TPU v7x, 32 devices: a whole 2x2x4 slice. The times are simulated.
32 devices in a mesh: groups: 2 (over y), tile: 4 (over z), sub: 2 (over x), rep: 2 (over core).
Axes of the slice: x: 2, y: 2, z: 4, core: 2. Of those that a mesh axis runs over, the one named last changes fastest.
Arguments:
- pressure: float32 [64, 32, 256], P(('groups', 'tile'), 'sub', 'rep'), parts along dimension 0, may hold values from -3 to 3
- previous_pressure: float32 [64, 32, 256], P(('groups', 'tile'), 'sub', 'rep'), parts along dimension 0, may hold values from -3 to 3
- courant_square: float32 [64, 32, 256], P(('groups', 'tile'), 'sub', 'rep'), parts along dimension 0, may hold values from 0.07 to 0.22
- node_area: float32 [12288], P(('groups', 'tile', 'sub', 'rep')), parts along dimension 0, may hold values from 0.25 to 4
- mode_shapes: bfloat16 [12288, 2048], P(('groups', 'tile', 'sub', 'rep')), parts along dimension 0, may hold values from -0.049804688 to 0.049804688
- frequency: float32 [4096], P('groups'), parts along dimension 0, may hold values from 0.4 to 1.3
- damping_ratio: float32 [4096], P('groups'), parts along dimension 0, may hold values from 0.02 to 0.4
- modal_start: float32 [2, 4096], P(None, 'groups'), parts along dimension 1, may hold values from -4 to 4
- slot_cell: int32 [8, 2, 2, 384], P(('groups', 'tile'), 'sub', 'rep'), parts along dimension 0, may hold values from 0 to 16383, as said below
- slot_owner: int32 [8, 2, 2, 384, 1], P(('groups', 'tile'), 'sub', 'rep'), parts along dimension 0, may hold values from 0 to 3; in each aligned block of 384 rows (0 to 383, 384 to 767, ..., all dimensions but the last counted through in order) at most 96 rows name the same one
- surface_count: int32 [4, 2, 4], P(('groups', 'sub'), 'rep', 'tile'), parts along dimension 0, may hold values from 1 to 384, 512 in all within a row
Outputs:
- final_pressure: float32 [64, 32, 256], P(('groups', 'tile'), 'sub', 'rep'), parts along dimension 0
- prior_pressure: float32 [64, 32, 256], P(('groups', 'tile'), 'sub', 'rep'), parts along dimension 0
- surface_accel: bfloat16 [8, 2, 2, 4, 384], P(('groups', 'tile'), 'sub', 'rep'), parts along dimension 0
- modal_state: float32 [2, 4096], P(None, ('groups', 'tile', 'sub', 'rep')), parts along dimension 1
There are 2 independent parts, one for each index of `groups`. A program takes and returns all parts, laid end to end along the dimension named above; each array names one. Nothing has to cross between parts.
Inputs may be any that keep to these rules, and one draw needn't show every extreme that they name: `slot_cell`: slot j of a block lies in the block's cells j * (42) to (j + 1) (42) - 1, so a block's slots name distinct cells. `slot_owner`: every owner index is named by exactly 96 of the 384 slots of each block (t, s, r). `surface_count`: for fixed s and r the counts over t sum to 128 times the number of tile indices, and one of them equals 384.
All inputs are finite; a program needn't handle non-finite values. No bound on the sum of `surface_count` on one device may be relied on, other than what follows from the above.
Results may differ from a plain program's by a relative error of at most 0.0098.
Values may be sent and summed in bfloat16 or wider, within the bound.
No kernel may reach another device: no remote copies, remote signals or barrier semaphores. Data moves between devices by JAX's collectives and lax.ppermute only.
A program may use at most 64 MiB of HBM per device.

v0:
```python
import jax
import jax.numpy as jnp
from jax import lax
from jax.sharding import PartitionSpec as P

STEPS = 4
HALO = 4


nonlinear = 0.03
viscous = 0.02


def extended(shard, sides, width):
    for axis, dim in sides:
        count, length = (lax.axis_size(axis), shard.shape[dim])
        up = [(i, (i + 1) % count) for i in range(count - 1)]
        down = [(j, i) for i, j in up]
        last = lax.slice_in_dim(shard, length - width, length, axis=dim)
        first = lax.slice_in_dim(shard, 0, width, axis=dim)
        before = lax.ppermute(last, axis, up)
        after = lax.ppermute(first, axis, down)
        shard = jnp.concatenate([before, shard, after], axis=dim)
    return shard


def laplace(padded):
    middle = padded[1:-1, 1:-1, 1:-1]
    summed = padded[2:, 1:-1, 1:-1] + padded[:-2, 1:-1, 1:-1]
    summed = summed + padded[1:-1, 2:, 1:-1] + padded[1:-1, :-2, 1:-1]
    summed = summed + padded[1:-1, 1:-1, 2:] + padded[1:-1, 1:-1, :-2]
    return summed - 6.0 * middle


def advance(wide_now, wide_before, coefficient):
    current = wide_now[1:-1, 1:-1, 1:-1]
    before = wide_before[1:-1, 1:-1, 1:-1]
    change = current - before
    driving = (
        coefficient * laplace(wide_now)
        + viscous * laplace(wide_now - wide_before)
        + 2.0 * nonlinear * change * change
    )
    return 2.0 * current - before + (1.0 + 2.0 * nonlinear * current) * driving


def routing(owners, live_count, tile_total):
    slot_total = owners.shape[0]
    bucket = slot_total // tile_total
    position = jnp.arange(slot_total, dtype=jnp.int32)
    is_live = position < live_count
    member = (
        (owners[:, None] == jnp.arange(tile_total, dtype=jnp.int32)[None, :]) & is_live[:, None]
    ).astype(jnp.float32)
    earlier = (position[None, :] < position[:, None]).astype(jnp.float32)
    before = jnp.dot(earlier, member, precision=lax.Precision.HIGHEST)
    bucket_rank = jnp.sum(before * member, axis=1).astype(jnp.int32)
    target = owners * bucket + bucket_rank
    return ((target[:, None] == position[None, :]) & is_live[:, None]).astype(jnp.bfloat16)


def oscillate(forces, frequency, damping_ratio, start_state):

    def advance_mode(carried, force_row):
        displace, velocity = carried
        acceleration = (
            force_row
            - 2.0 * damping_ratio * frequency * velocity
            - frequency * frequency * displace
        )
        velocity = velocity + acceleration
        displace = displace + velocity
        return ((displace, velocity), acceleration)

    (displace, velocity), modal_accel = lax.scan(
        advance_mode, (start_state[0], start_state[1]), forces
    )
    return (modal_accel, jnp.stack([displace, velocity]))


def trim_rim(array, depth):
    return array[
        depth : array.shape[0] - depth,
        depth : array.shape[1] - depth,
        depth : array.shape[2] - depth,
    ]


def inside_range(offset, length, axis_devices, margin):
    position = offset * length - margin + jnp.arange(length + 2 * margin, dtype=jnp.int32)
    return ((position >= 0) & (position < axis_devices * length)).astype(jnp.float32)


def body(
    pressure,
    previous_pressure,
    courant_square,
    node_area,
    mode_shapes,
    frequency,
    damping_ratio,
    modal_start,
    slot_cell,
    slot_owner,
    surface_count,
):
    tile_total = lax.axis_size("tile")
    extent_first, extent_second, extent_third = pressure.shape
    slot_total = slot_cell.shape[-1]
    bucket = slot_total // tile_total
    routing_matrix = routing(slot_owner.reshape(slot_total), surface_count.reshape(()), tile_total)
    cell_index = slot_cell.reshape(slot_total)
    fields = jnp.stack([pressure, previous_pressure])
    margin = HALO
    coef_wide = extended(courant_square, (("tile", 0), ("sub", 1), ("rep", 2)), margin)
    inside_first = inside_range(lax.axis_index("tile"), extent_first, lax.axis_size("tile"), margin)
    inside_second = inside_range(lax.axis_index("sub"), extent_second, lax.axis_size("sub"), margin)
    inside_third = inside_range(lax.axis_index("rep"), extent_third, lax.axis_size("rep"), margin)
    inside = (
        inside_first[:, None, None] * inside_second[None, :, None] * inside_third[None, None, :]
    )

    def deep_block(carried, unused):
        padded = extended(carried, (("tile", 1), ("sub", 2), ("rep", 3)), margin)
        recorded = []
        for layer_index in range(margin):
            edge_depth = layer_index + 1
            updated = advance(padded[0], padded[1], trim_rim(coef_wide, edge_depth)) * trim_rim(
                inside, edge_depth
            )
            interior = trim_rim(updated, margin - edge_depth)
            recorded.append(jnp.take(interior.reshape(-1), cell_index).astype(jnp.bfloat16))
            padded = jnp.stack([updated, trim_rim(padded[0], 1)])
        return (padded, jnp.stack(recorded))

    fields, history = lax.scan(deep_block, fields, None, length=STEPS // margin)
    history = history.reshape(STEPS, slot_total)
    final_field = fields[0]
    prior_field = fields[1]
    bucketed = jnp.dot(history, routing_matrix, preferred_element_type=jnp.float32).astype(
        jnp.bfloat16
    )
    bucketed = bucketed.reshape(STEPS, tile_total, bucket)
    arrived = lax.all_to_all(bucketed, "tile", split_axis=1, concat_axis=1, tiled=True)
    arrived_flat = arrived.reshape(arrived.shape[0], slot_total)
    weighted = (arrived_flat * node_area).astype(jnp.bfloat16)
    partial_forces = jnp.dot(weighted, mode_shapes, preferred_element_type=jnp.float32)
    device_total = lax.axis_size("tile") * lax.axis_size("sub") * lax.axis_size("rep")
    mode_count = mode_shapes.shape[1]
    mode_share = mode_count // device_total
    first_mode = lax.axis_index(("tile", "sub", "rep")) * mode_share
    forces = lax.psum_scatter(
        partial_forces, ("tile", "sub", "rep"), scatter_dimension=1, tiled=True
    )
    local_frequency = lax.dynamic_slice_in_dim(frequency, first_mode, mode_share, 0)
    local_damping = lax.dynamic_slice_in_dim(damping_ratio, first_mode, mode_share, 0)
    local_start = lax.dynamic_slice_in_dim(modal_start, first_mode, mode_share, 1)
    modal_accel, modal_state = oscillate(forces, local_frequency, local_damping, local_start)
    modal_rounded = modal_accel.astype(jnp.bfloat16)
    node_accel = lax.dot_general(
        lax.all_gather(modal_rounded, ("tile", "sub", "rep"), axis=1, tiled=True),
        mode_shapes,
        (((1,), (1,)), ((), ())),
        preferred_element_type=jnp.float32,
    )
    outgoing = node_accel.astype(jnp.bfloat16).reshape(STEPS, tile_total, bucket)
    returned = lax.all_to_all(outgoing, "tile", split_axis=1, concat_axis=1, tiled=True)
    surface = lax.dot_general(
        returned.reshape(STEPS, slot_total),
        routing_matrix,
        (((1,), (1,)), ((), ())),
        preferred_element_type=jnp.float32,
    )
    surface_accel = surface.astype(jnp.bfloat16).reshape(1, 1, 1, STEPS, slot_total)
    return (final_field, prior_field, surface_accel, modal_state)


def solution(mesh):
    in_specs = (
        P(("groups", "tile"), "sub", "rep"),
        P(("groups", "tile"), "sub", "rep"),
        P(("groups", "tile"), "sub", "rep"),
        P(("groups", "tile", "sub", "rep")),
        P(("groups", "tile", "sub", "rep"), None),
        P("groups"),
        P("groups"),
        P(None, "groups"),
        P(("groups", "tile"), "sub", "rep", None),
        P(("groups", "tile"), "sub", "rep", None, None),
        P(("groups", "sub"), "rep", "tile"),
    )
    out_specs = (
        P(("groups", "tile"), "sub", "rep"),
        P(("groups", "tile"), "sub", "rep"),
        P(("groups", "tile"), "sub", "rep", None, None),
        P(None, ("groups", "tile", "sub", "rep")),
    )
    return jax.shard_map(body, mesh=mesh, in_specs=in_specs, out_specs=out_specs, check_vma=False)
```

profile of v0, /device:TPU:0, one launch (start us, length us, event | category | flops | bytes accessed | tf_op | source)
XLA Modules:
  0.0 171.9 jit_solution(446253793117891918)
XLA Ops:
  8.1 4.9 %collective-permute-start = (f32[2,4,16,128]{3,2,1,0:T(8,128)S(1)}, f32[2,4,16,128]{3,2,1,0:T(8,128)S(1)}, u32[]{:S(2)}, u32[]{:S(2)}) collective-permute-start(f32[2,4,16,128]{3,2,1,0:T(8,128)S(1)} %get-tuple-element.142), channel_id=1, source_target_pairs={{0,4},{4,8},{8,12},{1,5},{5,9},{9,13},{2,6},{6,10},{10,14},{3,7},{... | collective-permute-start | bytes 196616 | tf_op jit(solution)/shard_map/while/body/eval_jaxpr/ppermute | solution.py:21
  13.1 1.3 collective-permute-start.1
  15.2 4.5 %collective-permute-start.6 = (f32[4,16,128]{2,1,0:T(8,128)S(1)}, f32[4,16,128]{2,1,0:T(8,128)S(1)}, u32[]{:S(2)}, u32[]{:S(2)}) collective-permute-start(f32[4,16,128]{2,1,0:T(8,128)S(1)} %get-tuple-element.145), channel_id=1, source_target_pairs={{0,4},{4,8},{8,12},{1,5},{5,9},{9,13},{2,6},{6,10},{10,14},{3,7},{... | collective-permute-start | bytes 98312 | tf_op jit(solution)/shard_map/ppermute | solution.py:21
  19.7 1.3 collective-permute-start.7
  25.5 3.4 %collective-permute-start.8 = (f32[16,4,128]{2,1,0:T(4,128)S(1)}, f32[16,4,128]{2,1,0:T(4,128)S(1)}, u32[]{:S(2)}, u32[]{:S(2)}) collective-permute-start(f32[16,4,128]{2,1,0:T(4,128)S(1)} %get-tuple-element.140), channel_id=1, source_target_pairs={{0,2},{1,3},{4,6},{5,7},{8,10},{9,11},{12,14},{13,15},{16,18},{17,... | collective-permute-start | bytes 98312 | tf_op jit(solution)/shard_map/ppermute | solution.py:21
  28.9 1.3 collective-permute-start.9
  31.1 4.5 %collective-permute-start.2 = (f32[2,16,4,128]{3,2,1,0:T(4,128)S(1)}, f32[2,16,4,128]{3,2,1,0:T(4,128)S(1)}, u32[]{:S(2)}, u32[]{:S(2)}) collective-permute-start(f32[2,16,4,128]{3,2,1,0:T(4,128)S(1)} %get-tuple-element.136), channel_id=1, source_target_pairs={{0,2},{1,3},{4,6},{5,7},{8,10},{9,11},{12,14},{13,15},{16,18},{17,... | collective-permute-start | bytes 196616 | tf_op jit(solution)/shard_map/while/body/eval_jaxpr/ppermute | solution.py:21
  35.7 1.3 collective-permute-start.3
  37.1 1.3 collective-permute-start.10
  39.8 2.1 %collective-permute-done.3 = f32[2,16,4,128]{3,2,1,0:T(4,128)S(1)} collective-permute-done((f32[2,16,4,128]{3,2,1,0:T(4,128)S(1)}, f32[2,16,4,128]{3,2,1,0:T(4,128)S(1)}, u32[]{:S(2)}, u32[]{:S(2)}) %collective-permute-start.3) | collective-permute-done | bytes 65568 | tf_op jit(solution)/shard_map/while/body/eval_jaxpr/ppermute | solution.py:22
  42.1 1.3 collective-permute-start.4
  45.0 2.0 %collective-permute-done.5 = f32[2,16,24,4]{3,2,1,0:T(8,128)S(1)} collective-permute-done((f32[2,16,24,4]{3,2,1,0:T(8,128)S(1)}, f32[2,16,24,4]{3,2,1,0:T(8,128)S(1)}, u32[]{:S(2)}, u32[]{:S(2)}) %collective-permute-start.5) | collective-permute-done | bytes 12320 | tf_op jit(solution)/shard_map/while/body/eval_jaxpr/ppermute | solution.py:22
  47.6 1.4 slice_subtract_fusion
  51.9 2.5 %gather_fusion.2 = bf16[384]{0:T(512)(128)(2,1)S(1)} fusion(f32[16384]{0:T(1024)S(1)} %bitcast.42, s32[1024]{0:T(1024)S(1)} %pad_clamp_fusion), kind=kCustom, calls=%fused_computation.2.clone | custom fusion | bytes 3072 | tf_op jit(solution)/shard_map/while/body/eval_jaxpr/jit(_take)/gather | solution.py:132
  54.4 2.5 %gather_fusion.3 = bf16[384]{0:T(512)(128)(2,1)S(1)} fusion(f32[16384]{0:T(1024)S(1)} %bitcast.41, s32[1024]{0:T(1024)S(1)} %pad_clamp_fusion), kind=kCustom, calls=%fused_computation.3.clone | custom fusion | bytes 3072 | tf_op jit(solution)/shard_map/while/body/eval_jaxpr/jit(_take)/gather | solution.py:132
  57.0 2.8 %gather_fusion.1 = bf16[384]{0:T(512)(128)(2,1)S(1)} fusion(bf16[16384]{0:T(1024)(128)(2,1)S(1)} %bitcast.40, s32[1024]{0:T(1024)S(1)} %pad_clamp_fusion), kind=kCustom, calls=%fused_computation.1.clone | custom fusion | bytes 3072 | tf_op jit(solution)/shard_map/while/body/eval_jaxpr/jit(_take)/gather | solution.py:132
  59.8 2.8 %gather_fusion = bf16[384]{0:T(512)(128)(2,1)S(1)} fusion(bf16[16384]{0:T(1024)(128)(2,1)S(1)} %bitcast.39, s32[1024]{0:T(1024)S(1)} %pad_clamp_fusion), kind=kCustom, calls=%fused_computation.clone | custom fusion | bytes 3072 | tf_op jit(solution)/shard_map/while/body/eval_jaxpr/jit(_take)/gather | solution.py:132
  63.7 5.5 %all-to-all-start = ((bf16[4,4,96]{2,0,1:T(4,128)(2,1)}), bf16[4,4,96]{2,0,1:T(4,128)(2,1)S(1)}, u32[]{:S(2)}, u32[]{:S(2)}) async-start(bf16[4,4,96]{2,0,1:T(4,128)(2,1)} %copy.17), calls=%async_computation | async-start | bytes 8192 | tf_op jit(solution)/shard_map/all_to_all | solution.py:144
  69.3 5.6 %all-to-all-done = bf16[4,4,96]{2,0,1:T(4,128)(2,1)S(1)} async-done(((bf16[4,4,96]{2,0,1:T(4,128)(2,1)}), bf16[4,4,96]{2,0,1:T(4,128)(2,1)S(1)}, u32[]{:S(2)}, u32[]{:S(2)}) %all-to-all-start) | async-done | bytes 3104 | tf_op jit(solution)/shard_map/all_to_all | solution.py:144
  74.9 1.7 %convolution_bitcast_fusion = f32[2048,4]{1,0:T(8,128)} fusion(bf16[384,2048]{1,0:T(8,128)(2,1)S(1)} %copy-done, f32[4,384]{1,0:T(4,128)S(1)} %reshape.139, f32[384]{0:T(512)S(1)} %copy-done.6), kind=kOutput, calls=%fused_computation.6 | convolution fusion | flops 6294528 | bytes 1613312
  78.2 55.2 %reduce-scatter.4.cloned.1.call-done = f32[128,4]{1,0:T(8,128)} async-done(((f32[2048,4]{1,0:T(8,128)}), f32[128,4]{1,0:T(8,128)}) %reduce-scatter.4.cloned.1.call-update) | async-done | bytes 2064
  134.6 19.5 %all_gather.3 = bf16[4,2048]{1,0:T(4,128)(2,1)S(1)} all-gather(bf16[4,128]{1,0:T(4,128)(2,1)S(1)} %get-tuple-element.98), channel_id=1, replica_groups=mesh['groups'=2,'tile'=4,'sub'=2,'rep'=2] {'tile','sub','rep'}, dimensions={1}, use_global_device_ids=true | all-gather | bytes 17408 | tf_op jit(solution)/shard_map/all_gather | solution.py:161
  155.3 3.2 %all-to-all-start.1 = ((bf16[4,4,96]{2,0,1:T(4,128)(2,1)}), bf16[4,4,96]{2,0,1:T(4,128)(2,1)S(1)}, u32[]{:S(2)}, u32[]{:S(2)}) async-start(bf16[4,4,96]{2,0,1:T(4,128)(2,1)} %copy.19), calls=%async_computation.1 | async-start | bytes 8192 | tf_op jit(solution)/shard_map/all_to_all | solution.py:167
  159.1 5.0 %all-to-all-done.1 = bf16[4,4,96]{2,0,1:T(4,128)(2,1)S(1)} async-done(((bf16[4,4,96]{2,0,1:T(4,128)(2,1)}), bf16[4,4,96]{2,0,1:T(4,128)(2,1)S(1)}, u32[]{:S(2)}, u32[]{:S(2)}) %all-to-all-start.1) | async-done | bytes 3104 | tf_op jit(solution)/shard_map/all_to_all | solution.py:167
  (93 shorter events, 19.9 us)
Async XLA Ops:
  7.2 67.8 %copy-start = (bf16[384,2048]{1,0:T(8,128)(2,1)S(1)}, bf16[384,2048]{1,0:T(8,128)(2,1)}, u32[]{:S(2)}) copy-start(bf16[384,2048]{1,0:T(8,128)(2,1)} %param.19) | copy-start | bytes 4718596
  7.2 34.6 %copy-start.3 = (f32[8,16,128]{2,1,0:T(8,128)S(1)}, f32[8,16,128]{2,1,0:T(8,128)}, u32[]{:S(2)}) copy-start(f32[8,16,128]{2,1,0:T(8,128)} %param.15) | copy-start | bytes 196612
  7.2 34.6 %copy-start.4 = (f32[8,16,128]{2,1,0:T(8,128)S(1)}, f32[8,16,128]{2,1,0:T(8,128)}, u32[]{:S(2)}) copy-start(f32[8,16,128]{2,1,0:T(8,128)} %param.16) | copy-start | bytes 196612
  8.1 22.1 %collective-permute-start = (f32[2,4,16,128]{3,2,1,0:T(8,128)S(1)}, f32[2,4,16,128]{3,2,1,0:T(8,128)S(1)}, u32[]{:S(2)}, u32[]{:S(2)}) collective-permute-start(f32[2,4,16,128]{3,2,1,0:T(8,128)S(1)} %get-tuple-element.142), channel_id=1, source_target_pairs={{0,4},{4,8},{8,12},{1,5},{5,9},{9,13},{2,6},{6,10},{10,14},{3,7},{... | collective-permute-start | bytes 196616 | tf_op jit(solution)/shard_map/while/body/eval_jaxpr/ppermute | solution.py:21
  13.1 17.2 %collective-permute-start.1 = (f32[2,4,16,128]{3,2,1,0:T(8,128)S(1)}, f32[2,4,16,128]{3,2,1,0:T(8,128)S(1)}, u32[]{:S(2)}, u32[]{:S(2)}) collective-permute-start(f32[2,4,16,128]{3,2,1,0:T(8,128)S(1)} %get-tuple-element.143), channel_id=1, source_target_pairs={{4,0},{8,4},{12,8},{5,1},{9,5},{13,9},{6,2},{10,6},{14,10},{7,3},{... | collective-permute-start | bytes 196616 | tf_op jit(solution)/shard_map/while/body/eval_jaxpr/ppermute | solution.py:22
  15.2 9.1 %collective-permute-start.6 = (f32[4,16,128]{2,1,0:T(8,128)S(1)}, f32[4,16,128]{2,1,0:T(8,128)S(1)}, u32[]{:S(2)}, u32[]{:S(2)}) collective-permute-start(f32[4,16,128]{2,1,0:T(8,128)S(1)} %get-tuple-element.145), channel_id=1, source_target_pairs={{0,4},{4,8},{8,12},{1,5},{5,9},{9,13},{2,6},{6,10},{10,14},{3,7},{... | collective-permute-start | bytes 98312 | tf_op jit(solution)/shard_map/ppermute | solution.py:21
  19.7 5.8 %collective-permute-start.7 = (f32[4,16,128]{2,1,0:T(8,128)S(1)}, f32[4,16,128]{2,1,0:T(8,128)S(1)}, u32[]{:S(2)}, u32[]{:S(2)}) collective-permute-start(f32[4,16,128]{2,1,0:T(8,128)S(1)} %get-tuple-element.144), channel_id=1, source_target_pairs={{4,0},{8,4},{12,8},{5,1},{9,5},{13,9},{6,2},{10,6},{14,10},{7,3},{... | collective-permute-start | bytes 98312 | tf_op jit(solution)/shard_map/ppermute | solution.py:22
  25.5 11.4 %collective-permute-start.8 = (f32[16,4,128]{2,1,0:T(4,128)S(1)}, f32[16,4,128]{2,1,0:T(4,128)S(1)}, u32[]{:S(2)}, u32[]{:S(2)}) collective-permute-start(f32[16,4,128]{2,1,0:T(4,128)S(1)} %get-tuple-element.140), channel_id=1, source_target_pairs={{0,2},{1,3},{4,6},{5,7},{8,10},{9,11},{12,14},{13,15},{16,18},{17,... | collective-permute-start | bytes 98312 | tf_op jit(solution)/shard_map/ppermute | solution.py:21
  28.9 8.0 %collective-permute-start.9 = (f32[16,4,128]{2,1,0:T(4,128)S(1)}, f32[16,4,128]{2,1,0:T(4,128)S(1)}, u32[]{:S(2)}, u32[]{:S(2)}) collective-permute-start(f32[16,4,128]{2,1,0:T(4,128)S(1)} %get-tuple-element.141), channel_id=1, source_target_pairs={{2,0},{3,1},{6,4},{7,5},{10,8},{11,9},{14,12},{15,13},{18,16},{19,... | collective-permute-start | bytes 98312 | tf_op jit(solution)/shard_map/ppermute | solution.py:22
  31.1 8.6 %collective-permute-start.2 = (f32[2,16,4,128]{3,2,1,0:T(4,128)S(1)}, f32[2,16,4,128]{3,2,1,0:T(4,128)S(1)}, u32[]{:S(2)}, u32[]{:S(2)}) collective-permute-start(f32[2,16,4,128]{3,2,1,0:T(4,128)S(1)} %get-tuple-element.136), channel_id=1, source_target_pairs={{0,2},{1,3},{4,6},{5,7},{8,10},{9,11},{12,14},{13,15},{16,18},{17,... | collective-permute-start | bytes 196616 | tf_op jit(solution)/shard_map/while/body/eval_jaxpr/ppermute | solution.py:21
  35.7 6.2 %collective-permute-start.3 = (f32[2,16,4,128]{3,2,1,0:T(4,128)S(1)}, f32[2,16,4,128]{3,2,1,0:T(4,128)S(1)}, u32[]{:S(2)}, u32[]{:S(2)}) collective-permute-start(f32[2,16,4,128]{3,2,1,0:T(4,128)S(1)} %get-tuple-element.137), channel_id=1, source_target_pairs={{2,0},{3,1},{6,4},{7,5},{10,8},{11,9},{14,12},{15,13},{18,16},{19,... | collective-permute-start | bytes 196616 | tf_op jit(solution)/shard_map/while/body/eval_jaxpr/ppermute | solution.py:22
  37.1 7.6 %collective-permute-start.10 = (f32[16,24,4]{2,1,0:T(8,128)S(1)}, f32[16,24,4]{2,1,0:T(8,128)S(1)}, u32[]{:S(2)}, u32[]{:S(2)}) collective-permute-start(f32[16,24,4]{2,1,0:T(8,128)S(1)} %get-tuple-element.138), channel_id=1, source_target_pairs={{0,1},{2,3},{4,5},{6,7},{8,9},{10,11},{12,13},{14,15},{16,17},{18,... | collective-permute-start | bytes 18440 | tf_op jit(solution)/shard_map/ppermute | solution.py:21
  38.4 6.3 %collective-permute-start.11 = (f32[16,24,4]{2,1,0:T(8,128)S(1)}, f32[16,24,4]{2,1,0:T(8,128)S(1)}, u32[]{:S(2)}, u32[]{:S(2)}) collective-permute-start(f32[16,24,4]{2,1,0:T(8,128)S(1)} %get-tuple-element.139), channel_id=1, source_target_pairs={{1,0},{3,2},{5,4},{7,6},{9,8},{11,10},{13,12},{15,14},{17,16},{19,... | collective-permute-start | bytes 18440 | tf_op jit(solution)/shard_map/ppermute | solution.py:22
  42.1 2.9 %collective-permute-start.4 = (f32[2,16,24,4]{3,2,1,0:T(8,128)S(1)}, f32[2,16,24,4]{3,2,1,0:T(8,128)S(1)}, u32[]{:S(2)}, u32[]{:S(2)}) collective-permute-start(f32[2,16,24,4]{3,2,1,0:T(8,128)S(1)} %get-tuple-element.134), channel_id=1, source_target_pairs={{0,1},{2,3},{4,5},{6,7},{8,9},{10,11},{12,13},{14,15},{16,17},{18,... | collective-permute-start | bytes 36872 | tf_op jit(solution)/shard_map/while/body/eval_jaxpr/ppermute | solution.py:21
  43.4 3.6 %collective-permute-start.5 = (f32[2,16,24,4]{3,2,1,0:T(8,128)S(1)}, f32[2,16,24,4]{3,2,1,0:T(8,128)S(1)}, u32[]{:S(2)}, u32[]{:S(2)}) collective-permute-start(f32[2,16,24,4]{3,2,1,0:T(8,128)S(1)} %get-tuple-element.135), channel_id=1, source_target_pairs={{1,0},{3,2},{5,4},{7,6},{9,8},{11,10},{13,12},{15,14},{17,16},{19,... | collective-permute-start | bytes 36872 | tf_op jit(solution)/shard_map/while/body/eval_jaxpr/ppermute | solution.py:22
  50.5 1.1 copy-start.5
  51.9 7.9 %copy-start.1 = (f32[8,16,128]{2,1,0:T(8,128)}, f32[8,16,128]{2,1,0:T(8,128)S(1)}, u32[]{:S(2)}) copy-start(f32[8,16,128]{2,1,0:T(8,128)S(1)} %get-tuple-element.124) | copy-start | bytes 196612
  51.9 7.9 %copy-start.2 = (f32[8,16,128]{2,1,0:T(8,128)}, f32[8,16,128]{2,1,0:T(8,128)S(1)}, u32[]{:S(2)}) copy-start(f32[8,16,128]{2,1,0:T(8,128)S(1)} %get-tuple-element.125) | copy-start | bytes 196612
  54.4 20.5 %copy-start.6 = (f32[384]{0:T(512)S(1)}, f32[384]{0:T(512)}, u32[]{:S(2)}) copy-start(f32[384]{0:T(512)} %param.18) | copy-start | bytes 4612
  63.7 11.1 %all-to-all-start = ((bf16[4,4,96]{2,0,1:T(4,128)(2,1)}), bf16[4,4,96]{2,0,1:T(4,128)(2,1)S(1)}, u32[]{:S(2)}, u32[]{:S(2)}) async-start(bf16[4,4,96]{2,0,1:T(4,128)(2,1)} %copy.17), calls=%async_computation | async-start | bytes 8192 | tf_op jit(solution)/shard_map/all_to_all | solution.py:144
  69.3 64.2 %reduce-scatter.4.cloned.1.call-start = ((), (), s32[]{:S(2)}) async-start(), calls=%async_computation.3 | async-start | bytes 1114112
  155.3 8.8 %all-to-all-start.1 = ((bf16[4,4,96]{2,0,1:T(4,128)(2,1)}), bf16[4,4,96]{2,0,1:T(4,128)(2,1)S(1)}, u32[]{:S(2)}, u32[]{:S(2)}) async-start(bf16[4,4,96]{2,0,1:T(4,128)(2,1)} %copy.19), calls=%async_computation.1 | async-start | bytes 8192 | tf_op jit(solution)/shard_map/all_to_all | solution.py:167
Sparse Core Ops, SparseCore 0:
  76.8 56.5 reduce-scatter.3
where the time goes:
time: 173 us; the launch traced here: 172 us
  waiting for transfers between devices  70.2 us (41%)
  starting transfers between devices  36.6 us (21%)
  blocking collectives  19.5 us (11%)
  local copies, waits for them, and re-layouts  17 us (10%)
  between operations  15.2 us (9%)
  other arithmetic  9.79 us (6%)
  matrix products  3.65 us (2%)
    unnamed x2, waiting for transfers between devices  55.2 us
    ppermute x6, starting transfers between devices, extended(): before = lax.ppermute(last, axis, up)  20 us
    all_gather x1, blocking collectives, body(): lax.all_gather(modal_rounded, ('tile', 'sub', 'rep'), axis=1, tiled=True)  19.5 us
    gather x4, local copies, waits for them, and re-layouts, deep_block(): jnp.take(interior.reshape(-1), cell_index).astype(jnp.bfloat16)  10.7 us
    ppermute x6, starting transfers between devices, extended(): after = lax.ppermute(first, axis, down)  7.75 us
    all_to_all x1, waiting for transfers between devices, body(): lax.all_to_all(bucketed, 'tile', split_axis=1, concat_axis=1, tiled=True)  5.57 us
    all_to_all x1, starting transfers between devices, body(): lax.all_to_all(bucketed, 'tile', split_axis=1, concat_axis=1, tiled=True)  5.54 us
    all_to_all x1, waiting for transfers between devices, body(): lax.all_to_all(outgoing, 'tile', split_axis=1, concat_axis=1, tiled=True)  4.97 us
  transfers between devices with their start and end apart: 15, of which 6 were waited for; matrix products, arithmetic and copies ran while one was open for 5% of the time, Pallas kernels for 0%

commit v1 on v0

v1 whole, which is shorter than its diff:
```python
import functools

import jax
import jax.numpy as jnp
from jax import lax
from jax.experimental import pallas as pl
from jax.experimental.pallas import tpu as pltpu
from jax.sharding import PartitionSpec as P

STEPS = 4
FIELDS = 3
SUBLANES = 8

nonlinear = 0.03
viscous = 0.02

f32 = jnp.float32
bf16 = jnp.bfloat16
VMEM = pl.BlockSpec(memory_space=pltpu.VMEM)
SMEM = pl.BlockSpec(memory_space=pltpu.SMEM)


def shift(count, by):
    return [(i, (i + by) % count) for i in range(count)]


def line(count, by):
    return [(i, i + by) for i in range(count) if 0 <= i + by < count]


def iota(shape, dim):
    return lax.broadcasted_iota(jnp.int32, shape, dim)


def dot(a, b, contract):
    return lax.dot_general(a, b, (((contract[0],), (contract[1],)), ((), ())), preferred_element_type=f32)


def call(kernel, out_shape, inputs, scratch=(), specs=None, flops=1_000_000):
    return pl.pallas_call(
        kernel,
        out_shape=out_shape,
        in_specs=specs or [VMEM] * len(inputs),
        out_specs=jax.tree.map(lambda _: VMEM, out_shape),
        scratch_shapes=list(scratch),
        cost_estimate=pl.CostEstimate(flops=flops, bytes_accessed=1_000_000, transcendentals=0),
        compiler_params=pltpu.CompilerParams(vmem_limit_bytes=32 * 1024 * 1024),
    )(*inputs)


def shape_of(dims, dtype):
    return jax.ShapeDtypeStruct(dims, dtype)


def both_ways(axis, ahead, behind):
    count = lax.axis_size(axis)
    after = lax.ppermute(behind, axis, line(count, -1))
    before = lax.ppermute(ahead, axis, line(count, 1))
    return after, before


def route_kernel(buckets, owner_ref, cell_ref, count_ref, route_ref, place_ref, *, lanes, rows):
    slots = owner_ref.shape[1]
    bucket = slots // buckets
    me = lax.axis_index("tile")
    owner = owner_ref[...]
    live = iota((1, slots), 1) < count_ref[0, 0]
    held = -(-buckets // SUBLANES) * SUBLANES
    member = jnp.where((iota((held, slots), 0) == owner) & live, 1.0, 0.0)
    earlier = jnp.where(iota((slots, slots), 0) < iota((slots, slots), 1), 1.0, 0.0).astype(bf16)
    before = dot(member.astype(bf16), earlier, (1, 0))
    rank = jnp.sum(before * member, axis=0, keepdims=True).astype(jnp.int32)
    away = owner - me
    away = jnp.where(away < 0, away + buckets, away)
    target = jnp.where(live, away * bucket + rank, -1)
    route = jnp.where(iota((slots, slots), 0) == target, 1.0, 0.0).astype(bf16)
    route_ref[...] = route
    cell = cell_ref[...]
    row = jnp.where(iota((rows, slots), 0) == cell // lanes, 1.0, 0.0)
    lane = jnp.where(iota((lanes, slots), 0) == cell % lanes, 1.0, 0.0)
    place_ref[:, :rows] = dot(route, row.astype(bf16), (1, 1)).astype(bf16)
    place_ref[:, rows:] = dot(route, lane.astype(bf16), (1, 1)).astype(bf16)


def pack_sub_kernel(ends, p_ref, q_ref, c_ref, *outs):
    layers, rows, lanes = p_ref.shape
    low = iota((SUBLANES, lanes), 0) < STEPS
    for at, ref in enumerate((p_ref, q_ref, c_ref)):
        for pair in range(layers // 2):
            tiles = []
            for layer in (2 * pair, 2 * pair + 1):
                last = pltpu.roll(ref[layer, rows - SUBLANES :, :], STEPS, 0)
                first = ref[layer, :SUBLANES, :]
                tiles.append((last, first))
            picked = [jnp.where(low, a, pltpu.roll(b, STEPS, 0)) for a, b in zip(*tiles)]
            if ends == 1:
                picked = [jnp.where(lax.axis_index("sub") == 0, picked[0], picked[1])]
            for out, value in zip(outs, picked):
                out[at, pair * SUBLANES : (pair + 1) * SUBLANES, :] = value.astype(bf16)


def side_rows(at, layer, after_ref, before_ref):
    start = layer // 2 * SUBLANES
    after = after_ref[at, start : start + SUBLANES, :].astype(f32)
    before = before_ref[at, start : start + SUBLANES, :].astype(f32)
    if layer % 2 == 0:
        before = pltpu.roll(before, STEPS, 0)
    else:
        after = pltpu.roll(after, STEPS, 0)
    me, count = lax.axis_index("sub"), lax.axis_size("sub")
    low = iota(after.shape, 0) < STEPS
    keep_after = jnp.where(me < count - 1, 1.0, 0.0)
    keep_before = jnp.where(me > 0, 1.0, 0.0)
    return jnp.where(low, after * keep_after, before * keep_before)


def pack_tile_kernel(p_ref, q_ref, c_ref, after_ref, before_ref, ahead_ref, behind_ref):
    layers = p_ref.shape[0]
    for out, base in ((ahead_ref, layers - STEPS), (behind_ref, 0)):
        for at, ref in enumerate((p_ref, q_ref, c_ref)):
            for k in range(STEPS):
                out[at * STEPS + k] = ref[base + k].astype(bf16)
            for k in range(0, STEPS, 2):
                beside = [side_rows(at, base + k + i, after_ref, before_ref) for i in range(2)]
                out[FIELDS * STEPS + (at * STEPS + k) // 2] = jnp.concatenate(beside, 0).astype(bf16)


def end_lanes(lanes):
    row = iota((2 * STEPS, lanes), 0)
    wanted = jnp.where(row < STEPS, row, lanes - 2 * STEPS + row)
    return jnp.where(iota((2 * STEPS, lanes), 1) == wanted, 1.0, 0.0).astype(bf16)


def pack_rep_kernel(p_ref, q_ref, c_ref, sub_after, sub_before, tile_after, tile_before, out_ref, wide):
    layers, rows, lanes = p_ref.shape
    beside = 2 * STEPS
    total = layers + 2 * STEPS
    picks = end_lanes(lanes)
    for at, ref in enumerate((p_ref, q_ref, c_ref)):
        for side, base in ((tile_before, 0), (tile_after, STEPS + layers)):
            wide[base * rows : (base + STEPS) * rows, :] = side[at * STEPS : (at + 1) * STEPS].reshape(STEPS * rows, lanes)
            start = total * rows + base * beside
            packed = FIELDS * STEPS + at * STEPS // 2
            wide[start : start + STEPS * beside, :] = side[packed : packed + STEPS // 2].reshape(STEPS * beside, lanes)
        for k in range(layers):
            wide[(STEPS + k) * rows : (STEPS + k + 1) * rows, :] = ref[k].astype(bf16)
        for k in range(0, layers, 2):
            start = total * rows + (STEPS + k) * beside
            pair = [side_rows(at, k + i, sub_after, sub_before) for i in range(2)]
            wide[start : start + 2 * beside, :] = jnp.concatenate(pair, 0).astype(bf16)
        width = wide.shape[0]
        out_ref[:, at * width : (at + 1) * width] = dot(picks, wide[...], (1, 1)).astype(bf16)


def window_kernel(
    p_ref, q_ref, c_ref, sub_after, sub_before, tile_after, tile_before, rep_after, rep_before, place_ref,
    final_ref, prior_ref, *rest,
):
    *sends, now, ago, coef, lapped, seen = rest
    layers, rows, lanes = p_ref.shape
    beside = 2 * STEPS
    total = layers + 2 * STEPS
    wide_rows, wide_lanes = rows + beside, 2 * lanes
    tile, tiles = lax.axis_index("tile"), lax.axis_size("tile")
    sub, subs = lax.axis_index("sub"), lax.axis_size("sub")
    rep, reps = lax.axis_index("rep"), lax.axis_size("rep")

    picks = end_lanes(lanes)
    width = total * wide_rows
    end = iota((2 * STEPS, width), 0) < STEPS
    keep_after = jnp.where(rep < reps - 1, 1.0, 0.0)
    keep_before = jnp.where(rep > 0, 1.0, 0.0)
    for at, (ref, out) in enumerate(((p_ref, now), (q_ref, ago), (c_ref, coef))):
        for k in range(layers):
            out[STEPS + k, :rows, :lanes] = ref[k]
            out[STEPS + k, rows:, :lanes] = side_rows(at, k, sub_after, sub_before)
        for side, base in ((tile_before, 0), (tile_after, STEPS + layers)):
            for k in range(STEPS):
                out[base + k, :rows, :lanes] = side[at * STEPS + k].astype(f32)
                pair = side[FIELDS * STEPS + (at * STEPS + k) // 2].astype(f32)
                out[base + k, rows:, :lanes] = pair[k % 2 * beside : (k % 2 + 1) * beside]
        after = rep_after[:, at * width : (at + 1) * width].astype(f32) * keep_after
        before = rep_before[:, at * width : (at + 1) * width].astype(f32) * keep_before
        strip = dot(jnp.where(end, after, before).astype(bf16), picks, (0, 0))
        for k in range(total):
            out[k, :rows, lanes:] = strip[k * rows : (k + 1) * rows]
            out[k, rows:, lanes:] = strip[total * rows + k * beside : total * rows + (k + 1) * beside]

    row = iota((wide_rows, wide_lanes), 0)
    lane = iota((wide_rows, wide_lanes), 1)
    inside = (row < rows) | ((row < rows + STEPS) & (sub < subs - 1)) | ((row >= rows + STEPS) & (sub > 0))
    inside &= (lane < lanes) | ((lane < lanes + STEPS) & (rep < reps - 1)) | ((lane >= wide_lanes - STEPS) & (rep > 0))
    inside = jnp.where(inside, 1.0, 0.0)
    inside_low = inside * jnp.where(tile > 0, 1.0, 0.0)
    inside_high = inside * jnp.where(tile < tiles - 1, 1.0, 0.0)

    def laplace(below, here, above):
        summed = below + above
        summed = summed + pltpu.roll(here, 1, 0) + pltpu.roll(here, wide_rows - 1, 0)
        summed = summed + pltpu.roll(here, 1, 1) + pltpu.roll(here, wide_lanes - 1, 1)
        return summed - 6.0 * here

    for k in range(1, total - 1):
        lapped[k] = laplace(ago[k - 1], ago[k], ago[k + 1])
    for step in range(STEPS):
        below = now[step]
        here = now[step + 1]
        for k in range(step + 1, total - step - 1):
            above = now[k + 1]
            before = ago[k]
            lap = laplace(below, here, above)
            change = here - before
            driving = coef[k] * lap + viscous * (lap - lapped[k]) + 2.0 * nonlinear * change * change
            updated = 2.0 * here - before + (1.0 + 2.0 * nonlinear * here) * driving
            mask = inside_low if k < STEPS else inside_high if k >= STEPS + layers else inside
            updated = updated * mask
            now[k] = updated
            ago[k] = here
            lapped[k] = lap
            own = k - STEPS
            if 0 <= own < layers:
                core = updated[:rows, :lanes]
                seen[own * rows : (own + 1) * rows, step * lanes : (step + 1) * lanes] = core.astype(bf16)
                if step == STEPS - 1:
                    final_ref[own] = core
                if step == STEPS - 2:
                    prior_ref[own] = core
            below, here = here, above

    cells = layers * rows
    steps_at = iota((SUBLANES, STEPS * lanes), 1) // lanes == iota((SUBLANES, STEPS * lanes), 0)
    steps_at = jnp.where(steps_at, 1.0, 0.0).astype(bf16)
    size = place_ref.shape[0] // len(sends)
    for at, send in enumerate(sends):
        part = place_ref[at * size : (at + 1) * size, :]
        found = dot(part[:, :cells], seen[...], (1, 0))
        lane_of = part[:, cells:].astype(f32)
        found = jnp.concatenate([found[:, i * lanes : (i + 1) * lanes] * lane_of for i in range(STEPS)], 1)
        send[...] = dot(steps_at, found.astype(bf16), (1, 1))[:STEPS].astype(bf16)


def spread(at, size, total, bucket):
    wanted = iota((size, 1), 0) + at * size + lax.axis_index("tile") * bucket
    wanted = jnp.where(wanted >= total, wanted - total, wanted)
    return jnp.where(iota((size, total), 1) == wanted, 1.0, 0.0).astype(bf16)


def project_kernel(buckets, area_ref, shapes_ref, *rest):
    *parts, out_ref = rest
    total = area_ref.shape[1]
    size = parts[0].shape[1]
    loads = 0.0
    for at, part in enumerate(parts):
        loads = loads + dot(part[...], spread(at, size, total, total // buckets), (1, 0))
    weighted = (loads * area_ref[...]).astype(bf16)
    out_ref[...] = dot(weighted, shapes_ref[...], (1, 0))


def respond_kernel(buckets, addends, freq_ref, damp_ref, start_ref, shapes_ref, *rest):
    forces_in, rest = rest[:addends], rest[addends:]
    state_ref, *sends, accel = rest
    forces = forces_in[0][...]
    for ref in forces_in[1:]:
        forces = forces + ref[...]
    frequency, damping = freq_ref[...], damp_ref[...]
    drag, stiffness = 2.0 * damping * frequency, frequency * frequency
    displace, velocity = start_ref[0:1, :], start_ref[1:2, :]
    accel[...] = jnp.zeros_like(accel)
    for step in range(STEPS):
        acceleration = forces[step : step + 1, :] - drag * velocity - stiffness * displace
        velocity = velocity + acceleration
        displace = displace + velocity
        accel[step : step + 1, :] = acceleration
    state_ref[0:1, :] = displace
    state_ref[1:2, :] = velocity
    node = dot(accel[...].astype(bf16), shapes_ref[...], (1, 1)).astype(bf16)
    total = node.shape[1]
    size = total // len(sends)
    for at, send in enumerate(sends):
        send[...] = dot(node, spread(at, size, total, total // buckets), (1, 1))[:STEPS].astype(bf16)


def return_kernel(route_ref, *rest):
    *parts, out_ref = rest
    size = parts[0].shape[1]
    surface = 0.0
    for at, part in enumerate(parts):
        surface = surface + dot(part[...], route_ref[at * size : (at + 1) * size, :], (1, 0))
    out_ref[...] = surface.astype(bf16)


def exchange(parts, buckets):
    if len(parts) == buckets:
        return [parts[0]] + [lax.ppermute(parts[-k], "tile", shift(buckets, -k)) for k in range(1, buckets)]
    me = lax.axis_index("tile")
    (whole,) = parts
    steps, total = whole.shape
    stacked = whole.reshape(steps, buckets, total // buckets).transpose(1, 0, 2)
    stacked = lax.all_to_all(jnp.roll(stacked, me, 0), "tile", 0, 0, tiled=True)
    return [jnp.roll(stacked, -me, 0).transpose(1, 0, 2).reshape(steps, total)]


def body(
    pressure,
    previous_pressure,
    courant_square,
    node_area,
    mode_shapes,
    frequency,
    damping_ratio,
    modal_start,
    slot_cell,
    slot_owner,
    surface_count,
):
    buckets, subs, reps = (lax.axis_size(axis) for axis in ("tile", "sub", "rep"))
    layers, rows, lanes = pressure.shape
    slots = slot_cell.shape[-1]
    modes = mode_shapes.shape[1]
    bucket = slots // buckets
    parts = buckets if buckets <= 4 and bucket % 16 == 0 else 1
    fields = (pressure, previous_pressure, courant_square)
    total = layers + 2 * STEPS
    wide_rows = rows + 2 * STEPS

    route, place = call(
        functools.partial(route_kernel, buckets, lanes=lanes, rows=layers * rows),
        (shape_of((slots, slots), bf16), shape_of((slots, layers * rows + lanes), bf16)),
        (slot_owner.reshape(1, slots), slot_cell.reshape(1, slots), surface_count.reshape(1, 1)),
        specs=[VMEM, VMEM, SMEM],
    )

    ends = 1 if subs == 2 else 2
    slab = shape_of((FIELDS, layers * STEPS, lanes), bf16)
    packed = call(functools.partial(pack_sub_kernel, ends), (slab,) * ends, fields)
    if subs == 2:
        sub_halo = (lax.ppermute(packed[0], "sub", shift(2, 1)),) * 2
    else:
        sub_halo = both_ways("sub", *packed)
    slab = shape_of((FIELDS * STEPS * 3 // 2, rows, lanes), bf16)
    packed = call(pack_tile_kernel, (slab, slab), (*fields, *sub_halo))
    tile_halo = both_ways("tile", *packed)
    packed = call(
        pack_rep_kernel,
        shape_of((2 * STEPS, FIELDS * total * wide_rows), bf16),
        (*fields, *sub_halo, *tile_halo),
        scratch=[pltpu.VMEM((total * wide_rows, lanes), bf16)],
    )
    if reps == 2:
        rep_halo = (lax.ppermute(packed, "rep", shift(2, 1)),) * 2
    else:
        rep_halo = both_ways("rep", packed, packed)

    wide = pltpu.VMEM((total, wide_rows, 2 * lanes), f32)
    part = shape_of((STEPS, slots // parts), bf16)
    block = shape_of(pressure.shape, f32)
    final_field, prior_field, *sends = call(
        window_kernel,
        (block, block) + (part,) * parts,
        (*fields, *sub_halo, *tile_halo, *rep_halo, place),
        scratch=[wide] * 4 + [pltpu.VMEM((layers * rows, STEPS * lanes), bf16)],
        flops=50_000_000,
    )

    forces = call(
        functools.partial(project_kernel, buckets),
        shape_of((STEPS, modes), f32),
        (node_area.reshape(1, slots), mode_shapes, *exchange(sends, buckets)),
    )
    addends = [forces]
    for axis in ("rep", "sub", "tile"):
        count = lax.axis_size(axis)
        forces = functools.reduce(jnp.add, addends)
        if count <= 4:
            addends = [forces] + [lax.ppermute(forces, axis, shift(count, k)) for k in range(1, count)]
        else:
            addends = [lax.psum(forces, axis)]

    state, *sends = call(
        functools.partial(respond_kernel, buckets, len(addends)),
        (shape_of((2, modes), f32),) + (part,) * parts,
        (frequency.reshape(1, modes), damping_ratio.reshape(1, modes), modal_start, mode_shapes, *addends),
        scratch=[pltpu.VMEM((SUBLANES, modes), f32)],
    )
    share = modes // (buckets * subs * reps)
    modal_state = lax.dynamic_slice_in_dim(state, lax.axis_index(("tile", "sub", "rep")) * share, share, 1)
    surface = call(return_kernel, shape_of((STEPS, slots), bf16), (route, *exchange(sends, buckets)))
    return (final_field, prior_field, surface.reshape(1, 1, 1, STEPS, slots), modal_state)


def solution(mesh):
    in_specs = (
        P(("groups", "tile"), "sub", "rep"),
        P(("groups", "tile"), "sub", "rep"),
        P(("groups", "tile"), "sub", "rep"),
        P(("groups", "tile", "sub", "rep")),
        P(("groups", "tile", "sub", "rep"), None),
        P("groups"),
        P("groups"),
        P(None, "groups"),
        P(("groups", "tile"), "sub", "rep", None),
        P(("groups", "tile"), "sub", "rep", None, None),
        P(("groups", "sub"), "rep", "tile"),
    )
    out_specs = (
        P(("groups", "tile"), "sub", "rep"),
        P(("groups", "tile"), "sub", "rep"),
        P(("groups", "tile"), "sub", "rep", None, None),
        P(None, ("groups", "tile", "sub", "rep")),
    )
    return jax.shard_map(body, mesh=mesh, in_specs=in_specs, out_specs=out_specs, check_vma=False)
```

time: 173 us -> 56.7 us (0.33)
  waiting for transfers between devices: 70.2 us -> 19.2 us
  blocking collectives: 19.5 us -> 0 us
  starting transfers between devices: 36.6 us -> 21.7 us
  between operations: 15.2 us -> 1.41 us
  other arithmetic: 9.79 us -> 0.02 us
  local copies, waits for them, and re-layouts: 17 us -> 9.06 us
  Pallas kernels: 0 us -> 4.77 us
  matrix products: 3.65 us -> 0 us
    unnamed x2 -> x0, waiting for transfers between devices: 55.2 us -> none
    all_gather x1 -> x0, blocking collectives: 19.5 us -> none  [body(): lax.all_gather(modal_rounded, ('tile', 'sub', 'rep'), axis=1, tiled=True)]
    ppermute x12 -> x15, waiting for transfers between devices: 4.48 us -> 19.2 us  [the longest x5 7.99 us: body(): lax.ppermute(forces, axis, shift(count, k))]
    gather x4 -> x0, local copies, waits for them, and re-layouts: 10.7 us -> none  [deep_block(): jnp.take(interior.reshape(-1), cell_index).astype(jnp.bfloat16)]
    all_to_all x2 -> x0, waiting for transfers between devices: 10.5 us -> none  [the longest x1 5.57 us: body(): lax.all_to_all(bucketed, 'tile', split_axis=1, concat_axis=1, tiled=True)]
    all_to_all x2 -> x0, starting transfers between devices: 8.79 us -> none  [the longest x1 5.54 us: body(): lax.all_to_all(bucketed, 'tile', split_axis=1, concat_axis=1, tiled=True)]
    ppermute x12 -> x15, starting transfers between devices: 27.8 us -> 21.7 us  [the longest x6 7.91 us: exchange(): lax.ppermute(parts[-k], 'tile', shift(buckets, -k))]
    unnamed x17 -> x26, local copies, waits for them, and re-layouts: 1.79 us -> 7.81 us
  transfers between devices with their start and end apart: 15 -> 15, of which waited for: 6 -> 13; matrix products, arithmetic and copies ran while one was open for 5% -> 2% of each run, Pallas kernels for 0% -> 1%
where the time goes in v1:
time: 56.7 us; the launch traced here: 56.2 us
  starting transfers between devices  21.7 us (38%)
  waiting for transfers between devices  19.2 us (34%)
  local copies, waits for them, and re-layouts  9.06 us (16%)
  Pallas kernels  4.77 us (8%)
  between operations  1.41 us (2%)
    ppermute x5, waiting for transfers between devices, body(): lax.ppermute(forces, axis, shift(count, k))  7.99 us
    ppermute x6, starting transfers between devices, exchange(): lax.ppermute(parts[-k], 'tile', shift(buckets, -k))  7.91 us
    unnamed x26, local copies, waits for them, and re-layouts  7.81 us
    ppermute x6, waiting for transfers between devices, exchange(): lax.ppermute(parts[-k], 'tile', shift(buckets, -k))  7.47 us
    ppermute x5, starting transfers between devices, body(): lax.ppermute(forces, axis, shift(count, k))  4.77 us
    pallas_call x8, Pallas kernels, call(): pl.pallas_call(kernel, out_shape=out_shape, in_specs=specs or [VMEM] * le...  4.77 us
    ppermute x1, starting transfers between devices, both_ways(): before = lax.ppermute(ahead, axis, line(count, 1))  4.64 us
    ppermute x1, starting transfers between devices, body(): sub_halo = (lax.ppermute(packed[0], 'sub', shift(2, 1)),) * 2  3 us
  transfers between devices with their start and end apart: 15, of which 13 were waited for; matrix products, arithmetic and copies ran while one was open for 2% of the time, Pallas kernels for 1%

profile of v1, /device:TPU:0, one launch (start us, length us, event | category | flops | bytes accessed | tf_op | source)
XLA Modules:
  0.0 56.2 jit_solution(5803902621322215664)
XLA Ops:
  1.5 0.8 %copy-done.4 = f32[8,16,128]{2,1,0:T(8,128)S(1)} copy-done((f32[8,16,128]{2,1,0:T(8,128)S(1)}, f32[8,16,128]{2,1,0:T(8,128)}, u32[]{:S(2)}) %copy-start.4) | copy-done | bytes 65560
  3.2 3.0 %collective-permute-start = (bf16[3,32,128]{2,1,0:T(8,128)(2,1)S(1)}, bf16[3,32,128]{2,1,0:T(8,128)(2,1)S(1)}, u32[]{:S(2)}, u32[]{:S(2)}) collective-permute-start(bf16[3,32,128]{2,1,0:T(8,128)(2,1)S(1)} %shard_map.138), channel_id=1, source_target_pairs={{0,2},{2,0},{1,3},{3,1},{4,6},{6,4},{5,7},{7,5},{8,10},{10,8},{9,1... | collective-permute-start | bytes 73736 | tf_op jit(solution)/shard_map/ppermute | solution.py:337
  6.2 1.8 %collective-permute-done.after_ref.before_ref.sub_after.sub_before = bf16[3,32,128]{2,1,0:T(8,128)(2,1)S(1)} collective-permute-done((bf16[3,32,128]{2,1,0:T(8,128)(2,1)S(1)}, bf16[3,32,128]{2,1,0:T(8,128)(2,1)S(1)}, u32[]{:S(2)}, u32[]{:S(2)}) %collective-permute-start) | collective-permute-done | bytes 24608 | tf_op jit(solution)/shard_map/ppermute | solution.py:337
  8.1 1.3 %collective-permute-start.1 = (bf16[18,16,128]{2,1,0:T(8,128)(2,1)S(1)}, bf16[18,16,128]{2,1,0:T(8,128)(2,1)S(1)}, u32[]{:S(2)}, u32[]{:S(2)}) collective-permute-start(bf16[18,16,128]{2,1,0:T(8,128)(2,1)S(1)} %get-tuple-element.19), channel_id=1, source_target_pairs={{4,0},{8,4},{12,8},{5,1},{9,5},{13,9},{6,2},{10,6},{14,10},{7,3},{... | collective-permute-start | bytes 221192 | tf_op jit(solution)/shard_map/ppermute | solution.py:57
  9.4 4.6 %collective-permute-start.2 = (bf16[18,16,128]{2,1,0:T(8,128)(2,1)S(1)}, bf16[18,16,128]{2,1,0:T(8,128)(2,1)S(1)}, u32[]{:S(2)}, u32[]{:S(2)}) collective-permute-start(bf16[18,16,128]{2,1,0:T(8,128)(2,1)S(1)} %get-tuple-element.20), channel_id=1, source_target_pairs={{0,4},{4,8},{8,12},{1,5},{5,9},{9,13},{2,6},{6,10},{10,14},{3,7},{... | collective-permute-start | bytes 221192 | tf_op jit(solution)/shard_map/ppermute | solution.py:58
  14.4 1.6 %collective-permute-done.2.tile_before = bf16[18,16,128]{2,1,0:T(8,128)(2,1)S(1)} collective-permute-done((bf16[18,16,128]{2,1,0:T(8,128)(2,1)S(1)}, bf16[18,16,128]{2,1,0:T(8,128)(2,1)S(1)}, u32[]{:S(2)}, u32[]{:S(2)}) %collective-permute-start.2) | collective-permute-done | bytes 73760 | tf_op jit(solution)/shard_map/ppermute | solution.py:58
  21.3 1.9 %shard_map.142 = (f32[8,16,128]{2,1,0:T(8,128)}, f32[8,16,128]{2,1,0:T(8,128)}, bf16[4,96]{1,0:T(4,128)(2,1)S(1)}, bf16[4,96]{1,0:T(4,128)(2,1)S(1)}, bf16[4,96]...) custom-call(f32[8,16,128]{2,1,0:T(8,128)S(1)} %copy-done.3, f32[8,16,128]{2,1,0:T(8,128)S(1)} %copy-done.5, ...), custom_call_target="tpu_custom_call" | custom-call | flops 50000000 | bytes 1000000 | tf_op jit(solution)/shard_map/pallas_call | solution.py:40
  23.2 4.8 %collective-permute-start.4 = (bf16[4,96]{1,0:T(4,128)(2,1)S(1)}, bf16[4,96]{1,0:T(4,128)(2,1)S(1)}, u32[]{:S(2)}, u32[]{:S(2)}) collective-permute-start(bf16[4,96]{1,0:T(4,128)(2,1)S(1)} %get-tuple-element.26), channel_id=1, source_target_pairs={{0,12},{4,0},{8,4},{12,8},{1,13},{5,1},{9,5},{13,9},{2,14},{6,2},{... | collective-permute-start | bytes 2312 | tf_op jit(solution)/shard_map/ppermute | solution.py:294
  28.0 1.0 %collective-permute-start.6 = (bf16[4,96]{1,0:T(4,128)(2,1)S(1)}, bf16[4,96]{1,0:T(4,128)(2,1)S(1)}, u32[]{:S(2)}, u32[]{:S(2)}) collective-permute-start(bf16[4,96]{1,0:T(4,128)(2,1)S(1)} %get-tuple-element.28), channel_id=1, source_target_pairs={{0,4},{4,8},{8,12},{12,0},{1,5},{5,9},{9,13},{13,1},{2,6},{6,10},{... | collective-permute-start | bytes 2312 | tf_op jit(solution)/shard_map/ppermute | solution.py:294
  29.7 2.8 %collective-permute-done.5.rest_2_ = bf16[4,96]{1,0:T(4,128)(2,1)S(1)} collective-permute-done((bf16[4,96]{1,0:T(4,128)(2,1)S(1)}, bf16[4,96]{1,0:T(4,128)(2,1)S(1)}, u32[]{:S(2)}, u32[]{:S(2)}) %collective-permute-start.5) | collective-permute-done | bytes 800 | tf_op jit(solution)/shard_map/ppermute | solution.py:294
  32.5 0.9 %collective-permute-done.6.rest_3_ = bf16[4,96]{1,0:T(4,128)(2,1)S(1)} collective-permute-done((bf16[4,96]{1,0:T(4,128)(2,1)S(1)}, bf16[4,96]{1,0:T(4,128)(2,1)S(1)}, u32[]{:S(2)}, u32[]{:S(2)}) %collective-permute-start.6) | collective-permute-done | bytes 800 | tf_op jit(solution)/shard_map/ppermute | solution.py:294
  33.4 1.4 %copy-done = bf16[384,2048]{1,0:T(8,128)(2,1)S(1)} copy-done((bf16[384,2048]{1,0:T(8,128)(2,1)S(1)}, bf16[384,2048]{1,0:T(8,128)(2,1)}, u32[]{:S(2)}) %copy-start) | copy-done | bytes 1572888
  35.3 1.2 %collective-permute-done.7 = f32[4,2048]{1,0:T(4,128)S(1)} collective-permute-done((f32[4,2048]{1,0:T(4,128)S(1)}, f32[4,2048]{1,0:T(4,128)S(1)}, u32[]{:S(2)}, u32[]{:S(2)}) %collective-permute-start.7) | collective-permute-done | bytes 32800 | tf_op jit(solution)/shard_map/ppermute | solution.py:375
  36.5 1.6 %collective-permute-start.8 = (f32[4,2048]{1,0:T(4,128)S(1)}, f32[4,2048]{1,0:T(4,128)S(1)}, u32[]{:S(2)}, u32[]{:S(2)}) collective-permute-start(f32[4,2048]{1,0:T(4,128)S(1)} %add.15), channel_id=1, source_target_pairs={{0,2},{2,0},{1,3},{3,1},{4,6},{6,4},{5,7},{7,5},{8,10},{10,8},{9,1... | collective-permute-start | bytes 98312 | tf_op jit(solution)/shard_map/ppermute | solution.py:375
  38.0 2.4 %collective-permute-done.8 = f32[4,2048]{1,0:T(4,128)S(1)} collective-permute-done((f32[4,2048]{1,0:T(4,128)S(1)}, f32[4,2048]{1,0:T(4,128)S(1)}, u32[]{:S(2)}, u32[]{:S(2)}) %collective-permute-start.8) | collective-permute-done | bytes 32800 | tf_op jit(solution)/shard_map/ppermute | solution.py:375
  40.5 1.2 %collective-permute-start.10 = (f32[4,2048]{1,0:T(4,128)S(1)}, f32[4,2048]{1,0:T(4,128)S(1)}, u32[]{:S(2)}, u32[]{:S(2)}) collective-permute-start(f32[4,2048]{1,0:T(4,128)S(1)} %add.16.rest_0_), channel_id=1, source_target_pairs={{0,8},{4,12},{8,0},{12,4},{1,9},{5,13},{9,1},{13,5},{2,10},{6,14},... | collective-permute-start | bytes 98312 | tf_op jit(solution)/shard_map/ppermute | solution.py:375
  42.3 1.4 %collective-permute-start.9 = (f32[4,2048]{1,0:T(4,128)S(1)}, f32[4,2048]{1,0:T(4,128)S(1)}, u32[]{:S(2)}, u32[]{:S(2)}) collective-permute-start(f32[4,2048]{1,0:T(4,128)S(1)} %add.16.rest_0_), channel_id=1, source_target_pairs={{0,4},{4,8},{8,12},{12,0},{1,5},{5,9},{9,13},{13,1},{2,6},{6,10},{... | collective-permute-start | bytes 98312 | tf_op jit(solution)/shard_map/ppermute | solution.py:375
  43.7 2.1 %collective-permute-done.10.rest_2_ = f32[4,2048]{1,0:T(4,128)S(1)} collective-permute-done((f32[4,2048]{1,0:T(4,128)S(1)}, f32[4,2048]{1,0:T(4,128)S(1)}, u32[]{:S(2)}, u32[]{:S(2)}) %collective-permute-start.10) | collective-permute-done | bytes 32800 | tf_op jit(solution)/shard_map/ppermute | solution.py:375
  46.1 2.0 %collective-permute-done.9.rest_1_ = f32[4,2048]{1,0:T(4,128)S(1)} collective-permute-done((f32[4,2048]{1,0:T(4,128)S(1)}, f32[4,2048]{1,0:T(4,128)S(1)}, u32[]{:S(2)}, u32[]{:S(2)}) %collective-permute-start.9) | collective-permute-done | bytes 32800 | tf_op jit(solution)/shard_map/ppermute | solution.py:375
  48.1 0.9 %shard_map.144 = (f32[2,2048]{1,0:T(2,128)S(1)}, bf16[4,96]{1,0:T(4,128)(2,1)S(1)}, bf16[4,96]{1,0:T(4,128)(2,1)S(1)}, bf16[4,96]{1,0:T(4,128)(2,1)S(1)}, bf16[4,96]{1,0:T(4,128)(2,1)S(1)}) custom-call(f32[1,2048]{1,0:T(1,128)S(1)} %bitcast.7, f32[1,2048]{1,0:T(1,128)S(1)} %bitcast.8, f32[2,2048]{1,0:T(2,128)S(1)} %copy-done.8, ...), custom_call_target="tpu_custom_call" | custom-call | flops 1000000 | bytes 1000000 | tf_op jit(solution)/shard_map/pallas_call | solution.py:40
  50.1 1.0 %collective-permute-start.14 = (bf16[4,96]{1,0:T(4,128)(2,1)S(1)}, bf16[4,96]{1,0:T(4,128)(2,1)S(1)}, u32[]{:S(2)}, u32[]{:S(2)}) collective-permute-start(bf16[4,96]{1,0:T(4,128)(2,1)S(1)} %get-tuple-element.32), channel_id=1, source_target_pairs={{0,4},{4,8},{8,12},{12,0},{1,5},{5,9},{9,13},{13,1},{2,6},{6,10},{... | collective-permute-start | bytes 2312 | tf_op jit(solution)/shard_map/ppermute | solution.py:294
  51.6 1.0 %collective-permute-done.12.rest_1_ = bf16[4,96]{1,0:T(4,128)(2,1)S(1)} collective-permute-done((bf16[4,96]{1,0:T(4,128)(2,1)S(1)}, bf16[4,96]{1,0:T(4,128)(2,1)S(1)}, u32[]{:S(2)}, u32[]{:S(2)}) %collective-permute-start.12) | collective-permute-done | bytes 800 | tf_op jit(solution)/shard_map/ppermute | solution.py:294
  52.6 1.7 %collective-permute-done.13.rest_2_ = bf16[4,96]{1,0:T(4,128)(2,1)S(1)} collective-permute-done((bf16[4,96]{1,0:T(4,128)(2,1)S(1)}, bf16[4,96]{1,0:T(4,128)(2,1)S(1)}, u32[]{:S(2)}, u32[]{:S(2)}) %collective-permute-start.13) | collective-permute-done | bytes 800 | tf_op jit(solution)/shard_map/ppermute | solution.py:294
  54.3 1.1 %collective-permute-done.14.rest_3_ = bf16[4,96]{1,0:T(4,128)(2,1)S(1)} collective-permute-done((bf16[4,96]{1,0:T(4,128)(2,1)S(1)}, bf16[4,96]{1,0:T(4,128)(2,1)S(1)}, u32[]{:S(2)}, u32[]{:S(2)}) %collective-permute-start.14) | collective-permute-done | bytes 800 | tf_op jit(solution)/shard_map/ppermute | solution.py:294
  (44 shorter events, 11.3 us)
Async XLA Ops:
  0.6 0.8 %copy-start.2 = (f32[8,16,128]{2,1,0:T(8,128)S(1)}, f32[8,16,128]{2,1,0:T(8,128)}, u32[]{:S(2)}) copy-start(f32[8,16,128]{2,1,0:T(8,128)} %p_ref.7) | copy-start | bytes 196612
  1.5 0.8 %copy-start.4 = (f32[8,16,128]{2,1,0:T(8,128)S(1)}, f32[8,16,128]{2,1,0:T(8,128)}, u32[]{:S(2)}) copy-start(f32[8,16,128]{2,1,0:T(8,128)} %q_ref.7) | copy-start | bytes 196612
  2.3 0.8 %copy-start.6 = (f32[8,16,128]{2,1,0:T(8,128)S(1)}, f32[8,16,128]{2,1,0:T(8,128)}, u32[]{:S(2)}) copy-start(f32[8,16,128]{2,1,0:T(8,128)} %c_ref.7) | copy-start | bytes 196612
  3.2 44.9 %copy-start.8 = (f32[2,2048]{1,0:T(2,128)S(1)}, f32[2,2048]{1,0:T(2,128)}, u32[]{:S(2)}) copy-start(f32[2,2048]{1,0:T(2,128)} %start_ref.1) | copy-start | bytes 49156
  3.2 44.9 %copy-start.9 = (f32[2048]{0:T(1024)S(1)}, f32[2048]{0:T(1024)}, u32[]{:S(2)}) copy-start(f32[2048]{0:T(1024)} %param.16) | copy-start | bytes 24580
  3.2 44.9 %copy-start.10 = (f32[2048]{0:T(1024)S(1)}, f32[2048]{0:T(1024)}, u32[]{:S(2)}) copy-start(f32[2048]{0:T(1024)} %param.17) | copy-start | bytes 24580
  3.2 4.8 %collective-permute-start = (bf16[3,32,128]{2,1,0:T(8,128)(2,1)S(1)}, bf16[3,32,128]{2,1,0:T(8,128)(2,1)S(1)}, u32[]{:S(2)}, u32[]{:S(2)}) collective-permute-start(bf16[3,32,128]{2,1,0:T(8,128)(2,1)S(1)} %shard_map.138), channel_id=1, source_target_pairs={{0,2},{2,0},{1,3},{3,1},{4,6},{6,4},{5,7},{7,5},{8,10},{10,8},{9,1... | collective-permute-start | bytes 73736 | tf_op jit(solution)/shard_map/ppermute | solution.py:337
  8.1 6.3 %collective-permute-start.1 = (bf16[18,16,128]{2,1,0:T(8,128)(2,1)S(1)}, bf16[18,16,128]{2,1,0:T(8,128)(2,1)S(1)}, u32[]{:S(2)}, u32[]{:S(2)}) collective-permute-start(bf16[18,16,128]{2,1,0:T(8,128)(2,1)S(1)} %get-tuple-element.19), channel_id=1, source_target_pairs={{4,0},{8,4},{12,8},{5,1},{9,5},{13,9},{6,2},{10,6},{14,10},{7,3},{... | collective-permute-start | bytes 221192 | tf_op jit(solution)/shard_map/ppermute | solution.py:57
  9.4 6.6 %collective-permute-start.2 = (bf16[18,16,128]{2,1,0:T(8,128)(2,1)S(1)}, bf16[18,16,128]{2,1,0:T(8,128)(2,1)S(1)}, u32[]{:S(2)}, u32[]{:S(2)}) collective-permute-start(bf16[18,16,128]{2,1,0:T(8,128)(2,1)S(1)} %get-tuple-element.20), channel_id=1, source_target_pairs={{0,4},{4,8},{8,12},{1,5},{5,9},{9,13},{2,6},{6,10},{10,14},{3,7},{... | collective-permute-start | bytes 221192 | tf_op jit(solution)/shard_map/ppermute | solution.py:58
  16.2 2.6 %collective-permute-start.3 = (bf16[8,1152]{1,0:T(8,128)(2,1)S(1)}, bf16[8,1152]{1,0:T(8,128)(2,1)S(1)}, u32[]{:S(2)}, u32[]{:S(2)}) collective-permute-start(bf16[8,1152]{1,0:T(8,128)(2,1)S(1)} %shard_map.140), channel_id=1, source_target_pairs={{0,1},{1,0},{2,3},{3,2},{4,5},{5,4},{6,7},{7,6},{8,9},{9,8},{10,11... | collective-permute-start | bytes 55304 | tf_op jit(solution)/shard_map/ppermute | solution.py:350
  18.8 0.8 %copy-start.3 = (f32[8,16,128]{2,1,0:T(8,128)S(1)}, f32[8,16,128]{2,1,0:T(8,128)}, u32[]{:S(2)}) copy-start(f32[8,16,128]{2,1,0:T(8,128)} %p_ref.7) | copy-start | bytes 196612
  23.2 6.5 %collective-permute-start.4 = (bf16[4,96]{1,0:T(4,128)(2,1)S(1)}, bf16[4,96]{1,0:T(4,128)(2,1)S(1)}, u32[]{:S(2)}, u32[]{:S(2)}) collective-permute-start(bf16[4,96]{1,0:T(4,128)(2,1)S(1)} %get-tuple-element.26), channel_id=1, source_target_pairs={{0,12},{4,0},{8,4},{12,8},{1,13},{5,1},{9,5},{13,9},{2,14},{6,2},{... | collective-permute-start | bytes 2312 | tf_op jit(solution)/shard_map/ppermute | solution.py:294
  28.0 4.5 %collective-permute-start.5 = (bf16[4,96]{1,0:T(4,128)(2,1)S(1)}, bf16[4,96]{1,0:T(4,128)(2,1)S(1)}, u32[]{:S(2)}, u32[]{:S(2)}) collective-permute-start(bf16[4,96]{1,0:T(4,128)(2,1)S(1)} %get-tuple-element.27), channel_id=1, source_target_pairs={{0,8},{4,12},{8,0},{12,4},{1,9},{5,13},{9,1},{13,5},{2,10},{6,14},... | collective-permute-start | bytes 2312 | tf_op jit(solution)/shard_map/ppermute | solution.py:294
  28.0 5.4 %collective-permute-start.6 = (bf16[4,96]{1,0:T(4,128)(2,1)S(1)}, bf16[4,96]{1,0:T(4,128)(2,1)S(1)}, u32[]{:S(2)}, u32[]{:S(2)}) collective-permute-start(bf16[4,96]{1,0:T(4,128)(2,1)S(1)} %get-tuple-element.28), channel_id=1, source_target_pairs={{0,4},{4,8},{8,12},{12,0},{1,5},{5,9},{9,13},{13,1},{2,6},{6,10},{... | collective-permute-start | bytes 2312 | tf_op jit(solution)/shard_map/ppermute | solution.py:294
  33.4 1.4 %copy-start = (bf16[384,2048]{1,0:T(8,128)(2,1)S(1)}, bf16[384,2048]{1,0:T(8,128)(2,1)}, u32[]{:S(2)}) copy-start(bf16[384,2048]{1,0:T(8,128)(2,1)} %shapes_ref.3) | copy-start | bytes 4718596
  34.8 13.3 %copy-start.1 = (bf16[384,2048]{1,0:T(8,128)(2,1)S(1)}, bf16[384,2048]{1,0:T(8,128)(2,1)}, u32[]{:S(2)}) copy-start(bf16[384,2048]{1,0:T(8,128)(2,1)} %shapes_ref.3) | copy-start | bytes 4718596
  35.3 1.2 %collective-permute-start.7 = (f32[4,2048]{1,0:T(4,128)S(1)}, f32[4,2048]{1,0:T(4,128)S(1)}, u32[]{:S(2)}, u32[]{:S(2)}) collective-permute-start(f32[4,2048]{1,0:T(4,128)S(1)} %shard_map.143), channel_id=1, source_target_pairs={{0,1},{1,0},{2,3},{3,2},{4,5},{5,4},{6,7},{7,6},{8,9},{9,8},{10,11... | collective-permute-start | bytes 98312 | tf_op jit(solution)/shard_map/ppermute | solution.py:375
  36.5 4.0 %collective-permute-start.8 = (f32[4,2048]{1,0:T(4,128)S(1)}, f32[4,2048]{1,0:T(4,128)S(1)}, u32[]{:S(2)}, u32[]{:S(2)}) collective-permute-start(f32[4,2048]{1,0:T(4,128)S(1)} %add.15), channel_id=1, source_target_pairs={{0,2},{2,0},{1,3},{3,1},{4,6},{6,4},{5,7},{7,5},{8,10},{10,8},{9,1... | collective-permute-start | bytes 98312 | tf_op jit(solution)/shard_map/ppermute | solution.py:375
  40.5 5.3 %collective-permute-start.10 = (f32[4,2048]{1,0:T(4,128)S(1)}, f32[4,2048]{1,0:T(4,128)S(1)}, u32[]{:S(2)}, u32[]{:S(2)}) collective-permute-start(f32[4,2048]{1,0:T(4,128)S(1)} %add.16.rest_0_), channel_id=1, source_target_pairs={{0,8},{4,12},{8,0},{12,4},{1,9},{5,13},{9,1},{13,5},{2,10},{6,14},... | collective-permute-start | bytes 98312 | tf_op jit(solution)/shard_map/ppermute | solution.py:375
  41.7 4.4 %collective-permute-start.11 = (f32[4,2048]{1,0:T(4,128)S(1)}, f32[4,2048]{1,0:T(4,128)S(1)}, u32[]{:S(2)}, u32[]{:S(2)}) collective-permute-start(f32[4,2048]{1,0:T(4,128)S(1)} %add.16.rest_0_), channel_id=1, source_target_pairs={{0,12},{4,0},{8,4},{12,8},{1,13},{5,1},{9,5},{13,9},{2,14},{6,2},{... | collective-permute-start | bytes 98312 | tf_op jit(solution)/shard_map/ppermute | solution.py:375
  42.3 5.7 %collective-permute-start.9 = (f32[4,2048]{1,0:T(4,128)S(1)}, f32[4,2048]{1,0:T(4,128)S(1)}, u32[]{:S(2)}, u32[]{:S(2)}) collective-permute-start(f32[4,2048]{1,0:T(4,128)S(1)} %add.16.rest_0_), channel_id=1, source_target_pairs={{0,4},{4,8},{8,12},{12,0},{1,5},{5,9},{9,13},{13,1},{2,6},{6,10},{... | collective-permute-start | bytes 98312 | tf_op jit(solution)/shard_map/ppermute | solution.py:375
  49.0 3.6 %collective-permute-start.12 = (bf16[4,96]{1,0:T(4,128)(2,1)S(1)}, bf16[4,96]{1,0:T(4,128)(2,1)S(1)}, u32[]{:S(2)}, u32[]{:S(2)}) collective-permute-start(bf16[4,96]{1,0:T(4,128)(2,1)S(1)} %get-tuple-element.30), channel_id=1, source_target_pairs={{0,12},{4,0},{8,4},{12,8},{1,13},{5,1},{9,5},{13,9},{2,14},{6,2},{... | collective-permute-start | bytes 2312 | tf_op jit(solution)/shard_map/ppermute | solution.py:294
  49.8 4.5 %collective-permute-start.13 = (bf16[4,96]{1,0:T(4,128)(2,1)S(1)}, bf16[4,96]{1,0:T(4,128)(2,1)S(1)}, u32[]{:S(2)}, u32[]{:S(2)}) collective-permute-start(bf16[4,96]{1,0:T(4,128)(2,1)S(1)} %get-tuple-element.31), channel_id=1, source_target_pairs={{0,8},{4,12},{8,0},{12,4},{1,9},{5,13},{9,1},{13,5},{2,10},{6,14},... | collective-permute-start | bytes 2312 | tf_op jit(solution)/shard_map/ppermute | solution.py:294
  50.1 5.4 %collective-permute-start.14 = (bf16[4,96]{1,0:T(4,128)(2,1)S(1)}, bf16[4,96]{1,0:T(4,128)(2,1)S(1)}, u32[]{:S(2)}, u32[]{:S(2)}) collective-permute-start(bf16[4,96]{1,0:T(4,128)(2,1)S(1)} %get-tuple-element.32), channel_id=1, source_target_pairs={{0,4},{4,8},{8,12},{12,0},{1,5},{5,9},{9,13},{13,1},{2,6},{6,10},{... | collective-permute-start | bytes 2312 | tf_op jit(solution)/shard_map/ppermute | solution.py:294
  (4 other events, 3.0 us)

commit v2 on v1

--- a/solution.py
+++ b/solution.py
@@ -17,7 +17,7 @@
 f32 = jnp.float32
 bf16 = jnp.bfloat16
 VMEM = pl.BlockSpec(memory_space=pltpu.VMEM)
-SMEM = pl.BlockSpec(memory_space=pltpu.SMEM)
+HBM = pl.BlockSpec(memory_space=pltpu.HBM)
 
 
 def shift(count, by):
@@ -36,20 +36,27 @@
     return lax.dot_general(a, b, (((contract[0],), (contract[1],)), ((), ())), preferred_element_type=f32)
 
 
-def call(kernel, out_shape, inputs, scratch=(), specs=None, flops=1_000_000):
+def call(kernel, out_shape, inputs, scratch=(), specs=None, out_specs=None, micros=1.0, vmem=32):
     return pl.pallas_call(
         kernel,
         out_shape=out_shape,
         in_specs=specs or [VMEM] * len(inputs),
-        out_specs=jax.tree.map(lambda _: VMEM, out_shape),
+        out_specs=out_specs or jax.tree.map(lambda _: VMEM, out_shape),
         scratch_shapes=list(scratch),
-        cost_estimate=pl.CostEstimate(flops=flops, bytes_accessed=1_000_000, transcendentals=0),
-        compiler_params=pltpu.CompilerParams(vmem_limit_bytes=32 * 1024 * 1024),
+        cost_estimate=pl.CostEstimate(flops=int(micros * 1e9), bytes_accessed=0, transcendentals=0),
+        compiler_params=pltpu.CompilerParams(vmem_limit_bytes=vmem * 1024 * 1024),
     )(*inputs)
 
 
 def shape_of(dims, dtype):
     return jax.ShapeDtypeStruct(dims, dtype)
+
+
+def fetch(pairs, sems):
+    copies = [pltpu.make_async_copy(a, b, sems.at[i]) for i, (a, b) in enumerate(pairs)]
+    for copy in copies:
+        copy.start()
+    return copies
 
 
 def both_ways(axis, ahead, behind):
@@ -59,12 +66,19 @@
     return after, before
 
 
-def route_kernel(buckets, owner_ref, cell_ref, count_ref, route_ref, place_ref, *, lanes, rows):
+def pairs(count, first):
+    swaps = []
+    for i in range(first, count - 1, 2):
+        swaps += [(i, i + 1), (i + 1, i)]
+    return swaps
+
+
+def route_kernel(buckets, lanes, rows, after_ref, owner_ref, cell_ref, count_ref, route_ref, place_ref):
     slots = owner_ref.shape[1]
     bucket = slots // buckets
     me = lax.axis_index("tile")
     owner = owner_ref[...]
-    live = iota((1, slots), 1) < count_ref[0, 0]
+    live = iota((1, slots), 1) < count_ref[...]
     held = -(-buckets // SUBLANES) * SUBLANES
     member = jnp.where((iota((held, slots), 0) == owner) & live, 1.0, 0.0)
     earlier = jnp.where(iota((slots, slots), 0) < iota((slots, slots), 1), 1.0, 0.0).astype(bf16)
@@ -82,15 +96,15 @@
     place_ref[:, rows:] = dot(route, lane.astype(bf16), (1, 1)).astype(bf16)
 
 
-def pack_sub_kernel(ends, p_ref, q_ref, c_ref, *outs):
-    layers, rows, lanes = p_ref.shape
+def pack_sub_kernel(ends, fields, *outs):
+    layers, rows, lanes = fields.shape[1:]
     low = iota((SUBLANES, lanes), 0) < STEPS
-    for at, ref in enumerate((p_ref, q_ref, c_ref)):
+    for at in range(FIELDS):
         for pair in range(layers // 2):
             tiles = []
             for layer in (2 * pair, 2 * pair + 1):
-                last = pltpu.roll(ref[layer, rows - SUBLANES :, :], STEPS, 0)
-                first = ref[layer, :SUBLANES, :]
+                last = pltpu.roll(fields[at, layer, rows - SUBLANES :, :], STEPS, 0)
+                first = fields[at, layer, :SUBLANES, :]
                 tiles.append((last, first))
             picked = [jnp.where(low, a, pltpu.roll(b, STEPS, 0)) for a, b in zip(*tiles)]
             if ends == 1:
@@ -99,11 +113,13 @@
                 out[at, pair * SUBLANES : (pair + 1) * SUBLANES, :] = value.astype(bf16)
 
 
-def side_rows(at, layer, after_ref, before_ref):
-    start = layer // 2 * SUBLANES
-    after = after_ref[at, start : start + SUBLANES, :].astype(f32)
-    before = before_ref[at, start : start + SUBLANES, :].astype(f32)
-    if layer % 2 == 0:
+def side_rows(at, base, k, after_ref, before_ref):
+    start = base // 2 * SUBLANES + k // 2 * SUBLANES
+    if not isinstance(start, int):
+        start = pl.multiple_of(start, SUBLANES)
+    after = after_ref[at, pl.ds(start, SUBLANES), :].astype(f32)
+    before = before_ref[at, pl.ds(start, SUBLANES), :].astype(f32)
+    if k % 2 == 0:
         before = pltpu.roll(before, STEPS, 0)
     else:
         after = pltpu.roll(after, STEPS, 0)
@@ -114,15 +130,22 @@
     return jnp.where(low, after * keep_after, before * keep_before)
 
 
-def pack_tile_kernel(p_ref, q_ref, c_ref, after_ref, before_ref, ahead_ref, behind_ref):
-    layers = p_ref.shape[0]
-    for out, base in ((ahead_ref, layers - STEPS), (behind_ref, 0)):
-        for at, ref in enumerate((p_ref, q_ref, c_ref)):
+def pack_tile_kernel(fields, after_ref, before_ref, ready_ref, *outs):
+    layers = fields.shape[1]
+    odd = lax.axis_index("tile") % 2
+    for out, base in zip(outs, ((1 - odd) * (layers - STEPS), odd * (layers - STEPS))):
+        for at in range(FIELDS):
             for k in range(STEPS):
-                out[at * STEPS + k] = ref[base + k].astype(bf16)
+                out[at * STEPS + k] = fields[at, base + k].astype(bf16)
             for k in range(0, STEPS, 2):
-                beside = [side_rows(at, base + k + i, after_ref, before_ref) for i in range(2)]
+                beside = [side_rows(at, base, k + i, after_ref, before_ref) for i in range(2)]
                 out[FIELDS * STEPS + (at * STEPS + k) // 2] = jnp.concatenate(beside, 0).astype(bf16)
+
+
+def sides(first, second, layers):
+    odd = lax.axis_index("tile") % 2
+    top = STEPS + layers
+    return (first, (1 - odd) * top), (second, odd * top)
 
 
 def end_lanes(lanes):
@@ -131,33 +154,33 @@
     return jnp.where(iota((2 * STEPS, lanes), 1) == wanted, 1.0, 0.0).astype(bf16)
 
 
-def pack_rep_kernel(p_ref, q_ref, c_ref, sub_after, sub_before, tile_after, tile_before, out_ref, wide):
-    layers, rows, lanes = p_ref.shape
+def pack_rep_kernel(fields, sub_after, sub_before, tile_first, tile_second, out_ref, wide):
+    layers, rows, lanes = fields.shape[1:]
     beside = 2 * STEPS
     total = layers + 2 * STEPS
     picks = end_lanes(lanes)
-    for at, ref in enumerate((p_ref, q_ref, c_ref)):
-        for side, base in ((tile_before, 0), (tile_after, STEPS + layers)):
-            wide[base * rows : (base + STEPS) * rows, :] = side[at * STEPS : (at + 1) * STEPS].reshape(STEPS * rows, lanes)
-            start = total * rows + base * beside
+    for at in range(FIELDS):
+        for side, base in sides(tile_first, tile_second, layers):
+            start = pl.multiple_of(base * rows, STEPS * rows)
+            wide[pl.ds(start, STEPS * rows), :] = side[at * STEPS : (at + 1) * STEPS].reshape(STEPS * rows, lanes)
+            start = pl.multiple_of(total * rows + base * beside, STEPS * beside)
             packed = FIELDS * STEPS + at * STEPS // 2
-            wide[start : start + STEPS * beside, :] = side[packed : packed + STEPS // 2].reshape(STEPS * beside, lanes)
+            wide[pl.ds(start, STEPS * beside), :] = side[packed : packed + STEPS // 2].reshape(STEPS * beside, lanes)
         for k in range(layers):
-            wide[(STEPS + k) * rows : (STEPS + k + 1) * rows, :] = ref[k].astype(bf16)
+            wide[(STEPS + k) * rows : (STEPS + k + 1) * rows, :] = fields[at, k].astype(bf16)
         for k in range(0, layers, 2):
             start = total * rows + (STEPS + k) * beside
-            pair = [side_rows(at, k + i, sub_after, sub_before) for i in range(2)]
+            pair = [side_rows(at, 0, k + i, sub_after, sub_before) for i in range(2)]
             wide[start : start + 2 * beside, :] = jnp.concatenate(pair, 0).astype(bf16)
         width = wide.shape[0]
         out_ref[:, at * width : (at + 1) * width] = dot(picks, wide[...], (1, 1)).astype(bf16)
 
 
 def window_kernel(
-    p_ref, q_ref, c_ref, sub_after, sub_before, tile_after, tile_before, rep_after, rep_before, place_ref,
-    final_ref, prior_ref, *rest,
+    fields, sub_after, sub_before, tile_first, tile_second, rep_after, rep_before, place_ref, states, *rest
 ):
     *sends, now, ago, coef, lapped, seen = rest
-    layers, rows, lanes = p_ref.shape
+    layers, rows, lanes = fields.shape[1:]
     beside = 2 * STEPS
     total = layers + 2 * STEPS
     wide_rows, wide_lanes = rows + beside, 2 * lanes
@@ -170,11 +193,11 @@
     end = iota((2 * STEPS, width), 0) < STEPS
     keep_after = jnp.where(rep < reps - 1, 1.0, 0.0)
     keep_before = jnp.where(rep > 0, 1.0, 0.0)
-    for at, (ref, out) in enumerate(((p_ref, now), (q_ref, ago), (c_ref, coef))):
+    for at, out in enumerate((now, ago, coef)):
         for k in range(layers):
-            out[STEPS + k, :rows, :lanes] = ref[k]
-            out[STEPS + k, rows:, :lanes] = side_rows(at, k, sub_after, sub_before)
-        for side, base in ((tile_before, 0), (tile_after, STEPS + layers)):
+            out[STEPS + k, :rows, :lanes] = fields[at, k]
+            out[STEPS + k, rows:, :lanes] = side_rows(at, 0, k, sub_after, sub_before)
+        for side, base in sides(tile_first, tile_second, layers):
             for k in range(STEPS):
                 out[base + k, :rows, :lanes] = side[at * STEPS + k].astype(f32)
                 pair = side[FIELDS * STEPS + (at * STEPS + k) // 2].astype(f32)
@@ -221,10 +244,8 @@
             if 0 <= own < layers:
                 core = updated[:rows, :lanes]
                 seen[own * rows : (own + 1) * rows, step * lanes : (step + 1) * lanes] = core.astype(bf16)
-                if step == STEPS - 1:
-                    final_ref[own] = core
-                if step == STEPS - 2:
-                    prior_ref[own] = core
+                if step >= STEPS - 2:
+                    states[STEPS - 1 - step, own] = core
             below, here = here, above
 
     cells = layers * rows
@@ -239,6 +260,11 @@
         send[...] = dot(steps_at, found.astype(bf16), (1, 1))[:STEPS].astype(bf16)
 
 
+def store_kernel(states, final_hbm, prior_hbm, sems):
+    for copy in fetch(((states.at[0], final_hbm), (states.at[1], prior_hbm)), sems):
+        copy.wait()
+
+
 def spread(at, size, total, bucket):
     wanted = iota((size, 1), 0) + at * size + lax.axis_index("tile") * bucket
     wanted = jnp.where(wanted >= total, wanted - total, wanted)
@@ -261,7 +287,7 @@
     state_ref, *sends, accel = rest
     forces = forces_in[0][...]
     for ref in forces_in[1:]:
-        forces = forces + ref[...]
+        forces = forces + ref[...].astype(f32)
     frequency, damping = freq_ref[...], damp_ref[...]
     drag, stiffness = 2.0 * damping * frequency, frequency * frequency
     displace, velocity = start_ref[0:1, :], start_ref[1:2, :]
@@ -319,31 +345,32 @@
     modes = mode_shapes.shape[1]
     bucket = slots // buckets
     parts = buckets if buckets <= 4 and bucket % 16 == 0 else 1
-    fields = (pressure, previous_pressure, courant_square)
     total = layers + 2 * STEPS
     wide_rows = rows + 2 * STEPS
 
-    route, place = call(
-        functools.partial(route_kernel, buckets, lanes=lanes, rows=layers * rows),
-        (shape_of((slots, slots), bf16), shape_of((slots, layers * rows + lanes), bf16)),
-        (slot_owner.reshape(1, slots), slot_cell.reshape(1, slots), surface_count.reshape(1, 1)),
-        specs=[VMEM, VMEM, SMEM],
-    )
-
     ends = 1 if subs == 2 else 2
     slab = shape_of((FIELDS, layers * STEPS, lanes), bf16)
-    packed = call(functools.partial(pack_sub_kernel, ends), (slab,) * ends, fields)
+    fields = jnp.stack([pressure, previous_pressure, courant_square])
+    packed = call(functools.partial(pack_sub_kernel, ends), (slab,) * ends, (fields,))
     if subs == 2:
         sub_halo = (lax.ppermute(packed[0], "sub", shift(2, 1)),) * 2
     else:
         sub_halo = both_ways("sub", *packed)
+
+    cells = layers * rows
+    route, place = call(
+        functools.partial(route_kernel, buckets, lanes, cells),
+        (shape_of((slots, slots), bf16), shape_of((slots, cells + lanes), bf16)),
+        (packed[0], slot_owner.reshape(1, slots), slot_cell.reshape(1, slots), surface_count.reshape(1, 1)),
+    )
+
     slab = shape_of((FIELDS * STEPS * 3 // 2, rows, lanes), bf16)
-    packed = call(pack_tile_kernel, (slab, slab), (*fields, *sub_halo))
-    tile_halo = both_ways("tile", *packed)
+    packed = call(pack_tile_kernel, (slab, slab), (fields, *sub_halo, route))
+    tile_halo = [lax.ppermute(value, "tile", pairs(buckets, i)) for i, value in enumerate(packed)]
     packed = call(
         pack_rep_kernel,
         shape_of((2 * STEPS, FIELDS * total * wide_rows), bf16),
-        (*fields, *sub_halo, *tile_halo),
+        (fields, *sub_halo, *tile_halo),
         scratch=[pltpu.VMEM((total * wide_rows, lanes), bf16)],
     )
     if reps == 2:
@@ -354,12 +381,15 @@
     wide = pltpu.VMEM((total, wide_rows, 2 * lanes), f32)
     part = shape_of((STEPS, slots // parts), bf16)
     block = shape_of(pressure.shape, f32)
-    final_field, prior_field, *sends = call(
+    states, *sends = call(
         window_kernel,
-        (block, block) + (part,) * parts,
-        (*fields, *sub_halo, *tile_halo, *rep_halo, place),
-        scratch=[wide] * 4 + [pltpu.VMEM((layers * rows, STEPS * lanes), bf16)],
-        flops=50_000_000,
+        (shape_of((2, layers, rows, lanes), f32),) + (part,) * parts,
+        (fields, *sub_halo, *tile_halo, *rep_halo, place),
+        scratch=[wide] * 4 + [pltpu.VMEM((cells, STEPS * lanes), bf16)],
+        micros=2.0,
+    )
+    final_field, prior_field = call(
+        store_kernel, (block, block), (states,), out_specs=(HBM, HBM), scratch=[pltpu.SemaphoreType.DMA((2,))]
     )
 
     forces = call(
@@ -372,7 +402,8 @@
         count = lax.axis_size(axis)
         forces = functools.reduce(jnp.add, addends)
         if count <= 4:
-            addends = [forces] + [lax.ppermute(forces, axis, shift(count, k)) for k in range(1, count)]
+            sent = forces.astype(bf16) if axis == "tile" else forces
+            addends = [forces] + [lax.ppermute(sent, axis, shift(count, k)) for k in range(1, count)]
         else:
             addends = [lax.psum(forces, axis)]
 

time: 56.7 us -> 48 us (0.85)
  local copies, waits for them, and re-layouts: 9.06 us -> 0.6 us
  starting transfers between devices: 21.7 us -> 20.7 us
  other arithmetic: 0.02 us -> 0.94 us
  Pallas kernels: 4.77 us -> 5.6 us
  waiting for transfers between devices: 19.2 us -> 18.6 us
    unnamed x26 -> x14, local copies, waits for them, and re-layouts: 7.81 us -> 0.03 us
    ppermute x7, starting transfers between devices: 10.7 us -> 7 us  [the longest x5 4.18 us: body(): lax.ppermute(sent, axis, shift(count, k))]
    ppermute x6, starting transfers between devices: 7.91 us -> 10.6 us  [exchange(): lax.ppermute(parts[-k], 'tile', shift(buckets, -k))]
    ppermute x1, waiting for transfers between devices: 1.81 us -> 0.54 us  [body(): sub_halo = (lax.ppermute(packed[0], 'sub', shift(2, 1)),) * 2]
    ppermute x1, waiting for transfers between devices: 0.01 us -> 1.17 us  [body(): rep_halo = (lax.ppermute(packed, 'rep', shift(2, 1)),) * 2]
    another operation x0 -> x1, other arithmetic: none -> 0.92 us  [body(): fields = jnp.stack([pressure, previous_pressure, courant_square])]
    pallas_call x8 -> x9, Pallas kernels: 4.77 us -> 5.6 us  [call(): pl.pallas_call(kernel, out_shape=out_shape, in_specs=specs or [VMEM] * le...]
    ppermute x6, waiting for transfers between devices: 7.47 us -> 6.7 us  [exchange(): lax.ppermute(parts[-k], 'tile', shift(buckets, -k))]
  transfers between devices with their start and end apart: 15 -> 15, of which waited for: 13 -> 11; matrix products, arithmetic and copies ran while one was open for 2% -> 1% of each run, Pallas kernels for 1% -> 3%
where the time goes in v2:
time: 48 us; the launch traced here: 47.8 us
  starting transfers between devices  20.7 us (43%)
  waiting for transfers between devices  18.6 us (39%)
  Pallas kernels  5.6 us (12%)
  between operations  1.41 us (3%)
  other arithmetic  0.94 us (2%)
  local copies, waits for them, and re-layouts  0.6 us (1%)
    ppermute x6, starting transfers between devices, exchange(): lax.ppermute(parts[-k], 'tile', shift(buckets, -k))  10.6 us
    ppermute x5, waiting for transfers between devices, body(): lax.ppermute(sent, axis, shift(count, k))  8.48 us
    ppermute x6, waiting for transfers between devices, exchange(): lax.ppermute(parts[-k], 'tile', shift(buckets, -k))  6.7 us
    pallas_call x9, Pallas kernels, call(): pl.pallas_call(kernel, out_shape=out_shape, in_specs=specs or [VMEM] * le...  5.6 us
    ppermute x5, starting transfers between devices, body(): lax.ppermute(sent, axis, shift(count, k))  4.18 us
    ppermute x1, starting transfers between devices, body(): sub_halo = (lax.ppermute(packed[0], 'sub', shift(2, 1)),) * 2  3 us
    ppermute x2, starting transfers between devices, body(): lax.ppermute(value, 'tile', pairs(buckets, i))  2.82 us
    ppermute x2, waiting for transfers between devices, body(): lax.ppermute(value, 'tile', pairs(buckets, i))  1.67 us
  transfers between devices with their start and end apart: 15, of which 11 were waited for; matrix products, arithmetic and copies ran while one was open for 1% of the time, Pallas kernels for 3%

profile of v2, /device:TPU:0, one launch (start us, length us, event | category | flops | bytes accessed | tf_op | source)
XLA Modules:
  0.0 47.8 jit_solution(12571958449656020762)
XLA Ops:
  0.6 0.9 %pad_maximum_fusion.fields = f32[3,8,16,128]{3,2,1,0:T(8,128)S(1)} fusion(f32[1,8,16,128]{3,2,1,0:T(8,128)} %bitcast.14, f32[1,8,16,128]{3,2,1,0:T(8,128)} %bitcast.15, f32[1,8,16,128]{3,2,1,0:T(8,128)} %bitcast.16), kind=kLoop, calls=%fused_computation | loop fusion | flops 98304 | bytes 393216 | tf_op jit(solution)/shard_map/stack | solution.py:353
  1.6 3.0 %collective-permute-start = (bf16[3,32,128]{2,1,0:T(8,128)(2,1)S(1)}, bf16[3,32,128]{2,1,0:T(8,128)(2,1)S(1)}, u32[]{:S(2)}, u32[]{:S(2)}) collective-permute-start(bf16[3,32,128]{2,1,0:T(8,128)(2,1)S(1)} %shard_map.138.after_ref), channel_id=1, source_target_pairs={{0,2},{2,0},{1,3},{3,1},{4,6},{6,4},{5,7},{7,5},{8,10},{10,8},{9,1... | collective-permute-start | bytes 73736 | tf_op jit(solution)/shard_map/ppermute | solution.py:356
  6.4 2.2 %collective-permute-start.1 = (bf16[18,16,128]{2,1,0:T(8,128)(2,1)S(1)}, bf16[18,16,128]{2,1,0:T(8,128)(2,1)S(1)}, u32[]{:S(2)}, u32[]{:S(2)}) collective-permute-start(bf16[18,16,128]{2,1,0:T(8,128)(2,1)S(1)} %get-tuple-element.21), channel_id=1, source_target_pairs={{0,4},{4,0},{8,12},{12,8},{1,5},{5,1},{9,13},{13,9},{2,6},{6,2},{1... | collective-permute-start | bytes 221192 | tf_op jit(solution)/shard_map/ppermute | solution.py:369
  8.6 0.7 %collective-permute-start.2 = (bf16[18,16,128]{2,1,0:T(8,128)(2,1)S(1)}, bf16[18,16,128]{2,1,0:T(8,128)(2,1)S(1)}, u32[]{:S(2)}, u32[]{:S(2)}) collective-permute-start(bf16[18,16,128]{2,1,0:T(8,128)(2,1)S(1)} %get-tuple-element.22), channel_id=1, source_target_pairs={{4,8},{8,4},{5,9},{9,5},{6,10},{10,6},{7,11},{11,7},{20,24},{24,20... | collective-permute-start | bytes 221192 | tf_op jit(solution)/shard_map/ppermute | solution.py:369
  9.3 1.7 %collective-permute-done.1.tile_first = bf16[18,16,128]{2,1,0:T(8,128)(2,1)S(1)} collective-permute-done((bf16[18,16,128]{2,1,0:T(8,128)(2,1)S(1)}, bf16[18,16,128]{2,1,0:T(8,128)(2,1)S(1)}, u32[]{:S(2)}, u32[]{:S(2)}) %collective-permute-start.1) | collective-permute-done | bytes 73760 | tf_op jit(solution)/shard_map/ppermute | solution.py:369
  11.3 1.2 %collective-permute-done.3.rep_after.rep_before = bf16[8,1152]{1,0:T(8,128)(2,1)S(1)} collective-permute-done((bf16[8,1152]{1,0:T(8,128)(2,1)S(1)}, bf16[8,1152]{1,0:T(8,128)(2,1)S(1)}, u32[]{:S(2)}, u32[]{:S(2)}) %collective-permute-start.3) | collective-permute-done | bytes 18464 | tf_op jit(solution)/shard_map/ppermute | solution.py:377
  12.4 1.9 %shard_map.142 = (f32[2,8,16,128]{3,2,1,0:T(8,128)S(1)}, bf16[4,96]{1,0:T(4,128)(2,1)S(1)}, bf16[4,96]{1,0:T(4,128)(2,1)S(1)}, bf16[4,96]{1,0:T(4,128)(2,1)S(1)}, bf16[4,96]{1,0:T(4,128)(2,1)S(1)}) custom-call(f32[3,8,16,128]{3,2,1,0:T(8,128)S(1)} %pad_maximum_fusion.fields, ...), custom_call_target="tpu_custom_call" | custom-call | flops 2000000000 | tf_op jit(solution)/shard_map/pallas_call | solution.py:40
  14.4 4.1 %collective-permute-start.4 = (bf16[4,96]{1,0:T(4,128)(2,1)S(1)}, bf16[4,96]{1,0:T(4,128)(2,1)S(1)}, u32[]{:S(2)}, u32[]{:S(2)}) collective-permute-start(bf16[4,96]{1,0:T(4,128)(2,1)S(1)} %get-tuple-element.28), channel_id=1, source_target_pairs={{0,12},{4,0},{8,4},{12,8},{1,13},{5,1},{9,5},{13,9},{2,14},{6,2},{... | collective-permute-start | bytes 2312 | tf_op jit(solution)/shard_map/ppermute | solution.py:320
  18.4 2.5 %collective-permute-start.5 = (bf16[4,96]{1,0:T(4,128)(2,1)S(1)}, bf16[4,96]{1,0:T(4,128)(2,1)S(1)}, u32[]{:S(2)}, u32[]{:S(2)}) collective-permute-start(bf16[4,96]{1,0:T(4,128)(2,1)S(1)} %get-tuple-element.29), channel_id=1, source_target_pairs={{0,8},{4,12},{8,0},{12,4},{1,9},{5,13},{9,1},{13,5},{2,10},{6,14},... | collective-permute-start | bytes 2312 | tf_op jit(solution)/shard_map/ppermute | solution.py:320
  20.9 2.0 %collective-permute-start.6 = (bf16[4,96]{1,0:T(4,128)(2,1)S(1)}, bf16[4,96]{1,0:T(4,128)(2,1)S(1)}, u32[]{:S(2)}, u32[]{:S(2)}) collective-permute-start(bf16[4,96]{1,0:T(4,128)(2,1)S(1)} %get-tuple-element.30), channel_id=1, source_target_pairs={{0,4},{4,8},{8,12},{12,0},{1,5},{5,9},{9,13},{13,1},{2,6},{6,10},{... | collective-permute-start | bytes 2312 | tf_op jit(solution)/shard_map/ppermute | solution.py:320
  22.9 3.3 %collective-permute-done.6.rest_3_ = bf16[4,96]{1,0:T(4,128)(2,1)S(1)} collective-permute-done((bf16[4,96]{1,0:T(4,128)(2,1)S(1)}, bf16[4,96]{1,0:T(4,128)(2,1)S(1)}, u32[]{:S(2)}, u32[]{:S(2)}) %collective-permute-start.6) | collective-permute-done | bytes 800 | tf_op jit(solution)/shard_map/ppermute | solution.py:320
  26.7 1.2 %collective-permute-done.7 = f32[4,2048]{1,0:T(4,128)S(1)} collective-permute-done((f32[4,2048]{1,0:T(4,128)S(1)}, f32[4,2048]{1,0:T(4,128)S(1)}, u32[]{:S(2)}, u32[]{:S(2)}) %collective-permute-start.7) | collective-permute-done | bytes 32800 | tf_op jit(solution)/shard_map/ppermute | solution.py:406
  28.0 1.6 %collective-permute-start.8 = (f32[4,2048]{1,0:T(4,128)S(1)}, f32[4,2048]{1,0:T(4,128)S(1)}, u32[]{:S(2)}, u32[]{:S(2)}) collective-permute-start(f32[4,2048]{1,0:T(4,128)S(1)} %add.15), channel_id=1, source_target_pairs={{0,2},{2,0},{1,3},{3,1},{4,6},{6,4},{5,7},{7,5},{8,10},{10,8},{9,1... | collective-permute-start | bytes 98312 | tf_op jit(solution)/shard_map/ppermute | solution.py:406
  29.5 2.4 %collective-permute-done.8 = f32[4,2048]{1,0:T(4,128)S(1)} collective-permute-done((f32[4,2048]{1,0:T(4,128)S(1)}, f32[4,2048]{1,0:T(4,128)S(1)}, u32[]{:S(2)}, u32[]{:S(2)}) %collective-permute-start.8) | collective-permute-done | bytes 32800 | tf_op jit(solution)/shard_map/ppermute | solution.py:406
  32.1 2.5 %collective-permute-start.11 = (bf16[4,2048]{1,0:T(4,128)(2,1)S(1)}, bf16[4,2048]{1,0:T(4,128)(2,1)S(1)}, u32[]{:S(2)}, u32[]{:S(2)}) collective-permute-start(bf16[4,2048]{1,0:T(4,128)(2,1)S(1)} %get-tuple-element.36), channel_id=1, source_target_pairs={{0,12},{4,0},{8,4},{12,8},{1,13},{5,1},{9,5},{13,9},{2,14},{6,2},{... | collective-permute-start | bytes 49160 | tf_op jit(solution)/shard_map/ppermute | solution.py:406
  34.6 0.7 %shard_map.143 = (f32[8,16,128]{2,1,0:T(8,128)}, f32[8,16,128]{2,1,0:T(8,128)}) custom-call(f32[2,8,16,128]{3,2,1,0:T(8,128)S(1)} %get-tuple-element.24.states), custom_call_target="tpu_custom_call" | custom-call | flops 1000000000 | tf_op jit(solution)/shard_map/pallas_call | solution.py:40
  35.3 1.4 %collective-permute-done.10.rest_2_ = bf16[4,2048]{1,0:T(4,128)(2,1)S(1)} collective-permute-done((bf16[4,2048]{1,0:T(4,128)(2,1)S(1)}, bf16[4,2048]{1,0:T(4,128)(2,1)S(1)}, u32[]{:S(2)}, u32[]{:S(2)}) %collective-permute-start.10) | collective-permute-done | bytes 16416 | tf_op jit(solution)/shard_map/ppermute | solution.py:406
  36.7 3.5 %collective-permute-done.9.rest_1_ = bf16[4,2048]{1,0:T(4,128)(2,1)S(1)} collective-permute-done((bf16[4,2048]{1,0:T(4,128)(2,1)S(1)}, bf16[4,2048]{1,0:T(4,128)(2,1)S(1)}, u32[]{:S(2)}, u32[]{:S(2)}) %collective-permute-start.9) | collective-permute-done | bytes 16416 | tf_op jit(solution)/shard_map/ppermute | solution.py:406
  40.1 0.9 %shard_map.145 = (f32[2,2048]{1,0:T(2,128)S(1)}, bf16[4,96]{1,0:T(4,128)(2,1)S(1)}, bf16[4,96]{1,0:T(4,128)(2,1)S(1)}, bf16[4,96]{1,0:T(4,128)(2,1)S(1)}, bf16[4,96]{1,0:T(4,128)(2,1)S(1)}) custom-call(f32[1,2048]{1,0:T(1,128)S(1)} %bitcast.10, f32[1,2048]{1,0:T(1,128)S(1)} %bitcast.11, f32[2,2048]{1,0:T(2,128)S(1)} %copy-done.1, ...), custom_call_target="tpu_custom_call" | custom-call | flops 1000000000 | tf_op jit(solution)/shard_map/pallas_call | solution.py:40
  41.3 1.9 %collective-permute-start.14 = (bf16[4,96]{1,0:T(4,128)(2,1)S(1)}, bf16[4,96]{1,0:T(4,128)(2,1)S(1)}, u32[]{:S(2)}, u32[]{:S(2)}) collective-permute-start(bf16[4,96]{1,0:T(4,128)(2,1)S(1)} %get-tuple-element.34), channel_id=1, source_target_pairs={{0,4},{4,8},{8,12},{12,0},{1,5},{5,9},{9,13},{13,1},{2,6},{6,10},{... | collective-permute-start | bytes 2312 | tf_op jit(solution)/shard_map/ppermute | solution.py:320
  43.7 1.0 %collective-permute-done.12.rest_1_ = bf16[4,96]{1,0:T(4,128)(2,1)S(1)} collective-permute-done((bf16[4,96]{1,0:T(4,128)(2,1)S(1)}, bf16[4,96]{1,0:T(4,128)(2,1)S(1)}, u32[]{:S(2)}, u32[]{:S(2)}) %collective-permute-start.12) | collective-permute-done | bytes 800 | tf_op jit(solution)/shard_map/ppermute | solution.py:320
  44.7 1.1 %collective-permute-done.13.rest_2_ = bf16[4,96]{1,0:T(4,128)(2,1)S(1)} collective-permute-done((bf16[4,96]{1,0:T(4,128)(2,1)S(1)}, bf16[4,96]{1,0:T(4,128)(2,1)S(1)}, u32[]{:S(2)}, u32[]{:S(2)}) %collective-permute-start.13) | collective-permute-done | bytes 800 | tf_op jit(solution)/shard_map/ppermute | solution.py:320
  45.8 1.3 %collective-permute-done.14.rest_3_ = bf16[4,96]{1,0:T(4,128)(2,1)S(1)} collective-permute-done((bf16[4,96]{1,0:T(4,128)(2,1)S(1)}, bf16[4,96]{1,0:T(4,128)(2,1)S(1)}, u32[]{:S(2)}, u32[]{:S(2)}) %collective-permute-start.14) | collective-permute-done | bytes 800 | tf_op jit(solution)/shard_map/ppermute | solution.py:320
  47.0 0.8 %shard_map.146 = bf16[4,384]{1,0:T(4,128)(2,1)} custom-call(bf16[384,384]{1,0:T(8,128)(2,1)S(1)} %get-tuple-element.20.ready_ref.route_ref, bf16[4,96]{1,0:T(4,128)(2,1)S(1)} %get-tuple-element.31.rest_0_, bf16[4,96]{1,0:T(4,128)(2,1)S(1)} %collective-permute-done.12.rest_1_, bf16[4,96]{1,0:T(4,128)(2,1)S(1)} %collective-permute-done.13.rest_2_, ...), custom_call_target="tpu_custom_call" | custom-call | flops 1000000000 | tf_op jit(solution)/shard_map/pallas_call | solution.py:40
  (34 shorter events, 2.9 us)
Async XLA Ops:
  1.6 3.7 %copy-start.4 = (s32[1,1,1,384,1]{3,4,2,1,0:T(1,128)S(1)}, s32[1,1,1,384,1]{3,4,2,1,0:T(1,128)}, u32[]{:S(2)}) copy-start(s32[1,1,1,384,1]{3,4,2,1,0:T(1,128)} %param.20) | copy-start | bytes 4612
  1.6 3.7 %copy-start.5 = (s32[1,1,1,384]{3,2,1,0:T(1,128)S(1)}, s32[1,1,1,384]{3,2,1,0:T(1,128)}, u32[]{:S(2)}) copy-start(s32[1,1,1,384]{3,2,1,0:T(1,128)} %param.19) | copy-start | bytes 4612
  1.6 4.8 %collective-permute-start = (bf16[3,32,128]{2,1,0:T(8,128)(2,1)S(1)}, bf16[3,32,128]{2,1,0:T(8,128)(2,1)S(1)}, u32[]{:S(2)}, u32[]{:S(2)}) collective-permute-start(bf16[3,32,128]{2,1,0:T(8,128)(2,1)S(1)} %shard_map.138.after_ref), channel_id=1, source_target_pairs={{0,2},{2,0},{1,3},{3,1},{4,6},{6,4},{5,7},{7,5},{8,10},{10,8},{9,1... | collective-permute-start | bytes 73736 | tf_op jit(solution)/shard_map/ppermute | solution.py:356
  6.4 4.5 %collective-permute-start.1 = (bf16[18,16,128]{2,1,0:T(8,128)(2,1)S(1)}, bf16[18,16,128]{2,1,0:T(8,128)(2,1)S(1)}, u32[]{:S(2)}, u32[]{:S(2)}) collective-permute-start(bf16[18,16,128]{2,1,0:T(8,128)(2,1)S(1)} %get-tuple-element.21), channel_id=1, source_target_pairs={{0,4},{4,0},{8,12},{12,8},{1,5},{5,1},{9,13},{13,9},{2,6},{6,2},{1... | collective-permute-start | bytes 221192 | tf_op jit(solution)/shard_map/ppermute | solution.py:369
  8.6 2.3 %collective-permute-start.2 = (bf16[18,16,128]{2,1,0:T(8,128)(2,1)S(1)}, bf16[18,16,128]{2,1,0:T(8,128)(2,1)S(1)}, u32[]{:S(2)}, u32[]{:S(2)}) collective-permute-start(bf16[18,16,128]{2,1,0:T(8,128)(2,1)S(1)} %get-tuple-element.22), channel_id=1, source_target_pairs={{4,8},{8,4},{5,9},{9,5},{6,10},{10,6},{7,11},{11,7},{20,24},{24,20... | collective-permute-start | bytes 221192 | tf_op jit(solution)/shard_map/ppermute | solution.py:369
  11.2 1.2 %collective-permute-start.3 = (bf16[8,1152]{1,0:T(8,128)(2,1)S(1)}, bf16[8,1152]{1,0:T(8,128)(2,1)S(1)}, u32[]{:S(2)}, u32[]{:S(2)}) collective-permute-start(bf16[8,1152]{1,0:T(8,128)(2,1)S(1)} %shard_map.141), channel_id=1, source_target_pairs={{0,1},{1,0},{2,3},{3,2},{4,5},{5,4},{6,7},{7,6},{8,9},{9,8},{10,11... | collective-permute-start | bytes 55304 | tf_op jit(solution)/shard_map/ppermute | solution.py:377
  12.4 10.5 %copy-start.6 = (f32[384]{0:T(512)S(1)}, f32[384]{0:T(512)}, u32[]{:S(2)}) copy-start(f32[384]{0:T(512)} %param.14) | copy-start | bytes 4612
  12.4 13.8 %copy-start = (bf16[384,2048]{1,0:T(8,128)(2,1)S(1)}, bf16[384,2048]{1,0:T(8,128)(2,1)}, u32[]{:S(2)}) copy-start(bf16[384,2048]{1,0:T(8,128)(2,1)} %shapes_ref.3) | copy-start | bytes 4718596
  14.4 8.6 %collective-permute-start.4 = (bf16[4,96]{1,0:T(4,128)(2,1)S(1)}, bf16[4,96]{1,0:T(4,128)(2,1)S(1)}, u32[]{:S(2)}, u32[]{:S(2)}) collective-permute-start(bf16[4,96]{1,0:T(4,128)(2,1)S(1)} %get-tuple-element.28), channel_id=1, source_target_pairs={{0,12},{4,0},{8,4},{12,8},{1,13},{5,1},{9,5},{13,9},{2,14},{6,2},{... | collective-permute-start | bytes 2312 | tf_op jit(solution)/shard_map/ppermute | solution.py:320
  18.4 4.5 %collective-permute-start.5 = (bf16[4,96]{1,0:T(4,128)(2,1)S(1)}, bf16[4,96]{1,0:T(4,128)(2,1)S(1)}, u32[]{:S(2)}, u32[]{:S(2)}) collective-permute-start(bf16[4,96]{1,0:T(4,128)(2,1)S(1)} %get-tuple-element.29), channel_id=1, source_target_pairs={{0,8},{4,12},{8,0},{12,4},{1,9},{5,13},{9,1},{13,5},{2,10},{6,14},... | collective-permute-start | bytes 2312 | tf_op jit(solution)/shard_map/ppermute | solution.py:320
  20.9 5.4 %collective-permute-start.6 = (bf16[4,96]{1,0:T(4,128)(2,1)S(1)}, bf16[4,96]{1,0:T(4,128)(2,1)S(1)}, u32[]{:S(2)}, u32[]{:S(2)}) collective-permute-start(bf16[4,96]{1,0:T(4,128)(2,1)S(1)} %get-tuple-element.30), channel_id=1, source_target_pairs={{0,4},{4,8},{8,12},{12,0},{1,5},{5,9},{9,13},{13,1},{2,6},{6,10},{... | collective-permute-start | bytes 2312 | tf_op jit(solution)/shard_map/ppermute | solution.py:320
  26.7 1.2 %collective-permute-start.7 = (f32[4,2048]{1,0:T(4,128)S(1)}, f32[4,2048]{1,0:T(4,128)S(1)}, u32[]{:S(2)}, u32[]{:S(2)}) collective-permute-start(f32[4,2048]{1,0:T(4,128)S(1)} %shard_map.144), channel_id=1, source_target_pairs={{0,1},{1,0},{2,3},{3,2},{4,5},{5,4},{6,7},{7,6},{8,9},{9,8},{10,11... | collective-permute-start | bytes 98312 | tf_op jit(solution)/shard_map/ppermute | solution.py:406
  28.0 4.0 %collective-permute-start.8 = (f32[4,2048]{1,0:T(4,128)S(1)}, f32[4,2048]{1,0:T(4,128)S(1)}, u32[]{:S(2)}, u32[]{:S(2)}) collective-permute-start(f32[4,2048]{1,0:T(4,128)S(1)} %add.15), channel_id=1, source_target_pairs={{0,2},{2,0},{1,3},{3,1},{4,6},{6,4},{5,7},{7,5},{8,10},{10,8},{9,1... | collective-permute-start | bytes 98312 | tf_op jit(solution)/shard_map/ppermute | solution.py:406
  32.0 4.7 %collective-permute-start.10 = (bf16[4,2048]{1,0:T(4,128)(2,1)S(1)}, bf16[4,2048]{1,0:T(4,128)(2,1)S(1)}, u32[]{:S(2)}, u32[]{:S(2)}) collective-permute-start(bf16[4,2048]{1,0:T(4,128)(2,1)S(1)} %get-tuple-element.36), channel_id=1, source_target_pairs={{0,8},{4,12},{8,0},{12,4},{1,9},{5,13},{9,1},{13,5},{2,10},{6,14},... | collective-permute-start | bytes 49160 | tf_op jit(solution)/shard_map/ppermute | solution.py:406
  32.1 4.6 %collective-permute-start.11 = (bf16[4,2048]{1,0:T(4,128)(2,1)S(1)}, bf16[4,2048]{1,0:T(4,128)(2,1)S(1)}, u32[]{:S(2)}, u32[]{:S(2)}) collective-permute-start(bf16[4,2048]{1,0:T(4,128)(2,1)S(1)} %get-tuple-element.36), channel_id=1, source_target_pairs={{0,12},{4,0},{8,4},{12,8},{1,13},{5,1},{9,5},{13,9},{2,14},{6,2},{... | collective-permute-start | bytes 49160 | tf_op jit(solution)/shard_map/ppermute | solution.py:406
  34.6 5.5 %collective-permute-start.9 = (bf16[4,2048]{1,0:T(4,128)(2,1)S(1)}, bf16[4,2048]{1,0:T(4,128)(2,1)S(1)}, u32[]{:S(2)}, u32[]{:S(2)}) collective-permute-start(bf16[4,2048]{1,0:T(4,128)(2,1)S(1)} %get-tuple-element.36), channel_id=1, source_target_pairs={{0,4},{4,8},{8,12},{12,0},{1,5},{5,9},{9,13},{13,1},{2,6},{6,10},{... | collective-permute-start | bytes 49160 | tf_op jit(solution)/shard_map/ppermute | solution.py:406
  34.6 5.5 %copy-start.1 = (f32[2,2048]{1,0:T(2,128)S(1)}, f32[2,2048]{1,0:T(2,128)}, u32[]{:S(2)}) copy-start(f32[2,2048]{1,0:T(2,128)} %start_ref.1) | copy-start | bytes 49156
  34.6 5.5 %copy-start.2 = (f32[2048]{0:T(1024)S(1)}, f32[2048]{0:T(1024)}, u32[]{:S(2)}) copy-start(f32[2048]{0:T(1024)} %param.16) | copy-start | bytes 24580
  34.6 5.5 %copy-start.3 = (f32[2048]{0:T(1024)S(1)}, f32[2048]{0:T(1024)}, u32[]{:S(2)}) copy-start(f32[2048]{0:T(1024)} %param.17) | copy-start | bytes 24580
  41.1 3.6 %collective-permute-start.12 = (bf16[4,96]{1,0:T(4,128)(2,1)S(1)}, bf16[4,96]{1,0:T(4,128)(2,1)S(1)}, u32[]{:S(2)}, u32[]{:S(2)}) collective-permute-start(bf16[4,96]{1,0:T(4,128)(2,1)S(1)} %get-tuple-element.32), channel_id=1, source_target_pairs={{0,12},{4,0},{8,4},{12,8},{1,13},{5,1},{9,5},{13,9},{2,14},{6,2},{... | collective-permute-start | bytes 2312 | tf_op jit(solution)/shard_map/ppermute | solution.py:320
  41.3 4.5 %collective-permute-start.13 = (bf16[4,96]{1,0:T(4,128)(2,1)S(1)}, bf16[4,96]{1,0:T(4,128)(2,1)S(1)}, u32[]{:S(2)}, u32[]{:S(2)}) collective-permute-start(bf16[4,96]{1,0:T(4,128)(2,1)S(1)} %get-tuple-element.33), channel_id=1, source_target_pairs={{0,8},{4,12},{8,0},{12,4},{1,9},{5,13},{9,1},{13,5},{2,10},{6,14},... | collective-permute-start | bytes 2312 | tf_op jit(solution)/shard_map/ppermute | solution.py:320
  41.3 5.8 %collective-permute-start.14 = (bf16[4,96]{1,0:T(4,128)(2,1)S(1)}, bf16[4,96]{1,0:T(4,128)(2,1)S(1)}, u32[]{:S(2)}, u32[]{:S(2)}) collective-permute-start(bf16[4,96]{1,0:T(4,128)(2,1)S(1)} %get-tuple-element.34), channel_id=1, source_target_pairs={{0,4},{4,8},{8,12},{12,0},{1,5},{5,9},{9,13},{13,1},{2,6},{6,10},{... | collective-permute-start | bytes 2312 | tf_op jit(solution)/shard_map/ppermute | solution.py:320

commit v3 on v2

--- a/solution.py
+++ b/solution.py
@@ -64,13 +64,6 @@
     after = lax.ppermute(behind, axis, line(count, -1))
     before = lax.ppermute(ahead, axis, line(count, 1))
     return after, before
-
-
-def pairs(count, first):
-    swaps = []
-    for i in range(first, count - 1, 2):
-        swaps += [(i, i + 1), (i + 1, i)]
-    return swaps
 
 
 def route_kernel(buckets, lanes, rows, after_ref, owner_ref, cell_ref, count_ref, route_ref, place_ref):
@@ -130,10 +123,9 @@
     return jnp.where(low, after * keep_after, before * keep_before)
 
 
-def pack_tile_kernel(fields, after_ref, before_ref, ready_ref, *outs):
+def pack_tile_kernel(fields, after_ref, before_ref, *outs):
     layers = fields.shape[1]
-    odd = lax.axis_index("tile") % 2
-    for out, base in zip(outs, ((1 - odd) * (layers - STEPS), odd * (layers - STEPS))):
+    for out, base in zip(outs, (layers - STEPS, 0)):
         for at in range(FIELDS):
             for k in range(STEPS):
                 out[at * STEPS + k] = fields[at, base + k].astype(bf16)
@@ -142,30 +134,24 @@
                 out[FIELDS * STEPS + (at * STEPS + k) // 2] = jnp.concatenate(beside, 0).astype(bf16)
 
 
-def sides(first, second, layers):
-    odd = lax.axis_index("tile") % 2
-    top = STEPS + layers
-    return (first, (1 - odd) * top), (second, odd * top)
-
-
 def end_lanes(lanes):
     row = iota((2 * STEPS, lanes), 0)
     wanted = jnp.where(row < STEPS, row, lanes - 2 * STEPS + row)
     return jnp.where(iota((2 * STEPS, lanes), 1) == wanted, 1.0, 0.0).astype(bf16)
 
 
-def pack_rep_kernel(fields, sub_after, sub_before, tile_first, tile_second, out_ref, wide):
+def pack_rep_kernel(fields, sub_after, sub_before, tile_before, tile_after, ready_ref, out_ref, wide):
     layers, rows, lanes = fields.shape[1:]
     beside = 2 * STEPS
     total = layers + 2 * STEPS
     picks = end_lanes(lanes)
     for at in range(FIELDS):
-        for side, base in sides(tile_first, tile_second, layers):
-            start = pl.multiple_of(base * rows, STEPS * rows)
-            wide[pl.ds(start, STEPS * rows), :] = side[at * STEPS : (at + 1) * STEPS].reshape(STEPS * rows, lanes)
-            start = pl.multiple_of(total * rows + base * beside, STEPS * beside)
+        for side, base in ((tile_before, 0), (tile_after, STEPS + layers)):
+            start = base * rows
+            wide[start : start + STEPS * rows, :] = side[at * STEPS : (at + 1) * STEPS].reshape(STEPS * rows, lanes)
+            start = total * rows + base * beside
             packed = FIELDS * STEPS + at * STEPS // 2
-            wide[pl.ds(start, STEPS * beside), :] = side[packed : packed + STEPS // 2].reshape(STEPS * beside, lanes)
+            wide[start : start + STEPS * beside, :] = side[packed : packed + STEPS // 2].reshape(STEPS * beside, lanes)
         for k in range(layers):
             wide[(STEPS + k) * rows : (STEPS + k + 1) * rows, :] = fields[at, k].astype(bf16)
         for k in range(0, layers, 2):
@@ -177,7 +163,7 @@
 
 
 def window_kernel(
-    fields, sub_after, sub_before, tile_first, tile_second, rep_after, rep_before, place_ref, states, *rest
+    fields, sub_after, sub_before, tile_before, tile_after, rep_after, rep_before, place_ref, states, *rest
 ):
     *sends, now, ago, coef, lapped, seen = rest
     layers, rows, lanes = fields.shape[1:]
@@ -188,6 +174,8 @@
     sub, subs = lax.axis_index("sub"), lax.axis_size("sub")
     rep, reps = lax.axis_index("rep"), lax.axis_size("rep")
 
+    keep_low = jnp.where(tile > 0, 1.0, 0.0)
+    keep_high = jnp.where(tile < tiles - 1, 1.0, 0.0)
     picks = end_lanes(lanes)
     width = total * wide_rows
     end = iota((2 * STEPS, width), 0) < STEPS
@@ -197,25 +185,25 @@
         for k in range(layers):
             out[STEPS + k, :rows, :lanes] = fields[at, k]
             out[STEPS + k, rows:, :lanes] = side_rows(at, 0, k, sub_after, sub_before)
-        for side, base in sides(tile_first, tile_second, layers):
+        for side, base, keep in ((tile_before, 0, keep_low), (tile_after, STEPS + layers, keep_high)):
             for k in range(STEPS):
-                out[base + k, :rows, :lanes] = side[at * STEPS + k].astype(f32)
-                pair = side[FIELDS * STEPS + (at * STEPS + k) // 2].astype(f32)
+                out[base + k, :rows, :lanes] = side[at * STEPS + k].astype(f32) * keep
+                pair = side[FIELDS * STEPS + (at * STEPS + k) // 2].astype(f32) * keep
                 out[base + k, rows:, :lanes] = pair[k % 2 * beside : (k % 2 + 1) * beside]
         after = rep_after[:, at * width : (at + 1) * width].astype(f32) * keep_after
         before = rep_before[:, at * width : (at + 1) * width].astype(f32) * keep_before
         strip = dot(jnp.where(end, after, before).astype(bf16), picks, (0, 0))
         for k in range(total):
-            out[k, :rows, lanes:] = strip[k * rows : (k + 1) * rows]
-            out[k, rows:, lanes:] = strip[total * rows + k * beside : total * rows + (k + 1) * beside]
+            keep = keep_low if k < STEPS else keep_high if k >= STEPS + layers else 1.0
+            out[k, :rows, lanes:] = strip[k * rows : (k + 1) * rows] * keep
+            out[k, rows:, lanes:] = strip[total * rows + k * beside : total * rows + (k + 1) * beside] * keep
 
     row = iota((wide_rows, wide_lanes), 0)
     lane = iota((wide_rows, wide_lanes), 1)
     inside = (row < rows) | ((row < rows + STEPS) & (sub < subs - 1)) | ((row >= rows + STEPS) & (sub > 0))
     inside &= (lane < lanes) | ((lane < lanes + STEPS) & (rep < reps - 1)) | ((lane >= wide_lanes - STEPS) & (rep > 0))
     inside = jnp.where(inside, 1.0, 0.0)
-    inside_low = inside * jnp.where(tile > 0, 1.0, 0.0)
-    inside_high = inside * jnp.where(tile < tiles - 1, 1.0, 0.0)
+    inside_low, inside_high = inside * keep_low, inside * keep_high
 
     def laplace(below, here, above):
         summed = below + above
@@ -358,19 +346,19 @@
         sub_halo = both_ways("sub", *packed)
 
     cells = layers * rows
+    slab = shape_of((FIELDS * STEPS * 3 // 2, rows, lanes), bf16)
+    packed = call(pack_tile_kernel, (slab, slab), (fields, *sub_halo))
     route, place = call(
         functools.partial(route_kernel, buckets, lanes, cells),
         (shape_of((slots, slots), bf16), shape_of((slots, cells + lanes), bf16)),
         (packed[0], slot_owner.reshape(1, slots), slot_cell.reshape(1, slots), surface_count.reshape(1, 1)),
     )
 
-    slab = shape_of((FIELDS * STEPS * 3 // 2, rows, lanes), bf16)
-    packed = call(pack_tile_kernel, (slab, slab), (fields, *sub_halo, route))
-    tile_halo = [lax.ppermute(value, "tile", pairs(buckets, i)) for i, value in enumerate(packed)]
+    tile_halo = [lax.ppermute(value, "tile", shift(buckets, by)) for value, by in zip(packed, (1, -1))]
     packed = call(
         pack_rep_kernel,
         shape_of((2 * STEPS, FIELDS * total * wide_rows), bf16),
-        (fields, *sub_halo, *tile_halo),
+        (fields, *sub_halo, *tile_halo, route),
         scratch=[pltpu.VMEM((total * wide_rows, lanes), bf16)],
     )
     if reps == 2:

time: 48 us -> 46.7 us (0.973)
  starting transfers between devices: 20.7 us -> 18.2 us
  waiting for transfers between devices: 18.6 us -> 20.2 us
    ppermute x6, starting transfers between devices: 10.6 us -> 5.92 us  [exchange(): lax.ppermute(parts[-k], 'tile', shift(buckets, -k))]
    ppermute x6, waiting for transfers between devices: 6.7 us -> 8.43 us  [exchange(): lax.ppermute(parts[-k], 'tile', shift(buckets, -k))]
    ppermute x5, waiting for transfers between devices: 8.48 us -> 6.98 us  [body(): lax.ppermute(sent, axis, shift(count, k))]
    ppermute x2, starting transfers between devices: 2.82 us -> 4.25 us  [body(): lax.ppermute(value, 'tile', shift(buckets, by))]
    ppermute x2, waiting for transfers between devices: 1.67 us -> 2.45 us  [body(): lax.ppermute(value, 'tile', shift(buckets, by))]
    ppermute x5, starting transfers between devices: 4.18 us -> 4.93 us  [body(): lax.ppermute(sent, axis, shift(count, k))]
    ppermute x1, waiting for transfers between devices: 0.54 us -> 1.13 us  [body(): sub_halo = (lax.ppermute(packed[0], 'sub', shift(2, 1)),) * 2]
  transfers between devices with their start and end apart: 15 -> 15, of which waited for: 11 -> 15; matrix products, arithmetic and copies ran while one was open for 1% -> 1% of each run, Pallas kernels for 3% -> 3%
where the time goes in v3:
time: 46.7 us; the launch traced here: 46.5 us
  waiting for transfers between devices  20.2 us (43%)
  starting transfers between devices  18.2 us (39%)
  Pallas kernels  5.29 us (11%)
  between operations  1.37 us (3%)
  other arithmetic  0.94 us (2%)
  local copies, waits for them, and re-layouts  0.6 us (1%)
    ppermute x6, waiting for transfers between devices, exchange(): lax.ppermute(parts[-k], 'tile', shift(buckets, -k))  8.43 us
    ppermute x5, waiting for transfers between devices, body(): lax.ppermute(sent, axis, shift(count, k))  6.98 us
    ppermute x6, starting transfers between devices, exchange(): lax.ppermute(parts[-k], 'tile', shift(buckets, -k))  5.92 us
    pallas_call x9, Pallas kernels, call(): pl.pallas_call(kernel, out_shape=out_shape, in_specs=specs or [VMEM] * le...  5.29 us
    ppermute x5, starting transfers between devices, body(): lax.ppermute(sent, axis, shift(count, k))  4.93 us
    ppermute x2, starting transfers between devices, body(): lax.ppermute(value, 'tile', shift(buckets, by))  4.25 us
    ppermute x1, starting transfers between devices, body(): sub_halo = (lax.ppermute(packed[0], 'sub', shift(2, 1)),) * 2  3 us
    ppermute x2, waiting for transfers between devices, body(): lax.ppermute(value, 'tile', shift(buckets, by))  2.45 us
  transfers between devices with their start and end apart: 15, of which 15 were waited for; matrix products, arithmetic and copies ran while one was open for 1% of the time, Pallas kernels for 3%

profile of v3, /device:TPU:0, one launch (start us, length us, event | category | flops | bytes accessed | tf_op | source)
XLA Modules:
  0.0 46.5 jit_solution(10563468947108545984)
XLA Ops:
  0.6 0.9 %pad_maximum_fusion.fields = f32[3,8,16,128]{3,2,1,0:T(8,128)S(1)} fusion(f32[1,8,16,128]{3,2,1,0:T(8,128)} %bitcast.14, f32[1,8,16,128]{3,2,1,0:T(8,128)} %bitcast.15, f32[1,8,16,128]{3,2,1,0:T(8,128)} %bitcast.16), kind=kLoop, calls=%fused_computation | loop fusion | flops 98304 | bytes 393216 | tf_op jit(solution)/shard_map/stack | solution.py:341
  1.6 3.0 %collective-permute-start = (bf16[3,32,128]{2,1,0:T(8,128)(2,1)S(1)}, bf16[3,32,128]{2,1,0:T(8,128)(2,1)S(1)}, u32[]{:S(2)}, u32[]{:S(2)}) collective-permute-start(bf16[3,32,128]{2,1,0:T(8,128)(2,1)S(1)} %shard_map.138), channel_id=1, source_target_pairs={{0,2},{2,0},{1,3},{3,1},{4,6},{6,4},{5,7},{7,5},{8,10},{10,8},{9,1... | collective-permute-start | bytes 73736 | tf_op jit(solution)/shard_map/ppermute | solution.py:344
  5.3 1.1 %collective-permute-done.after_ref.before_ref.sub_after.sub_before = bf16[3,32,128]{2,1,0:T(8,128)(2,1)S(1)} collective-permute-done((bf16[3,32,128]{2,1,0:T(8,128)(2,1)S(1)}, bf16[3,32,128]{2,1,0:T(8,128)(2,1)S(1)}, u32[]{:S(2)}, u32[]{:S(2)}) %collective-permute-start) | collective-permute-done | bytes 24608 | tf_op jit(solution)/shard_map/ppermute | solution.py:344
  6.4 2.2 %collective-permute-start.1 = (bf16[18,16,128]{2,1,0:T(8,128)(2,1)S(1)}, bf16[18,16,128]{2,1,0:T(8,128)(2,1)S(1)}, u32[]{:S(2)}, u32[]{:S(2)}) collective-permute-start(bf16[18,16,128]{2,1,0:T(8,128)(2,1)S(1)} %get-tuple-element.20.after_ref), channel_id=1, source_target_pairs={{0,4},{4,8},{8,12},{12,0},{1,5},{5,9},{9,13},{13,1},{2,6},{6,10},{... | collective-permute-start | bytes 221192 | tf_op jit(solution)/shard_map/ppermute | solution.py:357
  8.6 2.1 %collective-permute-start.2 = (bf16[18,16,128]{2,1,0:T(8,128)(2,1)S(1)}, bf16[18,16,128]{2,1,0:T(8,128)(2,1)S(1)}, u32[]{:S(2)}, u32[]{:S(2)}) collective-permute-start(bf16[18,16,128]{2,1,0:T(8,128)(2,1)S(1)} %get-tuple-element.21), channel_id=1, source_target_pairs={{0,12},{4,0},{8,4},{12,8},{1,13},{5,1},{9,5},{13,9},{2,14},{6,2},{... | collective-permute-start | bytes 221192 | tf_op jit(solution)/shard_map/ppermute | solution.py:357
  11.3 2.0 %collective-permute-done.1.tile_before = bf16[18,16,128]{2,1,0:T(8,128)(2,1)S(1)} collective-permute-done((bf16[18,16,128]{2,1,0:T(8,128)(2,1)S(1)}, bf16[18,16,128]{2,1,0:T(8,128)(2,1)S(1)}, u32[]{:S(2)}, u32[]{:S(2)}) %collective-permute-start.1) | collective-permute-done | bytes 73760 | tf_op jit(solution)/shard_map/ppermute | solution.py:357
  14.0 1.2 %collective-permute-done.3.rep_after.rep_before = bf16[8,1152]{1,0:T(8,128)(2,1)S(1)} collective-permute-done((bf16[8,1152]{1,0:T(8,128)(2,1)S(1)}, bf16[8,1152]{1,0:T(8,128)(2,1)S(1)}, u32[]{:S(2)}, u32[]{:S(2)}) %collective-permute-start.3) | collective-permute-done | bytes 18464 | tf_op jit(solution)/shard_map/ppermute | solution.py:365
  15.2 1.6 %shard_map.142 = (f32[2,8,16,128]{3,2,1,0:T(8,128)S(1)}, bf16[4,96]{1,0:T(4,128)(2,1)S(1)}, bf16[4,96]{1,0:T(4,128)(2,1)S(1)}, bf16[4,96]{1,0:T(4,128)(2,1)S(1)}, bf16[4,96]{1,0:T(4,128)(2,1)S(1)}) custom-call(f32[3,8,16,128]{3,2,1,0:T(8,128)S(1)} %pad_maximum_fusion.fields, ...), custom_call_target="tpu_custom_call" | custom-call | flops 2000000000 | tf_op jit(solution)/shard_map/pallas_call | solution.py:40
  16.8 3.1 %collective-permute-start.4 = (bf16[4,96]{1,0:T(4,128)(2,1)S(1)}, bf16[4,96]{1,0:T(4,128)(2,1)S(1)}, u32[]{:S(2)}, u32[]{:S(2)}) collective-permute-start(bf16[4,96]{1,0:T(4,128)(2,1)S(1)} %get-tuple-element.28), channel_id=1, source_target_pairs={{0,12},{4,0},{8,4},{12,8},{1,13},{5,1},{9,5},{13,9},{2,14},{6,2},{... | collective-permute-start | bytes 2312 | tf_op jit(solution)/shard_map/ppermute | solution.py:308
  21.3 3.2 %collective-permute-done.5.rest_2_ = bf16[4,96]{1,0:T(4,128)(2,1)S(1)} collective-permute-done((bf16[4,96]{1,0:T(4,128)(2,1)S(1)}, bf16[4,96]{1,0:T(4,128)(2,1)S(1)}, u32[]{:S(2)}, u32[]{:S(2)}) %collective-permute-start.5) | collective-permute-done | bytes 800 | tf_op jit(solution)/shard_map/ppermute | solution.py:308
  24.4 0.9 %collective-permute-done.6.rest_3_ = bf16[4,96]{1,0:T(4,128)(2,1)S(1)} collective-permute-done((bf16[4,96]{1,0:T(4,128)(2,1)S(1)}, bf16[4,96]{1,0:T(4,128)(2,1)S(1)}, u32[]{:S(2)}, u32[]{:S(2)}) %collective-permute-start.6) | collective-permute-done | bytes 800 | tf_op jit(solution)/shard_map/ppermute | solution.py:308
  25.8 1.2 %collective-permute-done.7 = f32[4,2048]{1,0:T(4,128)S(1)} collective-permute-done((f32[4,2048]{1,0:T(4,128)S(1)}, f32[4,2048]{1,0:T(4,128)S(1)}, u32[]{:S(2)}, u32[]{:S(2)}) %collective-permute-start.7) | collective-permute-done | bytes 32800 | tf_op jit(solution)/shard_map/ppermute | solution.py:394
  27.0 1.7 %collective-permute-start.8 = (f32[4,2048]{1,0:T(4,128)S(1)}, f32[4,2048]{1,0:T(4,128)S(1)}, u32[]{:S(2)}, u32[]{:S(2)}) collective-permute-start(f32[4,2048]{1,0:T(4,128)S(1)} %add.15), channel_id=1, source_target_pairs={{0,2},{2,0},{1,3},{3,1},{4,6},{6,4},{5,7},{7,5},{8,10},{10,8},{9,1... | collective-permute-start | bytes 98312 | tf_op jit(solution)/shard_map/ppermute | solution.py:394
  28.7 2.3 %collective-permute-done.8 = f32[4,2048]{1,0:T(4,128)S(1)} collective-permute-done((f32[4,2048]{1,0:T(4,128)S(1)}, f32[4,2048]{1,0:T(4,128)S(1)}, u32[]{:S(2)}, u32[]{:S(2)}) %collective-permute-start.8) | collective-permute-done | bytes 32800 | tf_op jit(solution)/shard_map/ppermute | solution.py:394
  31.0 1.2 %collective-permute-start.10 = (bf16[4,2048]{1,0:T(4,128)(2,1)S(1)}, bf16[4,2048]{1,0:T(4,128)(2,1)S(1)}, u32[]{:S(2)}, u32[]{:S(2)}) collective-permute-start(bf16[4,2048]{1,0:T(4,128)(2,1)S(1)} %get-tuple-element.36), channel_id=1, source_target_pairs={{0,8},{4,12},{8,0},{12,4},{1,9},{5,13},{9,1},{13,5},{2,10},{6,14},... | collective-permute-start | bytes 49160 | tf_op jit(solution)/shard_map/ppermute | solution.py:394
  32.9 1.4 %collective-permute-start.9 = (bf16[4,2048]{1,0:T(4,128)(2,1)S(1)}, bf16[4,2048]{1,0:T(4,128)(2,1)S(1)}, u32[]{:S(2)}, u32[]{:S(2)}) collective-permute-start(bf16[4,2048]{1,0:T(4,128)(2,1)S(1)} %get-tuple-element.36), channel_id=1, source_target_pairs={{0,4},{4,8},{8,12},{12,0},{1,5},{5,9},{9,13},{13,1},{2,6},{6,10},{... | collective-permute-start | bytes 49160 | tf_op jit(solution)/shard_map/ppermute | solution.py:394
  34.9 0.8 %collective-permute-done.10.rest_2_ = bf16[4,2048]{1,0:T(4,128)(2,1)S(1)} collective-permute-done((bf16[4,2048]{1,0:T(4,128)(2,1)S(1)}, bf16[4,2048]{1,0:T(4,128)(2,1)S(1)}, u32[]{:S(2)}, u32[]{:S(2)}) %collective-permute-start.10) | collective-permute-done | bytes 16416 | tf_op jit(solution)/shard_map/ppermute | solution.py:394
  36.1 2.3 %collective-permute-done.9.rest_1_ = bf16[4,2048]{1,0:T(4,128)(2,1)S(1)} collective-permute-done((bf16[4,2048]{1,0:T(4,128)(2,1)S(1)}, bf16[4,2048]{1,0:T(4,128)(2,1)S(1)}, u32[]{:S(2)}, u32[]{:S(2)}) %collective-permute-start.9) | collective-permute-done | bytes 16416 | tf_op jit(solution)/shard_map/ppermute | solution.py:394
  38.4 0.9 %shard_map.145 = (f32[2,2048]{1,0:T(2,128)S(1)}, bf16[4,96]{1,0:T(4,128)(2,1)S(1)}, bf16[4,96]{1,0:T(4,128)(2,1)S(1)}, bf16[4,96]{1,0:T(4,128)(2,1)S(1)}, bf16[4,96]{1,0:T(4,128)(2,1)S(1)}) custom-call(f32[1,2048]{1,0:T(1,128)S(1)} %bitcast.10, f32[1,2048]{1,0:T(1,128)S(1)} %bitcast.11, f32[2,2048]{1,0:T(2,128)S(1)} %copy-done.1, ...), custom_call_target="tpu_custom_call" | custom-call | flops 1000000000 | tf_op jit(solution)/shard_map/pallas_call | solution.py:40
  39.4 0.8 %collective-permute-start.12 = (bf16[4,96]{1,0:T(4,128)(2,1)S(1)}, bf16[4,96]{1,0:T(4,128)(2,1)S(1)}, u32[]{:S(2)}, u32[]{:S(2)}) collective-permute-start(bf16[4,96]{1,0:T(4,128)(2,1)S(1)} %get-tuple-element.32), channel_id=1, source_target_pairs={{0,12},{4,0},{8,4},{12,8},{1,13},{5,1},{9,5},{13,9},{2,14},{6,2},{... | collective-permute-start | bytes 2312 | tf_op jit(solution)/shard_map/ppermute | solution.py:308
  40.4 1.0 %collective-permute-start.14 = (bf16[4,96]{1,0:T(4,128)(2,1)S(1)}, bf16[4,96]{1,0:T(4,128)(2,1)S(1)}, u32[]{:S(2)}, u32[]{:S(2)}) collective-permute-start(bf16[4,96]{1,0:T(4,128)(2,1)S(1)} %get-tuple-element.34), channel_id=1, source_target_pairs={{0,4},{4,8},{8,12},{12,0},{1,5},{5,9},{9,13},{13,1},{2,6},{6,10},{... | collective-permute-start | bytes 2312 | tf_op jit(solution)/shard_map/ppermute | solution.py:308
  42.0 1.0 %collective-permute-done.12.rest_1_ = bf16[4,96]{1,0:T(4,128)(2,1)S(1)} collective-permute-done((bf16[4,96]{1,0:T(4,128)(2,1)S(1)}, bf16[4,96]{1,0:T(4,128)(2,1)S(1)}, u32[]{:S(2)}, u32[]{:S(2)}) %collective-permute-start.12) | collective-permute-done | bytes 800 | tf_op jit(solution)/shard_map/ppermute | solution.py:308
  43.0 1.7 %collective-permute-done.13.rest_2_ = bf16[4,96]{1,0:T(4,128)(2,1)S(1)} collective-permute-done((bf16[4,96]{1,0:T(4,128)(2,1)S(1)}, bf16[4,96]{1,0:T(4,128)(2,1)S(1)}, u32[]{:S(2)}, u32[]{:S(2)}) %collective-permute-start.13) | collective-permute-done | bytes 800 | tf_op jit(solution)/shard_map/ppermute | solution.py:308
  44.7 1.1 %collective-permute-done.14.rest_3_ = bf16[4,96]{1,0:T(4,128)(2,1)S(1)} collective-permute-done((bf16[4,96]{1,0:T(4,128)(2,1)S(1)}, bf16[4,96]{1,0:T(4,128)(2,1)S(1)}, u32[]{:S(2)}, u32[]{:S(2)}) %collective-permute-start.14) | collective-permute-done | bytes 800 | tf_op jit(solution)/shard_map/ppermute | solution.py:308
  (34 shorter events, 6.5 us)
Async XLA Ops:
  1.6 4.8 %collective-permute-start = (bf16[3,32,128]{2,1,0:T(8,128)(2,1)S(1)}, bf16[3,32,128]{2,1,0:T(8,128)(2,1)S(1)}, u32[]{:S(2)}, u32[]{:S(2)}) collective-permute-start(bf16[3,32,128]{2,1,0:T(8,128)(2,1)S(1)} %shard_map.138), channel_id=1, source_target_pairs={{0,2},{2,0},{1,3},{3,1},{4,6},{6,4},{5,7},{7,5},{8,10},{10,8},{9,1... | collective-permute-start | bytes 73736 | tf_op jit(solution)/shard_map/ppermute | solution.py:344
  5.2 5.4 %copy-start.4 = (s32[1,1,1,384,1]{3,4,2,1,0:T(1,128)S(1)}, s32[1,1,1,384,1]{3,4,2,1,0:T(1,128)}, u32[]{:S(2)}) copy-start(s32[1,1,1,384,1]{3,4,2,1,0:T(1,128)} %param.20) | copy-start | bytes 4612
  5.2 5.4 %copy-start.5 = (s32[1,1,1,384]{3,2,1,0:T(1,128)S(1)}, s32[1,1,1,384]{3,2,1,0:T(1,128)}, u32[]{:S(2)}) copy-start(s32[1,1,1,384]{3,2,1,0:T(1,128)} %param.19) | copy-start | bytes 4612
  6.4 6.8 %collective-permute-start.1 = (bf16[18,16,128]{2,1,0:T(8,128)(2,1)S(1)}, bf16[18,16,128]{2,1,0:T(8,128)(2,1)S(1)}, u32[]{:S(2)}, u32[]{:S(2)}) collective-permute-start(bf16[18,16,128]{2,1,0:T(8,128)(2,1)S(1)} %get-tuple-element.20.after_ref), channel_id=1, source_target_pairs={{0,4},{4,8},{8,12},{12,0},{1,5},{5,9},{9,13},{13,1},{2,6},{6,10},{... | collective-permute-start | bytes 221192 | tf_op jit(solution)/shard_map/ppermute | solution.py:357
  8.6 5.1 %collective-permute-start.2 = (bf16[18,16,128]{2,1,0:T(8,128)(2,1)S(1)}, bf16[18,16,128]{2,1,0:T(8,128)(2,1)S(1)}, u32[]{:S(2)}, u32[]{:S(2)}) collective-permute-start(bf16[18,16,128]{2,1,0:T(8,128)(2,1)S(1)} %get-tuple-element.21), channel_id=1, source_target_pairs={{0,12},{4,0},{8,4},{12,8},{1,13},{5,1},{9,5},{13,9},{2,14},{6,2},{... | collective-permute-start | bytes 221192 | tf_op jit(solution)/shard_map/ppermute | solution.py:357
  13.9 1.2 %collective-permute-start.3 = (bf16[8,1152]{1,0:T(8,128)(2,1)S(1)}, bf16[8,1152]{1,0:T(8,128)(2,1)S(1)}, u32[]{:S(2)}, u32[]{:S(2)}) collective-permute-start(bf16[8,1152]{1,0:T(8,128)(2,1)S(1)} %shard_map.141), channel_id=1, source_target_pairs={{0,1},{1,0},{2,3},{3,2},{4,5},{5,4},{6,7},{7,6},{8,9},{9,8},{10,11... | collective-permute-start | bytes 55304 | tf_op jit(solution)/shard_map/ppermute | solution.py:365
  15.2 5.5 %copy-start.6 = (f32[384]{0:T(512)S(1)}, f32[384]{0:T(512)}, u32[]{:S(2)}) copy-start(f32[384]{0:T(512)} %param.14) | copy-start | bytes 4612
  15.2 10.1 %copy-start = (bf16[384,2048]{1,0:T(8,128)(2,1)S(1)}, bf16[384,2048]{1,0:T(8,128)(2,1)}, u32[]{:S(2)}) copy-start(bf16[384,2048]{1,0:T(8,128)(2,1)} %shapes_ref.3) | copy-start | bytes 4718596
  16.8 4.4 %collective-permute-start.4 = (bf16[4,96]{1,0:T(4,128)(2,1)S(1)}, bf16[4,96]{1,0:T(4,128)(2,1)S(1)}, u32[]{:S(2)}, u32[]{:S(2)}) collective-permute-start(bf16[4,96]{1,0:T(4,128)(2,1)S(1)} %get-tuple-element.28), channel_id=1, source_target_pairs={{0,12},{4,0},{8,4},{12,8},{1,13},{5,1},{9,5},{13,9},{2,14},{6,2},{... | collective-permute-start | bytes 2312 | tf_op jit(solution)/shard_map/ppermute | solution.py:308
  20.0 4.5 %collective-permute-start.5 = (bf16[4,96]{1,0:T(4,128)(2,1)S(1)}, bf16[4,96]{1,0:T(4,128)(2,1)S(1)}, u32[]{:S(2)}, u32[]{:S(2)}) collective-permute-start(bf16[4,96]{1,0:T(4,128)(2,1)S(1)} %get-tuple-element.29), channel_id=1, source_target_pairs={{0,8},{4,12},{8,0},{12,4},{1,9},{5,13},{9,1},{13,5},{2,10},{6,14},... | collective-permute-start | bytes 2312 | tf_op jit(solution)/shard_map/ppermute | solution.py:308
  20.0 5.4 %collective-permute-start.6 = (bf16[4,96]{1,0:T(4,128)(2,1)S(1)}, bf16[4,96]{1,0:T(4,128)(2,1)S(1)}, u32[]{:S(2)}, u32[]{:S(2)}) collective-permute-start(bf16[4,96]{1,0:T(4,128)(2,1)S(1)} %get-tuple-element.30), channel_id=1, source_target_pairs={{0,4},{4,8},{8,12},{12,0},{1,5},{5,9},{9,13},{13,1},{2,6},{6,10},{... | collective-permute-start | bytes 2312 | tf_op jit(solution)/shard_map/ppermute | solution.py:308
  25.8 1.2 %collective-permute-start.7 = (f32[4,2048]{1,0:T(4,128)S(1)}, f32[4,2048]{1,0:T(4,128)S(1)}, u32[]{:S(2)}, u32[]{:S(2)}) collective-permute-start(f32[4,2048]{1,0:T(4,128)S(1)} %shard_map.144), channel_id=1, source_target_pairs={{0,1},{1,0},{2,3},{3,2},{4,5},{5,4},{6,7},{7,6},{8,9},{9,8},{10,11... | collective-permute-start | bytes 98312 | tf_op jit(solution)/shard_map/ppermute | solution.py:394
  27.0 4.0 %collective-permute-start.8 = (f32[4,2048]{1,0:T(4,128)S(1)}, f32[4,2048]{1,0:T(4,128)S(1)}, u32[]{:S(2)}, u32[]{:S(2)}) collective-permute-start(f32[4,2048]{1,0:T(4,128)S(1)} %add.15), channel_id=1, source_target_pairs={{0,2},{2,0},{1,3},{3,1},{4,6},{6,4},{5,7},{7,5},{8,10},{10,8},{9,1... | collective-permute-start | bytes 98312 | tf_op jit(solution)/shard_map/ppermute | solution.py:394
  31.0 4.7 %collective-permute-start.10 = (bf16[4,2048]{1,0:T(4,128)(2,1)S(1)}, bf16[4,2048]{1,0:T(4,128)(2,1)S(1)}, u32[]{:S(2)}, u32[]{:S(2)}) collective-permute-start(bf16[4,2048]{1,0:T(4,128)(2,1)S(1)} %get-tuple-element.36), channel_id=1, source_target_pairs={{0,8},{4,12},{8,0},{12,4},{1,9},{5,13},{9,1},{13,5},{2,10},{6,14},... | collective-permute-start | bytes 49160 | tf_op jit(solution)/shard_map/ppermute | solution.py:394
  32.2 3.9 %collective-permute-start.11 = (bf16[4,2048]{1,0:T(4,128)(2,1)S(1)}, bf16[4,2048]{1,0:T(4,128)(2,1)S(1)}, u32[]{:S(2)}, u32[]{:S(2)}) collective-permute-start(bf16[4,2048]{1,0:T(4,128)(2,1)S(1)} %get-tuple-element.36), channel_id=1, source_target_pairs={{0,12},{4,0},{8,4},{12,8},{1,13},{5,1},{9,5},{13,9},{2,14},{6,2},{... | collective-permute-start | bytes 49160 | tf_op jit(solution)/shard_map/ppermute | solution.py:394
  32.9 5.5 %collective-permute-start.9 = (bf16[4,2048]{1,0:T(4,128)(2,1)S(1)}, bf16[4,2048]{1,0:T(4,128)(2,1)S(1)}, u32[]{:S(2)}, u32[]{:S(2)}) collective-permute-start(bf16[4,2048]{1,0:T(4,128)(2,1)S(1)} %get-tuple-element.36), channel_id=1, source_target_pairs={{0,4},{4,8},{8,12},{12,0},{1,5},{5,9},{9,13},{13,1},{2,6},{6,10},{... | collective-permute-start | bytes 49160 | tf_op jit(solution)/shard_map/ppermute | solution.py:394
  34.2 4.2 %copy-start.1 = (f32[2,2048]{1,0:T(2,128)S(1)}, f32[2,2048]{1,0:T(2,128)}, u32[]{:S(2)}) copy-start(f32[2,2048]{1,0:T(2,128)} %start_ref.1) | copy-start | bytes 49156
  34.2 4.2 %copy-start.2 = (f32[2048]{0:T(1024)S(1)}, f32[2048]{0:T(1024)}, u32[]{:S(2)}) copy-start(f32[2048]{0:T(1024)} %param.16) | copy-start | bytes 24580
  34.2 4.2 %copy-start.3 = (f32[2048]{0:T(1024)S(1)}, f32[2048]{0:T(1024)}, u32[]{:S(2)}) copy-start(f32[2048]{0:T(1024)} %param.17) | copy-start | bytes 24580
  39.4 3.6 %collective-permute-start.12 = (bf16[4,96]{1,0:T(4,128)(2,1)S(1)}, bf16[4,96]{1,0:T(4,128)(2,1)S(1)}, u32[]{:S(2)}, u32[]{:S(2)}) collective-permute-start(bf16[4,96]{1,0:T(4,128)(2,1)S(1)} %get-tuple-element.32), channel_id=1, source_target_pairs={{0,12},{4,0},{8,4},{12,8},{1,13},{5,1},{9,5},{13,9},{2,14},{6,2},{... | collective-permute-start | bytes 2312 | tf_op jit(solution)/shard_map/ppermute | solution.py:308
  40.2 4.5 %collective-permute-start.13 = (bf16[4,96]{1,0:T(4,128)(2,1)S(1)}, bf16[4,96]{1,0:T(4,128)(2,1)S(1)}, u32[]{:S(2)}, u32[]{:S(2)}) collective-permute-start(bf16[4,96]{1,0:T(4,128)(2,1)S(1)} %get-tuple-element.33), channel_id=1, source_target_pairs={{0,8},{4,12},{8,0},{12,4},{1,9},{5,13},{9,1},{13,5},{2,10},{6,14},... | collective-permute-start | bytes 2312 | tf_op jit(solution)/shard_map/ppermute | solution.py:308
  40.4 5.4 %collective-permute-start.14 = (bf16[4,96]{1,0:T(4,128)(2,1)S(1)}, bf16[4,96]{1,0:T(4,128)(2,1)S(1)}, u32[]{:S(2)}, u32[]{:S(2)}) collective-permute-start(bf16[4,96]{1,0:T(4,128)(2,1)S(1)} %get-tuple-element.34), channel_id=1, source_target_pairs={{0,4},{4,8},{8,12},{12,0},{1,5},{5,9},{9,13},{13,1},{2,6},{6,10},{... | collective-permute-start | bytes 2312 | tf_op jit(solution)/shard_map/ppermute | solution.py:308

commit v4 on v3

v4 whole, which is shorter than its diff:
```python
import functools

import jax
import jax.numpy as jnp
from jax import lax
from jax.experimental import pallas as pl
from jax.experimental.pallas import tpu as pltpu
from jax.sharding import PartitionSpec as P

STEPS = 4
FIELDS = 3
SUBLANES = 8

nonlinear = 0.03
viscous = 0.02

f32 = jnp.float32
bf16 = jnp.bfloat16
VMEM = pl.BlockSpec(memory_space=pltpu.VMEM)
HBM = pl.BlockSpec(memory_space=pltpu.HBM)


def shift(count, by):
    return [(i, (i + by) % count) for i in range(count)]


def line(count, by):
    return [(i, i + by) for i in range(count) if 0 <= i + by < count]


def swaps(count, by):
    return [(i, i ^ by) for i in range(count)]


def iota(shape, dim):
    return lax.broadcasted_iota(jnp.int32, shape, dim)


def dot(a, b, contract):
    return lax.dot_general(a, b, (((contract[0],), (contract[1],)), ((), ())), preferred_element_type=f32)


def call(kernel, out_shape, inputs, scratch=(), specs=None, out_specs=None, micros=1.0, vmem=32):
    return pl.pallas_call(
        kernel,
        out_shape=out_shape,
        in_specs=specs or [VMEM] * len(inputs),
        out_specs=out_specs or jax.tree.map(lambda _: VMEM, out_shape),
        scratch_shapes=list(scratch),
        cost_estimate=pl.CostEstimate(flops=int(micros * 1e9), bytes_accessed=0, transcendentals=0),
        compiler_params=pltpu.CompilerParams(vmem_limit_bytes=vmem * 1024 * 1024),
    )(*inputs)


def shape_of(dims, dtype):
    return jax.ShapeDtypeStruct(dims, dtype)


def fetch(pairs, sems):
    copies = [pltpu.make_async_copy(a, b, sems.at[i]) for i, (a, b) in enumerate(pairs)]
    for copy in copies:
        copy.start()
    return copies


def both_ways(axis, ahead, behind):
    count = lax.axis_size(axis)
    after = lax.ppermute(behind, axis, line(count, -1))
    before = lax.ppermute(ahead, axis, line(count, 1))
    return after, before


def route_kernel(buckets, lanes, rows, after_ref, owner_ref, cell_ref, count_ref, route_ref, place_ref):
    slots = owner_ref.shape[1]
    bucket = slots // buckets
    me = lax.axis_index("tile")
    owner = owner_ref[...]
    live = iota((1, slots), 1) < count_ref[...]
    held = -(-buckets // SUBLANES) * SUBLANES
    member = jnp.where((iota((held, slots), 0) == owner) & live, 1.0, 0.0)
    earlier = jnp.where(iota((slots, slots), 0) < iota((slots, slots), 1), 1.0, 0.0).astype(bf16)
    before = dot(member.astype(bf16), earlier, (1, 0))
    rank = jnp.sum(before * member, axis=0, keepdims=True).astype(jnp.int32)
    target = jnp.where(live, (owner ^ me) * bucket + rank, -1)
    route = jnp.where(iota((slots, slots), 0) == target, 1.0, 0.0).astype(bf16)
    route_ref[...] = route
    cell = cell_ref[...]
    row = jnp.where(iota((rows, slots), 0) == cell // lanes, 1.0, 0.0)
    lane = jnp.where(iota((lanes, slots), 0) == cell % lanes, 1.0, 0.0)
    place_ref[:, :rows] = dot(route, row.astype(bf16), (1, 1)).astype(bf16)
    place_ref[:, rows:] = dot(route, lane.astype(bf16), (1, 1)).astype(bf16)


def pack_sub_kernel(sides, fields, *outs):
    layers, rows, lanes = fields.shape[1:]
    low = iota((SUBLANES, lanes), 0) < STEPS
    for at in range(FIELDS):
        for pair in range(layers // 2):
            tiles = []
            for layer in (2 * pair, 2 * pair + 1):
                last = pltpu.roll(fields[at, layer, rows - SUBLANES :, :], STEPS, 0)
                first = fields[at, layer, :SUBLANES, :]
                tiles.append((last, first))
            picked = [jnp.where(low, a, pltpu.roll(b, STEPS, 0)) for a, b in zip(*tiles)]
            if sides == 1:
                picked = [jnp.where(lax.axis_index("sub") == 0, picked[0], picked[1])]
            for out, value in zip(outs, picked):
                out[at, pair * SUBLANES : (pair + 1) * SUBLANES, :] = value.astype(bf16)


def side_rows(at, base, k, after_ref, before_ref):
    start = base // 2 * SUBLANES + k // 2 * SUBLANES
    if not isinstance(start, int):
        start = pl.multiple_of(start, SUBLANES)
    after = after_ref[at, pl.ds(start, SUBLANES), :].astype(f32)
    before = before_ref[at, pl.ds(start, SUBLANES), :].astype(f32)
    if k % 2 == 0:
        before = pltpu.roll(before, STEPS, 0)
    else:
        after = pltpu.roll(after, STEPS, 0)
    me, count = lax.axis_index("sub"), lax.axis_size("sub")
    low = iota(after.shape, 0) < STEPS
    keep_after = jnp.where(me < count - 1, 1.0, 0.0)
    keep_before = jnp.where(me > 0, 1.0, 0.0)
    return jnp.where(low, after * keep_after, before * keep_before)


def pack_tile_kernel(fields, after_ref, before_ref, *outs):
    layers = fields.shape[1]
    for out, base in zip(outs, (layers - STEPS, 0)):
        for at in range(FIELDS):
            for k in range(STEPS):
                out[at * STEPS + k] = fields[at, base + k].astype(bf16)
            for k in range(0, STEPS, 2):
                beside = [side_rows(at, base, k + i, after_ref, before_ref) for i in range(2)]
                out[FIELDS * STEPS + (at * STEPS + k) // 2] = jnp.concatenate(beside, 0).astype(bf16)


def pack_rep_kernel(fields, sub_after, sub_before, tile_before, tile_after, ready_ref, out_ref, ends_ref):
    layers, rows, lanes = fields.shape[1:]
    beside = 2 * STEPS
    total = layers + 2 * STEPS
    layer_of = iota((rows + beside, lanes), 1) // beside
    for at in range(FIELDS):
        packed = jnp.zeros((rows + beside, lanes), f32)
        for k in range(total):
            own = k - STEPS
            if 0 <= own < layers:
                here = fields[at, own], side_rows(at, 0, own, sub_after, sub_before)
            else:
                side, depth = (tile_before, k) if k < STEPS else (tile_after, own - layers)
                pair = side[FIELDS * STEPS + (at * STEPS + depth) // 2].astype(f32)
                here = side[at * STEPS + depth].astype(f32), pair[depth % 2 * beside : (depth % 2 + 1) * beside]
            here = jnp.concatenate(here, 0)
            packed = jnp.where(layer_of == k, pltpu.roll(here, (beside * k + STEPS) % lanes, 1), packed)
        out_ref[at] = packed.astype(bf16)
        ends_ref[at] = packed


def across(value):
    return pltpu.roll(value, 1, 0) + pltpu.roll(value, value.shape[0] - 1, 0)


def beside_lanes(value):
    lanes = value.shape[1]
    lane = iota(value.shape, 1)
    left = jnp.where(lane == 0, 0.0, pltpu.roll(value, 1, 1))
    right = jnp.where(lane == lanes - 1, 0.0, pltpu.roll(value, lanes - 1, 1))
    return left + right


def laplace(below, here, above):
    return below + above + across(here) + beside_lanes(here) - 6.0 * here


def row_masks(layers, rows, lanes):
    tile, sub = lax.axis_index("tile"), lax.axis_index("sub")
    keep_low, keep_high = jnp.where(tile > 0, 1.0, 0.0), jnp.where(tile < lax.axis_size("tile") - 1, 1.0, 0.0)
    keep_before, keep_after = jnp.where(sub > 0, 1.0, 0.0), jnp.where(sub < lax.axis_size("sub") - 1, 1.0, 0.0)
    row = iota((rows + 2 * STEPS, lanes), 0)
    inside = jnp.where(row < rows, 1.0, jnp.where(row < rows + STEPS, keep_after, keep_before))
    return inside * keep_low, inside, inside * keep_high


def assemble_kernel(
    fields, sub_after, sub_before, tile_before, tile_after, ready_ref, now, ago, coef, lapped, lapped_ago
):
    layers, rows, lanes = fields.shape[1:]
    beside = 2 * STEPS
    total = layers + 2 * STEPS
    tile = lax.axis_index("tile")
    keep_low, keep_high = jnp.where(tile > 0, 1.0, 0.0), jnp.where(tile < lax.axis_size("tile") - 1, 1.0, 0.0)
    for at, out in enumerate((now, ago, coef)):
        extra = viscous if at == 2 else 0.0
        for k in range(layers):
            out[STEPS + k, :rows] = fields[at, k] + extra
            out[STEPS + k, rows:] = side_rows(at, 0, k, sub_after, sub_before) + extra
        for side, base, keep in ((tile_before, 0, keep_low), (tile_after, STEPS + layers, keep_high)):
            for k in range(STEPS):
                out[base + k, :rows] = side[at * STEPS + k].astype(f32) * keep + extra
                pair = side[FIELDS * STEPS + (at * STEPS + k) // 2].astype(f32) * keep
                out[base + k, rows:] = pair[k % 2 * beside : (k % 2 + 1) * beside] + extra
    for value, out in ((now, lapped), (ago, lapped_ago)):
        for k in range(1, total - 1):
            out[k] = laplace(value[k - 1], value[k], value[k + 1])


def window_kernel(
    now_in, ago_in, coef, lapped_in, lapped_ago_in, ends_ref, rep_after, rep_before, place_ref, states, *rest
):
    *sends, now, ago, lapped, seen = rest
    layers, rows, lanes = states.shape[1:]
    beside = 2 * STEPS
    total, wide_rows = now.shape[:2]
    rep, reps = lax.axis_index("rep"), lax.axis_size("rep")
    keep_left, keep_right = jnp.where(rep > 0, 1.0, 0.0), jnp.where(rep < reps - 1, 1.0, 0.0)
    inside_low, inside, inside_high = row_masks(layers, rows, lanes)

    lane = iota((wide_rows, lanes), 1)
    layer_of = lane // beside
    outer = lane % beside < STEPS
    ending = (lane == 0) | (lane == lanes - 1)
    inside_side = jnp.where(layer_of < STEPS, inside_low, jnp.where(layer_of < STEPS + layers, inside, inside_high))
    inside_side = jnp.where(layer_of < total, inside_side, 0.0)
    inside_left = inside_side * jnp.where(outer, keep_left, 1.0)
    inside_right = inside_side * jnp.where(outer, 1.0, keep_right)
    lefts, rights = [], []
    for at in range(FIELDS):
        extra = viscous if at == 2 else 0.0
        left = jnp.where(outer, rep_before[at].astype(f32), ends_ref[at])
        right = jnp.where(outer, ends_ref[at], rep_after[at].astype(f32))
        lefts.append(left * inside_left + extra)
        rights.append(right * inside_right + extra)
    left_now, left_ago, left_coef = lefts
    right_now, right_ago, right_coef = rights

    def edges(left, right):
        return jnp.where(outer, pltpu.roll(right, lanes - 1, 1), pltpu.roll(left, 1, 1))

    def edge_of(k, edge):
        return jnp.where(ending, pltpu.roll(edge, (lanes - beside * k - STEPS) % lanes, 1), 0.0)

    def laplace_side(side):
        beyond = pltpu.roll(side, beside, 1) + pltpu.roll(side, lanes - beside, 1)
        return beyond + across(side) + pltpu.roll(side, 1, 1) + pltpu.roll(side, lanes - 1, 1) - 6.0 * side

    def advance(here, before, gain, lap, lap_before, mask):
        change = here - before
        driving = gain * lap - lap_before + 2.0 * nonlinear * change * change
        return (here + change + (1.0 + 2.0 * nonlinear * here) * driving) * mask

    edge_ago = edges(left_ago, right_ago)
    left_lapped, right_lapped = viscous * laplace_side(left_ago), viscous * laplace_side(right_ago)

    cells = layers * rows
    slots = place_ref.shape[0]
    lane_of = place_ref[:, cells:].astype(f32)
    loads = jnp.zeros((SUBLANES, slots), f32)
    for step in range(STEPS):
        edge = edges(left_now, right_now)
        source = now_in if step == 0 else now
        below, here = source[step], source[step + 1]
        for k in range(step + 1, total - step - 1):
            above = source[k + 1]
            if step == 0:
                lap, before = lapped_in[k], ago_in[k]
                lap_before = viscous * (lapped_ago_in[k] + edge_of(k, edge_ago))
            else:
                lap, before, lap_before = laplace(below, here, above), ago[k], lapped[k]
            lap = lap + edge_of(k, edge)
            mask = inside_low if k < STEPS else inside_high if k >= STEPS + layers else inside
            updated = advance(here, before, coef[k], lap, lap_before, mask)
            now[k] = updated
            ago[k] = here
            lapped[k] = viscous * lap
            own = k - STEPS
            if 0 <= own < layers:
                core = updated[:rows]
                seen[own * rows : (own + 1) * rows, :] = core.astype(bf16)
                if step >= STEPS - 2:
                    states[STEPS - 1 - step, own] = core
            below, here = here, above
        if step < STEPS - 1:
            lap = laplace_side(left_now)
            updated = advance(left_now, left_ago, left_coef, lap, left_lapped, inside_left)
            left_now, left_ago, left_lapped = updated, left_now, viscous * lap
            lap = laplace_side(right_now)
            updated = advance(right_now, right_ago, right_coef, lap, right_lapped, inside_right)
            right_now, right_ago, right_lapped = updated, right_now, viscous * lap
        found = (dot(place_ref[:, :cells], seen[...], (1, 0)) * lane_of).astype(bf16)
        summed = dot(jnp.ones((SUBLANES, lanes), bf16), found, (1, 1))
        loads = jnp.where(iota((SUBLANES, slots), 0) == step, summed, loads)

    size = slots // len(sends)
    for at, send in enumerate(sends):
        send[...] = loads[:STEPS, at * size : (at + 1) * size].astype(bf16)


def store_kernel(states, final_hbm, prior_hbm, sems):
    for copy in fetch(((states.at[0], final_hbm), (states.at[1], prior_hbm)), sems):
        copy.wait()


def spread(at, size, total, bucket):
    entry = iota((size, 1), 0) + at * size
    part = at if size == bucket else entry // bucket
    wanted = entry + ((part ^ lax.axis_index("tile")) - part) * bucket
    return jnp.where(iota((size, total), 1) == wanted, 1.0, 0.0).astype(bf16)


def project_kernel(order, buckets, area_ref, shapes_ref, *rest):
    *parts, out_ref = rest
    total = area_ref.shape[1]
    size = parts[0].shape[1]
    loads = 0.0
    for at, part in zip(order, parts):
        loads = loads + dot(part[...], spread(at, size, total, total // buckets), (1, 0))
    weighted = (loads * area_ref[...]).astype(bf16)
    out_ref[...] = dot(weighted, shapes_ref[...], (1, 0))


def respond_kernel(buckets, addends, freq_ref, damp_ref, start_ref, shapes_ref, *rest):
    forces_in, rest = rest[:addends], rest[addends:]
    state_ref, *sends, accel = rest
    forces = forces_in[0][...]
    for ref in forces_in[1:]:
        forces = forces + ref[...].astype(f32)
    frequency, damping = freq_ref[...], damp_ref[...]
    drag, stiffness = 2.0 * damping * frequency, frequency * frequency
    displace, velocity = start_ref[0:1, :], start_ref[1:2, :]
    accel[...] = jnp.zeros_like(accel)
    for step in range(STEPS):
        acceleration = forces[step : step + 1, :] - drag * velocity - stiffness * displace
        velocity = velocity + acceleration
        displace = displace + velocity
        accel[step : step + 1, :] = acceleration
    state_ref[0:1, :] = displace
    state_ref[1:2, :] = velocity
    node = dot(accel[...].astype(bf16), shapes_ref[...], (1, 1)).astype(bf16)
    total = node.shape[1]
    size = total // len(sends)
    for at, send in enumerate(sends):
        send[...] = dot(node, spread(at, size, total, total // buckets), (1, 1))[:STEPS].astype(bf16)


def return_kernel(order, route_ref, *rest):
    *parts, out_ref = rest
    size = parts[0].shape[1]
    surface = 0.0
    for at, part in zip(order, parts):
        surface = surface + dot(part[...], route_ref[at * size : (at + 1) * size, :], (1, 0))
    out_ref[...] = surface.astype(bf16)


def exchange(parts, order):
    buckets = lax.axis_size("tile")
    if len(parts) == buckets:
        return [lax.ppermute(parts[k], "tile", swaps(buckets, k)) if k else parts[0] for k in order]
    tiles = jnp.arange(buckets) ^ lax.axis_index("tile")
    (whole,) = parts
    steps, total = whole.shape
    stacked = whole.reshape(steps, buckets, total // buckets).transpose(1, 0, 2)
    stacked = lax.all_to_all(stacked[tiles], "tile", 0, 0, tiled=True)
    return [stacked[tiles].transpose(1, 0, 2).reshape(steps, total)]


def body(
    pressure,
    previous_pressure,
    courant_square,
    node_area,
    mode_shapes,
    frequency,
    damping_ratio,
    modal_start,
    slot_cell,
    slot_owner,
    surface_count,
):
    buckets, subs, reps = (lax.axis_size(axis) for axis in ("tile", "sub", "rep"))
    layers, rows, lanes = pressure.shape
    slots = slot_cell.shape[-1]
    modes = mode_shapes.shape[1]
    bucket = slots // buckets
    parts = buckets if buckets in (2, 4) and bucket % 16 == 0 else 1
    total = layers + 2 * STEPS
    wide_rows = rows + 2 * STEPS

    sides = 1 if subs == 2 else 2
    slab = shape_of((FIELDS, layers * STEPS, lanes), bf16)
    fields = jnp.stack([pressure, previous_pressure, courant_square])
    packed = call(functools.partial(pack_sub_kernel, sides), (slab,) * sides, (fields,))
    if subs == 2:
        sub_halo = (lax.ppermute(packed[0], "sub", shift(2, 1)),) * 2
    else:
        sub_halo = both_ways("sub", *packed)

    cells = layers * rows
    slab = shape_of((FIELDS * STEPS * 3 // 2, rows, lanes), bf16)
    packed = call(pack_tile_kernel, (slab, slab), (fields, *sub_halo))
    route, place = call(
        functools.partial(route_kernel, buckets, lanes, cells),
        (shape_of((slots, slots), bf16), shape_of((slots, cells + lanes), bf16)),
        (packed[0], slot_owner.reshape(1, slots), slot_cell.reshape(1, slots), surface_count.reshape(1, 1)),
    )

    tile_halo = [lax.ppermute(value, "tile", shift(buckets, by)) for value, by in zip(packed, (1, -1))]
    packed, ends = call(
        pack_rep_kernel,
        (shape_of((FIELDS, wide_rows, lanes), bf16), shape_of((FIELDS, wide_rows, lanes), f32)),
        (fields, *sub_halo, *tile_halo, route),
    )
    if reps == 2:
        rep_halo = (lax.ppermute(packed, "rep", shift(2, 1)),) * 2
    else:
        rep_halo = both_ways("rep", packed, packed)

    wide = shape_of((total, wide_rows, lanes), f32)
    assembled = call(assemble_kernel, (wide,) * 5, (fields, *sub_halo, *tile_halo, packed))
    wide = pltpu.VMEM(wide.shape, f32)
    part = shape_of((STEPS, slots // parts), bf16)
    block = shape_of(pressure.shape, f32)
    states, *sends = call(
        window_kernel,
        (shape_of((2, layers, rows, lanes), f32),) + (part,) * parts,
        (*assembled, ends, *rep_halo, place),
        scratch=[wide] * 3 + [pltpu.VMEM((cells, lanes), bf16)],
        micros=2.0,
    )
    final_field, prior_field = call(
        store_kernel, (block, block), (states,), out_specs=(HBM, HBM), scratch=[pltpu.SemaphoreType.DMA((2,))]
    )

    order = [k for k in (0, 2, 3, 1) if k < parts]
    forces = call(
        functools.partial(project_kernel, order, buckets),
        shape_of((STEPS, modes), f32),
        (node_area.reshape(1, slots), mode_shapes, *exchange(sends, order)),
    )
    addends = [forces]
    for axis in ("rep", "sub", "tile"):
        count = lax.axis_size(axis)
        forces = functools.reduce(jnp.add, addends)
        if count in (2, 4):
            sent = forces.astype(bf16) if axis != "rep" else forces
            addends = [forces] + [lax.ppermute(sent, axis, swaps(count, k)) for k in (1, 3, 2) if k < count]
        else:
            addends = [lax.psum(forces, axis)]

    state, *sends = call(
        functools.partial(respond_kernel, buckets, len(addends)),
        (shape_of((2, modes), f32),) + (part,) * parts,
        (frequency.reshape(1, modes), damping_ratio.reshape(1, modes), modal_start, mode_shapes, *addends),
        scratch=[pltpu.VMEM((SUBLANES, modes), f32)],
    )
    share = modes // (buckets * subs * reps)
    modal_state = lax.dynamic_slice_in_dim(state, lax.axis_index(("tile", "sub", "rep")) * share, share, 1)
    order = [k for k in (0, 3, 2, 1) if k < parts]
    surface = call(
        functools.partial(return_kernel, order), shape_of((STEPS, slots), bf16), (route, *exchange(sends, order))
    )
    return (final_field, prior_field, surface.reshape(1, 1, 1, STEPS, slots), modal_state)


def solution(mesh):
    in_specs = (
        P(("groups", "tile"), "sub", "rep"),
        P(("groups", "tile"), "sub", "rep"),
        P(("groups", "tile"), "sub", "rep"),
        P(("groups", "tile", "sub", "rep")),
        P(("groups", "tile", "sub", "rep"), None),
        P("groups"),
        P("groups"),
        P(None, "groups"),
        P(("groups", "tile"), "sub", "rep", None),
        P(("groups", "tile"), "sub", "rep", None, None),
        P(("groups", "sub"), "rep", "tile"),
    )
    out_specs = (
        P(("groups", "tile"), "sub", "rep"),
        P(("groups", "tile"), "sub", "rep"),
        P(("groups", "tile"), "sub", "rep", None, None),
        P(None, ("groups", "tile", "sub", "rep")),
    )
    return jax.shard_map(body, mesh=mesh, in_specs=in_specs, out_specs=out_specs, check_vma=False)
```

time: 46.7 us -> 44.4 us (0.951)
  waiting for transfers between devices: 20.2 us -> 14.6 us
  starting transfers between devices: 18.2 us -> 21.4 us
    ppermute x11, waiting for transfers between devices: 15.4 us -> 10.1 us  [the longest x5 5.06 us: body(): lax.ppermute(sent, axis, swaps(count, k))]
    ppermute x11, starting transfers between devices: 10.9 us -> 14.1 us  [the longest x6 8.11 us: exchange(): lax.ppermute(parts[k], 'tile', swaps(buckets, k))]
    pallas_call x9 -> x10, Pallas kernels: 5.29 us -> 5.24 us  [call(): pl.pallas_call(kernel, out_shape=out_shape, in_specs=specs or [VMEM] * le...]
  transfers between devices with their start and end apart: 15 -> 15, of which waited for: 15 -> 13; matrix products, arithmetic and copies ran while one was open for 1% -> 1% of each run, Pallas kernels for 3% -> 3%
where the time goes in v4:
time: 44.4 us; the launch traced here: 44.2 us
  starting transfers between devices  21.4 us (48%)
  waiting for transfers between devices  14.6 us (33%)
  Pallas kernels  5.24 us (12%)
  between operations  1.39 us (3%)
  other arithmetic  0.95 us (2%)
  local copies, waits for them, and re-layouts  0.6 us (1%)
    ppermute x6, starting transfers between devices, exchange(): lax.ppermute(parts[k], 'tile', swaps(buckets, k))  8.11 us
    ppermute x5, starting transfers between devices, body(): lax.ppermute(sent, axis, swaps(count, k))  6.01 us
    pallas_call x10, Pallas kernels, call(): pl.pallas_call(kernel, out_shape=out_shape, in_specs=specs or [VMEM] * le...  5.24 us
    ppermute x5, waiting for transfers between devices, body(): lax.ppermute(sent, axis, swaps(count, k))  5.06 us
    ppermute x6, waiting for transfers between devices, exchange(): lax.ppermute(parts[k], 'tile', swaps(buckets, k))  5.03 us
    ppermute x2, starting transfers between devices, body(): lax.ppermute(value, 'tile', shift(buckets, by))  4.25 us
    ppermute x1, starting transfers between devices, body(): sub_halo = (lax.ppermute(packed[0], 'sub', shift(2, 1)),) * 2  3 us
    ppermute x2, waiting for transfers between devices, body(): lax.ppermute(value, 'tile', shift(buckets, by))  2.45 us
  transfers between devices with their start and end apart: 15, of which 13 were waited for; matrix products, arithmetic and copies ran while one was open for 1% of the time, Pallas kernels for 3%

profile of v4, /device:TPU:0, one launch (start us, length us, event | category | flops | bytes accessed | tf_op | source)
XLA Modules:
  0.0 44.2 jit_solution(733597334092439641)
XLA Ops:
  0.6 0.9 %pad_maximum_fusion.fields = f32[3,8,16,128]{3,2,1,0:T(8,128)S(1)} fusion(f32[1,8,16,128]{3,2,1,0:T(8,128)} %bitcast.14, f32[1,8,16,128]{3,2,1,0:T(8,128)} %bitcast.15, f32[1,8,16,128]{3,2,1,0:T(8,128)} %bitcast.16), kind=kLoop, calls=%fused_computation | loop fusion | flops 98304 | bytes 393216 | tf_op jit(solution)/shard_map/stack | solution.py:391
  1.6 3.0 %collective-permute-start = (bf16[3,32,128]{2,1,0:T(8,128)(2,1)S(1)}, bf16[3,32,128]{2,1,0:T(8,128)(2,1)S(1)}, u32[]{:S(2)}, u32[]{:S(2)}) collective-permute-start(bf16[3,32,128]{2,1,0:T(8,128)(2,1)S(1)} %shard_map.138), channel_id=1, source_target_pairs={{0,2},{2,0},{1,3},{3,1},{4,6},{6,4},{5,7},{7,5},{8,10},{10,8},{9,1... | collective-permute-start | bytes 73736 | tf_op jit(solution)/shard_map/ppermute | solution.py:394
  5.3 1.1 %collective-permute-done.after_ref.before_ref.sub_after.sub_before = bf16[3,32,128]{2,1,0:T(8,128)(2,1)S(1)} collective-permute-done((bf16[3,32,128]{2,1,0:T(8,128)(2,1)S(1)}, bf16[3,32,128]{2,1,0:T(8,128)(2,1)S(1)}, u32[]{:S(2)}, u32[]{:S(2)}) %collective-permute-start) | collective-permute-done | bytes 24608 | tf_op jit(solution)/shard_map/ppermute | solution.py:394
  6.4 2.2 %collective-permute-start.1 = (bf16[18,16,128]{2,1,0:T(8,128)(2,1)S(1)}, bf16[18,16,128]{2,1,0:T(8,128)(2,1)S(1)}, u32[]{:S(2)}, u32[]{:S(2)}) collective-permute-start(bf16[18,16,128]{2,1,0:T(8,128)(2,1)S(1)} %get-tuple-element.27.after_ref), channel_id=1, source_target_pairs={{0,4},{4,8},{8,12},{12,0},{1,5},{5,9},{9,13},{13,1},{2,6},{6,10},{... | collective-permute-start | bytes 221192 | tf_op jit(solution)/shard_map/ppermute | solution.py:407
  8.6 2.1 %collective-permute-start.2 = (bf16[18,16,128]{2,1,0:T(8,128)(2,1)S(1)}, bf16[18,16,128]{2,1,0:T(8,128)(2,1)S(1)}, u32[]{:S(2)}, u32[]{:S(2)}) collective-permute-start(bf16[18,16,128]{2,1,0:T(8,128)(2,1)S(1)} %get-tuple-element.28), channel_id=1, source_target_pairs={{0,12},{4,0},{8,4},{12,8},{1,13},{5,1},{9,5},{13,9},{2,14},{6,2},{... | collective-permute-start | bytes 221192 | tf_op jit(solution)/shard_map/ppermute | solution.py:407
  11.3 2.0 %collective-permute-done.1.tile_before = bf16[18,16,128]{2,1,0:T(8,128)(2,1)S(1)} collective-permute-done((bf16[18,16,128]{2,1,0:T(8,128)(2,1)S(1)}, bf16[18,16,128]{2,1,0:T(8,128)(2,1)S(1)}, u32[]{:S(2)}, u32[]{:S(2)}) %collective-permute-start.1) | collective-permute-done | bytes 73760 | tf_op jit(solution)/shard_map/ppermute | solution.py:407
  14.3 0.9 %collective-permute-done.3.rep_after.rep_before = bf16[3,24,128]{2,1,0:T(8,128)(2,1)S(1)} collective-permute-done((bf16[3,24,128]{2,1,0:T(8,128)(2,1)S(1)}, bf16[3,24,128]{2,1,0:T(8,128)(2,1)S(1)}, u32[]{:S(2)}, u32[]{:S(2)}) %collective-permute-start.3) | collective-permute-done | bytes 18464 | tf_op jit(solution)/shard_map/ppermute | solution.py:414
  15.2 1.3 %shard_map.143 = (f32[2,8,16,128]{3,2,1,0:T(8,128)S(1)}, bf16[4,96]{1,0:T(4,128)(2,1)S(1)}, bf16[4,96]{1,0:T(4,128)(2,1)S(1)}, bf16[4,96]{1,0:T(4,128)(2,1)S(1)}, bf16[4,96]{1,0:T(4,128)(2,1)S(1)}) custom-call(f32[16,24,128]{2,1,0:T(8,128)S(1)} %get-tuple-element.31.now_in, f32[16,24,128]{2,1,0:T(8,128)S(1)} %get-tuple-element.32.ago_in, ...), custom_call_target="tpu_custom_call" | custom-call | flops 2000000000 | tf_op jit(solution)/shard_map/pallas_call | solution.py:44
  16.5 1.8 %collective-permute-start.4 = (bf16[4,96]{1,0:T(4,128)(2,1)S(1)}, bf16[4,96]{1,0:T(4,128)(2,1)S(1)}, u32[]{:S(2)}, u32[]{:S(2)}) collective-permute-start(bf16[4,96]{1,0:T(4,128)(2,1)S(1)} %get-tuple-element.42), channel_id=1, source_target_pairs={{0,8},{4,12},{8,0},{12,4},{1,9},{5,13},{9,1},{13,5},{2,10},{6,14},... | collective-permute-start | bytes 2312 | tf_op jit(solution)/shard_map/ppermute | solution.py:358
  18.3 1.4 %collective-permute-start.5 = (bf16[4,96]{1,0:T(4,128)(2,1)S(1)}, bf16[4,96]{1,0:T(4,128)(2,1)S(1)}, u32[]{:S(2)}, u32[]{:S(2)}) collective-permute-start(bf16[4,96]{1,0:T(4,128)(2,1)S(1)} %get-tuple-element.43), channel_id=1, source_target_pairs={{0,12},{4,8},{8,4},{12,0},{1,13},{5,9},{9,5},{13,1},{2,14},{6,10},... | collective-permute-start | bytes 2312 | tf_op jit(solution)/shard_map/ppermute | solution.py:358
  20.2 0.8 %collective-permute-done.4.rest_1_ = bf16[4,96]{1,0:T(4,128)(2,1)S(1)} collective-permute-done((bf16[4,96]{1,0:T(4,128)(2,1)S(1)}, bf16[4,96]{1,0:T(4,128)(2,1)S(1)}, u32[]{:S(2)}, u32[]{:S(2)}) %collective-permute-start.4) | collective-permute-done | bytes 800 | tf_op jit(solution)/shard_map/ppermute | solution.py:358
  21.0 2.7 %collective-permute-done.5.rest_2_ = bf16[4,96]{1,0:T(4,128)(2,1)S(1)} collective-permute-done((bf16[4,96]{1,0:T(4,128)(2,1)S(1)}, bf16[4,96]{1,0:T(4,128)(2,1)S(1)}, u32[]{:S(2)}, u32[]{:S(2)}) %collective-permute-start.5) | collective-permute-done | bytes 800 | tf_op jit(solution)/shard_map/ppermute | solution.py:358
  24.2 1.2 %collective-permute-done.7 = f32[4,2048]{1,0:T(4,128)S(1)} collective-permute-done((f32[4,2048]{1,0:T(4,128)S(1)}, f32[4,2048]{1,0:T(4,128)S(1)}, u32[]{:S(2)}, u32[]{:S(2)}) %collective-permute-start.7) | collective-permute-done | bytes 32800 | tf_op jit(solution)/shard_map/ppermute | solution.py:446
  25.4 1.6 %collective-permute-start.8 = (bf16[4,2048]{1,0:T(4,128)(2,1)S(1)}, bf16[4,2048]{1,0:T(4,128)(2,1)S(1)}, u32[]{:S(2)}, u32[]{:S(2)}) collective-permute-start(bf16[4,2048]{1,0:T(4,128)(2,1)S(1)} %get-tuple-element.52), channel_id=1, source_target_pairs={{0,2},{2,0},{1,3},{3,1},{4,6},{6,4},{5,7},{7,5},{8,10},{10,8},{9,1... | collective-permute-start | bytes 49160 | tf_op jit(solution)/shard_map/ppermute | solution.py:446
  27.0 2.2 %collective-permute-done.8 = bf16[4,2048]{1,0:T(4,128)(2,1)S(1)} collective-permute-done((bf16[4,2048]{1,0:T(4,128)(2,1)S(1)}, bf16[4,2048]{1,0:T(4,128)(2,1)S(1)}, u32[]{:S(2)}, u32[]{:S(2)}) %collective-permute-start.8) | collective-permute-done | bytes 16416 | tf_op jit(solution)/shard_map/ppermute | solution.py:446
  29.2 2.1 %collective-permute-start.10 = (bf16[4,2048]{1,0:T(4,128)(2,1)S(1)}, bf16[4,2048]{1,0:T(4,128)(2,1)S(1)}, u32[]{:S(2)}, u32[]{:S(2)}) collective-permute-start(bf16[4,2048]{1,0:T(4,128)(2,1)S(1)} %get-tuple-element.50), channel_id=1, source_target_pairs={{0,12},{4,8},{8,4},{12,0},{1,13},{5,9},{9,5},{13,1},{2,14},{6,10},... | collective-permute-start | bytes 49160 | tf_op jit(solution)/shard_map/ppermute | solution.py:446
  31.3 2.4 %collective-permute-start.9 = (bf16[4,2048]{1,0:T(4,128)(2,1)S(1)}, bf16[4,2048]{1,0:T(4,128)(2,1)S(1)}, u32[]{:S(2)}, u32[]{:S(2)}) collective-permute-start(bf16[4,2048]{1,0:T(4,128)(2,1)S(1)} %get-tuple-element.50), channel_id=1, source_target_pairs={{0,4},{4,0},{8,12},{12,8},{1,5},{5,1},{9,13},{13,9},{2,6},{6,2},{1... | collective-permute-start | bytes 49160 | tf_op jit(solution)/shard_map/ppermute | solution.py:446
  34.9 1.0 %collective-permute-done.11.rest_3_ = bf16[4,2048]{1,0:T(4,128)(2,1)S(1)} collective-permute-done((bf16[4,2048]{1,0:T(4,128)(2,1)S(1)}, bf16[4,2048]{1,0:T(4,128)(2,1)S(1)}, u32[]{:S(2)}, u32[]{:S(2)}) %collective-permute-start.11) | collective-permute-done | bytes 16416 | tf_op jit(solution)/shard_map/ppermute | solution.py:446
  36.0 0.9 %shard_map.146 = (f32[2,2048]{1,0:T(2,128)S(1)}, bf16[4,96]{1,0:T(4,128)(2,1)S(1)}, bf16[4,96]{1,0:T(4,128)(2,1)S(1)}, bf16[4,96]{1,0:T(4,128)(2,1)S(1)}, bf16[4,96]{1,0:T(4,128)(2,1)S(1)}) custom-call(f32[1,2048]{1,0:T(1,128)S(1)} %bitcast.10, f32[1,2048]{1,0:T(1,128)S(1)} %bitcast.11, f32[2,2048]{1,0:T(2,128)S(1)} %copy-done.1, ...), custom_call_target="tpu_custom_call" | custom-call | flops 1000000000 | tf_op jit(solution)/shard_map/pallas_call | solution.py:44
  36.9 1.8 %collective-permute-start.12 = (bf16[4,96]{1,0:T(4,128)(2,1)S(1)}, bf16[4,96]{1,0:T(4,128)(2,1)S(1)}, u32[]{:S(2)}, u32[]{:S(2)}) collective-permute-start(bf16[4,96]{1,0:T(4,128)(2,1)S(1)} %get-tuple-element.46), channel_id=1, source_target_pairs={{0,12},{4,8},{8,4},{12,0},{1,13},{5,9},{9,5},{13,1},{2,14},{6,10},... | collective-permute-start | bytes 2312 | tf_op jit(solution)/shard_map/ppermute | solution.py:358
  38.7 1.1 %collective-permute-start.13 = (bf16[4,96]{1,0:T(4,128)(2,1)S(1)}, bf16[4,96]{1,0:T(4,128)(2,1)S(1)}, u32[]{:S(2)}, u32[]{:S(2)}) collective-permute-start(bf16[4,96]{1,0:T(4,128)(2,1)S(1)} %get-tuple-element.47), channel_id=1, source_target_pairs={{0,8},{4,12},{8,0},{12,4},{1,9},{5,13},{9,1},{13,5},{2,10},{6,14},... | collective-permute-start | bytes 2312 | tf_op jit(solution)/shard_map/ppermute | solution.py:358
  39.9 1.5 %collective-permute-start.14 = (bf16[4,96]{1,0:T(4,128)(2,1)S(1)}, bf16[4,96]{1,0:T(4,128)(2,1)S(1)}, u32[]{:S(2)}, u32[]{:S(2)}) collective-permute-start(bf16[4,96]{1,0:T(4,128)(2,1)S(1)} %get-tuple-element.48), channel_id=1, source_target_pairs={{0,4},{4,0},{8,12},{12,8},{1,5},{5,1},{9,13},{13,9},{2,6},{6,2},{1... | collective-permute-start | bytes 2312 | tf_op jit(solution)/shard_map/ppermute | solution.py:358
  42.3 0.9 %collective-permute-done.13.rest_2_ = bf16[4,96]{1,0:T(4,128)(2,1)S(1)} collective-permute-done((bf16[4,96]{1,0:T(4,128)(2,1)S(1)}, bf16[4,96]{1,0:T(4,128)(2,1)S(1)}, u32[]{:S(2)}, u32[]{:S(2)}) %collective-permute-start.13) | collective-permute-done | bytes 800 | tf_op jit(solution)/shard_map/ppermute | solution.py:358
  43.4 0.8 %shard_map.147 = bf16[4,384]{1,0:T(4,128)(2,1)} custom-call(bf16[384,384]{1,0:T(8,128)(2,1)S(1)} %get-tuple-element.29.ready_ref.route_ref, bf16[4,96]{1,0:T(4,128)(2,1)S(1)} %get-tuple-element.45.rest_0_, bf16[4,96]{1,0:T(4,128)(2,1)S(1)} %collective-permute-done.12.rest_1_, bf16[4,96]{1,0:T(4,128)(2,1)S(1)} %collective-permute-done.13.rest_2_, ...), custom_call_target="tpu_custom_call" | custom-call | flops 1000000000 | tf_op jit(solution)/shard_map/pallas_call | solution.py:44
  (35 shorter events, 5.1 us)
Async XLA Ops:
  1.6 4.8 %collective-permute-start = (bf16[3,32,128]{2,1,0:T(8,128)(2,1)S(1)}, bf16[3,32,128]{2,1,0:T(8,128)(2,1)S(1)}, u32[]{:S(2)}, u32[]{:S(2)}) collective-permute-start(bf16[3,32,128]{2,1,0:T(8,128)(2,1)S(1)} %shard_map.138), channel_id=1, source_target_pairs={{0,2},{2,0},{1,3},{3,1},{4,6},{6,4},{5,7},{7,5},{8,10},{10,8},{9,1... | collective-permute-start | bytes 73736 | tf_op jit(solution)/shard_map/ppermute | solution.py:394
  5.2 5.4 %copy-start.4 = (s32[1,1,1,384,1]{3,4,2,1,0:T(1,128)S(1)}, s32[1,1,1,384,1]{3,4,2,1,0:T(1,128)}, u32[]{:S(2)}) copy-start(s32[1,1,1,384,1]{3,4,2,1,0:T(1,128)} %param.20) | copy-start | bytes 4612
  5.2 5.4 %copy-start.5 = (s32[1,1,1,384]{3,2,1,0:T(1,128)S(1)}, s32[1,1,1,384]{3,2,1,0:T(1,128)}, u32[]{:S(2)}) copy-start(s32[1,1,1,384]{3,2,1,0:T(1,128)} %param.19) | copy-start | bytes 4612
  6.4 6.8 %collective-permute-start.1 = (bf16[18,16,128]{2,1,0:T(8,128)(2,1)S(1)}, bf16[18,16,128]{2,1,0:T(8,128)(2,1)S(1)}, u32[]{:S(2)}, u32[]{:S(2)}) collective-permute-start(bf16[18,16,128]{2,1,0:T(8,128)(2,1)S(1)} %get-tuple-element.27.after_ref), channel_id=1, source_target_pairs={{0,4},{4,8},{8,12},{12,0},{1,5},{5,9},{9,13},{13,1},{2,6},{6,10},{... | collective-permute-start | bytes 221192 | tf_op jit(solution)/shard_map/ppermute | solution.py:407
  8.6 5.1 %collective-permute-start.2 = (bf16[18,16,128]{2,1,0:T(8,128)(2,1)S(1)}, bf16[18,16,128]{2,1,0:T(8,128)(2,1)S(1)}, u32[]{:S(2)}, u32[]{:S(2)}) collective-permute-start(bf16[18,16,128]{2,1,0:T(8,128)(2,1)S(1)} %get-tuple-element.28), channel_id=1, source_target_pairs={{0,12},{4,0},{8,4},{12,8},{1,13},{5,1},{9,5},{13,9},{2,14},{6,2},{... | collective-permute-start | bytes 221192 | tf_op jit(solution)/shard_map/ppermute | solution.py:407
  13.9 1.3 %collective-permute-start.3 = (bf16[3,24,128]{2,1,0:T(8,128)(2,1)S(1)}, bf16[3,24,128]{2,1,0:T(8,128)(2,1)S(1)}, u32[]{:S(2)}, u32[]{:S(2)}) collective-permute-start(bf16[3,24,128]{2,1,0:T(8,128)(2,1)S(1)} %get-tuple-element.30.ready_ref), channel_id=1, source_target_pairs={{0,1},{1,0},{2,3},{3,2},{4,5},{5,4},{6,7},{7,6},{8,9},{9,8},{10,11... | collective-permute-start | bytes 55304 | tf_op jit(solution)/shard_map/ppermute | solution.py:414
  15.2 5.0 %copy-start.6 = (f32[384]{0:T(512)S(1)}, f32[384]{0:T(512)}, u32[]{:S(2)}) copy-start(f32[384]{0:T(512)} %param.14) | copy-start | bytes 4612
  15.2 8.5 %copy-start = (bf16[384,2048]{1,0:T(8,128)(2,1)S(1)}, bf16[384,2048]{1,0:T(8,128)(2,1)}, u32[]{:S(2)}) copy-start(bf16[384,2048]{1,0:T(8,128)(2,1)} %shapes_ref.3) | copy-start | bytes 4718596
  16.5 4.5 %collective-permute-start.4 = (bf16[4,96]{1,0:T(4,128)(2,1)S(1)}, bf16[4,96]{1,0:T(4,128)(2,1)S(1)}, u32[]{:S(2)}, u32[]{:S(2)}) collective-permute-start(bf16[4,96]{1,0:T(4,128)(2,1)S(1)} %get-tuple-element.42), channel_id=1, source_target_pairs={{0,8},{4,12},{8,0},{12,4},{1,9},{5,13},{9,1},{13,5},{2,10},{6,14},... | collective-permute-start | bytes 2312 | tf_op jit(solution)/shard_map/ppermute | solution.py:358
  18.3 5.4 %collective-permute-start.5 = (bf16[4,96]{1,0:T(4,128)(2,1)S(1)}, bf16[4,96]{1,0:T(4,128)(2,1)S(1)}, u32[]{:S(2)}, u32[]{:S(2)}) collective-permute-start(bf16[4,96]{1,0:T(4,128)(2,1)S(1)} %get-tuple-element.43), channel_id=1, source_target_pairs={{0,12},{4,8},{8,4},{12,0},{1,13},{5,9},{9,5},{13,1},{2,14},{6,10},... | collective-permute-start | bytes 2312 | tf_op jit(solution)/shard_map/ppermute | solution.py:358
  19.7 4.0 %collective-permute-start.6 = (bf16[4,96]{1,0:T(4,128)(2,1)S(1)}, bf16[4,96]{1,0:T(4,128)(2,1)S(1)}, u32[]{:S(2)}, u32[]{:S(2)}) collective-permute-start(bf16[4,96]{1,0:T(4,128)(2,1)S(1)} %get-tuple-element.44), channel_id=1, source_target_pairs={{0,4},{4,0},{8,12},{12,8},{1,5},{5,1},{9,13},{13,9},{2,6},{6,2},{1... | collective-permute-start | bytes 2312 | tf_op jit(solution)/shard_map/ppermute | solution.py:358
  24.2 1.2 %collective-permute-start.7 = (f32[4,2048]{1,0:T(4,128)S(1)}, f32[4,2048]{1,0:T(4,128)S(1)}, u32[]{:S(2)}, u32[]{:S(2)}) collective-permute-start(f32[4,2048]{1,0:T(4,128)S(1)} %shard_map.145), channel_id=1, source_target_pairs={{0,1},{1,0},{2,3},{3,2},{4,5},{5,4},{6,7},{7,6},{8,9},{9,8},{10,11... | collective-permute-start | bytes 98312 | tf_op jit(solution)/shard_map/ppermute | solution.py:446
  25.4 3.8 %collective-permute-start.8 = (bf16[4,2048]{1,0:T(4,128)(2,1)S(1)}, bf16[4,2048]{1,0:T(4,128)(2,1)S(1)}, u32[]{:S(2)}, u32[]{:S(2)}) collective-permute-start(bf16[4,2048]{1,0:T(4,128)(2,1)S(1)} %get-tuple-element.52), channel_id=1, source_target_pairs={{0,2},{2,0},{1,3},{3,1},{4,6},{6,4},{5,7},{7,5},{8,10},{10,8},{9,1... | collective-permute-start | bytes 49160 | tf_op jit(solution)/shard_map/ppermute | solution.py:446
  29.2 5.7 %collective-permute-start.10 = (bf16[4,2048]{1,0:T(4,128)(2,1)S(1)}, bf16[4,2048]{1,0:T(4,128)(2,1)S(1)}, u32[]{:S(2)}, u32[]{:S(2)}) collective-permute-start(bf16[4,2048]{1,0:T(4,128)(2,1)S(1)} %get-tuple-element.50), channel_id=1, source_target_pairs={{0,12},{4,8},{8,4},{12,0},{1,13},{5,9},{9,5},{13,1},{2,14},{6,10},... | collective-permute-start | bytes 49160 | tf_op jit(solution)/shard_map/ppermute | solution.py:446
  31.3 4.6 %collective-permute-start.11 = (bf16[4,2048]{1,0:T(4,128)(2,1)S(1)}, bf16[4,2048]{1,0:T(4,128)(2,1)S(1)}, u32[]{:S(2)}, u32[]{:S(2)}) collective-permute-start(bf16[4,2048]{1,0:T(4,128)(2,1)S(1)} %get-tuple-element.50), channel_id=1, source_target_pairs={{0,8},{4,12},{8,0},{12,4},{1,9},{5,13},{9,1},{13,5},{2,10},{6,14},... | collective-permute-start | bytes 49160 | tf_op jit(solution)/shard_map/ppermute | solution.py:446
  31.3 4.6 %collective-permute-start.9 = (bf16[4,2048]{1,0:T(4,128)(2,1)S(1)}, bf16[4,2048]{1,0:T(4,128)(2,1)S(1)}, u32[]{:S(2)}, u32[]{:S(2)}) collective-permute-start(bf16[4,2048]{1,0:T(4,128)(2,1)S(1)} %get-tuple-element.50), channel_id=1, source_target_pairs={{0,4},{4,0},{8,12},{12,8},{1,5},{5,1},{9,13},{13,9},{2,6},{6,2},{1... | collective-permute-start | bytes 49160 | tf_op jit(solution)/shard_map/ppermute | solution.py:446
  33.7 2.3 %copy-start.1 = (f32[2,2048]{1,0:T(2,128)S(1)}, f32[2,2048]{1,0:T(2,128)}, u32[]{:S(2)}) copy-start(f32[2,2048]{1,0:T(2,128)} %start_ref.1) | copy-start | bytes 49156
  33.7 2.3 %copy-start.2 = (f32[2048]{0:T(1024)S(1)}, f32[2048]{0:T(1024)}, u32[]{:S(2)}) copy-start(f32[2048]{0:T(1024)} %param.16) | copy-start | bytes 24580
  33.7 2.3 %copy-start.3 = (f32[2048]{0:T(1024)S(1)}, f32[2048]{0:T(1024)}, u32[]{:S(2)}) copy-start(f32[2048]{0:T(1024)} %param.17) | copy-start | bytes 24580
  36.9 5.4 %collective-permute-start.12 = (bf16[4,96]{1,0:T(4,128)(2,1)S(1)}, bf16[4,96]{1,0:T(4,128)(2,1)S(1)}, u32[]{:S(2)}, u32[]{:S(2)}) collective-permute-start(bf16[4,96]{1,0:T(4,128)(2,1)S(1)} %get-tuple-element.46), channel_id=1, source_target_pairs={{0,12},{4,8},{8,4},{12,0},{1,13},{5,9},{9,5},{13,1},{2,14},{6,10},... | collective-permute-start | bytes 2312 | tf_op jit(solution)/shard_map/ppermute | solution.py:358
  38.7 4.5 %collective-permute-start.13 = (bf16[4,96]{1,0:T(4,128)(2,1)S(1)}, bf16[4,96]{1,0:T(4,128)(2,1)S(1)}, u32[]{:S(2)}, u32[]{:S(2)}) collective-permute-start(bf16[4,96]{1,0:T(4,128)(2,1)S(1)} %get-tuple-element.47), channel_id=1, source_target_pairs={{0,8},{4,12},{8,0},{12,4},{1,9},{5,13},{9,1},{13,5},{2,10},{6,14},... | collective-permute-start | bytes 2312 | tf_op jit(solution)/shard_map/ppermute | solution.py:358
  39.9 3.6 %collective-permute-start.14 = (bf16[4,96]{1,0:T(4,128)(2,1)S(1)}, bf16[4,96]{1,0:T(4,128)(2,1)S(1)}, u32[]{:S(2)}, u32[]{:S(2)}) collective-permute-start(bf16[4,96]{1,0:T(4,128)(2,1)S(1)} %get-tuple-element.48), channel_id=1, source_target_pairs={{0,4},{4,0},{8,12},{12,8},{1,5},{5,1},{9,13},{13,9},{2,6},{6,2},{1... | collective-permute-start | bytes 2312 | tf_op jit(solution)/shard_map/ppermute | solution.py:358

commit v5 on v4

--- a/solution.py
+++ b/solution.py
@@ -87,20 +87,37 @@
     cell = cell_ref[...]
     row = jnp.where(iota((rows, slots), 0) == cell // lanes, 1.0, 0.0)
     lane = jnp.where(iota((lanes, slots), 0) == cell % lanes, 1.0, 0.0)
-    place_ref[:, :rows] = dot(route, row.astype(bf16), (1, 1)).astype(bf16)
-    place_ref[:, rows:] = dot(route, lane.astype(bf16), (1, 1)).astype(bf16)
-
-
-def pack_sub_kernel(sides, fields, *outs):
+    place_ref[:rows] = dot(row.astype(bf16), route, (1, 1)).astype(bf16)
+    place_ref[rows:] = dot(lane.astype(bf16), route, (1, 1)).astype(bf16)
+
+
+def pack_tile_kernel(fields, ahead, behind):
+    layers = fields.shape[1]
+    for out, base, unused in ((ahead, layers - STEPS, 0), (behind, 0, STEPS - 1)):
+        kept = [(at, k) for at in range(FIELDS) for k in range(STEPS) if at < 2 or k != unused]
+        for entry, (at, k) in enumerate(kept):
+            out[entry] = fields[at, base + k].astype(bf16)
+
+
+def layer_of_block(at, k, fields, tile_before, tile_after):
+    layers = fields.shape[1]
+    if STEPS <= k < STEPS + layers:
+        return fields[at, k - STEPS]
+    side, depth, unused = (tile_before, k, 0) if k < STEPS else (tile_after, k - STEPS - layers, STEPS - 1)
+    if at == 2 and depth == unused:
+        return jnp.zeros(fields.shape[2:], f32)
+    return side[at * STEPS + depth - (at == 2 and unused == 0)].astype(f32)
+
+
+def pack_sub_kernel(sides, fields, tile_before, tile_after, ready_ref, *outs):
     layers, rows, lanes = fields.shape[1:]
     low = iota((SUBLANES, lanes), 0) < STEPS
     for at in range(FIELDS):
-        for pair in range(layers // 2):
+        for pair in range(layers // 2 + STEPS):
             tiles = []
             for layer in (2 * pair, 2 * pair + 1):
-                last = pltpu.roll(fields[at, layer, rows - SUBLANES :, :], STEPS, 0)
-                first = fields[at, layer, :SUBLANES, :]
-                tiles.append((last, first))
+                here = layer_of_block(at, layer, fields, tile_before, tile_after)
+                tiles.append((pltpu.roll(here[rows - SUBLANES :], STEPS, 0), here[:SUBLANES]))
             picked = [jnp.where(low, a, pltpu.roll(b, STEPS, 0)) for a, b in zip(*tiles)]
             if sides == 1:
                 picked = [jnp.where(lax.axis_index("sub") == 0, picked[0], picked[1])]
@@ -108,12 +125,10 @@
                 out[at, pair * SUBLANES : (pair + 1) * SUBLANES, :] = value.astype(bf16)
 
 
-def side_rows(at, base, k, after_ref, before_ref):
-    start = base // 2 * SUBLANES + k // 2 * SUBLANES
-    if not isinstance(start, int):
-        start = pl.multiple_of(start, SUBLANES)
-    after = after_ref[at, pl.ds(start, SUBLANES), :].astype(f32)
-    before = before_ref[at, pl.ds(start, SUBLANES), :].astype(f32)
+def side_rows(at, k, after_ref, before_ref):
+    start = k // 2 * SUBLANES
+    after = after_ref[at, start : start + SUBLANES, :].astype(f32)
+    before = before_ref[at, start : start + SUBLANES, :].astype(f32)
     if k % 2 == 0:
         before = pltpu.roll(before, STEPS, 0)
     else:
@@ -125,34 +140,17 @@
     return jnp.where(low, after * keep_after, before * keep_before)
 
 
-def pack_tile_kernel(fields, after_ref, before_ref, *outs):
-    layers = fields.shape[1]
-    for out, base in zip(outs, (layers - STEPS, 0)):
-        for at in range(FIELDS):
-            for k in range(STEPS):
-                out[at * STEPS + k] = fields[at, base + k].astype(bf16)
-            for k in range(0, STEPS, 2):
-                beside = [side_rows(at, base, k + i, after_ref, before_ref) for i in range(2)]
-                out[FIELDS * STEPS + (at * STEPS + k) // 2] = jnp.concatenate(beside, 0).astype(bf16)
-
-
-def pack_rep_kernel(fields, sub_after, sub_before, tile_before, tile_after, ready_ref, out_ref, ends_ref):
+def pack_rep_kernel(fields, tile_before, tile_after, sub_after, sub_before, ready_ref, out_ref, ends_ref):
     layers, rows, lanes = fields.shape[1:]
     beside = 2 * STEPS
     total = layers + 2 * STEPS
-    layer_of = iota((rows + beside, lanes), 1) // beside
+    layer_at = iota((rows + beside, lanes), 1) // beside
     for at in range(FIELDS):
         packed = jnp.zeros((rows + beside, lanes), f32)
         for k in range(total):
-            own = k - STEPS
-            if 0 <= own < layers:
-                here = fields[at, own], side_rows(at, 0, own, sub_after, sub_before)
-            else:
-                side, depth = (tile_before, k) if k < STEPS else (tile_after, own - layers)
-                pair = side[FIELDS * STEPS + (at * STEPS + depth) // 2].astype(f32)
-                here = side[at * STEPS + depth].astype(f32), pair[depth % 2 * beside : (depth % 2 + 1) * beside]
-            here = jnp.concatenate(here, 0)
-            packed = jnp.where(layer_of == k, pltpu.roll(here, (beside * k + STEPS) % lanes, 1), packed)
+            here = layer_of_block(at, k, fields, tile_before, tile_after), side_rows(at, k, sub_after, sub_before)
+            here = pltpu.roll(jnp.concatenate(here, 0), (beside * k + STEPS) % lanes, 1)
+            packed = jnp.where(layer_at == k, here, packed)
         out_ref[at] = packed.astype(bf16)
         ends_ref[at] = packed
 
@@ -183,23 +181,18 @@
 
 
 def assemble_kernel(
-    fields, sub_after, sub_before, tile_before, tile_after, ready_ref, now, ago, coef, lapped, lapped_ago
+    fields, tile_before, tile_after, sub_after, sub_before, ready_ref, now, ago, coef, lapped, lapped_ago
 ):
     layers, rows, lanes = fields.shape[1:]
-    beside = 2 * STEPS
     total = layers + 2 * STEPS
     tile = lax.axis_index("tile")
     keep_low, keep_high = jnp.where(tile > 0, 1.0, 0.0), jnp.where(tile < lax.axis_size("tile") - 1, 1.0, 0.0)
     for at, out in enumerate((now, ago, coef)):
         extra = viscous if at == 2 else 0.0
-        for k in range(layers):
-            out[STEPS + k, :rows] = fields[at, k] + extra
-            out[STEPS + k, rows:] = side_rows(at, 0, k, sub_after, sub_before) + extra
-        for side, base, keep in ((tile_before, 0, keep_low), (tile_after, STEPS + layers, keep_high)):
-            for k in range(STEPS):
-                out[base + k, :rows] = side[at * STEPS + k].astype(f32) * keep + extra
-                pair = side[FIELDS * STEPS + (at * STEPS + k) // 2].astype(f32) * keep
-                out[base + k, rows:] = pair[k % 2 * beside : (k % 2 + 1) * beside] + extra
+        for k in range(total):
+            keep = keep_low if k < STEPS else keep_high if k >= STEPS + layers else 1.0
+            out[k, :rows] = layer_of_block(at, k, fields, tile_before, tile_after) * keep + extra
+            out[k, rows:] = side_rows(at, k, sub_after, sub_before) * keep + extra
     for value, out in ((now, lapped), (ago, lapped_ago)):
         for k in range(1, total - 1):
             out[k] = laplace(value[k - 1], value[k], value[k + 1])
@@ -208,7 +201,7 @@
 def window_kernel(
     now_in, ago_in, coef, lapped_in, lapped_ago_in, ends_ref, rep_after, rep_before, place_ref, states, *rest
 ):
-    *sends, now, ago, lapped, seen = rest
+    *sends, now, ago, lapped = rest
     layers, rows, lanes = states.shape[1:]
     beside = 2 * STEPS
     total, wide_rows = now.shape[:2]
@@ -253,11 +246,12 @@
     left_lapped, right_lapped = viscous * laplace_side(left_ago), viscous * laplace_side(right_ago)
 
     cells = layers * rows
-    slots = place_ref.shape[0]
-    lane_of = place_ref[:, cells:].astype(f32)
+    slots = place_ref.shape[1]
+    lane_of = place_ref[cells:]
     loads = jnp.zeros((SUBLANES, slots), f32)
     for step in range(STEPS):
         edge = edges(left_now, right_now)
+        found = jnp.zeros((rows, slots), f32)
         source = now_in if step == 0 else now
         below, here = source[step], source[step + 1]
         for k in range(step + 1, total - step - 1):
@@ -276,7 +270,8 @@
             own = k - STEPS
             if 0 <= own < layers:
                 core = updated[:rows]
-                seen[own * rows : (own + 1) * rows, :] = core.astype(bf16)
+                row_of = place_ref[own * rows : (own + 1) * rows].astype(f32)
+                found = found + dot(core.astype(bf16), lane_of, (1, 0)) * row_of
                 if step >= STEPS - 2:
                     states[STEPS - 1 - step, own] = core
             below, here = here, above
@@ -287,9 +282,7 @@
             lap = laplace_side(right_now)
             updated = advance(right_now, right_ago, right_coef, lap, right_lapped, inside_right)
             right_now, right_ago, right_lapped = updated, right_now, viscous * lap
-        found = (dot(place_ref[:, :cells], seen[...], (1, 0)) * lane_of).astype(bf16)
-        summed = dot(jnp.ones((SUBLANES, lanes), bf16), found, (1, 1))
-        loads = jnp.where(iota((SUBLANES, slots), 0) == step, summed, loads)
+        loads = jnp.where(iota((SUBLANES, slots), 0) == step, jnp.sum(found, axis=0, keepdims=True), loads)
 
     size = slots // len(sends)
     for at, send in enumerate(sends):
@@ -301,25 +294,32 @@
         copy.wait()
 
 
-def spread(at, size, total, bucket):
-    entry = iota((size, 1), 0) + at * size
-    part = at if size == bucket else entry // bucket
+def turn_kernel(buckets, ready_ref, shapes_ref, area_ref, turned_ref, flipped_ref, area_out):
+    total = shapes_ref.shape[0]
+    bucket = total // buckets
+    entry = iota((total, 1), 0)
+    part = entry // bucket
     wanted = entry + ((part ^ lax.axis_index("tile")) - part) * bucket
-    return jnp.where(iota((size, total), 1) == wanted, 1.0, 0.0).astype(bf16)
-
-
-def project_kernel(order, buckets, area_ref, shapes_ref, *rest):
+    picks = jnp.where(iota((total, total), 1) == wanted, 1.0, 0.0)
+    turned = dot(picks.astype(bf16), shapes_ref[...], (1, 0))
+    turned_ref[...] = turned.astype(bf16)
+    flipped_ref[...] = turned.T.astype(bf16)
+    area_out[...] = lax.dot_general(
+        area_ref[...], picks, (((1,), (1,)), ((), ())), precision=lax.Precision.HIGHEST, preferred_element_type=f32
+    )
+
+
+def project_kernel(order, area_ref, turned_ref, *rest):
     *parts, out_ref = rest
-    total = area_ref.shape[1]
     size = parts[0].shape[1]
-    loads = 0.0
+    forces = 0.0
     for at, part in zip(order, parts):
-        loads = loads + dot(part[...], spread(at, size, total, total // buckets), (1, 0))
-    weighted = (loads * area_ref[...]).astype(bf16)
-    out_ref[...] = dot(weighted, shapes_ref[...], (1, 0))
-
-
-def respond_kernel(buckets, addends, freq_ref, damp_ref, start_ref, shapes_ref, *rest):
+        weighted = (part[...].astype(f32) * area_ref[:, at * size : (at + 1) * size]).astype(bf16)
+        forces = forces + dot(weighted, turned_ref[at * size : (at + 1) * size, :], (1, 0))
+    out_ref[...] = forces
+
+
+def respond_kernel(addends, freq_ref, damp_ref, start_ref, flipped_ref, *rest):
     forces_in, rest = rest[:addends], rest[addends:]
     state_ref, *sends, accel = rest
     forces = forces_in[0][...]
@@ -336,11 +336,10 @@
         accel[step : step + 1, :] = acceleration
     state_ref[0:1, :] = displace
     state_ref[1:2, :] = velocity
-    node = dot(accel[...].astype(bf16), shapes_ref[...], (1, 1)).astype(bf16)
-    total = node.shape[1]
-    size = total // len(sends)
+    node = dot(accel[...].astype(bf16), flipped_ref[...], (1, 0))
+    size = node.shape[1] // len(sends)
     for at, send in enumerate(sends):
-        send[...] = dot(node, spread(at, size, total, total // buckets), (1, 1))[:STEPS].astype(bf16)
+        send[...] = node[:STEPS, at * size : (at + 1) * size].astype(bf16)
 
 
 def return_kernel(order, route_ref, *rest):
@@ -386,29 +385,35 @@
     total = layers + 2 * STEPS
     wide_rows = rows + 2 * STEPS
 
+    cells = layers * rows
+    fields = jnp.stack([pressure, previous_pressure, courant_square])
+    slab = shape_of((FIELDS * STEPS - 1, rows, lanes), bf16)
+    packed = call(pack_tile_kernel, (slab, slab), (fields,))
+    route, place = call(
+        functools.partial(route_kernel, buckets, lanes, cells),
+        (shape_of((slots, slots), bf16), shape_of((cells + lanes, slots), bf16)),
+        (packed[0], slot_owner.reshape(1, slots), slot_cell.reshape(1, slots), surface_count.reshape(1, 1)),
+    )
+    tile_halo = [lax.ppermute(value, "tile", shift(buckets, by)) for value, by in zip(packed, (1, -1))]
+
     sides = 1 if subs == 2 else 2
-    slab = shape_of((FIELDS, layers * STEPS, lanes), bf16)
-    fields = jnp.stack([pressure, previous_pressure, courant_square])
-    packed = call(functools.partial(pack_sub_kernel, sides), (slab,) * sides, (fields,))
+    slab = shape_of((FIELDS, total * STEPS, lanes), bf16)
+    packed = call(functools.partial(pack_sub_kernel, sides), (slab,) * sides, (fields, *tile_halo, route))
     if subs == 2:
         sub_halo = (lax.ppermute(packed[0], "sub", shift(2, 1)),) * 2
     else:
         sub_halo = both_ways("sub", *packed)
 
-    cells = layers * rows
-    slab = shape_of((FIELDS * STEPS * 3 // 2, rows, lanes), bf16)
-    packed = call(pack_tile_kernel, (slab, slab), (fields, *sub_halo))
-    route, place = call(
-        functools.partial(route_kernel, buckets, lanes, cells),
-        (shape_of((slots, slots), bf16), shape_of((slots, cells + lanes), bf16)),
-        (packed[0], slot_owner.reshape(1, slots), slot_cell.reshape(1, slots), surface_count.reshape(1, 1)),
-    )
-
-    tile_halo = [lax.ppermute(value, "tile", shift(buckets, by)) for value, by in zip(packed, (1, -1))]
+    turned, flipped, area = call(
+        functools.partial(turn_kernel, buckets),
+        (shape_of(mode_shapes.shape, bf16), shape_of(mode_shapes.shape[::-1], bf16), shape_of((1, slots), f32)),
+        (packed[0], mode_shapes, node_area.reshape(1, slots)),
+    )
+
     packed, ends = call(
         pack_rep_kernel,
         (shape_of((FIELDS, wide_rows, lanes), bf16), shape_of((FIELDS, wide_rows, lanes), f32)),
-        (fields, *sub_halo, *tile_halo, route),
+        (fields, *tile_halo, *sub_halo, area),
     )
     if reps == 2:
         rep_halo = (lax.ppermute(packed, "rep", shift(2, 1)),) * 2
@@ -416,7 +421,7 @@
         rep_halo = both_ways("rep", packed, packed)
 
     wide = shape_of((total, wide_rows, lanes), f32)
-    assembled = call(assemble_kernel, (wide,) * 5, (fields, *sub_halo, *tile_halo, packed))
+    assembled = call(assemble_kernel, (wide,) * 5, (fields, *tile_halo, *sub_halo, packed))
     wide = pltpu.VMEM(wide.shape, f32)
     part = shape_of((STEPS, slots // parts), bf16)
     block = shape_of(pressure.shape, f32)
@@ -424,7 +429,7 @@
         window_kernel,
         (shape_of((2, layers, rows, lanes), f32),) + (part,) * parts,
         (*assembled, ends, *rep_halo, place),
-        scratch=[wide] * 3 + [pltpu.VMEM((cells, lanes), bf16)],
+        scratch=[wide] * 3,
         micros=2.0,
     )
     final_field, prior_field = call(
@@ -433,9 +438,9 @@
 
     order = [k for k in (0, 2, 3, 1) if k < parts]
     forces = call(
-        functools.partial(project_kernel, order, buckets),
+        functools.partial(project_kernel, order),
         shape_of((STEPS, modes), f32),
-        (node_area.reshape(1, slots), mode_shapes, *exchange(sends, order)),
+        (area, turned, *exchange(sends, order)),
     )
     addends = [forces]
     for axis in ("rep", "sub", "tile"):
@@ -448,9 +453,9 @@
             addends = [lax.psum(forces, axis)]
 
     state, *sends = call(
-        functools.partial(respond_kernel, buckets, len(addends)),
+        functools.partial(respond_kernel, len(addends)),
         (shape_of((2, modes), f32),) + (part,) * parts,
-        (frequency.reshape(1, modes), damping_ratio.reshape(1, modes), modal_start, mode_shapes, *addends),
+        (frequency.reshape(1, modes), damping_ratio.reshape(1, modes), modal_start, flipped, *addends),
         scratch=[pltpu.VMEM((SUBLANES, modes), f32)],
     )
     share = modes // (buckets * subs * reps)

time: 44.4 us -> 43.6 us (0.982)
  waiting for transfers between devices: 14.6 us -> 13.2 us
  Pallas kernels: 5.24 us -> 5.93 us
    ppermute x1, starting transfers between devices: 3 us -> 1.56 us  [body(): sub_halo = (lax.ppermute(packed[0], 'sub', shift(2, 1)),) * 2]
    ppermute x2, waiting for transfers between devices: 2.45 us -> 1.08 us  [body(): lax.ppermute(value, 'tile', shift(buckets, by))]
    ppermute x2, starting transfers between devices: 4.25 us -> 5.17 us  [body(): lax.ppermute(value, 'tile', shift(buckets, by))]
    pallas_call x10 -> x11, Pallas kernels: 5.24 us -> 5.93 us  [call(): pl.pallas_call(kernel, out_shape=out_shape, in_specs=specs or [VMEM] * le...]
  transfers between devices with their start and end apart: 15 -> 15, of which waited for: 13 -> 13; matrix products, arithmetic and copies ran while one was open for 1% -> 1% of each run, Pallas kernels for 3% -> 7%
where the time goes in v5:
time: 43.6 us; the launch traced here: 43.4 us
  starting transfers between devices  21.3 us (49%)
  waiting for transfers between devices  13.2 us (30%)
  Pallas kernels  5.93 us (14%)
  between operations  1.42 us (3%)
  other arithmetic  0.95 us (2%)
  local copies, waits for them, and re-layouts  0.65 us (1%)
    ppermute x6, starting transfers between devices, exchange(): lax.ppermute(parts[k], 'tile', swaps(buckets, k))  8.39 us
    ppermute x5, starting transfers between devices, body(): lax.ppermute(sent, axis, swaps(count, k))  6.07 us
    pallas_call x11, Pallas kernels, call(): pl.pallas_call(kernel, out_shape=out_shape, in_specs=specs or [VMEM] * le...  5.93 us
    ppermute x2, starting transfers between devices, body(): lax.ppermute(value, 'tile', shift(buckets, by))  5.17 us
    ppermute x6, waiting for transfers between devices, exchange(): lax.ppermute(parts[k], 'tile', swaps(buckets, k))  5.04 us
    ppermute x5, waiting for transfers between devices, body(): lax.ppermute(sent, axis, swaps(count, k))  5.03 us
    ppermute x1, starting transfers between devices, body(): sub_halo = (lax.ppermute(packed[0], 'sub', shift(2, 1)),) * 2  1.56 us
    ppermute x1, waiting for transfers between devices, body(): sub_halo = (lax.ppermute(packed[0], 'sub', shift(2, 1)),) * 2  1.12 us
  transfers between devices with their start and end apart: 15, of which 13 were waited for; matrix products, arithmetic and copies ran while one was open for 1% of the time, Pallas kernels for 7%

profile of v5, /device:TPU:0, one launch (start us, length us, event | category | flops | bytes accessed | tf_op | source)
XLA Modules:
  0.0 43.4 jit_solution(4758623833596163873)
XLA Ops:
  0.6 0.9 %pad_maximum_fusion.fields = f32[3,8,16,128]{3,2,1,0:T(8,128)S(1)} fusion(f32[1,8,16,128]{3,2,1,0:T(8,128)} %bitcast.14, f32[1,8,16,128]{3,2,1,0:T(8,128)} %bitcast.15, f32[1,8,16,128]{3,2,1,0:T(8,128)} %bitcast.16), kind=kLoop, calls=%fused_computation | loop fusion | flops 98304 | bytes 393216 | tf_op jit(solution)/shard_map/stack | solution.py:389
  1.6 3.1 %collective-permute-start = (bf16[11,16,128]{2,1,0:T(8,128)(2,1)S(1)}, bf16[11,16,128]{2,1,0:T(8,128)(2,1)S(1)}, u32[]{:S(2)}, u32[]{:S(2)}) collective-permute-start(bf16[11,16,128]{2,1,0:T(8,128)(2,1)S(1)} %get-tuple-element.30.after_ref), channel_id=1, source_target_pairs={{0,4},{4,8},{8,12},{12,0},{1,5},{5,9},{9,13},{13,1},{2,6},{6,10},{... | collective-permute-start | bytes 135176 | tf_op jit(solution)/shard_map/ppermute | solution.py:397
  4.7 2.1 %collective-permute-start.1 = (bf16[11,16,128]{2,1,0:T(8,128)(2,1)S(1)}, bf16[11,16,128]{2,1,0:T(8,128)(2,1)S(1)}, u32[]{:S(2)}, u32[]{:S(2)}) collective-permute-start(bf16[11,16,128]{2,1,0:T(8,128)(2,1)S(1)} %get-tuple-element.31), channel_id=1, source_target_pairs={{0,12},{4,0},{8,4},{12,8},{1,13},{5,1},{9,5},{13,9},{2,14},{6,2},{... | collective-permute-start | bytes 135176 | tf_op jit(solution)/shard_map/ppermute | solution.py:397
  8.1 0.7 %collective-permute-done.tile_before = bf16[11,16,128]{2,1,0:T(8,128)(2,1)S(1)} collective-permute-done((bf16[11,16,128]{2,1,0:T(8,128)(2,1)S(1)}, bf16[11,16,128]{2,1,0:T(8,128)(2,1)S(1)}, u32[]{:S(2)}, u32[]{:S(2)}) %collective-permute-start) | collective-permute-done | bytes 45088 | tf_op jit(solution)/shard_map/ppermute | solution.py:397
  9.2 1.6 %collective-permute-start.2 = (bf16[3,64,128]{2,1,0:T(8,128)(2,1)S(1)}, bf16[3,64,128]{2,1,0:T(8,128)(2,1)S(1)}, u32[]{:S(2)}, u32[]{:S(2)}) collective-permute-start(bf16[3,64,128]{2,1,0:T(8,128)(2,1)S(1)} %shard_map.140.ready_ref), channel_id=1, source_target_pairs={{0,2},{2,0},{1,3},{3,1},{4,6},{6,4},{5,7},{7,5},{8,10},{10,8},{9,1... | collective-permute-start | bytes 147464 | tf_op jit(solution)/shard_map/ppermute | solution.py:403
  10.8 1.5 %shard_map.141 = (bf16[384,2048]{1,0:T(8,128)(2,1)S(1)}, bf16[2048,384]{1,0:T(8,128)(2,1)S(1)}, f32[1,384]{1,0:T(1,128)S(1)}) custom-call(bf16[3,64,128]{2,1,0:T(8,128)(2,1)S(1)} %shard_map.140.ready_ref, bf16[384,2048]{1,0:T(8,128)(2,1)S(1)} %copy-done, f32[1,384]{1,0:T(1,128)S(1)} %reshape.32.area_ref), custom_call_target="tpu_custom_call" | custom-call | flops 1000000000 | tf_op jit(solution)/shard_map/pallas_call | solution.py:44
  12.3 1.1 %collective-permute-done.2.sub_after.sub_before = bf16[3,64,128]{2,1,0:T(8,128)(2,1)S(1)} collective-permute-done((bf16[3,64,128]{2,1,0:T(8,128)(2,1)S(1)}, bf16[3,64,128]{2,1,0:T(8,128)(2,1)S(1)}, u32[]{:S(2)}, u32[]{:S(2)}) %collective-permute-start.2) | collective-permute-done | bytes 49184 | tf_op jit(solution)/shard_map/ppermute | solution.py:403
  14.0 0.9 %collective-permute-done.3.rep_after.rep_before = bf16[3,24,128]{2,1,0:T(8,128)(2,1)S(1)} collective-permute-done((bf16[3,24,128]{2,1,0:T(8,128)(2,1)S(1)}, bf16[3,24,128]{2,1,0:T(8,128)(2,1)S(1)}, u32[]{:S(2)}, u32[]{:S(2)}) %collective-permute-start.3) | collective-permute-done | bytes 18464 | tf_op jit(solution)/shard_map/ppermute | solution.py:419
  14.8 1.1 %shard_map.144 = (f32[2,8,16,128]{3,2,1,0:T(8,128)S(1)}, bf16[4,96]{1,0:T(4,128)(2,1)S(1)}, bf16[4,96]{1,0:T(4,128)(2,1)S(1)}, bf16[4,96]{1,0:T(4,128)(2,1)S(1)}, bf16[4,96]{1,0:T(4,128)(2,1)S(1)}) custom-call(f32[16,24,128]{2,1,0:T(8,128)S(1)} %get-tuple-element.35.now_in, f32[16,24,128]{2,1,0:T(8,128)S(1)} %get-tuple-element.36.ago_in, ...), custom_call_target="tpu_custom_call" | custom-call | flops 2000000000 | tf_op jit(solution)/shard_map/pallas_call | solution.py:44
  16.0 2.1 %collective-permute-start.4 = (bf16[4,96]{1,0:T(4,128)(2,1)S(1)}, bf16[4,96]{1,0:T(4,128)(2,1)S(1)}, u32[]{:S(2)}, u32[]{:S(2)}) collective-permute-start(bf16[4,96]{1,0:T(4,128)(2,1)S(1)} %get-tuple-element.48), channel_id=1, source_target_pairs={{0,8},{4,12},{8,0},{12,4},{1,9},{5,13},{9,1},{13,5},{2,10},{6,14},... | collective-permute-start | bytes 2312 | tf_op jit(solution)/shard_map/ppermute | solution.py:357
  18.1 1.4 %collective-permute-start.5 = (bf16[4,96]{1,0:T(4,128)(2,1)S(1)}, bf16[4,96]{1,0:T(4,128)(2,1)S(1)}, u32[]{:S(2)}, u32[]{:S(2)}) collective-permute-start(bf16[4,96]{1,0:T(4,128)(2,1)S(1)} %get-tuple-element.49), channel_id=1, source_target_pairs={{0,12},{4,8},{8,4},{12,0},{1,13},{5,9},{9,5},{13,1},{2,14},{6,10},... | collective-permute-start | bytes 2312 | tf_op jit(solution)/shard_map/ppermute | solution.py:357
  20.5 3.0 %collective-permute-done.5.rest_2_ = bf16[4,96]{1,0:T(4,128)(2,1)S(1)} collective-permute-done((bf16[4,96]{1,0:T(4,128)(2,1)S(1)}, bf16[4,96]{1,0:T(4,128)(2,1)S(1)}, u32[]{:S(2)}, u32[]{:S(2)}) %collective-permute-start.5) | collective-permute-done | bytes 800 | tf_op jit(solution)/shard_map/ppermute | solution.py:357
  23.9 1.2 %collective-permute-done.7 = f32[4,2048]{1,0:T(4,128)S(1)} collective-permute-done((f32[4,2048]{1,0:T(4,128)S(1)}, f32[4,2048]{1,0:T(4,128)S(1)}, u32[]{:S(2)}, u32[]{:S(2)}) %collective-permute-start.7) | collective-permute-done | bytes 32800 | tf_op jit(solution)/shard_map/ppermute | solution.py:451
  25.1 1.6 %collective-permute-start.8 = (bf16[4,2048]{1,0:T(4,128)(2,1)S(1)}, bf16[4,2048]{1,0:T(4,128)(2,1)S(1)}, u32[]{:S(2)}, u32[]{:S(2)}) collective-permute-start(bf16[4,2048]{1,0:T(4,128)(2,1)S(1)} %get-tuple-element.58), channel_id=1, source_target_pairs={{0,2},{2,0},{1,3},{3,1},{4,6},{6,4},{5,7},{7,5},{8,10},{10,8},{9,1... | collective-permute-start | bytes 49160 | tf_op jit(solution)/shard_map/ppermute | solution.py:451
  26.7 2.2 %collective-permute-done.8 = bf16[4,2048]{1,0:T(4,128)(2,1)S(1)} collective-permute-done((bf16[4,2048]{1,0:T(4,128)(2,1)S(1)}, bf16[4,2048]{1,0:T(4,128)(2,1)S(1)}, u32[]{:S(2)}, u32[]{:S(2)}) %collective-permute-start.8) | collective-permute-done | bytes 16416 | tf_op jit(solution)/shard_map/ppermute | solution.py:451
  28.9 2.1 %collective-permute-start.10 = (bf16[4,2048]{1,0:T(4,128)(2,1)S(1)}, bf16[4,2048]{1,0:T(4,128)(2,1)S(1)}, u32[]{:S(2)}, u32[]{:S(2)}) collective-permute-start(bf16[4,2048]{1,0:T(4,128)(2,1)S(1)} %get-tuple-element.56), channel_id=1, source_target_pairs={{0,12},{4,8},{8,4},{12,0},{1,13},{5,9},{9,5},{13,1},{2,14},{6,10},... | collective-permute-start | bytes 49160 | tf_op jit(solution)/shard_map/ppermute | solution.py:451
  31.0 2.4 %collective-permute-start.9 = (bf16[4,2048]{1,0:T(4,128)(2,1)S(1)}, bf16[4,2048]{1,0:T(4,128)(2,1)S(1)}, u32[]{:S(2)}, u32[]{:S(2)}) collective-permute-start(bf16[4,2048]{1,0:T(4,128)(2,1)S(1)} %get-tuple-element.56), channel_id=1, source_target_pairs={{0,4},{4,0},{8,12},{12,8},{1,5},{5,1},{9,13},{13,9},{2,6},{6,2},{1... | collective-permute-start | bytes 49160 | tf_op jit(solution)/shard_map/ppermute | solution.py:451
  33.4 0.7 %shard_map.145 = (f32[8,16,128]{2,1,0:T(8,128)}, f32[8,16,128]{2,1,0:T(8,128)}) custom-call(f32[2,8,16,128]{3,2,1,0:T(8,128)S(1)} %get-tuple-element.42.states), custom_call_target="tpu_custom_call" | custom-call | flops 1000000000 | tf_op jit(solution)/shard_map/pallas_call | solution.py:44
  34.6 1.0 %collective-permute-done.11.rest_3_ = bf16[4,2048]{1,0:T(4,128)(2,1)S(1)} collective-permute-done((bf16[4,2048]{1,0:T(4,128)(2,1)S(1)}, bf16[4,2048]{1,0:T(4,128)(2,1)S(1)}, u32[]{:S(2)}, u32[]{:S(2)}) %collective-permute-start.11) | collective-permute-done | bytes 16416 | tf_op jit(solution)/shard_map/ppermute | solution.py:451
  36.1 1.8 %collective-permute-start.12 = (bf16[4,96]{1,0:T(4,128)(2,1)S(1)}, bf16[4,96]{1,0:T(4,128)(2,1)S(1)}, u32[]{:S(2)}, u32[]{:S(2)}) collective-permute-start(bf16[4,96]{1,0:T(4,128)(2,1)S(1)} %get-tuple-element.52), channel_id=1, source_target_pairs={{0,12},{4,8},{8,4},{12,0},{1,13},{5,9},{9,5},{13,1},{2,14},{6,10},... | collective-permute-start | bytes 2312 | tf_op jit(solution)/shard_map/ppermute | solution.py:357
  37.9 1.1 %collective-permute-start.13 = (bf16[4,96]{1,0:T(4,128)(2,1)S(1)}, bf16[4,96]{1,0:T(4,128)(2,1)S(1)}, u32[]{:S(2)}, u32[]{:S(2)}) collective-permute-start(bf16[4,96]{1,0:T(4,128)(2,1)S(1)} %get-tuple-element.53), channel_id=1, source_target_pairs={{0,8},{4,12},{8,0},{12,4},{1,9},{5,13},{9,1},{13,5},{2,10},{6,14},... | collective-permute-start | bytes 2312 | tf_op jit(solution)/shard_map/ppermute | solution.py:357
  39.0 1.5 %collective-permute-start.14 = (bf16[4,96]{1,0:T(4,128)(2,1)S(1)}, bf16[4,96]{1,0:T(4,128)(2,1)S(1)}, u32[]{:S(2)}, u32[]{:S(2)}) collective-permute-start(bf16[4,96]{1,0:T(4,128)(2,1)S(1)} %get-tuple-element.54), channel_id=1, source_target_pairs={{0,4},{4,0},{8,12},{12,8},{1,5},{5,1},{9,13},{13,9},{2,6},{6,2},{1... | collective-permute-start | bytes 2312 | tf_op jit(solution)/shard_map/ppermute | solution.py:357
  41.5 0.9 %collective-permute-done.13.rest_2_ = bf16[4,96]{1,0:T(4,128)(2,1)S(1)} collective-permute-done((bf16[4,96]{1,0:T(4,128)(2,1)S(1)}, bf16[4,96]{1,0:T(4,128)(2,1)S(1)}, u32[]{:S(2)}, u32[]{:S(2)}) %collective-permute-start.13) | collective-permute-done | bytes 800 | tf_op jit(solution)/shard_map/ppermute | solution.py:357
  42.6 0.8 %shard_map.148 = bf16[4,384]{1,0:T(4,128)(2,1)} custom-call(bf16[384,384]{1,0:T(8,128)(2,1)S(1)} %get-tuple-element.32.ready_ref.route_ref, bf16[4,96]{1,0:T(4,128)(2,1)S(1)} %get-tuple-element.51.rest_0_, bf16[4,96]{1,0:T(4,128)(2,1)S(1)} %collective-permute-done.12.rest_1_, bf16[4,96]{1,0:T(4,128)(2,1)S(1)} %collective-permute-done.13.rest_2_, ...), custom_call_target="tpu_custom_call" | custom-call | flops 1000000000 | tf_op jit(solution)/shard_map/pallas_call | solution.py:44
  (36 shorter events, 5.3 us)
Async XLA Ops:
  1.6 5.9 %copy-start.4 = (s32[1,1,1,384,1]{3,4,2,1,0:T(1,128)S(1)}, s32[1,1,1,384,1]{3,4,2,1,0:T(1,128)}, u32[]{:S(2)}) copy-start(s32[1,1,1,384,1]{3,4,2,1,0:T(1,128)} %param.20) | copy-start | bytes 4612
  1.6 5.9 %copy-start.5 = (s32[1,1,1,384]{3,2,1,0:T(1,128)S(1)}, s32[1,1,1,384]{3,2,1,0:T(1,128)}, u32[]{:S(2)}) copy-start(s32[1,1,1,384]{3,2,1,0:T(1,128)} %param.19) | copy-start | bytes 4612
  1.6 7.2 %collective-permute-start = (bf16[11,16,128]{2,1,0:T(8,128)(2,1)S(1)}, bf16[11,16,128]{2,1,0:T(8,128)(2,1)S(1)}, u32[]{:S(2)}, u32[]{:S(2)}) collective-permute-start(bf16[11,16,128]{2,1,0:T(8,128)(2,1)S(1)} %get-tuple-element.30.after_ref), channel_id=1, source_target_pairs={{0,4},{4,8},{8,12},{12,0},{1,5},{5,9},{9,13},{13,1},{2,6},{6,10},{... | collective-permute-start | bytes 135176 | tf_op jit(solution)/shard_map/ppermute | solution.py:397
  4.7 4.5 %collective-permute-start.1 = (bf16[11,16,128]{2,1,0:T(8,128)(2,1)S(1)}, bf16[11,16,128]{2,1,0:T(8,128)(2,1)S(1)}, u32[]{:S(2)}, u32[]{:S(2)}) collective-permute-start(bf16[11,16,128]{2,1,0:T(8,128)(2,1)S(1)} %get-tuple-element.31), channel_id=1, source_target_pairs={{0,12},{4,0},{8,4},{12,8},{1,13},{5,1},{9,5},{13,9},{2,14},{6,2},{... | collective-permute-start | bytes 135176 | tf_op jit(solution)/shard_map/ppermute | solution.py:397
  7.4 0.7 %copy-start.6 = (f32[384]{0:T(512)S(1)}, f32[384]{0:T(512)}, u32[]{:S(2)}) copy-start(f32[384]{0:T(512)} %param.14) | copy-start | bytes 4612
  9.2 1.6 %copy-start = (bf16[384,2048]{1,0:T(8,128)(2,1)S(1)}, bf16[384,2048]{1,0:T(8,128)(2,1)}, u32[]{:S(2)}) copy-start(bf16[384,2048]{1,0:T(8,128)(2,1)} %shapes_ref.1) | copy-start | bytes 4718596
  9.2 4.2 %collective-permute-start.2 = (bf16[3,64,128]{2,1,0:T(8,128)(2,1)S(1)}, bf16[3,64,128]{2,1,0:T(8,128)(2,1)S(1)}, u32[]{:S(2)}, u32[]{:S(2)}) collective-permute-start(bf16[3,64,128]{2,1,0:T(8,128)(2,1)S(1)} %shard_map.140.ready_ref), channel_id=1, source_target_pairs={{0,2},{2,0},{1,3},{3,1},{4,6},{6,4},{5,7},{7,5},{8,10},{10,8},{9,1... | collective-permute-start | bytes 147464 | tf_op jit(solution)/shard_map/ppermute | solution.py:403
  13.6 1.3 %collective-permute-start.3 = (bf16[3,24,128]{2,1,0:T(8,128)(2,1)S(1)}, bf16[3,24,128]{2,1,0:T(8,128)(2,1)S(1)}, u32[]{:S(2)}, u32[]{:S(2)}) collective-permute-start(bf16[3,24,128]{2,1,0:T(8,128)(2,1)S(1)} %get-tuple-element.34.ready_ref), channel_id=1, source_target_pairs={{0,1},{1,0},{2,3},{3,2},{4,5},{5,4},{6,7},{7,6},{8,9},{9,8},{10,11... | collective-permute-start | bytes 55304 | tf_op jit(solution)/shard_map/ppermute | solution.py:419
  16.0 4.5 %collective-permute-start.4 = (bf16[4,96]{1,0:T(4,128)(2,1)S(1)}, bf16[4,96]{1,0:T(4,128)(2,1)S(1)}, u32[]{:S(2)}, u32[]{:S(2)}) collective-permute-start(bf16[4,96]{1,0:T(4,128)(2,1)S(1)} %get-tuple-element.48), channel_id=1, source_target_pairs={{0,8},{4,12},{8,0},{12,4},{1,9},{5,13},{9,1},{13,5},{2,10},{6,14},... | collective-permute-start | bytes 2312 | tf_op jit(solution)/shard_map/ppermute | solution.py:357
  18.1 5.4 %collective-permute-start.5 = (bf16[4,96]{1,0:T(4,128)(2,1)S(1)}, bf16[4,96]{1,0:T(4,128)(2,1)S(1)}, u32[]{:S(2)}, u32[]{:S(2)}) collective-permute-start(bf16[4,96]{1,0:T(4,128)(2,1)S(1)} %get-tuple-element.49), channel_id=1, source_target_pairs={{0,12},{4,8},{8,4},{12,0},{1,13},{5,9},{9,5},{13,1},{2,14},{6,10},... | collective-permute-start | bytes 2312 | tf_op jit(solution)/shard_map/ppermute | solution.py:357
  19.5 4.0 %collective-permute-start.6 = (bf16[4,96]{1,0:T(4,128)(2,1)S(1)}, bf16[4,96]{1,0:T(4,128)(2,1)S(1)}, u32[]{:S(2)}, u32[]{:S(2)}) collective-permute-start(bf16[4,96]{1,0:T(4,128)(2,1)S(1)} %get-tuple-element.50), channel_id=1, source_target_pairs={{0,4},{4,0},{8,12},{12,8},{1,5},{5,1},{9,13},{13,9},{2,6},{6,2},{1... | collective-permute-start | bytes 2312 | tf_op jit(solution)/shard_map/ppermute | solution.py:357
  23.8 1.3 %collective-permute-start.7 = (f32[4,2048]{1,0:T(4,128)S(1)}, f32[4,2048]{1,0:T(4,128)S(1)}, u32[]{:S(2)}, u32[]{:S(2)}) collective-permute-start(f32[4,2048]{1,0:T(4,128)S(1)} %shard_map.146), channel_id=1, source_target_pairs={{0,1},{1,0},{2,3},{3,2},{4,5},{5,4},{6,7},{7,6},{8,9},{9,8},{10,11... | collective-permute-start | bytes 98312 | tf_op jit(solution)/shard_map/ppermute | solution.py:451
  25.1 3.8 %collective-permute-start.8 = (bf16[4,2048]{1,0:T(4,128)(2,1)S(1)}, bf16[4,2048]{1,0:T(4,128)(2,1)S(1)}, u32[]{:S(2)}, u32[]{:S(2)}) collective-permute-start(bf16[4,2048]{1,0:T(4,128)(2,1)S(1)} %get-tuple-element.58), channel_id=1, source_target_pairs={{0,2},{2,0},{1,3},{3,1},{4,6},{6,4},{5,7},{7,5},{8,10},{10,8},{9,1... | collective-permute-start | bytes 49160 | tf_op jit(solution)/shard_map/ppermute | solution.py:451
  28.9 5.7 %collective-permute-start.10 = (bf16[4,2048]{1,0:T(4,128)(2,1)S(1)}, bf16[4,2048]{1,0:T(4,128)(2,1)S(1)}, u32[]{:S(2)}, u32[]{:S(2)}) collective-permute-start(bf16[4,2048]{1,0:T(4,128)(2,1)S(1)} %get-tuple-element.56), channel_id=1, source_target_pairs={{0,12},{4,8},{8,4},{12,0},{1,13},{5,9},{9,5},{13,1},{2,14},{6,10},... | collective-permute-start | bytes 49160 | tf_op jit(solution)/shard_map/ppermute | solution.py:451
  31.0 4.6 %collective-permute-start.11 = (bf16[4,2048]{1,0:T(4,128)(2,1)S(1)}, bf16[4,2048]{1,0:T(4,128)(2,1)S(1)}, u32[]{:S(2)}, u32[]{:S(2)}) collective-permute-start(bf16[4,2048]{1,0:T(4,128)(2,1)S(1)} %get-tuple-element.56), channel_id=1, source_target_pairs={{0,8},{4,12},{8,0},{12,4},{1,9},{5,13},{9,1},{13,5},{2,10},{6,14},... | collective-permute-start | bytes 49160 | tf_op jit(solution)/shard_map/ppermute | solution.py:451
  31.0 4.6 %collective-permute-start.9 = (bf16[4,2048]{1,0:T(4,128)(2,1)S(1)}, bf16[4,2048]{1,0:T(4,128)(2,1)S(1)}, u32[]{:S(2)}, u32[]{:S(2)}) collective-permute-start(bf16[4,2048]{1,0:T(4,128)(2,1)S(1)} %get-tuple-element.56), channel_id=1, source_target_pairs={{0,4},{4,0},{8,12},{12,8},{1,5},{5,1},{9,13},{13,9},{2,6},{6,2},{1... | collective-permute-start | bytes 49160 | tf_op jit(solution)/shard_map/ppermute | solution.py:451
  33.4 2.3 %copy-start.1 = (f32[2,2048]{1,0:T(2,128)S(1)}, f32[2,2048]{1,0:T(2,128)}, u32[]{:S(2)}) copy-start(f32[2,2048]{1,0:T(2,128)} %start_ref.1) | copy-start | bytes 49156
  33.4 2.3 %copy-start.2 = (f32[2048]{0:T(1024)S(1)}, f32[2048]{0:T(1024)}, u32[]{:S(2)}) copy-start(f32[2048]{0:T(1024)} %param.16) | copy-start | bytes 24580
  33.4 2.3 %copy-start.3 = (f32[2048]{0:T(1024)S(1)}, f32[2048]{0:T(1024)}, u32[]{:S(2)}) copy-start(f32[2048]{0:T(1024)} %param.17) | copy-start | bytes 24580
  36.1 5.4 %collective-permute-start.12 = (bf16[4,96]{1,0:T(4,128)(2,1)S(1)}, bf16[4,96]{1,0:T(4,128)(2,1)S(1)}, u32[]{:S(2)}, u32[]{:S(2)}) collective-permute-start(bf16[4,96]{1,0:T(4,128)(2,1)S(1)} %get-tuple-element.52), channel_id=1, source_target_pairs={{0,12},{4,8},{8,4},{12,0},{1,13},{5,9},{9,5},{13,1},{2,14},{6,10},... | collective-permute-start | bytes 2312 | tf_op jit(solution)/shard_map/ppermute | solution.py:357
  37.9 4.5 %collective-permute-start.13 = (bf16[4,96]{1,0:T(4,128)(2,1)S(1)}, bf16[4,96]{1,0:T(4,128)(2,1)S(1)}, u32[]{:S(2)}, u32[]{:S(2)}) collective-permute-start(bf16[4,96]{1,0:T(4,128)(2,1)S(1)} %get-tuple-element.53), channel_id=1, source_target_pairs={{0,8},{4,12},{8,0},{12,4},{1,9},{5,13},{9,1},{13,5},{2,10},{6,14},... | collective-permute-start | bytes 2312 | tf_op jit(solution)/shard_map/ppermute | solution.py:357
  39.0 3.6 %collective-permute-start.14 = (bf16[4,96]{1,0:T(4,128)(2,1)S(1)}, bf16[4,96]{1,0:T(4,128)(2,1)S(1)}, u32[]{:S(2)}, u32[]{:S(2)}) collective-permute-start(bf16[4,96]{1,0:T(4,128)(2,1)S(1)} %get-tuple-element.54), channel_id=1, source_target_pairs={{0,4},{4,0},{8,12},{12,8},{1,5},{5,1},{9,13},{13,9},{2,6},{6,2},{1... | collective-permute-start | bytes 2312 | tf_op jit(solution)/shard_map/ppermute | solution.py:357

commit v6 on v5

--- a/solution.py
+++ b/solution.py
@@ -351,8 +351,16 @@
     out_ref[...] = surface.astype(bf16)
 
 
-def exchange(parts, order):
+def crossed_swap(value, axis, by):
+    count = lax.axis_size(axis)
+    places = [(2 * i + r, 2 * (i ^ by) + 1 - r) for i in range(count) for r in range(2)]
+    return lax.ppermute(value, (axis, "rep"), places)
+
+
+def exchange(parts, order, crossed):
     buckets = lax.axis_size("tile")
+    if crossed:
+        return [crossed_swap(parts[k], "tile", k) if k else lax.ppermute(parts[0], "rep", swaps(2, 1)) for k in order]
     if len(parts) == buckets:
         return [lax.ppermute(parts[k], "tile", swaps(buckets, k)) if k else parts[0] for k in order]
     tiles = jnp.arange(buckets) ^ lax.axis_index("tile")
@@ -384,6 +392,9 @@
     parts = buckets if buckets in (2, 4) and bucket % 16 == 0 else 1
     total = layers + 2 * STEPS
     wide_rows = rows + 2 * STEPS
+    crossed = parts > 1 and reps == 2
+    if crossed:
+        mode_shapes, node_area = (lax.ppermute(value, "rep", swaps(2, 1)) for value in (mode_shapes, node_area))
 
     cells = layers * rows
     fields = jnp.stack([pressure, previous_pressure, courant_square])
@@ -436,11 +447,11 @@
         store_kernel, (block, block), (states,), out_specs=(HBM, HBM), scratch=[pltpu.SemaphoreType.DMA((2,))]
     )
 
-    order = [k for k in (0, 2, 3, 1) if k < parts]
+    order = [k for k in (2, 3, 1, 0) if k < parts]
     forces = call(
         functools.partial(project_kernel, order),
         shape_of((STEPS, modes), f32),
-        (area, turned, *exchange(sends, order)),
+        (area, turned, *exchange(sends, order, crossed)),
     )
     addends = [forces]
     for axis in ("rep", "sub", "tile"):
@@ -448,7 +459,10 @@
         forces = functools.reduce(jnp.add, addends)
         if count in (2, 4):
             sent = forces.astype(bf16) if axis != "rep" else forces
-            addends = [forces] + [lax.ppermute(sent, axis, swaps(count, k)) for k in (1, 3, 2) if k < count]
+            if axis != "rep" and reps == 2:
+                addends = [forces] + [crossed_swap(sent, axis, k) for k in (1, 3, 2) if k < count]
+            else:
+                addends = [forces] + [lax.ppermute(sent, axis, swaps(count, k)) for k in (1, 3, 2) if k < count]
         else:
             addends = [lax.psum(forces, axis)]
 
@@ -460,9 +474,9 @@
     )
     share = modes // (buckets * subs * reps)
     modal_state = lax.dynamic_slice_in_dim(state, lax.axis_index(("tile", "sub", "rep")) * share, share, 1)
-    order = [k for k in (0, 3, 2, 1) if k < parts]
+    order = [k for k in (3, 2, 1, 0) if k < parts]
     surface = call(
-        functools.partial(return_kernel, order), shape_of((STEPS, slots), bf16), (route, *exchange(sends, order))
+        functools.partial(return_kernel, order), shape_of((STEPS, slots), bf16), (route, *exchange(sends, order, crossed))
     )
     return (final_field, prior_field, surface.reshape(1, 1, 1, STEPS, slots), modal_state)
 

time: 43.6 us -> 41.1 us (0.943)
  waiting for transfers between devices: 13.2 us -> 11.9 us
  starting transfers between devices: 21.3 us -> 20.1 us
    ppermute x5 -> x1, starting transfers between devices: 6.07 us -> 0.4 us  [body(): lax.ppermute(sent, axis, swaps(count, k))]
    ppermute x6 -> x14, starting transfers between devices: 8.39 us -> 13.3 us  [the longest x10 12 us: crossed_swap(): return lax.ppermute(value, (axis, 'rep'), places)]
    ppermute x5 -> x1, waiting for transfers between devices: 5.03 us -> 0.86 us  [body(): lax.ppermute(sent, axis, swaps(count, k))]
    ppermute x6 -> x14, waiting for transfers between devices: 5.04 us -> 7.83 us  [the longest x10 7.82 us: crossed_swap(): return lax.ppermute(value, (axis, 'rep'), places)]
    ppermute x2, starting transfers between devices: 5.17 us -> 4.73 us  [body(): lax.ppermute(value, 'tile', shift(buckets, by))]
  transfers between devices with their start and end apart: 15 -> 19, of which waited for: 13 -> 12; matrix products, arithmetic and copies ran while one was open for 1% -> 4% of each run, Pallas kernels for 7% -> 8%
where the time goes in v6:
time: 41.1 us; the launch traced here: 40.9 us
  starting transfers between devices  20.1 us (49%)
  waiting for transfers between devices  11.9 us (29%)
  Pallas kernels  5.93 us (14%)
  between operations  1.43 us (3%)
  other arithmetic  0.94 us (2%)
  local copies, waits for them, and re-layouts  0.6 us (1%)
    ppermute x10, starting transfers between devices, crossed_swap(): return lax.ppermute(value, (axis, 'rep'), places)  12 us
    ppermute x10, waiting for transfers between devices, crossed_swap(): return lax.ppermute(value, (axis, 'rep'), places)  7.82 us
    pallas_call x11, Pallas kernels, call(): pl.pallas_call(kernel, out_shape=out_shape, in_specs=specs or [VMEM] * le...  5.93 us
    ppermute x2, starting transfers between devices, body(): lax.ppermute(value, 'tile', shift(buckets, by))  4.73 us
    ppermute x1, starting transfers between devices, body(): sub_halo = (lax.ppermute(packed[0], 'sub', shift(2, 1)),) * 2  1.56 us
    ppermute x2, waiting for transfers between devices, body(): lax.ppermute(value, 'tile', shift(buckets, by))  1.2 us
    ppermute x1, waiting for transfers between devices, body(): sub_halo = (lax.ppermute(packed[0], 'sub', shift(2, 1)),) * 2  1.12 us
    another operation x1, other arithmetic, body(): fields = jnp.stack([pressure, previous_pressure, courant_square])  0.92 us
  transfers between devices with their start and end apart: 19, of which 12 were waited for; matrix products, arithmetic and copies ran while one was open for 4% of the time, Pallas kernels for 8%

profile of v6, /device:TPU:0, one launch (start us, length us, event | category | flops | bytes accessed | tf_op | source)
XLA Modules:
  0.0 40.9 jit_solution(16723854106560332168)
XLA Ops:
  1.1 0.9 %pad_maximum_fusion.fields = f32[3,8,16,128]{3,2,1,0:T(8,128)S(1)} fusion(f32[1,8,16,128]{3,2,1,0:T(8,128)} %bitcast.14, f32[1,8,16,128]{3,2,1,0:T(8,128)} %bitcast.15, f32[1,8,16,128]{3,2,1,0:T(8,128)} %bitcast.16), kind=kLoop, calls=%fused_computation | loop fusion | flops 98304 | bytes 393216 | tf_op jit(solution)/shard_map/stack | solution.py:400
  2.1 2.6 %collective-permute-start = (bf16[11,16,128]{2,1,0:T(8,128)(2,1)S(1)}, bf16[11,16,128]{2,1,0:T(8,128)(2,1)S(1)}, u32[]{:S(2)}, u32[]{:S(2)}) collective-permute-start(bf16[11,16,128]{2,1,0:T(8,128)(2,1)S(1)} %get-tuple-element.30.after_ref), channel_id=1, source_target_pairs={{0,4},{4,8},{8,12},{12,0},{1,5},{5,9},{9,13},{13,1},{2,6},{6,10},{... | collective-permute-start | bytes 135176 | tf_op jit(solution)/shard_map/ppermute | solution.py:408
  4.8 2.1 %collective-permute-start.1 = (bf16[11,16,128]{2,1,0:T(8,128)(2,1)S(1)}, bf16[11,16,128]{2,1,0:T(8,128)(2,1)S(1)}, u32[]{:S(2)}, u32[]{:S(2)}) collective-permute-start(bf16[11,16,128]{2,1,0:T(8,128)(2,1)S(1)} %get-tuple-element.31), channel_id=1, source_target_pairs={{0,12},{4,0},{8,4},{12,8},{1,13},{5,1},{9,5},{13,9},{2,14},{6,2},{... | collective-permute-start | bytes 135176 | tf_op jit(solution)/shard_map/ppermute | solution.py:408
  7.7 0.6 %shard_map.139 = (bf16[384,384]{1,0:T(8,128)(2,1)S(1)}, bf16[256,384]{1,0:T(8,128)(2,1)S(1)}) custom-call(bf16[11,16,128]{2,1,0:T(8,128)(2,1)S(1)} %get-tuple-element.30.after_ref, s32[1,384]{1,0:T(1,128)S(1)} %bitcast.12, s32[1,384]{1,0:T(1,128)S(1)} %bitcast.13, s32[1,1]{1,0:T(1,128)} %bitcast.9.count_ref), custom_call_target="tpu_custom_call" | custom-call | flops 1000000000 | tf_op jit(solution)/shard_map/pallas_call | solution.py:44
  8.4 0.8 %collective-permute-done.tile_before = bf16[11,16,128]{2,1,0:T(8,128)(2,1)S(1)} collective-permute-done((bf16[11,16,128]{2,1,0:T(8,128)(2,1)S(1)}, bf16[11,16,128]{2,1,0:T(8,128)(2,1)S(1)}, u32[]{:S(2)}, u32[]{:S(2)}) %collective-permute-start) | collective-permute-done | bytes 45088 | tf_op jit(solution)/shard_map/ppermute | solution.py:408
  9.6 1.6 %collective-permute-start.2 = (bf16[3,64,128]{2,1,0:T(8,128)(2,1)S(1)}, bf16[3,64,128]{2,1,0:T(8,128)(2,1)S(1)}, u32[]{:S(2)}, u32[]{:S(2)}) collective-permute-start(bf16[3,64,128]{2,1,0:T(8,128)(2,1)S(1)} %shard_map.140.ready_ref), channel_id=1, source_target_pairs={{0,2},{2,0},{1,3},{3,1},{4,6},{6,4},{5,7},{7,5},{8,10},{10,8},{9,1... | collective-permute-start | bytes 147464 | tf_op jit(solution)/shard_map/ppermute | solution.py:414
  11.2 1.5 %shard_map.141 = (bf16[384,2048]{1,0:T(8,128)(2,1)S(1)}, bf16[2048,384]{1,0:T(8,128)(2,1)S(1)}, f32[1,384]{1,0:T(1,128)S(1)}) custom-call(bf16[3,64,128]{2,1,0:T(8,128)(2,1)S(1)} %shard_map.140.ready_ref, bf16[384,2048]{1,0:T(8,128)(2,1)S(1)} %collective-permute-done.3.shapes_ref, f32[1,384]{1,0:T(1,128)S(1)} %reshape.32.area_ref), custom_call_target="tpu_custom_call" | custom-call | flops 1000000000 | tf_op jit(solution)/shard_map/pallas_call | solution.py:44
  12.7 1.1 %collective-permute-done.2.sub_after.sub_before = bf16[3,64,128]{2,1,0:T(8,128)(2,1)S(1)} collective-permute-done((bf16[3,64,128]{2,1,0:T(8,128)(2,1)S(1)}, bf16[3,64,128]{2,1,0:T(8,128)(2,1)S(1)}, u32[]{:S(2)}, u32[]{:S(2)}) %collective-permute-start.2) | collective-permute-done | bytes 49184 | tf_op jit(solution)/shard_map/ppermute | solution.py:414
  14.3 0.9 %collective-permute-done.5.rep_after.rep_before = bf16[3,24,128]{2,1,0:T(8,128)(2,1)S(1)} collective-permute-done((bf16[3,24,128]{2,1,0:T(8,128)(2,1)S(1)}, bf16[3,24,128]{2,1,0:T(8,128)(2,1)S(1)}, u32[]{:S(2)}, u32[]{:S(2)}) %collective-permute-start.5) | collective-permute-done | bytes 18464 | tf_op jit(solution)/shard_map/ppermute | solution.py:430
  15.2 1.1 %shard_map.144 = (f32[2,8,16,128]{3,2,1,0:T(8,128)S(1)}, bf16[4,96]{1,0:T(4,128)(2,1)S(1)}, bf16[4,96]{1,0:T(4,128)(2,1)S(1)}, bf16[4,96]{1,0:T(4,128)(2,1)S(1)}, bf16[4,96]{1,0:T(4,128)(2,1)S(1)}) custom-call(f32[16,24,128]{2,1,0:T(8,128)S(1)} %get-tuple-element.35.now_in, f32[16,24,128]{2,1,0:T(8,128)S(1)} %get-tuple-element.36.ago_in, ...), custom_call_target="tpu_custom_call" | custom-call | flops 2000000000 | tf_op jit(solution)/shard_map/pallas_call | solution.py:44
  16.4 1.6 %collective-permute-start.6 = (bf16[4,96]{1,0:T(4,128)(2,1)S(1)}, bf16[4,96]{1,0:T(4,128)(2,1)S(1)}, u32[]{:S(2)}, u32[]{:S(2)}) collective-permute-start(bf16[4,96]{1,0:T(4,128)(2,1)S(1)} %get-tuple-element.47), channel_id=1, source_target_pairs={{0,9},{1,8},{4,13},{5,12},{8,1},{9,0},{12,5},{13,4},{2,11},{3,10},... | collective-permute-start | bytes 2312 | tf_op jit(solution)/shard_map/ppermute | solution.py:357
  18.0 1.5 %collective-permute-start.7 = (bf16[4,96]{1,0:T(4,128)(2,1)S(1)}, bf16[4,96]{1,0:T(4,128)(2,1)S(1)}, u32[]{:S(2)}, u32[]{:S(2)}) collective-permute-start(bf16[4,96]{1,0:T(4,128)(2,1)S(1)} %get-tuple-element.48), channel_id=1, source_target_pairs={{0,13},{1,12},{4,9},{5,8},{8,5},{9,4},{12,1},{13,0},{2,15},{3,14},... | collective-permute-start | bytes 2312 | tf_op jit(solution)/shard_map/ppermute | solution.py:357
  20.3 2.5 %collective-permute-done.7.rest_1_ = bf16[4,96]{1,0:T(4,128)(2,1)S(1)} collective-permute-done((bf16[4,96]{1,0:T(4,128)(2,1)S(1)}, bf16[4,96]{1,0:T(4,128)(2,1)S(1)}, u32[]{:S(2)}, u32[]{:S(2)}) %collective-permute-start.7) | collective-permute-done | bytes 800 | tf_op jit(solution)/shard_map/ppermute | solution.py:357
  23.5 0.9 %collective-permute-done.10 = f32[4,2048]{1,0:T(4,128)S(1)} collective-permute-done((f32[4,2048]{1,0:T(4,128)S(1)}, f32[4,2048]{1,0:T(4,128)S(1)}, u32[]{:S(2)}, u32[]{:S(2)}) %collective-permute-start.10) | collective-permute-done | bytes 32800 | tf_op jit(solution)/shard_map/ppermute | solution.py:465
  24.4 1.5 %collective-permute-start.11 = (bf16[4,2048]{1,0:T(4,128)(2,1)S(1)}, bf16[4,2048]{1,0:T(4,128)(2,1)S(1)}, u32[]{:S(2)}, u32[]{:S(2)}) collective-permute-start(bf16[4,2048]{1,0:T(4,128)(2,1)S(1)} %get-tuple-element.58), channel_id=1, source_target_pairs={{0,3},{1,2},{2,1},{3,0},{4,7},{5,6},{6,5},{7,4},{8,11},{9,10},{10,... | collective-permute-start | bytes 49160 | tf_op jit(solution)/shard_map/ppermute | solution.py:357
  25.9 1.7 %collective-permute-done.11 = bf16[4,2048]{1,0:T(4,128)(2,1)S(1)} collective-permute-done((bf16[4,2048]{1,0:T(4,128)(2,1)S(1)}, bf16[4,2048]{1,0:T(4,128)(2,1)S(1)}, u32[]{:S(2)}, u32[]{:S(2)}) %collective-permute-start.11) | collective-permute-done | bytes 16416 | tf_op jit(solution)/shard_map/ppermute | solution.py:357
  27.7 2.6 %collective-permute-start.13 = (bf16[4,2048]{1,0:T(4,128)(2,1)S(1)}, bf16[4,2048]{1,0:T(4,128)(2,1)S(1)}, u32[]{:S(2)}, u32[]{:S(2)}) collective-permute-start(bf16[4,2048]{1,0:T(4,128)(2,1)S(1)} %get-tuple-element.56), channel_id=1, source_target_pairs={{0,13},{1,12},{4,9},{5,8},{8,5},{9,4},{12,1},{13,0},{2,15},{3,14},... | collective-permute-start | bytes 49160 | tf_op jit(solution)/shard_map/ppermute | solution.py:357
  30.9 0.7 %shard_map.145 = (f32[8,16,128]{2,1,0:T(8,128)}, f32[8,16,128]{2,1,0:T(8,128)}) custom-call(f32[2,8,16,128]{3,2,1,0:T(8,128)S(1)} %get-tuple-element.42.states), custom_call_target="tpu_custom_call" | custom-call | flops 1000000000 | tf_op jit(solution)/shard_map/pallas_call | solution.py:44
  31.6 1.2 %collective-permute-done.13.rest_2_ = bf16[4,2048]{1,0:T(4,128)(2,1)S(1)} collective-permute-done((bf16[4,2048]{1,0:T(4,128)(2,1)S(1)}, bf16[4,2048]{1,0:T(4,128)(2,1)S(1)}, u32[]{:S(2)}, u32[]{:S(2)}) %collective-permute-start.13) | collective-permute-done | bytes 16416 | tf_op jit(solution)/shard_map/ppermute | solution.py:357
  32.8 1.7 %collective-permute-done.14.rest_3_ = bf16[4,2048]{1,0:T(4,128)(2,1)S(1)} collective-permute-done((bf16[4,2048]{1,0:T(4,128)(2,1)S(1)}, bf16[4,2048]{1,0:T(4,128)(2,1)S(1)}, u32[]{:S(2)}, u32[]{:S(2)}) %collective-permute-start.14) | collective-permute-done | bytes 16416 | tf_op jit(solution)/shard_map/ppermute | solution.py:357
  35.0 1.1 %collective-permute-start.15 = (bf16[4,96]{1,0:T(4,128)(2,1)S(1)}, bf16[4,96]{1,0:T(4,128)(2,1)S(1)}, u32[]{:S(2)}, u32[]{:S(2)}) collective-permute-start(bf16[4,96]{1,0:T(4,128)(2,1)S(1)} %get-tuple-element.51), channel_id=1, source_target_pairs={{0,13},{1,12},{4,9},{5,8},{8,5},{9,4},{12,1},{13,0},{2,15},{3,14},... | collective-permute-start | bytes 2312 | tf_op jit(solution)/shard_map/ppermute | solution.py:357
  36.2 2.6 %collective-permute-start.17 = (bf16[4,96]{1,0:T(4,128)(2,1)S(1)}, bf16[4,96]{1,0:T(4,128)(2,1)S(1)}, u32[]{:S(2)}, u32[]{:S(2)}) collective-permute-start(bf16[4,96]{1,0:T(4,128)(2,1)S(1)} %get-tuple-element.53), channel_id=1, source_target_pairs={{0,5},{1,4},{4,1},{5,0},{8,13},{9,12},{12,9},{13,8},{2,7},{3,6},{6... | collective-permute-start | bytes 2312 | tf_op jit(solution)/shard_map/ppermute | solution.py:357
  39.3 0.6 %constant_dynamic-slice_fusion = f32[2,128]{1,0:T(2,128)} fusion(f32[2,2048]{1,0:T(2,128)S(1)} %get-tuple-element.55, s32[]{:T(128)S(6)} %select_n.3), kind=kLoop, calls=%fused_computation.2 | loop fusion | bytes 2052 | tf_op jit(solution)/shard_map/dynamic_slice | solution.py:476
  40.1 0.8 %shard_map.148 = bf16[4,384]{1,0:T(4,128)(2,1)} custom-call(bf16[384,384]{1,0:T(8,128)(2,1)S(1)} %get-tuple-element.32.ready_ref.route_ref, bf16[4,96]{1,0:T(4,128)(2,1)S(1)} %collective-permute-done.15.rest_0_, bf16[4,96]{1,0:T(4,128)(2,1)S(1)} %collective-permute-done.16.rest_1_, bf16[4,96]{1,0:T(4,128)(2,1)S(1)} %collective-permute-done.17.rest_2_, ...), custom_call_target="tpu_custom_call" | custom-call | flops 1000000000 | tf_op jit(solution)/shard_map/pallas_call | solution.py:44
  (42 shorter events, 5.2 us)
Async XLA Ops:
  0.6 10.5 %collective-permute-start.3 = (bf16[384,2048]{1,0:T(8,128)(2,1)}, bf16[384,2048]{1,0:T(8,128)(2,1)S(1)}, u32[]{:S(2)}, u32[]{:S(2)}) collective-permute-start(bf16[384,2048]{1,0:T(8,128)(2,1)} %param.15), channel_id=1, source_target_pairs={{0,1},{1,0},{2,3},{3,2},{4,5},{5,4},{6,7},{7,6},{8,9},{9,8},{10,11... | collective-permute-start | bytes 4718600 | tf_op jit(solution)/shard_map/ppermute | solution.py:397
  2.1 4.8 %copy-start.5 = (f32[384]{0:T(512)S(1)}, f32[384]{0:T(512)}, u32[]{:S(2)}) copy-start(f32[384]{0:T(512)} %param.14) | copy-start | bytes 4612
  2.1 5.6 %copy-start.3 = (s32[1,1,1,384,1]{3,4,2,1,0:T(1,128)S(1)}, s32[1,1,1,384,1]{3,4,2,1,0:T(1,128)}, u32[]{:S(2)}) copy-start(s32[1,1,1,384,1]{3,4,2,1,0:T(1,128)} %param.20) | copy-start | bytes 4612
  2.1 5.6 %copy-start.4 = (s32[1,1,1,384]{3,2,1,0:T(1,128)S(1)}, s32[1,1,1,384]{3,2,1,0:T(1,128)}, u32[]{:S(2)}) copy-start(s32[1,1,1,384]{3,2,1,0:T(1,128)} %param.19) | copy-start | bytes 4612
  2.1 7.1 %collective-permute-start = (bf16[11,16,128]{2,1,0:T(8,128)(2,1)S(1)}, bf16[11,16,128]{2,1,0:T(8,128)(2,1)S(1)}, u32[]{:S(2)}, u32[]{:S(2)}) collective-permute-start(bf16[11,16,128]{2,1,0:T(8,128)(2,1)S(1)} %get-tuple-element.30.after_ref), channel_id=1, source_target_pairs={{0,4},{4,8},{8,12},{12,0},{1,5},{5,9},{9,13},{13,1},{2,6},{6,10},{... | collective-permute-start | bytes 135176 | tf_op jit(solution)/shard_map/ppermute | solution.py:408
  4.8 4.8 %collective-permute-start.1 = (bf16[11,16,128]{2,1,0:T(8,128)(2,1)S(1)}, bf16[11,16,128]{2,1,0:T(8,128)(2,1)S(1)}, u32[]{:S(2)}, u32[]{:S(2)}) collective-permute-start(bf16[11,16,128]{2,1,0:T(8,128)(2,1)S(1)} %get-tuple-element.31), channel_id=1, source_target_pairs={{0,12},{4,0},{8,4},{12,8},{1,13},{5,1},{9,5},{13,9},{2,14},{6,2},{... | collective-permute-start | bytes 135176 | tf_op jit(solution)/shard_map/ppermute | solution.py:408
  6.9 1.5 %collective-permute-start.4 = (f32[384]{0:T(512)S(1)}, f32[384]{0:T(512)S(1)}, u32[]{:S(2)}, u32[]{:S(2)}) collective-permute-start(f32[384]{0:T(512)S(1)} %copy-done.5), channel_id=1, source_target_pairs={{0,1},{1,0},{2,3},{3,2},{4,5},{5,4},{6,7},{7,6},{8,9},{9,8},{10,11... | collective-permute-start | bytes 4616 | tf_op jit(solution)/shard_map/ppermute | solution.py:397
  9.6 4.2 %collective-permute-start.2 = (bf16[3,64,128]{2,1,0:T(8,128)(2,1)S(1)}, bf16[3,64,128]{2,1,0:T(8,128)(2,1)S(1)}, u32[]{:S(2)}, u32[]{:S(2)}) collective-permute-start(bf16[3,64,128]{2,1,0:T(8,128)(2,1)S(1)} %shard_map.140.ready_ref), channel_id=1, source_target_pairs={{0,2},{2,0},{1,3},{3,1},{4,6},{6,4},{5,7},{7,5},{8,10},{10,8},{9,1... | collective-permute-start | bytes 147464 | tf_op jit(solution)/shard_map/ppermute | solution.py:414
  14.0 1.3 %collective-permute-start.5 = (bf16[3,24,128]{2,1,0:T(8,128)(2,1)S(1)}, bf16[3,24,128]{2,1,0:T(8,128)(2,1)S(1)}, u32[]{:S(2)}, u32[]{:S(2)}) collective-permute-start(bf16[3,24,128]{2,1,0:T(8,128)(2,1)S(1)} %get-tuple-element.34.ready_ref), channel_id=1, source_target_pairs={{0,1},{1,0},{2,3},{3,2},{4,5},{5,4},{6,7},{7,6},{8,9},{9,8},{10,11... | collective-permute-start | bytes 55304 | tf_op jit(solution)/shard_map/ppermute | solution.py:430
  16.4 3.9 %collective-permute-start.6 = (bf16[4,96]{1,0:T(4,128)(2,1)S(1)}, bf16[4,96]{1,0:T(4,128)(2,1)S(1)}, u32[]{:S(2)}, u32[]{:S(2)}) collective-permute-start(bf16[4,96]{1,0:T(4,128)(2,1)S(1)} %get-tuple-element.47), channel_id=1, source_target_pairs={{0,9},{1,8},{4,13},{5,12},{8,1},{9,0},{12,5},{13,4},{2,11},{3,10},... | collective-permute-start | bytes 2312 | tf_op jit(solution)/shard_map/ppermute | solution.py:357
  18.0 4.8 %collective-permute-start.7 = (bf16[4,96]{1,0:T(4,128)(2,1)S(1)}, bf16[4,96]{1,0:T(4,128)(2,1)S(1)}, u32[]{:S(2)}, u32[]{:S(2)}) collective-permute-start(bf16[4,96]{1,0:T(4,128)(2,1)S(1)} %get-tuple-element.48), channel_id=1, source_target_pairs={{0,13},{1,12},{4,9},{5,8},{8,5},{9,4},{12,1},{13,0},{2,15},{3,14},... | collective-permute-start | bytes 2312 | tf_op jit(solution)/shard_map/ppermute | solution.py:357
  19.5 3.2 %collective-permute-start.8 = (bf16[4,96]{1,0:T(4,128)(2,1)S(1)}, bf16[4,96]{1,0:T(4,128)(2,1)S(1)}, u32[]{:S(2)}, u32[]{:S(2)}) collective-permute-start(bf16[4,96]{1,0:T(4,128)(2,1)S(1)} %get-tuple-element.49), channel_id=1, source_target_pairs={{0,5},{1,4},{4,1},{5,0},{8,13},{9,12},{12,9},{13,8},{2,7},{3,6},{6... | collective-permute-start | bytes 2312 | tf_op jit(solution)/shard_map/ppermute | solution.py:357
  19.8 3.0 %collective-permute-start.9 = (bf16[4,96]{1,0:T(4,128)(2,1)S(1)}, bf16[4,96]{1,0:T(4,128)(2,1)S(1)}, u32[]{:S(2)}, u32[]{:S(2)}) collective-permute-start(bf16[4,96]{1,0:T(4,128)(2,1)S(1)} %get-tuple-element.50), channel_id=1, source_target_pairs={{0,1},{1,0},{2,3},{3,2},{4,5},{5,4},{6,7},{7,6},{8,9},{9,8},{10,11... | collective-permute-start | bytes 2312 | tf_op jit(solution)/shard_map/ppermute | solution.py:363
  23.1 1.3 %collective-permute-start.10 = (f32[4,2048]{1,0:T(4,128)S(1)}, f32[4,2048]{1,0:T(4,128)S(1)}, u32[]{:S(2)}, u32[]{:S(2)}) collective-permute-start(f32[4,2048]{1,0:T(4,128)S(1)} %shard_map.146), channel_id=1, source_target_pairs={{0,1},{1,0},{2,3},{3,2},{4,5},{5,4},{6,7},{7,6},{8,9},{9,8},{10,11... | collective-permute-start | bytes 98312 | tf_op jit(solution)/shard_map/ppermute | solution.py:465
  24.4 3.2 %collective-permute-start.11 = (bf16[4,2048]{1,0:T(4,128)(2,1)S(1)}, bf16[4,2048]{1,0:T(4,128)(2,1)S(1)}, u32[]{:S(2)}, u32[]{:S(2)}) collective-permute-start(bf16[4,2048]{1,0:T(4,128)(2,1)S(1)} %get-tuple-element.58), channel_id=1, source_target_pairs={{0,3},{1,2},{2,1},{3,0},{4,7},{5,6},{6,5},{7,4},{8,11},{9,10},{10,... | collective-permute-start | bytes 49160 | tf_op jit(solution)/shard_map/ppermute | solution.py:357
  27.7 3.9 %collective-permute-start.12 = (bf16[4,2048]{1,0:T(4,128)(2,1)S(1)}, bf16[4,2048]{1,0:T(4,128)(2,1)S(1)}, u32[]{:S(2)}, u32[]{:S(2)}) collective-permute-start(bf16[4,2048]{1,0:T(4,128)(2,1)S(1)} %get-tuple-element.56), channel_id=1, source_target_pairs={{0,5},{1,4},{4,1},{5,0},{8,13},{9,12},{12,9},{13,8},{2,7},{3,6},{6... | collective-permute-start | bytes 49160 | tf_op jit(solution)/shard_map/ppermute | solution.py:357
  27.7 5.1 %collective-permute-start.13 = (bf16[4,2048]{1,0:T(4,128)(2,1)S(1)}, bf16[4,2048]{1,0:T(4,128)(2,1)S(1)}, u32[]{:S(2)}, u32[]{:S(2)}) collective-permute-start(bf16[4,2048]{1,0:T(4,128)(2,1)S(1)} %get-tuple-element.56), channel_id=1, source_target_pairs={{0,13},{1,12},{4,9},{5,8},{8,5},{9,4},{12,1},{13,0},{2,15},{3,14},... | collective-permute-start | bytes 49160 | tf_op jit(solution)/shard_map/ppermute | solution.py:357
  30.4 4.2 %collective-permute-start.14 = (bf16[4,2048]{1,0:T(4,128)(2,1)S(1)}, bf16[4,2048]{1,0:T(4,128)(2,1)S(1)}, u32[]{:S(2)}, u32[]{:S(2)}) collective-permute-start(bf16[4,2048]{1,0:T(4,128)(2,1)S(1)} %get-tuple-element.56), channel_id=1, source_target_pairs={{0,9},{1,8},{4,13},{5,12},{8,1},{9,0},{12,5},{13,4},{2,11},{3,10},... | collective-permute-start | bytes 49160 | tf_op jit(solution)/shard_map/ppermute | solution.py:357
  30.9 3.7 %copy-start.1 = (f32[2048]{0:T(1024)S(1)}, f32[2048]{0:T(1024)}, u32[]{:S(2)}) copy-start(f32[2048]{0:T(1024)} %param.16) | copy-start | bytes 24580
  30.9 3.7 %copy-start.2 = (f32[2048]{0:T(1024)S(1)}, f32[2048]{0:T(1024)}, u32[]{:S(2)}) copy-start(f32[2048]{0:T(1024)} %param.17) | copy-start | bytes 24580
  35.0 4.8 %collective-permute-start.15 = (bf16[4,96]{1,0:T(4,128)(2,1)S(1)}, bf16[4,96]{1,0:T(4,128)(2,1)S(1)}, u32[]{:S(2)}, u32[]{:S(2)}) collective-permute-start(bf16[4,96]{1,0:T(4,128)(2,1)S(1)} %get-tuple-element.51), channel_id=1, source_target_pairs={{0,13},{1,12},{4,9},{5,8},{8,5},{9,4},{12,1},{13,0},{2,15},{3,14},... | collective-permute-start | bytes 2312 | tf_op jit(solution)/shard_map/ppermute | solution.py:357
  36.1 3.9 %collective-permute-start.16 = (bf16[4,96]{1,0:T(4,128)(2,1)S(1)}, bf16[4,96]{1,0:T(4,128)(2,1)S(1)}, u32[]{:S(2)}, u32[]{:S(2)}) collective-permute-start(bf16[4,96]{1,0:T(4,128)(2,1)S(1)} %get-tuple-element.52), channel_id=1, source_target_pairs={{0,9},{1,8},{4,13},{5,12},{8,1},{9,0},{12,5},{13,4},{2,11},{3,10},... | collective-permute-start | bytes 2312 | tf_op jit(solution)/shard_map/ppermute | solution.py:357
  36.2 3.9 %collective-permute-start.17 = (bf16[4,96]{1,0:T(4,128)(2,1)S(1)}, bf16[4,96]{1,0:T(4,128)(2,1)S(1)}, u32[]{:S(2)}, u32[]{:S(2)}) collective-permute-start(bf16[4,96]{1,0:T(4,128)(2,1)S(1)} %get-tuple-element.53), channel_id=1, source_target_pairs={{0,5},{1,4},{4,1},{5,0},{8,13},{9,12},{12,9},{13,8},{2,7},{3,6},{6... | collective-permute-start | bytes 2312 | tf_op jit(solution)/shard_map/ppermute | solution.py:357
  38.8 1.3 %collective-permute-start.18 = (bf16[4,96]{1,0:T(4,128)(2,1)S(1)}, bf16[4,96]{1,0:T(4,128)(2,1)S(1)}, u32[]{:S(2)}, u32[]{:S(2)}) collective-permute-start(bf16[4,96]{1,0:T(4,128)(2,1)S(1)} %get-tuple-element.54), channel_id=1, source_target_pairs={{0,1},{1,0},{2,3},{3,2},{4,5},{5,4},{6,7},{7,6},{8,9},{9,8},{10,11... | collective-permute-start | bytes 2312 | tf_op jit(solution)/shard_map/ppermute | solution.py:363
  (1 other events, 3.7 us)

commit v7 on v6

--- a/solution.py
+++ b/solution.py
@@ -63,10 +63,16 @@
     return copies
 
 
-def both_ways(axis, ahead, behind):
+def send(value, axis, places, crossed):
+    if not crossed:
+        return lax.ppermute(value, axis, places)
+    return lax.ppermute(value, (axis, "rep"), [(2 * i + r, 2 * j + 1 - r) for i, j in places for r in range(2)])
+
+
+def both_ways(axis, ahead, behind, crossed=False):
     count = lax.axis_size(axis)
-    after = lax.ppermute(behind, axis, line(count, -1))
-    before = lax.ppermute(ahead, axis, line(count, 1))
+    after = send(behind, axis, line(count, -1), crossed)
+    before = send(ahead, axis, line(count, 1), crossed)
     return after, before
 
 
@@ -91,38 +97,54 @@
     place_ref[rows:] = dot(lane.astype(bf16), route, (1, 1)).astype(bf16)
 
 
-def pack_tile_kernel(fields, ahead, behind):
+def end_rows(layers, outs):
+    rows, lanes = layers[0].shape
+    low = iota((SUBLANES, lanes), 0) < STEPS
+    last = [pltpu.roll(layer[rows - SUBLANES :], STEPS, 0) for layer in layers]
+    picked = [jnp.where(low, a, pltpu.roll(b, STEPS, 0)) for a, b in (last, [layer[:SUBLANES] for layer in layers])]
+    if outs == 1:
+        picked = [jnp.where(lax.axis_index("sub") == 0, *picked)]
+    return picked
+
+
+def pack_tile_kernel(fields, ahead, behind, *ends):
     layers = fields.shape[1]
     for out, base, unused in ((ahead, layers - STEPS, 0), (behind, 0, STEPS - 1)):
         kept = [(at, k) for at in range(FIELDS) for k in range(STEPS) if at < 2 or k != unused]
         for entry, (at, k) in enumerate(kept):
             out[entry] = fields[at, base + k].astype(bf16)
+    for at in range(FIELDS):
+        for pair in range(layers // 2):
+            picked = end_rows([fields[at, 2 * pair], fields[at, 2 * pair + 1]], len(ends))
+            for out, value in zip(ends, picked):
+                out[at, pair * SUBLANES : (pair + 1) * SUBLANES, :] = value.astype(bf16)
+
+
+def layer_beside(at, k, layers, tile_before, tile_after):
+    side, depth, unused = (tile_before, k, 0) if k < STEPS else (tile_after, k - STEPS - layers, STEPS - 1)
+    if at == 2 and depth == unused:
+        return jnp.zeros(side.shape[1:], f32)
+    return side[at * STEPS + depth - (at == 2 and unused == 0)].astype(f32)
 
 
 def layer_of_block(at, k, fields, tile_before, tile_after):
     layers = fields.shape[1]
     if STEPS <= k < STEPS + layers:
         return fields[at, k - STEPS]
-    side, depth, unused = (tile_before, k, 0) if k < STEPS else (tile_after, k - STEPS - layers, STEPS - 1)
-    if at == 2 and depth == unused:
-        return jnp.zeros(fields.shape[2:], f32)
-    return side[at * STEPS + depth - (at == 2 and unused == 0)].astype(f32)
-
-
-def pack_sub_kernel(sides, fields, tile_before, tile_after, ready_ref, *outs):
-    layers, rows, lanes = fields.shape[1:]
-    low = iota((SUBLANES, lanes), 0) < STEPS
+    return layer_beside(at, k, layers, tile_before, tile_after)
+
+
+def pack_sub_kernel(sides, tile_before, tile_after, ready_ref, *rest):
+    ends, outs = rest[:sides], rest[sides:]
+    held = ends[0].shape[1]
+    layers = held // STEPS
     for at in range(FIELDS):
-        for pair in range(layers // 2 + STEPS):
-            tiles = []
-            for layer in (2 * pair, 2 * pair + 1):
-                here = layer_of_block(at, layer, fields, tile_before, tile_after)
-                tiles.append((pltpu.roll(here[rows - SUBLANES :], STEPS, 0), here[:SUBLANES]))
-            picked = [jnp.where(low, a, pltpu.roll(b, STEPS, 0)) for a, b in zip(*tiles)]
-            if sides == 1:
-                picked = [jnp.where(lax.axis_index("sub") == 0, picked[0], picked[1])]
-            for out, value in zip(outs, picked):
-                out[at, pair * SUBLANES : (pair + 1) * SUBLANES, :] = value.astype(bf16)
+        for out, own in zip(outs, ends):
+            out[at, STEPS * STEPS : STEPS * STEPS + held, :] = own[at]
+        for first in (*range(0, STEPS, 2), *range(STEPS + layers, 2 * STEPS + layers, 2)):
+            beside = [layer_beside(at, k, layers, tile_before, tile_after) for k in (first, first + 1)]
+            for out, value in zip(outs, end_rows(beside, sides)):
+                out[at, first * STEPS : first * STEPS + SUBLANES, :] = value.astype(bf16)
 
 
 def side_rows(at, k, after_ref, before_ref):
@@ -351,18 +373,11 @@
     out_ref[...] = surface.astype(bf16)
 
 
-def crossed_swap(value, axis, by):
-    count = lax.axis_size(axis)
-    places = [(2 * i + r, 2 * (i ^ by) + 1 - r) for i in range(count) for r in range(2)]
-    return lax.ppermute(value, (axis, "rep"), places)
-
-
 def exchange(parts, order, crossed):
     buckets = lax.axis_size("tile")
-    if crossed:
-        return [crossed_swap(parts[k], "tile", k) if k else lax.ppermute(parts[0], "rep", swaps(2, 1)) for k in order]
     if len(parts) == buckets:
-        return [lax.ppermute(parts[k], "tile", swaps(buckets, k)) if k else parts[0] for k in order]
+        own = lax.ppermute(parts[0], "rep", swaps(2, 1)) if crossed else parts[0]
+        return [send(parts[k], "tile", swaps(buckets, k), crossed) if k else own for k in order]
     tiles = jnp.arange(buckets) ^ lax.axis_index("tile")
     (whole,) = parts
     steps, total = whole.shape
@@ -398,22 +413,27 @@
 
     cells = layers * rows
     fields = jnp.stack([pressure, previous_pressure, courant_square])
+    sides = 1 if subs == 2 else 2
     slab = shape_of((FIELDS * STEPS - 1, rows, lanes), bf16)
-    packed = call(pack_tile_kernel, (slab, slab), (fields,))
+    held = shape_of((FIELDS, layers * STEPS, lanes), bf16)
+    ahead, behind, *ends = call(pack_tile_kernel, (slab, slab) + (held,) * sides, (fields,))
     route, place = call(
         functools.partial(route_kernel, buckets, lanes, cells),
         (shape_of((slots, slots), bf16), shape_of((cells + lanes, slots), bf16)),
-        (packed[0], slot_owner.reshape(1, slots), slot_cell.reshape(1, slots), surface_count.reshape(1, 1)),
-    )
-    tile_halo = [lax.ppermute(value, "tile", shift(buckets, by)) for value, by in zip(packed, (1, -1))]
-
-    sides = 1 if subs == 2 else 2
+        (ahead, slot_owner.reshape(1, slots), slot_cell.reshape(1, slots), surface_count.reshape(1, 1)),
+    )
+    two = reps == 2
+    tile_halo = [send(value, "tile", shift(buckets, by), two) for value, by in ((ahead, 1), (behind, -1))]
+    if two:
+        ends = [lax.ppermute(value, "rep", swaps(2, 1)) for value in ends]
     slab = shape_of((FIELDS, total * STEPS, lanes), bf16)
-    packed = call(functools.partial(pack_sub_kernel, sides), (slab,) * sides, (fields, *tile_halo, route))
-    if subs == 2:
-        sub_halo = (lax.ppermute(packed[0], "sub", shift(2, 1)),) * 2
+    packed = call(functools.partial(pack_sub_kernel, sides), (slab,) * sides, (*tile_halo, route, *ends))
+    if sides == 1:
+        sub_halo = (send(packed[0], "sub", swaps(2, 1), two),) * 2
     else:
-        sub_halo = both_ways("sub", *packed)
+        sub_halo = both_ways("sub", *packed, two)
+    if two:
+        tile_halo = [lax.ppermute(value, "rep", swaps(2, 1)) for value in tile_halo]
 
     turned, flipped, area = call(
         functools.partial(turn_kernel, buckets),
@@ -447,7 +467,7 @@
         store_kernel, (block, block), (states,), out_specs=(HBM, HBM), scratch=[pltpu.SemaphoreType.DMA((2,))]
     )
 
-    order = [k for k in (2, 3, 1, 0) if k < parts]
+    order = [k for k in (0, 2, 3, 1) if k < parts]
     forces = call(
         functools.partial(project_kernel, order),
         shape_of((STEPS, modes), f32),
@@ -459,10 +479,8 @@
         forces = functools.reduce(jnp.add, addends)
         if count in (2, 4):
             sent = forces.astype(bf16) if axis != "rep" else forces
-            if axis != "rep" and reps == 2:
-                addends = [forces] + [crossed_swap(sent, axis, k) for k in (1, 3, 2) if k < count]
-            else:
-                addends = [forces] + [lax.ppermute(sent, axis, swaps(count, k)) for k in (1, 3, 2) if k < count]
+            places = [swaps(count, k) for k in (2, 3, 1) if k < count]
+            addends = [forces] + [send(sent, axis, swap, reps == 2 and axis != "rep") for swap in places]
         else:
             addends = [lax.psum(forces, axis)]
 

time: 41.1 us -> 40.1 us (0.976)
  waiting for transfers between devices: 11.9 us -> 10.5 us
    ppermute x16 -> x19, waiting for transfers between devices: 11 us -> 9.72 us  [the longest x13 8.85 us: send(): lax.ppermute(value, (axis, 'rep'), [(2 * i + r, 2 * j + 1 - r) for i, j i...]
    ppermute x16 -> x19, starting transfers between devices: 19.3 us -> 19.3 us  [the longest x13 18 us: send(): lax.ppermute(value, (axis, 'rep'), [(2 * i + r, 2 * j + 1 - r) for i, j i...]
  transfers between devices with their start and end apart: 19 -> 22, of which waited for: 12 -> 11; matrix products, arithmetic and copies ran while one was open for 4% -> 4% of each run, Pallas kernels for 8% -> 8%
where the time goes in v7:
time: 40.1 us; the launch traced here: 40 us
  starting transfers between devices  20.5 us (51%)
  waiting for transfers between devices  10.5 us (26%)
  Pallas kernels  5.94 us (15%)
  between operations  1.44 us (4%)
  other arithmetic  0.94 us (2%)
  local copies, waits for them, and re-layouts  0.6 us (1%)
    ppermute x13, starting transfers between devices, send(): lax.ppermute(value, (axis, 'rep'), [(2 * i + r, 2 * j + 1 - r) for i, j i...  18 us
    ppermute x13, waiting for transfers between devices, send(): lax.ppermute(value, (axis, 'rep'), [(2 * i + r, 2 * j + 1 - r) for i, j i...  8.85 us
    pallas_call x11, Pallas kernels, call(): pl.pallas_call(kernel, out_shape=out_shape, in_specs=specs or [VMEM] * le...  5.94 us
    ppermute x2, starting transfers between devices, body(): lax.ppermute(value, 'rep', swaps(2, 1))  1.01 us
    another operation x1, other arithmetic, body(): fields = jnp.stack([pressure, previous_pressure, courant_square])  0.92 us
    ppermute x1, waiting for transfers between devices, send(): return lax.ppermute(value, axis, places)  0.86 us
  transfers between devices with their start and end apart: 22, of which 11 were waited for; matrix products, arithmetic and copies ran while one was open for 4% of the time, Pallas kernels for 8%

profile of v7, /device:TPU:0, one launch (start us, length us, event | category | flops | bytes accessed | tf_op | source)
XLA Modules:
  0.0 40.0 jit_solution(1958622770581737443)
XLA Ops:
  1.1 0.9 %pad_maximum_fusion.fields = f32[3,8,16,128]{3,2,1,0:T(8,128)S(1)} fusion(f32[1,8,16,128]{3,2,1,0:T(8,128)} %bitcast.14, f32[1,8,16,128]{3,2,1,0:T(8,128)} %bitcast.15, f32[1,8,16,128]{3,2,1,0:T(8,128)} %bitcast.16), kind=kLoop, calls=%fused_computation | loop fusion | flops 98304 | bytes 393216 | tf_op jit(solution)/shard_map/stack | solution.py:415
  2.1 2.7 %collective-permute-start = (bf16[11,16,128]{2,1,0:T(8,128)(2,1)S(1)}, bf16[11,16,128]{2,1,0:T(8,128)(2,1)S(1)}, u32[]{:S(2)}, u32[]{:S(2)}) collective-permute-start(bf16[11,16,128]{2,1,0:T(8,128)(2,1)S(1)} %get-tuple-element.31.after_ref), channel_id=1, source_target_pairs={{0,5},{1,4},{4,9},{5,8},{8,13},{9,12},{12,1},{13,0},{2,7},{3,6},{6... | collective-permute-start | bytes 135176 | tf_op jit(solution)/shard_map/ppermute | solution.py:69
  4.9 2.1 %collective-permute-start.2 = (bf16[11,16,128]{2,1,0:T(8,128)(2,1)S(1)}, bf16[11,16,128]{2,1,0:T(8,128)(2,1)S(1)}, u32[]{:S(2)}, u32[]{:S(2)}) collective-permute-start(bf16[11,16,128]{2,1,0:T(8,128)(2,1)S(1)} %get-tuple-element.32), channel_id=1, source_target_pairs={{0,13},{1,12},{4,1},{5,0},{8,5},{9,4},{12,9},{13,8},{2,15},{3,14},... | collective-permute-start | bytes 135176 | tf_op jit(solution)/shard_map/ppermute | solution.py:69
  8.1 0.6 %shard_map.139 = (bf16[384,384]{1,0:T(8,128)(2,1)S(1)}, bf16[256,384]{1,0:T(8,128)(2,1)S(1)}) custom-call(bf16[11,16,128]{2,1,0:T(8,128)(2,1)S(1)} %get-tuple-element.31.after_ref, s32[1,384]{1,0:T(1,128)S(1)} %bitcast.12, s32[1,384]{1,0:T(1,128)S(1)} %bitcast.13, s32[1,1]{1,0:T(1,128)} %bitcast.9.count_ref), custom_call_target="tpu_custom_call" | custom-call | flops 1000000000 | tf_op jit(solution)/shard_map/pallas_call | solution.py:44
  9.0 0.6 %collective-permute-done.2.tile_after = bf16[11,16,128]{2,1,0:T(8,128)(2,1)S(1)} collective-permute-done((bf16[11,16,128]{2,1,0:T(8,128)(2,1)S(1)}, bf16[11,16,128]{2,1,0:T(8,128)(2,1)S(1)}, u32[]{:S(2)}, u32[]{:S(2)}) %collective-permute-start.2) | collective-permute-done | bytes 45088 | tf_op jit(solution)/shard_map/ppermute | solution.py:69
  9.6 1.3 %collective-permute-start.5 = (bf16[3,64,128]{2,1,0:T(8,128)(2,1)S(1)}, bf16[3,64,128]{2,1,0:T(8,128)(2,1)S(1)}, u32[]{:S(2)}, u32[]{:S(2)}) collective-permute-start(bf16[3,64,128]{2,1,0:T(8,128)(2,1)S(1)} %shard_map.140.ready_ref), channel_id=1, source_target_pairs={{0,3},{1,2},{2,1},{3,0},{4,7},{5,6},{6,5},{7,4},{8,11},{9,10},{10,... | collective-permute-start | bytes 147464 | tf_op jit(solution)/shard_map/ppermute | solution.py:69
  11.4 1.5 %shard_map.141 = (bf16[384,2048]{1,0:T(8,128)(2,1)S(1)}, bf16[2048,384]{1,0:T(8,128)(2,1)S(1)}, f32[1,384]{1,0:T(1,128)S(1)}) custom-call(bf16[3,64,128]{2,1,0:T(8,128)(2,1)S(1)} %shard_map.140.ready_ref, bf16[384,2048]{1,0:T(8,128)(2,1)S(1)} %collective-permute-done.6.shapes_ref, f32[1,384]{1,0:T(1,128)S(1)} %reshape.32.area_ref), custom_call_target="tpu_custom_call" | custom-call | flops 1000000000 | tf_op jit(solution)/shard_map/pallas_call | solution.py:44
  14.1 0.8 %collective-permute-done.8.rep_after.rep_before = bf16[3,24,128]{2,1,0:T(8,128)(2,1)S(1)} collective-permute-done((bf16[3,24,128]{2,1,0:T(8,128)(2,1)S(1)}, bf16[3,24,128]{2,1,0:T(8,128)(2,1)S(1)}, u32[]{:S(2)}, u32[]{:S(2)}) %collective-permute-start.8) | collective-permute-done | bytes 18464 | tf_op jit(solution)/shard_map/ppermute | solution.py:450
  14.9 1.1 %shard_map.144 = (f32[2,8,16,128]{3,2,1,0:T(8,128)S(1)}, bf16[4,96]{1,0:T(4,128)(2,1)S(1)}, bf16[4,96]{1,0:T(4,128)(2,1)S(1)}, bf16[4,96]{1,0:T(4,128)(2,1)S(1)}, bf16[4,96]{1,0:T(4,128)(2,1)S(1)}) custom-call(f32[16,24,128]{2,1,0:T(8,128)S(1)} %get-tuple-element.37.now_in, f32[16,24,128]{2,1,0:T(8,128)S(1)} %get-tuple-element.38.ago_in, ...), custom_call_target="tpu_custom_call" | custom-call | flops 2000000000 | tf_op jit(solution)/shard_map/pallas_call | solution.py:44
  16.0 1.4 %collective-permute-start.10 = (bf16[4,96]{1,0:T(4,128)(2,1)S(1)}, bf16[4,96]{1,0:T(4,128)(2,1)S(1)}, u32[]{:S(2)}, u32[]{:S(2)}) collective-permute-start(bf16[4,96]{1,0:T(4,128)(2,1)S(1)} %get-tuple-element.50), channel_id=1, source_target_pairs={{0,9},{1,8},{4,13},{5,12},{8,1},{9,0},{12,5},{13,4},{2,11},{3,10},... | collective-permute-start | bytes 2312 | tf_op jit(solution)/shard_map/ppermute | solution.py:69
  17.4 1.7 %collective-permute-start.11 = (bf16[4,96]{1,0:T(4,128)(2,1)S(1)}, bf16[4,96]{1,0:T(4,128)(2,1)S(1)}, u32[]{:S(2)}, u32[]{:S(2)}) collective-permute-start(bf16[4,96]{1,0:T(4,128)(2,1)S(1)} %get-tuple-element.51), channel_id=1, source_target_pairs={{0,13},{1,12},{4,9},{5,8},{8,5},{9,4},{12,1},{13,0},{2,15},{3,14},... | collective-permute-start | bytes 2312 | tf_op jit(solution)/shard_map/ppermute | solution.py:69
  19.9 2.3 %collective-permute-done.11.rest_2_ = bf16[4,96]{1,0:T(4,128)(2,1)S(1)} collective-permute-done((bf16[4,96]{1,0:T(4,128)(2,1)S(1)}, bf16[4,96]{1,0:T(4,128)(2,1)S(1)}, u32[]{:S(2)}, u32[]{:S(2)}) %collective-permute-start.11) | collective-permute-done | bytes 800 | tf_op jit(solution)/shard_map/ppermute | solution.py:69
  23.0 0.9 %collective-permute-done.13 = f32[4,2048]{1,0:T(4,128)S(1)} collective-permute-done((f32[4,2048]{1,0:T(4,128)S(1)}, f32[4,2048]{1,0:T(4,128)S(1)}, u32[]{:S(2)}, u32[]{:S(2)}) %collective-permute-start.13) | collective-permute-done | bytes 32800 | tf_op jit(solution)/shard_map/ppermute | solution.py:68
  23.9 1.5 %collective-permute-start.14 = (bf16[4,2048]{1,0:T(4,128)(2,1)S(1)}, bf16[4,2048]{1,0:T(4,128)(2,1)S(1)}, u32[]{:S(2)}, u32[]{:S(2)}) collective-permute-start(bf16[4,2048]{1,0:T(4,128)(2,1)S(1)} %get-tuple-element.60), channel_id=1, source_target_pairs={{0,3},{1,2},{2,1},{3,0},{4,7},{5,6},{6,5},{7,4},{8,11},{9,10},{10,... | collective-permute-start | bytes 49160 | tf_op jit(solution)/shard_map/ppermute | solution.py:69
  25.4 1.7 %collective-permute-done.14 = bf16[4,2048]{1,0:T(4,128)(2,1)S(1)} collective-permute-done((bf16[4,2048]{1,0:T(4,128)(2,1)S(1)}, bf16[4,2048]{1,0:T(4,128)(2,1)S(1)}, u32[]{:S(2)}, u32[]{:S(2)}) %collective-permute-start.14) | collective-permute-done | bytes 16416 | tf_op jit(solution)/shard_map/ppermute | solution.py:69
  27.1 1.0 %collective-permute-start.15 = (bf16[4,2048]{1,0:T(4,128)(2,1)S(1)}, bf16[4,2048]{1,0:T(4,128)(2,1)S(1)}, u32[]{:S(2)}, u32[]{:S(2)}) collective-permute-start(bf16[4,2048]{1,0:T(4,128)(2,1)S(1)} %get-tuple-element.58), channel_id=1, source_target_pairs={{0,9},{1,8},{4,13},{5,12},{8,1},{9,0},{12,5},{13,4},{2,11},{3,10},... | collective-permute-start | bytes 49160 | tf_op jit(solution)/shard_map/ppermute | solution.py:69
  28.2 1.1 %collective-permute-start.16 = (bf16[4,2048]{1,0:T(4,128)(2,1)S(1)}, bf16[4,2048]{1,0:T(4,128)(2,1)S(1)}, u32[]{:S(2)}, u32[]{:S(2)}) collective-permute-start(bf16[4,2048]{1,0:T(4,128)(2,1)S(1)} %get-tuple-element.58), channel_id=1, source_target_pairs={{0,13},{1,12},{4,9},{5,8},{8,5},{9,4},{12,1},{13,0},{2,15},{3,14},... | collective-permute-start | bytes 49160 | tf_op jit(solution)/shard_map/ppermute | solution.py:69
  29.3 1.1 %collective-permute-start.17 = (bf16[4,2048]{1,0:T(4,128)(2,1)S(1)}, bf16[4,2048]{1,0:T(4,128)(2,1)S(1)}, u32[]{:S(2)}, u32[]{:S(2)}) collective-permute-start(bf16[4,2048]{1,0:T(4,128)(2,1)S(1)} %get-tuple-element.58), channel_id=1, source_target_pairs={{0,5},{1,4},{4,1},{5,0},{8,13},{9,12},{12,9},{13,8},{2,7},{3,6},{6... | collective-permute-start | bytes 49160 | tf_op jit(solution)/shard_map/ppermute | solution.py:69
  30.4 0.7 %shard_map.145 = (f32[8,16,128]{2,1,0:T(8,128)}, f32[8,16,128]{2,1,0:T(8,128)}) custom-call(f32[2,8,16,128]{3,2,1,0:T(8,128)S(1)} %get-tuple-element.44.states), custom_call_target="tpu_custom_call" | custom-call | flops 1000000000 | tf_op jit(solution)/shard_map/pallas_call | solution.py:44
  31.4 1.8 %collective-permute-done.16.rest_2_ = bf16[4,2048]{1,0:T(4,128)(2,1)S(1)} collective-permute-done((bf16[4,2048]{1,0:T(4,128)(2,1)S(1)}, bf16[4,2048]{1,0:T(4,128)(2,1)S(1)}, u32[]{:S(2)}, u32[]{:S(2)}) %collective-permute-start.16) | collective-permute-done | bytes 16416 | tf_op jit(solution)/shard_map/ppermute | solution.py:69
  33.6 1.8 %collective-permute-start.18 = (bf16[4,96]{1,0:T(4,128)(2,1)S(1)}, bf16[4,96]{1,0:T(4,128)(2,1)S(1)}, u32[]{:S(2)}, u32[]{:S(2)}) collective-permute-start(bf16[4,96]{1,0:T(4,128)(2,1)S(1)} %get-tuple-element.53), channel_id=1, source_target_pairs={{0,13},{1,12},{4,9},{5,8},{8,5},{9,4},{12,1},{13,0},{2,15},{3,14},... | collective-permute-start | bytes 2312 | tf_op jit(solution)/shard_map/ppermute | solution.py:69
  35.3 2.3 %collective-permute-start.20 = (bf16[4,96]{1,0:T(4,128)(2,1)S(1)}, bf16[4,96]{1,0:T(4,128)(2,1)S(1)}, u32[]{:S(2)}, u32[]{:S(2)}) collective-permute-start(bf16[4,96]{1,0:T(4,128)(2,1)S(1)} %get-tuple-element.55), channel_id=1, source_target_pairs={{0,5},{1,4},{4,1},{5,0},{8,13},{9,12},{12,9},{13,8},{2,7},{3,6},{6... | collective-permute-start | bytes 2312 | tf_op jit(solution)/shard_map/ppermute | solution.py:69
  38.4 0.8 %collective-permute-done.19.rest_1_ = bf16[4,96]{1,0:T(4,128)(2,1)S(1)} collective-permute-done((bf16[4,96]{1,0:T(4,128)(2,1)S(1)}, bf16[4,96]{1,0:T(4,128)(2,1)S(1)}, u32[]{:S(2)}, u32[]{:S(2)}) %collective-permute-start.19) | collective-permute-done | bytes 800 | tf_op jit(solution)/shard_map/ppermute | solution.py:69
  39.2 0.8 %shard_map.148 = bf16[4,384]{1,0:T(4,128)(2,1)} custom-call(bf16[384,384]{1,0:T(8,128)(2,1)S(1)} %get-tuple-element.33.ready_ref.route_ref, bf16[4,96]{1,0:T(4,128)(2,1)S(1)} %collective-permute-done.18.rest_0_, bf16[4,96]{1,0:T(4,128)(2,1)S(1)} %collective-permute-done.19.rest_1_, bf16[4,96]{1,0:T(4,128)(2,1)S(1)} %collective-permute-done.20.rest_2_, ...), custom_call_target="tpu_custom_call" | custom-call | flops 1000000000 | tf_op jit(solution)/shard_map/pallas_call | solution.py:44
  (48 shorter events, 6.1 us)
Async XLA Ops:
  0.6 10.8 %collective-permute-start.6 = (bf16[384,2048]{1,0:T(8,128)(2,1)}, bf16[384,2048]{1,0:T(8,128)(2,1)S(1)}, u32[]{:S(2)}, u32[]{:S(2)}) collective-permute-start(bf16[384,2048]{1,0:T(8,128)(2,1)} %param.15), channel_id=1, source_target_pairs={{0,1},{1,0},{2,3},{3,2},{4,5},{5,4},{6,7},{7,6},{8,9},{9,8},{10,11... | collective-permute-start | bytes 4718600 | tf_op jit(solution)/shard_map/ppermute | solution.py:412
  2.1 6.0 %copy-start.3 = (s32[1,1,1,384,1]{3,4,2,1,0:T(1,128)S(1)}, s32[1,1,1,384,1]{3,4,2,1,0:T(1,128)}, u32[]{:S(2)}) copy-start(s32[1,1,1,384,1]{3,4,2,1,0:T(1,128)} %param.20) | copy-start | bytes 4612
  2.1 6.0 %copy-start.4 = (s32[1,1,1,384]{3,2,1,0:T(1,128)S(1)}, s32[1,1,1,384]{3,2,1,0:T(1,128)}, u32[]{:S(2)}) copy-start(s32[1,1,1,384]{3,2,1,0:T(1,128)} %param.19) | copy-start | bytes 4612
  2.1 6.9 %collective-permute-start = (bf16[11,16,128]{2,1,0:T(8,128)(2,1)S(1)}, bf16[11,16,128]{2,1,0:T(8,128)(2,1)S(1)}, u32[]{:S(2)}, u32[]{:S(2)}) collective-permute-start(bf16[11,16,128]{2,1,0:T(8,128)(2,1)S(1)} %get-tuple-element.31.after_ref), channel_id=1, source_target_pairs={{0,5},{1,4},{4,9},{5,8},{8,13},{9,12},{12,1},{13,0},{2,7},{3,6},{6... | collective-permute-start | bytes 135176 | tf_op jit(solution)/shard_map/ppermute | solution.py:69
  4.9 4.7 %collective-permute-start.2 = (bf16[11,16,128]{2,1,0:T(8,128)(2,1)S(1)}, bf16[11,16,128]{2,1,0:T(8,128)(2,1)S(1)}, u32[]{:S(2)}, u32[]{:S(2)}) collective-permute-start(bf16[11,16,128]{2,1,0:T(8,128)(2,1)S(1)} %get-tuple-element.32), channel_id=1, source_target_pairs={{0,13},{1,12},{4,1},{5,0},{8,5},{9,4},{12,9},{13,8},{2,15},{3,14},... | collective-permute-start | bytes 135176 | tf_op jit(solution)/shard_map/ppermute | solution.py:69
  7.0 1.8 %collective-permute-start.4 = (bf16[3,32,128]{2,1,0:T(8,128)(2,1)S(1)}, bf16[3,32,128]{2,1,0:T(8,128)(2,1)S(1)}, u32[]{:S(2)}, u32[]{:S(2)}) collective-permute-start(bf16[3,32,128]{2,1,0:T(8,128)(2,1)S(1)} %get-tuple-element.34), channel_id=1, source_target_pairs={{0,1},{1,0},{2,3},{3,2},{4,5},{5,4},{6,7},{7,6},{8,9},{9,8},{10,11... | collective-permute-start | bytes 73736 | tf_op jit(solution)/shard_map/ppermute | solution.py:428
  7.0 1.8 %collective-permute-start.7 = (f32[384]{0:T(512)S(1)}, f32[384]{0:T(512)S(1)}, u32[]{:S(2)}, u32[]{:S(2)}) collective-permute-start(f32[384]{0:T(512)S(1)} %copy-done.5), channel_id=1, source_target_pairs={{0,1},{1,0},{2,3},{3,2},{4,5},{5,4},{6,7},{7,6},{8,9},{9,8},{10,11... | collective-permute-start | bytes 4616 | tf_op jit(solution)/shard_map/ppermute | solution.py:412
  9.6 3.8 %collective-permute-start.5 = (bf16[3,64,128]{2,1,0:T(8,128)(2,1)S(1)}, bf16[3,64,128]{2,1,0:T(8,128)(2,1)S(1)}, u32[]{:S(2)}, u32[]{:S(2)}) collective-permute-start(bf16[3,64,128]{2,1,0:T(8,128)(2,1)S(1)} %shard_map.140.ready_ref), channel_id=1, source_target_pairs={{0,3},{1,2},{2,1},{3,0},{4,7},{5,6},{6,5},{7,4},{8,11},{9,10},{10,... | collective-permute-start | bytes 147464 | tf_op jit(solution)/shard_map/ppermute | solution.py:69
  10.9 2.0 %collective-permute-start.1 = (bf16[11,16,128]{2,1,0:T(8,128)(2,1)S(1)}, bf16[11,16,128]{2,1,0:T(8,128)(2,1)S(1)}, u32[]{:S(2)}, u32[]{:S(2)}) collective-permute-start(bf16[11,16,128]{2,1,0:T(8,128)(2,1)S(1)} %collective-permute-done.tile_before), channel_id=1, source_target_pairs={{0,1},{1,0},{2,3},{3,2},{4,5},{5,4},{6,7},{7,6},{8,9},{9,8},{10,11... | collective-permute-start | bytes 135176 | tf_op jit(solution)/shard_map/ppermute | solution.py:436
  11.3 1.6 %collective-permute-start.3 = (bf16[11,16,128]{2,1,0:T(8,128)(2,1)S(1)}, bf16[11,16,128]{2,1,0:T(8,128)(2,1)S(1)}, u32[]{:S(2)}, u32[]{:S(2)}) collective-permute-start(bf16[11,16,128]{2,1,0:T(8,128)(2,1)S(1)} %collective-permute-done.2.tile_after), channel_id=1, source_target_pairs={{0,1},{1,0},{2,3},{3,2},{4,5},{5,4},{6,7},{7,6},{8,9},{9,8},{10,11... | collective-permute-start | bytes 135176 | tf_op jit(solution)/shard_map/ppermute | solution.py:436
  13.6 1.3 %collective-permute-start.8 = (bf16[3,24,128]{2,1,0:T(8,128)(2,1)S(1)}, bf16[3,24,128]{2,1,0:T(8,128)(2,1)S(1)}, u32[]{:S(2)}, u32[]{:S(2)}) collective-permute-start(bf16[3,24,128]{2,1,0:T(8,128)(2,1)S(1)} %get-tuple-element.36.ready_ref), channel_id=1, source_target_pairs={{0,1},{1,0},{2,3},{3,2},{4,5},{5,4},{6,7},{7,6},{8,9},{9,8},{10,11... | collective-permute-start | bytes 55304 | tf_op jit(solution)/shard_map/ppermute | solution.py:450
  16.0 3.9 %collective-permute-start.10 = (bf16[4,96]{1,0:T(4,128)(2,1)S(1)}, bf16[4,96]{1,0:T(4,128)(2,1)S(1)}, u32[]{:S(2)}, u32[]{:S(2)}) collective-permute-start(bf16[4,96]{1,0:T(4,128)(2,1)S(1)} %get-tuple-element.50), channel_id=1, source_target_pairs={{0,9},{1,8},{4,13},{5,12},{8,1},{9,0},{12,5},{13,4},{2,11},{3,10},... | collective-permute-start | bytes 2312 | tf_op jit(solution)/shard_map/ppermute | solution.py:69
  17.4 4.8 %collective-permute-start.11 = (bf16[4,96]{1,0:T(4,128)(2,1)S(1)}, bf16[4,96]{1,0:T(4,128)(2,1)S(1)}, u32[]{:S(2)}, u32[]{:S(2)}) collective-permute-start(bf16[4,96]{1,0:T(4,128)(2,1)S(1)} %get-tuple-element.51), channel_id=1, source_target_pairs={{0,13},{1,12},{4,9},{5,8},{8,5},{9,4},{12,1},{13,0},{2,15},{3,14},... | collective-permute-start | bytes 2312 | tf_op jit(solution)/shard_map/ppermute | solution.py:69
  19.1 3.1 %collective-permute-start.12 = (bf16[4,96]{1,0:T(4,128)(2,1)S(1)}, bf16[4,96]{1,0:T(4,128)(2,1)S(1)}, u32[]{:S(2)}, u32[]{:S(2)}) collective-permute-start(bf16[4,96]{1,0:T(4,128)(2,1)S(1)} %get-tuple-element.52), channel_id=1, source_target_pairs={{0,5},{1,4},{4,1},{5,0},{8,13},{9,12},{12,9},{13,8},{2,7},{3,6},{6... | collective-permute-start | bytes 2312 | tf_op jit(solution)/shard_map/ppermute | solution.py:69
  19.2 3.1 %collective-permute-start.9 = (bf16[4,96]{1,0:T(4,128)(2,1)S(1)}, bf16[4,96]{1,0:T(4,128)(2,1)S(1)}, u32[]{:S(2)}, u32[]{:S(2)}) collective-permute-start(bf16[4,96]{1,0:T(4,128)(2,1)S(1)} %get-tuple-element.49), channel_id=1, source_target_pairs={{0,1},{1,0},{2,3},{3,2},{4,5},{5,4},{6,7},{7,6},{8,9},{9,8},{10,11... | collective-permute-start | bytes 2312 | tf_op jit(solution)/shard_map/ppermute | solution.py:379
  22.6 1.3 %collective-permute-start.13 = (f32[4,2048]{1,0:T(4,128)S(1)}, f32[4,2048]{1,0:T(4,128)S(1)}, u32[]{:S(2)}, u32[]{:S(2)}) collective-permute-start(f32[4,2048]{1,0:T(4,128)S(1)} %shard_map.146), channel_id=1, source_target_pairs={{0,1},{1,0},{2,3},{3,2},{4,5},{5,4},{6,7},{7,6},{8,9},{9,8},{10,11... | collective-permute-start | bytes 98312 | tf_op jit(solution)/shard_map/ppermute | solution.py:68
  23.9 3.2 %collective-permute-start.14 = (bf16[4,2048]{1,0:T(4,128)(2,1)S(1)}, bf16[4,2048]{1,0:T(4,128)(2,1)S(1)}, u32[]{:S(2)}, u32[]{:S(2)}) collective-permute-start(bf16[4,2048]{1,0:T(4,128)(2,1)S(1)} %get-tuple-element.60), channel_id=1, source_target_pairs={{0,3},{1,2},{2,1},{3,0},{4,7},{5,6},{6,5},{7,4},{8,11},{9,10},{10,... | collective-permute-start | bytes 49160 | tf_op jit(solution)/shard_map/ppermute | solution.py:69
  27.1 4.2 %collective-permute-start.15 = (bf16[4,2048]{1,0:T(4,128)(2,1)S(1)}, bf16[4,2048]{1,0:T(4,128)(2,1)S(1)}, u32[]{:S(2)}, u32[]{:S(2)}) collective-permute-start(bf16[4,2048]{1,0:T(4,128)(2,1)S(1)} %get-tuple-element.58), channel_id=1, source_target_pairs={{0,9},{1,8},{4,13},{5,12},{8,1},{9,0},{12,5},{13,4},{2,11},{3,10},... | collective-permute-start | bytes 49160 | tf_op jit(solution)/shard_map/ppermute | solution.py:69
  28.2 5.0 %collective-permute-start.16 = (bf16[4,2048]{1,0:T(4,128)(2,1)S(1)}, bf16[4,2048]{1,0:T(4,128)(2,1)S(1)}, u32[]{:S(2)}, u32[]{:S(2)}) collective-permute-start(bf16[4,2048]{1,0:T(4,128)(2,1)S(1)} %get-tuple-element.58), channel_id=1, source_target_pairs={{0,13},{1,12},{4,9},{5,8},{8,5},{9,4},{12,1},{13,0},{2,15},{3,14},... | collective-permute-start | bytes 49160 | tf_op jit(solution)/shard_map/ppermute | solution.py:69
  29.3 3.8 %collective-permute-start.17 = (bf16[4,2048]{1,0:T(4,128)(2,1)S(1)}, bf16[4,2048]{1,0:T(4,128)(2,1)S(1)}, u32[]{:S(2)}, u32[]{:S(2)}) collective-permute-start(bf16[4,2048]{1,0:T(4,128)(2,1)S(1)} %get-tuple-element.58), channel_id=1, source_target_pairs={{0,5},{1,4},{4,1},{5,0},{8,13},{9,12},{12,9},{13,8},{2,7},{3,6},{6... | collective-permute-start | bytes 49160 | tf_op jit(solution)/shard_map/ppermute | solution.py:69
  33.6 4.8 %collective-permute-start.18 = (bf16[4,96]{1,0:T(4,128)(2,1)S(1)}, bf16[4,96]{1,0:T(4,128)(2,1)S(1)}, u32[]{:S(2)}, u32[]{:S(2)}) collective-permute-start(bf16[4,96]{1,0:T(4,128)(2,1)S(1)} %get-tuple-element.53), channel_id=1, source_target_pairs={{0,13},{1,12},{4,9},{5,8},{8,5},{9,4},{12,1},{13,0},{2,15},{3,14},... | collective-permute-start | bytes 2312 | tf_op jit(solution)/shard_map/ppermute | solution.py:69
  35.3 3.9 %collective-permute-start.19 = (bf16[4,96]{1,0:T(4,128)(2,1)S(1)}, bf16[4,96]{1,0:T(4,128)(2,1)S(1)}, u32[]{:S(2)}, u32[]{:S(2)}) collective-permute-start(bf16[4,96]{1,0:T(4,128)(2,1)S(1)} %get-tuple-element.54), channel_id=1, source_target_pairs={{0,9},{1,8},{4,13},{5,12},{8,1},{9,0},{12,5},{13,4},{2,11},{3,10},... | collective-permute-start | bytes 2312 | tf_op jit(solution)/shard_map/ppermute | solution.py:69
  35.3 3.9 %collective-permute-start.20 = (bf16[4,96]{1,0:T(4,128)(2,1)S(1)}, bf16[4,96]{1,0:T(4,128)(2,1)S(1)}, u32[]{:S(2)}, u32[]{:S(2)}) collective-permute-start(bf16[4,96]{1,0:T(4,128)(2,1)S(1)} %get-tuple-element.55), channel_id=1, source_target_pairs={{0,5},{1,4},{4,1},{5,0},{8,13},{9,12},{12,9},{13,8},{2,7},{3,6},{6... | collective-permute-start | bytes 2312 | tf_op jit(solution)/shard_map/ppermute | solution.py:69
  37.6 1.6 %collective-permute-start.21 = (bf16[4,96]{1,0:T(4,128)(2,1)S(1)}, bf16[4,96]{1,0:T(4,128)(2,1)S(1)}, u32[]{:S(2)}, u32[]{:S(2)}) collective-permute-start(bf16[4,96]{1,0:T(4,128)(2,1)S(1)} %get-tuple-element.56), channel_id=1, source_target_pairs={{0,1},{1,0},{2,3},{3,2},{4,5},{5,4},{6,7},{7,6},{8,9},{9,8},{10,11... | collective-permute-start | bytes 2312 | tf_op jit(solution)/shard_map/ppermute | solution.py:379
  (4 other events, 13.2 us)

commit v8 on v7

--- a/solution.py
+++ b/solution.py
@@ -134,27 +134,45 @@
     return layer_beside(at, k, layers, tile_before, tile_after)
 
 
+NEAR, NEXT = 4, 6
+
+
+def beside_tile(nearest, outs):
+    rows, lanes = nearest[0].shape
+    row = iota((SUBLANES, lanes), 0)
+    picked = []
+    for pieces, rolls in (([a[rows - SUBLANES :] for a in nearest], (4, 6, 0)), ([a[:SUBLANES] for a in nearest], (0, 4, 6))):
+        a, b, c = (pltpu.roll(piece, by, 0) if by else piece for piece, by in zip(pieces, rolls))
+        picked.append(jnp.where(row < NEAR, a, jnp.where(row < NEXT, b, c)))
+    if outs == 1:
+        picked = [jnp.where(lax.axis_index("sub") == 0, *picked)]
+    return picked
+
+
 def pack_sub_kernel(sides, tile_before, tile_after, ready_ref, *rest):
     ends, outs = rest[:sides], rest[sides:]
     held = ends[0].shape[1]
     layers = held // STEPS
     for at in range(FIELDS):
-        for out, own in zip(outs, ends):
-            out[at, STEPS * STEPS : STEPS * STEPS + held, :] = own[at]
-        for first in (*range(0, STEPS, 2), *range(STEPS + layers, 2 * STEPS + layers, 2)):
-            beside = [layer_beside(at, k, layers, tile_before, tile_after) for k in (first, first + 1)]
-            for out, value in zip(outs, end_rows(beside, sides)):
-                out[at, first * STEPS : first * STEPS + SUBLANES, :] = value.astype(bf16)
-
-
-def side_rows(at, k, after_ref, before_ref):
-    start = k // 2 * SUBLANES
+        before = [layer_beside(at, STEPS - 1 - k, layers, tile_before, tile_after) for k in range(STEPS - 1)]
+        after = [layer_beside(at, STEPS + layers + k, layers, tile_before, tile_after) for k in range(STEPS - 1)]
+        for out, own, a, b in zip(outs, ends, beside_tile(before, sides), beside_tile(after, sides)):
+            out[at, :held, :] = own[at]
+            out[at, held:, :] = jnp.concatenate([a, b], 0).astype(bf16)
+
+
+def side_rows(at, k, layers, after_ref, before_ref):
+    own = k - STEPS
+    if 0 <= own < layers:
+        start, rolls = own // 2 * SUBLANES, ((0, 4), (4, 0))[own % 2]
+    else:
+        depth = -own if own < 0 else own - layers + 1
+        if depth == STEPS:
+            return jnp.zeros((SUBLANES, after_ref.shape[2]), f32)
+        start, rolls = layers * STEPS + (own > 0) * SUBLANES, ((0, 4), (4, 2), (2, 0))[depth - 1]
     after = after_ref[at, start : start + SUBLANES, :].astype(f32)
     before = before_ref[at, start : start + SUBLANES, :].astype(f32)
-    if k % 2 == 0:
-        before = pltpu.roll(before, STEPS, 0)
-    else:
-        after = pltpu.roll(after, STEPS, 0)
+    after, before = (pltpu.roll(value, by, 0) if by else value for value, by in zip((after, before), rolls))
     me, count = lax.axis_index("sub"), lax.axis_size("sub")
     low = iota(after.shape, 0) < STEPS
     keep_after = jnp.where(me < count - 1, 1.0, 0.0)
@@ -170,7 +188,7 @@
     for at in range(FIELDS):
         packed = jnp.zeros((rows + beside, lanes), f32)
         for k in range(total):
-            here = layer_of_block(at, k, fields, tile_before, tile_after), side_rows(at, k, sub_after, sub_before)
+            here = layer_of_block(at, k, fields, tile_before, tile_after), side_rows(at, k, layers, sub_after, sub_before)
             here = pltpu.roll(jnp.concatenate(here, 0), (beside * k + STEPS) % lanes, 1)
             packed = jnp.where(layer_at == k, here, packed)
         out_ref[at] = packed.astype(bf16)
@@ -214,7 +232,7 @@
         for k in range(total):
             keep = keep_low if k < STEPS else keep_high if k >= STEPS + layers else 1.0
             out[k, :rows] = layer_of_block(at, k, fields, tile_before, tile_after) * keep + extra
-            out[k, rows:] = side_rows(at, k, sub_after, sub_before) * keep + extra
+            out[k, rows:] = side_rows(at, k, layers, sub_after, sub_before) * keep + extra
     for value, out in ((now, lapped), (ago, lapped_ago)):
         for k in range(1, total - 1):
             out[k] = laplace(value[k - 1], value[k], value[k + 1])
@@ -319,16 +337,25 @@
 def turn_kernel(buckets, ready_ref, shapes_ref, area_ref, turned_ref, flipped_ref, area_out):
     total = shapes_ref.shape[0]
     bucket = total // buckets
-    entry = iota((total, 1), 0)
-    part = entry // bucket
-    wanted = entry + ((part ^ lax.axis_index("tile")) - part) * bucket
-    picks = jnp.where(iota((total, total), 1) == wanted, 1.0, 0.0)
-    turned = dot(picks.astype(bf16), shapes_ref[...], (1, 0))
-    turned_ref[...] = turned.astype(bf16)
-    flipped_ref[...] = turned.T.astype(bf16)
-    area_out[...] = lax.dot_general(
-        area_ref[...], picks, (((1,), (1,)), ((), ())), precision=lax.Precision.HIGHEST, preferred_element_type=f32
-    )
+    me = lax.axis_index("tile")
+    if bucket % 16 == 0:
+        for k in range(buckets):
+            first = pl.multiple_of((me ^ k) * bucket, 16)
+            turned_ref[k * bucket : (k + 1) * bucket, :] = shapes_ref[pl.ds(first, bucket), :]
+            area = jnp.zeros((1, bucket), f32)
+            for part in range(buckets):
+                area = jnp.where((me ^ k) == part, area_ref[:, part * bucket : (part + 1) * bucket], area)
+            area_out[:, k * bucket : (k + 1) * bucket] = area
+    else:
+        entry = iota((total, 1), 0)
+        part = entry // bucket
+        wanted = entry + ((part ^ me) - part) * bucket
+        picks = jnp.where(iota((total, total), 1) == wanted, 1.0, 0.0)
+        turned_ref[...] = dot(picks.astype(bf16), shapes_ref[...], (1, 0)).astype(bf16)
+        area_out[...] = lax.dot_general(
+            area_ref[...], picks, (((1,), (1,)), ((), ())), precision=lax.Precision.HIGHEST, preferred_element_type=f32
+        )
+    flipped_ref[...] = turned_ref[...].astype(f32).T.astype(bf16)
 
 
 def project_kernel(order, area_ref, turned_ref, *rest):
@@ -426,7 +453,7 @@
     tile_halo = [send(value, "tile", shift(buckets, by), two) for value, by in ((ahead, 1), (behind, -1))]
     if two:
         ends = [lax.ppermute(value, "rep", swaps(2, 1)) for value in ends]
-    slab = shape_of((FIELDS, total * STEPS, lanes), bf16)
+    slab = shape_of((FIELDS, layers * STEPS + 2 * SUBLANES, lanes), bf16)
     packed = call(functools.partial(pack_sub_kernel, sides), (slab,) * sides, (*tile_halo, route, *ends))
     if sides == 1:
         sub_halo = (send(packed[0], "sub", swaps(2, 1), two),) * 2

time: 40.1 us -> 40 us (level)
  Pallas kernels: 5.94 us -> 5.2 us
  waiting for transfers between devices: 10.5 us -> 11.1 us
    pallas_call x11, Pallas kernels: 5.94 us -> 5.2 us  [call(): pl.pallas_call(kernel, out_shape=out_shape, in_specs=specs or [VMEM] * le...]
    ppermute x13, waiting for transfers between devices: 8.85 us -> 9.45 us  [send(): lax.ppermute(value, (axis, 'rep'), [(2 * i + r, 2 * j + 1 - r) for i, j i...]
  transfers between devices with their start and end apart: 22 -> 22, of which waited for: 11 -> 11; matrix products, arithmetic and copies ran while one was open for 4% -> 4% of each run, Pallas kernels for 8% -> 6%
where the time goes in v8:
time: 40 us; the launch traced here: 39.8 us
  starting transfers between devices  20.5 us (51%)
  waiting for transfers between devices  11.1 us (28%)
  Pallas kernels  5.2 us (13%)
  between operations  1.43 us (4%)
  other arithmetic  0.94 us (2%)
  local copies, waits for them, and re-layouts  0.6 us (2%)
    ppermute x13, starting transfers between devices, send(): lax.ppermute(value, (axis, 'rep'), [(2 * i + r, 2 * j + 1 - r) for i, j i...  18 us
    ppermute x13, waiting for transfers between devices, send(): lax.ppermute(value, (axis, 'rep'), [(2 * i + r, 2 * j + 1 - r) for i, j i...  9.45 us
    pallas_call x11, Pallas kernels, call(): pl.pallas_call(kernel, out_shape=out_shape, in_specs=specs or [VMEM] * le...  5.2 us
    ppermute x2, starting transfers between devices, body(): lax.ppermute(value, 'rep', swaps(2, 1))  1.01 us
    another operation x1, other arithmetic, body(): fields = jnp.stack([pressure, previous_pressure, courant_square])  0.92 us
    ppermute x1, waiting for transfers between devices, send(): return lax.ppermute(value, axis, places)  0.86 us
    ppermute x1, waiting for transfers between devices, body(): rep_halo = (lax.ppermute(packed, 'rep', shift(2, 1)),) * 2  0.8 us
  transfers between devices with their start and end apart: 22, of which 11 were waited for; matrix products, arithmetic and copies ran while one was open for 4% of the time, Pallas kernels for 6%

profile of v8, /device:TPU:0, one launch (start us, length us, event | category | flops | bytes accessed | tf_op | source)
XLA Modules:
  0.0 39.8 jit_solution(11962756284841039175)
XLA Ops:
  1.1 0.9 %pad_maximum_fusion.fields = f32[3,8,16,128]{3,2,1,0:T(8,128)S(1)} fusion(f32[1,8,16,128]{3,2,1,0:T(8,128)} %bitcast.14, f32[1,8,16,128]{3,2,1,0:T(8,128)} %bitcast.15, f32[1,8,16,128]{3,2,1,0:T(8,128)} %bitcast.16), kind=kLoop, calls=%fused_computation | loop fusion | flops 98304 | bytes 393216 | tf_op jit(solution)/shard_map/stack | solution.py:442
  2.1 2.7 %collective-permute-start = (bf16[11,16,128]{2,1,0:T(8,128)(2,1)S(1)}, bf16[11,16,128]{2,1,0:T(8,128)(2,1)S(1)}, u32[]{:S(2)}, u32[]{:S(2)}) collective-permute-start(bf16[11,16,128]{2,1,0:T(8,128)(2,1)S(1)} %get-tuple-element.31.after_ref), channel_id=1, source_target_pairs={{0,5},{1,4},{4,9},{5,8},{8,13},{9,12},{12,1},{13,0},{2,7},{3,6},{6... | collective-permute-start | bytes 135176 | tf_op jit(solution)/shard_map/ppermute | solution.py:69
  4.9 2.1 %collective-permute-start.2 = (bf16[11,16,128]{2,1,0:T(8,128)(2,1)S(1)}, bf16[11,16,128]{2,1,0:T(8,128)(2,1)S(1)}, u32[]{:S(2)}, u32[]{:S(2)}) collective-permute-start(bf16[11,16,128]{2,1,0:T(8,128)(2,1)S(1)} %get-tuple-element.32), channel_id=1, source_target_pairs={{0,13},{1,12},{4,1},{5,0},{8,5},{9,4},{12,9},{13,8},{2,15},{3,14},... | collective-permute-start | bytes 135176 | tf_op jit(solution)/shard_map/ppermute | solution.py:69
  8.1 0.6 %shard_map.139 = (bf16[384,384]{1,0:T(8,128)(2,1)S(1)}, bf16[256,384]{1,0:T(8,128)(2,1)S(1)}) custom-call(bf16[11,16,128]{2,1,0:T(8,128)(2,1)S(1)} %get-tuple-element.31.after_ref, s32[1,384]{1,0:T(1,128)S(1)} %bitcast.12, s32[1,384]{1,0:T(1,128)S(1)} %bitcast.13, s32[1,1]{1,0:T(1,128)} %bitcast.9.count_ref), custom_call_target="tpu_custom_call" | custom-call | flops 1000000000 | tf_op jit(solution)/shard_map/pallas_call | solution.py:44
  9.6 1.3 %collective-permute-start.5 = (bf16[3,48,128]{2,1,0:T(8,128)(2,1)S(1)}, bf16[3,48,128]{2,1,0:T(8,128)(2,1)S(1)}, u32[]{:S(2)}, u32[]{:S(2)}) collective-permute-start(bf16[3,48,128]{2,1,0:T(8,128)(2,1)S(1)} %shard_map.140.ready_ref), channel_id=1, source_target_pairs={{0,3},{1,2},{2,1},{3,0},{4,7},{5,6},{6,5},{7,4},{8,11},{9,10},{10,... | collective-permute-start | bytes 110600 | tf_op jit(solution)/shard_map/ppermute | solution.py:69
  11.4 0.7 %shard_map.141 = (bf16[384,2048]{1,0:T(8,128)(2,1)S(1)}, bf16[2048,384]{1,0:T(8,128)(2,1)S(1)}, f32[1,384]{1,0:T(1,128)S(1)}) custom-call(bf16[3,48,128]{2,1,0:T(8,128)(2,1)S(1)} %shard_map.140.ready_ref, bf16[384,2048]{1,0:T(8,128)(2,1)S(1)} %collective-permute-done.6.shapes_ref, f32[1,384]{1,0:T(1,128)S(1)} %reshape.32.area_ref), custom_call_target="tpu_custom_call" | custom-call | flops 1000000000 | tf_op jit(solution)/shard_map/pallas_call | solution.py:44
  12.2 1.0 %collective-permute-done.5.sub_after.sub_before = bf16[3,48,128]{2,1,0:T(8,128)(2,1)S(1)} collective-permute-done((bf16[3,48,128]{2,1,0:T(8,128)(2,1)S(1)}, bf16[3,48,128]{2,1,0:T(8,128)(2,1)S(1)}, u32[]{:S(2)}, u32[]{:S(2)}) %collective-permute-start.5) | collective-permute-done | bytes 36896 | tf_op jit(solution)/shard_map/ppermute | solution.py:69
  13.8 0.8 %collective-permute-done.8.rep_after.rep_before = bf16[3,24,128]{2,1,0:T(8,128)(2,1)S(1)} collective-permute-done((bf16[3,24,128]{2,1,0:T(8,128)(2,1)S(1)}, bf16[3,24,128]{2,1,0:T(8,128)(2,1)S(1)}, u32[]{:S(2)}, u32[]{:S(2)}) %collective-permute-start.8) | collective-permute-done | bytes 18464 | tf_op jit(solution)/shard_map/ppermute | solution.py:477
  14.6 1.1 %shard_map.144 = (f32[2,8,16,128]{3,2,1,0:T(8,128)S(1)}, bf16[4,96]{1,0:T(4,128)(2,1)S(1)}, bf16[4,96]{1,0:T(4,128)(2,1)S(1)}, bf16[4,96]{1,0:T(4,128)(2,1)S(1)}, bf16[4,96]{1,0:T(4,128)(2,1)S(1)}) custom-call(f32[16,24,128]{2,1,0:T(8,128)S(1)} %get-tuple-element.37.now_in, f32[16,24,128]{2,1,0:T(8,128)S(1)} %get-tuple-element.38.ago_in, ...), custom_call_target="tpu_custom_call" | custom-call | flops 2000000000 | tf_op jit(solution)/shard_map/pallas_call | solution.py:44
  15.8 1.4 %collective-permute-start.10 = (bf16[4,96]{1,0:T(4,128)(2,1)S(1)}, bf16[4,96]{1,0:T(4,128)(2,1)S(1)}, u32[]{:S(2)}, u32[]{:S(2)}) collective-permute-start(bf16[4,96]{1,0:T(4,128)(2,1)S(1)} %get-tuple-element.50), channel_id=1, source_target_pairs={{0,9},{1,8},{4,13},{5,12},{8,1},{9,0},{12,5},{13,4},{2,11},{3,10},... | collective-permute-start | bytes 2312 | tf_op jit(solution)/shard_map/ppermute | solution.py:69
  17.2 1.7 %collective-permute-start.11 = (bf16[4,96]{1,0:T(4,128)(2,1)S(1)}, bf16[4,96]{1,0:T(4,128)(2,1)S(1)}, u32[]{:S(2)}, u32[]{:S(2)}) collective-permute-start(bf16[4,96]{1,0:T(4,128)(2,1)S(1)} %get-tuple-element.51), channel_id=1, source_target_pairs={{0,13},{1,12},{4,9},{5,8},{8,5},{9,4},{12,1},{13,0},{2,15},{3,14},... | collective-permute-start | bytes 2312 | tf_op jit(solution)/shard_map/ppermute | solution.py:69
  19.7 2.3 %collective-permute-done.11.rest_2_ = bf16[4,96]{1,0:T(4,128)(2,1)S(1)} collective-permute-done((bf16[4,96]{1,0:T(4,128)(2,1)S(1)}, bf16[4,96]{1,0:T(4,128)(2,1)S(1)}, u32[]{:S(2)}, u32[]{:S(2)}) %collective-permute-start.11) | collective-permute-done | bytes 800 | tf_op jit(solution)/shard_map/ppermute | solution.py:69
  22.7 0.9 %collective-permute-done.13 = f32[4,2048]{1,0:T(4,128)S(1)} collective-permute-done((f32[4,2048]{1,0:T(4,128)S(1)}, f32[4,2048]{1,0:T(4,128)S(1)}, u32[]{:S(2)}, u32[]{:S(2)}) %collective-permute-start.13) | collective-permute-done | bytes 32800 | tf_op jit(solution)/shard_map/ppermute | solution.py:68
  23.6 1.5 %collective-permute-start.14 = (bf16[4,2048]{1,0:T(4,128)(2,1)S(1)}, bf16[4,2048]{1,0:T(4,128)(2,1)S(1)}, u32[]{:S(2)}, u32[]{:S(2)}) collective-permute-start(bf16[4,2048]{1,0:T(4,128)(2,1)S(1)} %get-tuple-element.60), channel_id=1, source_target_pairs={{0,3},{1,2},{2,1},{3,0},{4,7},{5,6},{6,5},{7,4},{8,11},{9,10},{10,... | collective-permute-start | bytes 49160 | tf_op jit(solution)/shard_map/ppermute | solution.py:69
  25.1 1.7 %collective-permute-done.14 = bf16[4,2048]{1,0:T(4,128)(2,1)S(1)} collective-permute-done((bf16[4,2048]{1,0:T(4,128)(2,1)S(1)}, bf16[4,2048]{1,0:T(4,128)(2,1)S(1)}, u32[]{:S(2)}, u32[]{:S(2)}) %collective-permute-start.14) | collective-permute-done | bytes 16416 | tf_op jit(solution)/shard_map/ppermute | solution.py:69
  26.9 1.2 %collective-permute-start.15 = (bf16[4,2048]{1,0:T(4,128)(2,1)S(1)}, bf16[4,2048]{1,0:T(4,128)(2,1)S(1)}, u32[]{:S(2)}, u32[]{:S(2)}) collective-permute-start(bf16[4,2048]{1,0:T(4,128)(2,1)S(1)} %get-tuple-element.58), channel_id=1, source_target_pairs={{0,9},{1,8},{4,13},{5,12},{8,1},{9,0},{12,5},{13,4},{2,11},{3,10},... | collective-permute-start | bytes 49160 | tf_op jit(solution)/shard_map/ppermute | solution.py:69
  28.0 1.0 %collective-permute-start.16 = (bf16[4,2048]{1,0:T(4,128)(2,1)S(1)}, bf16[4,2048]{1,0:T(4,128)(2,1)S(1)}, u32[]{:S(2)}, u32[]{:S(2)}) collective-permute-start(bf16[4,2048]{1,0:T(4,128)(2,1)S(1)} %get-tuple-element.58), channel_id=1, source_target_pairs={{0,13},{1,12},{4,9},{5,8},{8,5},{9,4},{12,1},{13,0},{2,15},{3,14},... | collective-permute-start | bytes 49160 | tf_op jit(solution)/shard_map/ppermute | solution.py:69
  29.0 1.1 %collective-permute-start.17 = (bf16[4,2048]{1,0:T(4,128)(2,1)S(1)}, bf16[4,2048]{1,0:T(4,128)(2,1)S(1)}, u32[]{:S(2)}, u32[]{:S(2)}) collective-permute-start(bf16[4,2048]{1,0:T(4,128)(2,1)S(1)} %get-tuple-element.58), channel_id=1, source_target_pairs={{0,5},{1,4},{4,1},{5,0},{8,13},{9,12},{12,9},{13,8},{2,7},{3,6},{6... | collective-permute-start | bytes 49160 | tf_op jit(solution)/shard_map/ppermute | solution.py:69
  30.1 0.7 %shard_map.145 = (f32[8,16,128]{2,1,0:T(8,128)}, f32[8,16,128]{2,1,0:T(8,128)}) custom-call(f32[2,8,16,128]{3,2,1,0:T(8,128)S(1)} %get-tuple-element.44.states), custom_call_target="tpu_custom_call" | custom-call | flops 1000000000 | tf_op jit(solution)/shard_map/pallas_call | solution.py:44
  31.1 1.9 %collective-permute-done.16.rest_2_ = bf16[4,2048]{1,0:T(4,128)(2,1)S(1)} collective-permute-done((bf16[4,2048]{1,0:T(4,128)(2,1)S(1)}, bf16[4,2048]{1,0:T(4,128)(2,1)S(1)}, u32[]{:S(2)}, u32[]{:S(2)}) %collective-permute-start.16) | collective-permute-done | bytes 16416 | tf_op jit(solution)/shard_map/ppermute | solution.py:69
  33.4 1.8 %collective-permute-start.18 = (bf16[4,96]{1,0:T(4,128)(2,1)S(1)}, bf16[4,96]{1,0:T(4,128)(2,1)S(1)}, u32[]{:S(2)}, u32[]{:S(2)}) collective-permute-start(bf16[4,96]{1,0:T(4,128)(2,1)S(1)} %get-tuple-element.53), channel_id=1, source_target_pairs={{0,13},{1,12},{4,9},{5,8},{8,5},{9,4},{12,1},{13,0},{2,15},{3,14},... | collective-permute-start | bytes 2312 | tf_op jit(solution)/shard_map/ppermute | solution.py:69
  35.2 2.2 %collective-permute-start.20 = (bf16[4,96]{1,0:T(4,128)(2,1)S(1)}, bf16[4,96]{1,0:T(4,128)(2,1)S(1)}, u32[]{:S(2)}, u32[]{:S(2)}) collective-permute-start(bf16[4,96]{1,0:T(4,128)(2,1)S(1)} %get-tuple-element.55), channel_id=1, source_target_pairs={{0,5},{1,4},{4,1},{5,0},{8,13},{9,12},{12,9},{13,8},{2,7},{3,6},{6... | collective-permute-start | bytes 2312 | tf_op jit(solution)/shard_map/ppermute | solution.py:69
  38.2 0.8 %collective-permute-done.19.rest_1_ = bf16[4,96]{1,0:T(4,128)(2,1)S(1)} collective-permute-done((bf16[4,96]{1,0:T(4,128)(2,1)S(1)}, bf16[4,96]{1,0:T(4,128)(2,1)S(1)}, u32[]{:S(2)}, u32[]{:S(2)}) %collective-permute-start.19) | collective-permute-done | bytes 800 | tf_op jit(solution)/shard_map/ppermute | solution.py:69
  39.1 0.8 %shard_map.148 = bf16[4,384]{1,0:T(4,128)(2,1)} custom-call(bf16[384,384]{1,0:T(8,128)(2,1)S(1)} %get-tuple-element.33.ready_ref.route_ref, bf16[4,96]{1,0:T(4,128)(2,1)S(1)} %collective-permute-done.18.rest_0_, bf16[4,96]{1,0:T(4,128)(2,1)S(1)} %collective-permute-done.19.rest_1_, bf16[4,96]{1,0:T(4,128)(2,1)S(1)} %collective-permute-done.20.rest_2_, ...), custom_call_target="tpu_custom_call" | custom-call | flops 1000000000 | tf_op jit(solution)/shard_map/pallas_call | solution.py:44
  (48 shorter events, 6.2 us)
Async XLA Ops:
  0.6 10.8 %collective-permute-start.6 = (bf16[384,2048]{1,0:T(8,128)(2,1)}, bf16[384,2048]{1,0:T(8,128)(2,1)S(1)}, u32[]{:S(2)}, u32[]{:S(2)}) collective-permute-start(bf16[384,2048]{1,0:T(8,128)(2,1)} %param.15), channel_id=1, source_target_pairs={{0,1},{1,0},{2,3},{3,2},{4,5},{5,4},{6,7},{7,6},{8,9},{9,8},{10,11... | collective-permute-start | bytes 4718600 | tf_op jit(solution)/shard_map/ppermute | solution.py:439
  2.1 6.0 %copy-start.3 = (s32[1,1,1,384,1]{3,4,2,1,0:T(1,128)S(1)}, s32[1,1,1,384,1]{3,4,2,1,0:T(1,128)}, u32[]{:S(2)}) copy-start(s32[1,1,1,384,1]{3,4,2,1,0:T(1,128)} %param.20) | copy-start | bytes 4612
  2.1 6.0 %copy-start.4 = (s32[1,1,1,384]{3,2,1,0:T(1,128)S(1)}, s32[1,1,1,384]{3,2,1,0:T(1,128)}, u32[]{:S(2)}) copy-start(s32[1,1,1,384]{3,2,1,0:T(1,128)} %param.19) | copy-start | bytes 4612
  2.1 6.9 %collective-permute-start = (bf16[11,16,128]{2,1,0:T(8,128)(2,1)S(1)}, bf16[11,16,128]{2,1,0:T(8,128)(2,1)S(1)}, u32[]{:S(2)}, u32[]{:S(2)}) collective-permute-start(bf16[11,16,128]{2,1,0:T(8,128)(2,1)S(1)} %get-tuple-element.31.after_ref), channel_id=1, source_target_pairs={{0,5},{1,4},{4,9},{5,8},{8,13},{9,12},{12,1},{13,0},{2,7},{3,6},{6... | collective-permute-start | bytes 135176 | tf_op jit(solution)/shard_map/ppermute | solution.py:69
  4.9 4.7 %collective-permute-start.2 = (bf16[11,16,128]{2,1,0:T(8,128)(2,1)S(1)}, bf16[11,16,128]{2,1,0:T(8,128)(2,1)S(1)}, u32[]{:S(2)}, u32[]{:S(2)}) collective-permute-start(bf16[11,16,128]{2,1,0:T(8,128)(2,1)S(1)} %get-tuple-element.32), channel_id=1, source_target_pairs={{0,13},{1,12},{4,1},{5,0},{8,5},{9,4},{12,9},{13,8},{2,15},{3,14},... | collective-permute-start | bytes 135176 | tf_op jit(solution)/shard_map/ppermute | solution.py:69
  7.0 1.8 %collective-permute-start.4 = (bf16[3,32,128]{2,1,0:T(8,128)(2,1)S(1)}, bf16[3,32,128]{2,1,0:T(8,128)(2,1)S(1)}, u32[]{:S(2)}, u32[]{:S(2)}) collective-permute-start(bf16[3,32,128]{2,1,0:T(8,128)(2,1)S(1)} %get-tuple-element.34), channel_id=1, source_target_pairs={{0,1},{1,0},{2,3},{3,2},{4,5},{5,4},{6,7},{7,6},{8,9},{9,8},{10,11... | collective-permute-start | bytes 73736 | tf_op jit(solution)/shard_map/ppermute | solution.py:455
  7.0 1.8 %collective-permute-start.7 = (f32[384]{0:T(512)S(1)}, f32[384]{0:T(512)S(1)}, u32[]{:S(2)}, u32[]{:S(2)}) collective-permute-start(f32[384]{0:T(512)S(1)} %copy-done.5), channel_id=1, source_target_pairs={{0,1},{1,0},{2,3},{3,2},{4,5},{5,4},{6,7},{7,6},{8,9},{9,8},{10,11... | collective-permute-start | bytes 4616 | tf_op jit(solution)/shard_map/ppermute | solution.py:439
  9.6 3.5 %collective-permute-start.5 = (bf16[3,48,128]{2,1,0:T(8,128)(2,1)S(1)}, bf16[3,48,128]{2,1,0:T(8,128)(2,1)S(1)}, u32[]{:S(2)}, u32[]{:S(2)}) collective-permute-start(bf16[3,48,128]{2,1,0:T(8,128)(2,1)S(1)} %shard_map.140.ready_ref), channel_id=1, source_target_pairs={{0,3},{1,2},{2,1},{3,0},{4,7},{5,6},{6,5},{7,4},{8,11},{9,10},{10,... | collective-permute-start | bytes 110600 | tf_op jit(solution)/shard_map/ppermute | solution.py:69
  10.9 2.3 %collective-permute-start.1 = (bf16[11,16,128]{2,1,0:T(8,128)(2,1)S(1)}, bf16[11,16,128]{2,1,0:T(8,128)(2,1)S(1)}, u32[]{:S(2)}, u32[]{:S(2)}) collective-permute-start(bf16[11,16,128]{2,1,0:T(8,128)(2,1)S(1)} %collective-permute-done.tile_before), channel_id=1, source_target_pairs={{0,1},{1,0},{2,3},{3,2},{4,5},{5,4},{6,7},{7,6},{8,9},{9,8},{10,11... | collective-permute-start | bytes 135176 | tf_op jit(solution)/shard_map/ppermute | solution.py:463
  11.3 1.9 %collective-permute-start.3 = (bf16[11,16,128]{2,1,0:T(8,128)(2,1)S(1)}, bf16[11,16,128]{2,1,0:T(8,128)(2,1)S(1)}, u32[]{:S(2)}, u32[]{:S(2)}) collective-permute-start(bf16[11,16,128]{2,1,0:T(8,128)(2,1)S(1)} %collective-permute-done.2.tile_after), channel_id=1, source_target_pairs={{0,1},{1,0},{2,3},{3,2},{4,5},{5,4},{6,7},{7,6},{8,9},{9,8},{10,11... | collective-permute-start | bytes 135176 | tf_op jit(solution)/shard_map/ppermute | solution.py:463
  13.4 1.3 %collective-permute-start.8 = (bf16[3,24,128]{2,1,0:T(8,128)(2,1)S(1)}, bf16[3,24,128]{2,1,0:T(8,128)(2,1)S(1)}, u32[]{:S(2)}, u32[]{:S(2)}) collective-permute-start(bf16[3,24,128]{2,1,0:T(8,128)(2,1)S(1)} %get-tuple-element.36.ready_ref), channel_id=1, source_target_pairs={{0,1},{1,0},{2,3},{3,2},{4,5},{5,4},{6,7},{7,6},{8,9},{9,8},{10,11... | collective-permute-start | bytes 55304 | tf_op jit(solution)/shard_map/ppermute | solution.py:477
  15.8 3.9 %collective-permute-start.10 = (bf16[4,96]{1,0:T(4,128)(2,1)S(1)}, bf16[4,96]{1,0:T(4,128)(2,1)S(1)}, u32[]{:S(2)}, u32[]{:S(2)}) collective-permute-start(bf16[4,96]{1,0:T(4,128)(2,1)S(1)} %get-tuple-element.50), channel_id=1, source_target_pairs={{0,9},{1,8},{4,13},{5,12},{8,1},{9,0},{12,5},{13,4},{2,11},{3,10},... | collective-permute-start | bytes 2312 | tf_op jit(solution)/shard_map/ppermute | solution.py:69
  17.2 4.8 %collective-permute-start.11 = (bf16[4,96]{1,0:T(4,128)(2,1)S(1)}, bf16[4,96]{1,0:T(4,128)(2,1)S(1)}, u32[]{:S(2)}, u32[]{:S(2)}) collective-permute-start(bf16[4,96]{1,0:T(4,128)(2,1)S(1)} %get-tuple-element.51), channel_id=1, source_target_pairs={{0,13},{1,12},{4,9},{5,8},{8,5},{9,4},{12,1},{13,0},{2,15},{3,14},... | collective-permute-start | bytes 2312 | tf_op jit(solution)/shard_map/ppermute | solution.py:69
  18.9 3.1 %collective-permute-start.12 = (bf16[4,96]{1,0:T(4,128)(2,1)S(1)}, bf16[4,96]{1,0:T(4,128)(2,1)S(1)}, u32[]{:S(2)}, u32[]{:S(2)}) collective-permute-start(bf16[4,96]{1,0:T(4,128)(2,1)S(1)} %get-tuple-element.52), channel_id=1, source_target_pairs={{0,5},{1,4},{4,1},{5,0},{8,13},{9,12},{12,9},{13,8},{2,7},{3,6},{6... | collective-permute-start | bytes 2312 | tf_op jit(solution)/shard_map/ppermute | solution.py:69
  18.9 3.1 %collective-permute-start.9 = (bf16[4,96]{1,0:T(4,128)(2,1)S(1)}, bf16[4,96]{1,0:T(4,128)(2,1)S(1)}, u32[]{:S(2)}, u32[]{:S(2)}) collective-permute-start(bf16[4,96]{1,0:T(4,128)(2,1)S(1)} %get-tuple-element.49), channel_id=1, source_target_pairs={{0,1},{1,0},{2,3},{3,2},{4,5},{5,4},{6,7},{7,6},{8,9},{9,8},{10,11... | collective-permute-start | bytes 2312 | tf_op jit(solution)/shard_map/ppermute | solution.py:406
  22.3 1.3 %collective-permute-start.13 = (f32[4,2048]{1,0:T(4,128)S(1)}, f32[4,2048]{1,0:T(4,128)S(1)}, u32[]{:S(2)}, u32[]{:S(2)}) collective-permute-start(f32[4,2048]{1,0:T(4,128)S(1)} %shard_map.146), channel_id=1, source_target_pairs={{0,1},{1,0},{2,3},{3,2},{4,5},{5,4},{6,7},{7,6},{8,9},{9,8},{10,11... | collective-permute-start | bytes 98312 | tf_op jit(solution)/shard_map/ppermute | solution.py:68
  23.6 3.2 %collective-permute-start.14 = (bf16[4,2048]{1,0:T(4,128)(2,1)S(1)}, bf16[4,2048]{1,0:T(4,128)(2,1)S(1)}, u32[]{:S(2)}, u32[]{:S(2)}) collective-permute-start(bf16[4,2048]{1,0:T(4,128)(2,1)S(1)} %get-tuple-element.60), channel_id=1, source_target_pairs={{0,3},{1,2},{2,1},{3,0},{4,7},{5,6},{6,5},{7,4},{8,11},{9,10},{10,... | collective-permute-start | bytes 49160 | tf_op jit(solution)/shard_map/ppermute | solution.py:69
  26.9 4.2 %collective-permute-start.15 = (bf16[4,2048]{1,0:T(4,128)(2,1)S(1)}, bf16[4,2048]{1,0:T(4,128)(2,1)S(1)}, u32[]{:S(2)}, u32[]{:S(2)}) collective-permute-start(bf16[4,2048]{1,0:T(4,128)(2,1)S(1)} %get-tuple-element.58), channel_id=1, source_target_pairs={{0,9},{1,8},{4,13},{5,12},{8,1},{9,0},{12,5},{13,4},{2,11},{3,10},... | collective-permute-start | bytes 49160 | tf_op jit(solution)/shard_map/ppermute | solution.py:69
  28.0 5.0 %collective-permute-start.16 = (bf16[4,2048]{1,0:T(4,128)(2,1)S(1)}, bf16[4,2048]{1,0:T(4,128)(2,1)S(1)}, u32[]{:S(2)}, u32[]{:S(2)}) collective-permute-start(bf16[4,2048]{1,0:T(4,128)(2,1)S(1)} %get-tuple-element.58), channel_id=1, source_target_pairs={{0,13},{1,12},{4,9},{5,8},{8,5},{9,4},{12,1},{13,0},{2,15},{3,14},... | collective-permute-start | bytes 49160 | tf_op jit(solution)/shard_map/ppermute | solution.py:69
  29.0 4.0 %collective-permute-start.17 = (bf16[4,2048]{1,0:T(4,128)(2,1)S(1)}, bf16[4,2048]{1,0:T(4,128)(2,1)S(1)}, u32[]{:S(2)}, u32[]{:S(2)}) collective-permute-start(bf16[4,2048]{1,0:T(4,128)(2,1)S(1)} %get-tuple-element.58), channel_id=1, source_target_pairs={{0,5},{1,4},{4,1},{5,0},{8,13},{9,12},{12,9},{13,8},{2,7},{3,6},{6... | collective-permute-start | bytes 49160 | tf_op jit(solution)/shard_map/ppermute | solution.py:69
  33.4 4.8 %collective-permute-start.18 = (bf16[4,96]{1,0:T(4,128)(2,1)S(1)}, bf16[4,96]{1,0:T(4,128)(2,1)S(1)}, u32[]{:S(2)}, u32[]{:S(2)}) collective-permute-start(bf16[4,96]{1,0:T(4,128)(2,1)S(1)} %get-tuple-element.53), channel_id=1, source_target_pairs={{0,13},{1,12},{4,9},{5,8},{8,5},{9,4},{12,1},{13,0},{2,15},{3,14},... | collective-permute-start | bytes 2312 | tf_op jit(solution)/shard_map/ppermute | solution.py:69
  35.2 3.9 %collective-permute-start.19 = (bf16[4,96]{1,0:T(4,128)(2,1)S(1)}, bf16[4,96]{1,0:T(4,128)(2,1)S(1)}, u32[]{:S(2)}, u32[]{:S(2)}) collective-permute-start(bf16[4,96]{1,0:T(4,128)(2,1)S(1)} %get-tuple-element.54), channel_id=1, source_target_pairs={{0,9},{1,8},{4,13},{5,12},{8,1},{9,0},{12,5},{13,4},{2,11},{3,10},... | collective-permute-start | bytes 2312 | tf_op jit(solution)/shard_map/ppermute | solution.py:69
  35.2 3.9 %collective-permute-start.20 = (bf16[4,96]{1,0:T(4,128)(2,1)S(1)}, bf16[4,96]{1,0:T(4,128)(2,1)S(1)}, u32[]{:S(2)}, u32[]{:S(2)}) collective-permute-start(bf16[4,96]{1,0:T(4,128)(2,1)S(1)} %get-tuple-element.55), channel_id=1, source_target_pairs={{0,5},{1,4},{4,1},{5,0},{8,13},{9,12},{12,9},{13,8},{2,7},{3,6},{6... | collective-permute-start | bytes 2312 | tf_op jit(solution)/shard_map/ppermute | solution.py:69
  37.4 1.7 %collective-permute-start.21 = (bf16[4,96]{1,0:T(4,128)(2,1)S(1)}, bf16[4,96]{1,0:T(4,128)(2,1)S(1)}, u32[]{:S(2)}, u32[]{:S(2)}) collective-permute-start(bf16[4,96]{1,0:T(4,128)(2,1)S(1)} %get-tuple-element.56), channel_id=1, source_target_pairs={{0,1},{1,0},{2,3},{3,2},{4,5},{5,4},{6,7},{7,6},{8,9},{9,8},{10,11... | collective-permute-start | bytes 2312 | tf_op jit(solution)/shard_map/ppermute | solution.py:406
  (4 other events, 13.6 us)

commit v9 on v8

--- a/solution.py
+++ b/solution.py
@@ -114,10 +114,10 @@
         for entry, (at, k) in enumerate(kept):
             out[entry] = fields[at, base + k].astype(bf16)
     for at in range(FIELDS):
-        for pair in range(layers // 2):
-            picked = end_rows([fields[at, 2 * pair], fields[at, 2 * pair + 1]], len(ends))
-            for out, value in zip(ends, picked):
-                out[at, pair * SUBLANES : (pair + 1) * SUBLANES, :] = value.astype(bf16)
+        for first in range(0, layers, STEPS):
+            halves = [end_rows([fields[at, k], fields[at, k + 1]], len(ends)) for k in (first, first + 2)]
+            for out, *value in zip(ends, *halves):
+                out[at, first * STEPS : (first + STEPS) * STEPS, :] = jnp.concatenate(value, 0).astype(bf16)
 
 
 def layer_beside(at, k, layers, tile_before, tile_after):
@@ -170,8 +170,8 @@
         if depth == STEPS:
             return jnp.zeros((SUBLANES, after_ref.shape[2]), f32)
         start, rolls = layers * STEPS + (own > 0) * SUBLANES, ((0, 4), (4, 2), (2, 0))[depth - 1]
-    after = after_ref[at, start : start + SUBLANES, :].astype(f32)
-    before = before_ref[at, start : start + SUBLANES, :].astype(f32)
+    tile, half = start // (2 * SUBLANES) * 2 * SUBLANES, start % (2 * SUBLANES)
+    after, before = (ref[at, tile : tile + 2 * SUBLANES, :].astype(f32)[half : half + SUBLANES] for ref in (after_ref, before_ref))
     after, before = (pltpu.roll(value, by, 0) if by else value for value, by in zip((after, before), rolls))
     me, count = lax.axis_index("sub"), lax.axis_size("sub")
     low = iota(after.shape, 0) < STEPS
@@ -180,7 +180,7 @@
     return jnp.where(low, after * keep_after, before * keep_before)
 
 
-def pack_rep_kernel(fields, tile_before, tile_after, sub_after, sub_before, ready_ref, out_ref, ends_ref):
+def pack_rep_kernel(fields, tile_before, tile_after, sub_after, sub_before, ready_ref, ends_ref):
     layers, rows, lanes = fields.shape[1:]
     beside = 2 * STEPS
     total = layers + 2 * STEPS
@@ -191,7 +191,6 @@
             here = layer_of_block(at, k, fields, tile_before, tile_after), side_rows(at, k, layers, sub_after, sub_before)
             here = pltpu.roll(jnp.concatenate(here, 0), (beside * k + STEPS) % lanes, 1)
             packed = jnp.where(layer_at == k, here, packed)
-        out_ref[at] = packed.astype(bf16)
         ends_ref[at] = packed
 
 
@@ -260,8 +259,8 @@
     lefts, rights = [], []
     for at in range(FIELDS):
         extra = viscous if at == 2 else 0.0
-        left = jnp.where(outer, rep_before[at].astype(f32), ends_ref[at])
-        right = jnp.where(outer, ends_ref[at], rep_after[at].astype(f32))
+        left = jnp.where(outer, rep_before[at], ends_ref[at])
+        right = jnp.where(outer, ends_ref[at], rep_after[at])
         lefts.append(left * inside_left + extra)
         rights.append(right * inside_right + extra)
     left_now, left_ago, left_coef = lefts
@@ -468,18 +467,18 @@
         (packed[0], mode_shapes, node_area.reshape(1, slots)),
     )
 
-    packed, ends = call(
+    ends = call(
         pack_rep_kernel,
-        (shape_of((FIELDS, wide_rows, lanes), bf16), shape_of((FIELDS, wide_rows, lanes), f32)),
+        shape_of((FIELDS, wide_rows, lanes), f32),
         (fields, *tile_halo, *sub_halo, area),
     )
     if reps == 2:
-        rep_halo = (lax.ppermute(packed, "rep", shift(2, 1)),) * 2
+        rep_halo = (lax.ppermute(ends, "rep", swaps(2, 1)),) * 2
     else:
-        rep_halo = both_ways("rep", packed, packed)
+        rep_halo = both_ways("rep", ends, ends)
 
     wide = shape_of((total, wide_rows, lanes), f32)
-    assembled = call(assemble_kernel, (wide,) * 5, (fields, *tile_halo, *sub_halo, packed))
+    assembled = call(assemble_kernel, (wide,) * 5, (fields, *tile_halo, *sub_halo, ends))
     wide = pltpu.VMEM(wide.shape, f32)
     part = shape_of((STEPS, slots // parts), bf16)
     block = shape_of(pressure.shape, f32)

time: 40 us -> 40 us (level)
  no operation moved by 1% of the time
where the time goes in v9:
time: 40 us; the launch traced here: 39.9 us
  starting transfers between devices  20.5 us (51%)
  waiting for transfers between devices  11.1 us (28%)
  Pallas kernels  5.2 us (13%)
  between operations  1.43 us (4%)
  other arithmetic  0.94 us (2%)
  local copies, waits for them, and re-layouts  0.6 us (2%)
    ppermute x13, starting transfers between devices, send(): lax.ppermute(value, (axis, 'rep'), [(2 * i + r, 2 * j + 1 - r) for i, j i...  18 us
    ppermute x13, waiting for transfers between devices, send(): lax.ppermute(value, (axis, 'rep'), [(2 * i + r, 2 * j + 1 - r) for i, j i...  9.44 us
    pallas_call x11, Pallas kernels, call(): pl.pallas_call(kernel, out_shape=out_shape, in_specs=specs or [VMEM] * le...  5.2 us
    ppermute x2, starting transfers between devices, body(): lax.ppermute(value, 'rep', swaps(2, 1))  1.01 us
    another operation x1, other arithmetic, body(): fields = jnp.stack([pressure, previous_pressure, courant_square])  0.92 us
    ppermute x1, waiting for transfers between devices, send(): return lax.ppermute(value, axis, places)  0.86 us
    ppermute x1, waiting for transfers between devices, body(): rep_halo = (lax.ppermute(ends, 'rep', swaps(2, 1)),) * 2  0.83 us
  transfers between devices with their start and end apart: 22, of which 11 were waited for; matrix products, arithmetic and copies ran while one was open for 4% of the time, Pallas kernels for 6%

profile of v9, /device:TPU:0, one launch (start us, length us, event | category | flops | bytes accessed | tf_op | source)
XLA Modules:
  0.0 39.9 jit_solution(13618778729109928095)
XLA Ops:
  1.1 0.9 %pad_maximum_fusion.fields = f32[3,8,16,128]{3,2,1,0:T(8,128)S(1)} fusion(f32[1,8,16,128]{3,2,1,0:T(8,128)} %bitcast.14, f32[1,8,16,128]{3,2,1,0:T(8,128)} %bitcast.15, f32[1,8,16,128]{3,2,1,0:T(8,128)} %bitcast.16), kind=kLoop, calls=%fused_computation | loop fusion | flops 98304 | bytes 393216 | tf_op jit(solution)/shard_map/stack | solution.py:441
  2.1 2.7 %collective-permute-start = (bf16[11,16,128]{2,1,0:T(8,128)(2,1)S(1)}, bf16[11,16,128]{2,1,0:T(8,128)(2,1)S(1)}, u32[]{:S(2)}, u32[]{:S(2)}) collective-permute-start(bf16[11,16,128]{2,1,0:T(8,128)(2,1)S(1)} %get-tuple-element.29.after_ref), channel_id=1, source_target_pairs={{0,5},{1,4},{4,9},{5,8},{8,13},{9,12},{12,1},{13,0},{2,7},{3,6},{6... | collective-permute-start | bytes 135176 | tf_op jit(solution)/shard_map/ppermute | solution.py:69
  4.9 2.1 %collective-permute-start.2 = (bf16[11,16,128]{2,1,0:T(8,128)(2,1)S(1)}, bf16[11,16,128]{2,1,0:T(8,128)(2,1)S(1)}, u32[]{:S(2)}, u32[]{:S(2)}) collective-permute-start(bf16[11,16,128]{2,1,0:T(8,128)(2,1)S(1)} %get-tuple-element.30), channel_id=1, source_target_pairs={{0,13},{1,12},{4,1},{5,0},{8,5},{9,4},{12,9},{13,8},{2,15},{3,14},... | collective-permute-start | bytes 135176 | tf_op jit(solution)/shard_map/ppermute | solution.py:69
  8.1 0.6 %shard_map.139 = (bf16[384,384]{1,0:T(8,128)(2,1)S(1)}, bf16[256,384]{1,0:T(8,128)(2,1)S(1)}) custom-call(bf16[11,16,128]{2,1,0:T(8,128)(2,1)S(1)} %get-tuple-element.29.after_ref, s32[1,384]{1,0:T(1,128)S(1)} %bitcast.12, s32[1,384]{1,0:T(1,128)S(1)} %bitcast.13, s32[1,1]{1,0:T(1,128)} %bitcast.9.count_ref), custom_call_target="tpu_custom_call" | custom-call | flops 1000000000 | tf_op jit(solution)/shard_map/pallas_call | solution.py:44
  9.6 1.3 %collective-permute-start.5 = (bf16[3,48,128]{2,1,0:T(8,128)(2,1)S(1)}, bf16[3,48,128]{2,1,0:T(8,128)(2,1)S(1)}, u32[]{:S(2)}, u32[]{:S(2)}) collective-permute-start(bf16[3,48,128]{2,1,0:T(8,128)(2,1)S(1)} %shard_map.140.ready_ref), channel_id=1, source_target_pairs={{0,3},{1,2},{2,1},{3,0},{4,7},{5,6},{6,5},{7,4},{8,11},{9,10},{10,... | collective-permute-start | bytes 110600 | tf_op jit(solution)/shard_map/ppermute | solution.py:69
  11.4 0.7 %shard_map.141 = (bf16[384,2048]{1,0:T(8,128)(2,1)S(1)}, bf16[2048,384]{1,0:T(8,128)(2,1)S(1)}, f32[1,384]{1,0:T(1,128)S(1)}) custom-call(bf16[3,48,128]{2,1,0:T(8,128)(2,1)S(1)} %shard_map.140.ready_ref, bf16[384,2048]{1,0:T(8,128)(2,1)S(1)} %collective-permute-done.6.shapes_ref, f32[1,384]{1,0:T(1,128)S(1)} %reshape.32.area_ref), custom_call_target="tpu_custom_call" | custom-call | flops 1000000000 | tf_op jit(solution)/shard_map/pallas_call | solution.py:44
  12.2 1.0 %collective-permute-done.5.sub_after.sub_before = bf16[3,48,128]{2,1,0:T(8,128)(2,1)S(1)} collective-permute-done((bf16[3,48,128]{2,1,0:T(8,128)(2,1)S(1)}, bf16[3,48,128]{2,1,0:T(8,128)(2,1)S(1)}, u32[]{:S(2)}, u32[]{:S(2)}) %collective-permute-start.5) | collective-permute-done | bytes 36896 | tf_op jit(solution)/shard_map/ppermute | solution.py:69
  13.8 0.8 %collective-permute-done.8.rep_after.rep_before = f32[3,24,128]{2,1,0:T(8,128)S(1)} collective-permute-done((f32[3,24,128]{2,1,0:T(8,128)S(1)}, f32[3,24,128]{2,1,0:T(8,128)S(1)}, u32[]{:S(2)}, u32[]{:S(2)}) %collective-permute-start.8) | collective-permute-done | bytes 36896 | tf_op jit(solution)/shard_map/ppermute | solution.py:476
  14.6 1.2 %shard_map.144 = (f32[2,8,16,128]{3,2,1,0:T(8,128)S(1)}, bf16[4,96]{1,0:T(4,128)(2,1)S(1)}, bf16[4,96]{1,0:T(4,128)(2,1)S(1)}, bf16[4,96]{1,0:T(4,128)(2,1)S(1)}, bf16[4,96]{1,0:T(4,128)(2,1)S(1)}) custom-call(f32[16,24,128]{2,1,0:T(8,128)S(1)} %get-tuple-element.34.now_in, f32[16,24,128]{2,1,0:T(8,128)S(1)} %get-tuple-element.35.ago_in, ...), custom_call_target="tpu_custom_call" | custom-call | flops 2000000000 | tf_op jit(solution)/shard_map/pallas_call | solution.py:44
  15.8 1.4 %collective-permute-start.10 = (bf16[4,96]{1,0:T(4,128)(2,1)S(1)}, bf16[4,96]{1,0:T(4,128)(2,1)S(1)}, u32[]{:S(2)}, u32[]{:S(2)}) collective-permute-start(bf16[4,96]{1,0:T(4,128)(2,1)S(1)} %get-tuple-element.46), channel_id=1, source_target_pairs={{0,9},{1,8},{4,13},{5,12},{8,1},{9,0},{12,5},{13,4},{2,11},{3,10},... | collective-permute-start | bytes 2312 | tf_op jit(solution)/shard_map/ppermute | solution.py:69
  17.2 1.7 %collective-permute-start.11 = (bf16[4,96]{1,0:T(4,128)(2,1)S(1)}, bf16[4,96]{1,0:T(4,128)(2,1)S(1)}, u32[]{:S(2)}, u32[]{:S(2)}) collective-permute-start(bf16[4,96]{1,0:T(4,128)(2,1)S(1)} %get-tuple-element.47), channel_id=1, source_target_pairs={{0,13},{1,12},{4,9},{5,8},{8,5},{9,4},{12,1},{13,0},{2,15},{3,14},... | collective-permute-start | bytes 2312 | tf_op jit(solution)/shard_map/ppermute | solution.py:69
  19.7 2.3 %collective-permute-done.11.rest_2_ = bf16[4,96]{1,0:T(4,128)(2,1)S(1)} collective-permute-done((bf16[4,96]{1,0:T(4,128)(2,1)S(1)}, bf16[4,96]{1,0:T(4,128)(2,1)S(1)}, u32[]{:S(2)}, u32[]{:S(2)}) %collective-permute-start.11) | collective-permute-done | bytes 800 | tf_op jit(solution)/shard_map/ppermute | solution.py:69
  22.8 0.9 %collective-permute-done.13 = f32[4,2048]{1,0:T(4,128)S(1)} collective-permute-done((f32[4,2048]{1,0:T(4,128)S(1)}, f32[4,2048]{1,0:T(4,128)S(1)}, u32[]{:S(2)}, u32[]{:S(2)}) %collective-permute-start.13) | collective-permute-done | bytes 32800 | tf_op jit(solution)/shard_map/ppermute | solution.py:68
  23.6 1.5 %collective-permute-start.14 = (bf16[4,2048]{1,0:T(4,128)(2,1)S(1)}, bf16[4,2048]{1,0:T(4,128)(2,1)S(1)}, u32[]{:S(2)}, u32[]{:S(2)}) collective-permute-start(bf16[4,2048]{1,0:T(4,128)(2,1)S(1)} %get-tuple-element.56), channel_id=1, source_target_pairs={{0,3},{1,2},{2,1},{3,0},{4,7},{5,6},{6,5},{7,4},{8,11},{9,10},{10,... | collective-permute-start | bytes 49160 | tf_op jit(solution)/shard_map/ppermute | solution.py:69
  25.2 1.7 %collective-permute-done.14 = bf16[4,2048]{1,0:T(4,128)(2,1)S(1)} collective-permute-done((bf16[4,2048]{1,0:T(4,128)(2,1)S(1)}, bf16[4,2048]{1,0:T(4,128)(2,1)S(1)}, u32[]{:S(2)}, u32[]{:S(2)}) %collective-permute-start.14) | collective-permute-done | bytes 16416 | tf_op jit(solution)/shard_map/ppermute | solution.py:69
  26.9 1.2 %collective-permute-start.15 = (bf16[4,2048]{1,0:T(4,128)(2,1)S(1)}, bf16[4,2048]{1,0:T(4,128)(2,1)S(1)}, u32[]{:S(2)}, u32[]{:S(2)}) collective-permute-start(bf16[4,2048]{1,0:T(4,128)(2,1)S(1)} %get-tuple-element.54), channel_id=1, source_target_pairs={{0,9},{1,8},{4,13},{5,12},{8,1},{9,0},{12,5},{13,4},{2,11},{3,10},... | collective-permute-start | bytes 49160 | tf_op jit(solution)/shard_map/ppermute | solution.py:69
  28.1 1.0 %collective-permute-start.16 = (bf16[4,2048]{1,0:T(4,128)(2,1)S(1)}, bf16[4,2048]{1,0:T(4,128)(2,1)S(1)}, u32[]{:S(2)}, u32[]{:S(2)}) collective-permute-start(bf16[4,2048]{1,0:T(4,128)(2,1)S(1)} %get-tuple-element.54), channel_id=1, source_target_pairs={{0,13},{1,12},{4,9},{5,8},{8,5},{9,4},{12,1},{13,0},{2,15},{3,14},... | collective-permute-start | bytes 49160 | tf_op jit(solution)/shard_map/ppermute | solution.py:69
  29.1 1.1 %collective-permute-start.17 = (bf16[4,2048]{1,0:T(4,128)(2,1)S(1)}, bf16[4,2048]{1,0:T(4,128)(2,1)S(1)}, u32[]{:S(2)}, u32[]{:S(2)}) collective-permute-start(bf16[4,2048]{1,0:T(4,128)(2,1)S(1)} %get-tuple-element.54), channel_id=1, source_target_pairs={{0,5},{1,4},{4,1},{5,0},{8,13},{9,12},{12,9},{13,8},{2,7},{3,6},{6... | collective-permute-start | bytes 49160 | tf_op jit(solution)/shard_map/ppermute | solution.py:69
  30.1 0.7 %shard_map.145 = (f32[8,16,128]{2,1,0:T(8,128)}, f32[8,16,128]{2,1,0:T(8,128)}) custom-call(f32[2,8,16,128]{3,2,1,0:T(8,128)S(1)} %get-tuple-element.40.states), custom_call_target="tpu_custom_call" | custom-call | flops 1000000000 | tf_op jit(solution)/shard_map/pallas_call | solution.py:44
  31.1 1.9 %collective-permute-done.16.rest_2_ = bf16[4,2048]{1,0:T(4,128)(2,1)S(1)} collective-permute-done((bf16[4,2048]{1,0:T(4,128)(2,1)S(1)}, bf16[4,2048]{1,0:T(4,128)(2,1)S(1)}, u32[]{:S(2)}, u32[]{:S(2)}) %collective-permute-start.16) | collective-permute-done | bytes 16416 | tf_op jit(solution)/shard_map/ppermute | solution.py:69
  33.5 1.8 %collective-permute-start.18 = (bf16[4,96]{1,0:T(4,128)(2,1)S(1)}, bf16[4,96]{1,0:T(4,128)(2,1)S(1)}, u32[]{:S(2)}, u32[]{:S(2)}) collective-permute-start(bf16[4,96]{1,0:T(4,128)(2,1)S(1)} %get-tuple-element.49), channel_id=1, source_target_pairs={{0,13},{1,12},{4,9},{5,8},{8,5},{9,4},{12,1},{13,0},{2,15},{3,14},... | collective-permute-start | bytes 2312 | tf_op jit(solution)/shard_map/ppermute | solution.py:69
  35.2 2.2 %collective-permute-start.20 = (bf16[4,96]{1,0:T(4,128)(2,1)S(1)}, bf16[4,96]{1,0:T(4,128)(2,1)S(1)}, u32[]{:S(2)}, u32[]{:S(2)}) collective-permute-start(bf16[4,96]{1,0:T(4,128)(2,1)S(1)} %get-tuple-element.51), channel_id=1, source_target_pairs={{0,5},{1,4},{4,1},{5,0},{8,13},{9,12},{12,9},{13,8},{2,7},{3,6},{6... | collective-permute-start | bytes 2312 | tf_op jit(solution)/shard_map/ppermute | solution.py:69
  38.3 0.8 %collective-permute-done.19.rest_1_ = bf16[4,96]{1,0:T(4,128)(2,1)S(1)} collective-permute-done((bf16[4,96]{1,0:T(4,128)(2,1)S(1)}, bf16[4,96]{1,0:T(4,128)(2,1)S(1)}, u32[]{:S(2)}, u32[]{:S(2)}) %collective-permute-start.19) | collective-permute-done | bytes 800 | tf_op jit(solution)/shard_map/ppermute | solution.py:69
  39.1 0.8 %shard_map.148 = bf16[4,384]{1,0:T(4,128)(2,1)} custom-call(bf16[384,384]{1,0:T(8,128)(2,1)S(1)} %get-tuple-element.31.ready_ref.route_ref, bf16[4,96]{1,0:T(4,128)(2,1)S(1)} %collective-permute-done.18.rest_0_, bf16[4,96]{1,0:T(4,128)(2,1)S(1)} %collective-permute-done.19.rest_1_, bf16[4,96]{1,0:T(4,128)(2,1)S(1)} %collective-permute-done.20.rest_2_, ...), custom_call_target="tpu_custom_call" | custom-call | flops 1000000000 | tf_op jit(solution)/shard_map/pallas_call | solution.py:44
  (48 shorter events, 6.2 us)
Async XLA Ops:
  0.6 10.8 %collective-permute-start.6 = (bf16[384,2048]{1,0:T(8,128)(2,1)}, bf16[384,2048]{1,0:T(8,128)(2,1)S(1)}, u32[]{:S(2)}, u32[]{:S(2)}) collective-permute-start(bf16[384,2048]{1,0:T(8,128)(2,1)} %param.15), channel_id=1, source_target_pairs={{0,1},{1,0},{2,3},{3,2},{4,5},{5,4},{6,7},{7,6},{8,9},{9,8},{10,11... | collective-permute-start | bytes 4718600 | tf_op jit(solution)/shard_map/ppermute | solution.py:438
  2.1 6.0 %copy-start.3 = (s32[1,1,1,384,1]{3,4,2,1,0:T(1,128)S(1)}, s32[1,1,1,384,1]{3,4,2,1,0:T(1,128)}, u32[]{:S(2)}) copy-start(s32[1,1,1,384,1]{3,4,2,1,0:T(1,128)} %param.20) | copy-start | bytes 4612
  2.1 6.0 %copy-start.4 = (s32[1,1,1,384]{3,2,1,0:T(1,128)S(1)}, s32[1,1,1,384]{3,2,1,0:T(1,128)}, u32[]{:S(2)}) copy-start(s32[1,1,1,384]{3,2,1,0:T(1,128)} %param.19) | copy-start | bytes 4612
  2.1 6.9 %collective-permute-start = (bf16[11,16,128]{2,1,0:T(8,128)(2,1)S(1)}, bf16[11,16,128]{2,1,0:T(8,128)(2,1)S(1)}, u32[]{:S(2)}, u32[]{:S(2)}) collective-permute-start(bf16[11,16,128]{2,1,0:T(8,128)(2,1)S(1)} %get-tuple-element.29.after_ref), channel_id=1, source_target_pairs={{0,5},{1,4},{4,9},{5,8},{8,13},{9,12},{12,1},{13,0},{2,7},{3,6},{6... | collective-permute-start | bytes 135176 | tf_op jit(solution)/shard_map/ppermute | solution.py:69
  4.9 4.7 %collective-permute-start.2 = (bf16[11,16,128]{2,1,0:T(8,128)(2,1)S(1)}, bf16[11,16,128]{2,1,0:T(8,128)(2,1)S(1)}, u32[]{:S(2)}, u32[]{:S(2)}) collective-permute-start(bf16[11,16,128]{2,1,0:T(8,128)(2,1)S(1)} %get-tuple-element.30), channel_id=1, source_target_pairs={{0,13},{1,12},{4,1},{5,0},{8,5},{9,4},{12,9},{13,8},{2,15},{3,14},... | collective-permute-start | bytes 135176 | tf_op jit(solution)/shard_map/ppermute | solution.py:69
  7.0 1.8 %collective-permute-start.4 = (bf16[3,32,128]{2,1,0:T(8,128)(2,1)S(1)}, bf16[3,32,128]{2,1,0:T(8,128)(2,1)S(1)}, u32[]{:S(2)}, u32[]{:S(2)}) collective-permute-start(bf16[3,32,128]{2,1,0:T(8,128)(2,1)S(1)} %get-tuple-element.32), channel_id=1, source_target_pairs={{0,1},{1,0},{2,3},{3,2},{4,5},{5,4},{6,7},{7,6},{8,9},{9,8},{10,11... | collective-permute-start | bytes 73736 | tf_op jit(solution)/shard_map/ppermute | solution.py:454
  7.0 1.8 %collective-permute-start.7 = (f32[384]{0:T(512)S(1)}, f32[384]{0:T(512)S(1)}, u32[]{:S(2)}, u32[]{:S(2)}) collective-permute-start(f32[384]{0:T(512)S(1)} %copy-done.5), channel_id=1, source_target_pairs={{0,1},{1,0},{2,3},{3,2},{4,5},{5,4},{6,7},{7,6},{8,9},{9,8},{10,11... | collective-permute-start | bytes 4616 | tf_op jit(solution)/shard_map/ppermute | solution.py:438
  9.6 3.5 %collective-permute-start.5 = (bf16[3,48,128]{2,1,0:T(8,128)(2,1)S(1)}, bf16[3,48,128]{2,1,0:T(8,128)(2,1)S(1)}, u32[]{:S(2)}, u32[]{:S(2)}) collective-permute-start(bf16[3,48,128]{2,1,0:T(8,128)(2,1)S(1)} %shard_map.140.ready_ref), channel_id=1, source_target_pairs={{0,3},{1,2},{2,1},{3,0},{4,7},{5,6},{6,5},{7,4},{8,11},{9,10},{10,... | collective-permute-start | bytes 110600 | tf_op jit(solution)/shard_map/ppermute | solution.py:69
  10.9 2.3 %collective-permute-start.1 = (bf16[11,16,128]{2,1,0:T(8,128)(2,1)S(1)}, bf16[11,16,128]{2,1,0:T(8,128)(2,1)S(1)}, u32[]{:S(2)}, u32[]{:S(2)}) collective-permute-start(bf16[11,16,128]{2,1,0:T(8,128)(2,1)S(1)} %collective-permute-done.tile_before), channel_id=1, source_target_pairs={{0,1},{1,0},{2,3},{3,2},{4,5},{5,4},{6,7},{7,6},{8,9},{9,8},{10,11... | collective-permute-start | bytes 135176 | tf_op jit(solution)/shard_map/ppermute | solution.py:462
  11.3 1.9 %collective-permute-start.3 = (bf16[11,16,128]{2,1,0:T(8,128)(2,1)S(1)}, bf16[11,16,128]{2,1,0:T(8,128)(2,1)S(1)}, u32[]{:S(2)}, u32[]{:S(2)}) collective-permute-start(bf16[11,16,128]{2,1,0:T(8,128)(2,1)S(1)} %collective-permute-done.2.tile_after), channel_id=1, source_target_pairs={{0,1},{1,0},{2,3},{3,2},{4,5},{5,4},{6,7},{7,6},{8,9},{9,8},{10,11... | collective-permute-start | bytes 135176 | tf_op jit(solution)/shard_map/ppermute | solution.py:462
  13.4 1.3 %collective-permute-start.8 = (f32[3,24,128]{2,1,0:T(8,128)S(1)}, f32[3,24,128]{2,1,0:T(8,128)S(1)}, u32[]{:S(2)}, u32[]{:S(2)}) collective-permute-start(f32[3,24,128]{2,1,0:T(8,128)S(1)} %shard_map.142.ready_ref.ends_ref), channel_id=1, source_target_pairs={{0,1},{1,0},{2,3},{3,2},{4,5},{5,4},{6,7},{7,6},{8,9},{9,8},{10,11... | collective-permute-start | bytes 110600 | tf_op jit(solution)/shard_map/ppermute | solution.py:476
  15.8 3.9 %collective-permute-start.10 = (bf16[4,96]{1,0:T(4,128)(2,1)S(1)}, bf16[4,96]{1,0:T(4,128)(2,1)S(1)}, u32[]{:S(2)}, u32[]{:S(2)}) collective-permute-start(bf16[4,96]{1,0:T(4,128)(2,1)S(1)} %get-tuple-element.46), channel_id=1, source_target_pairs={{0,9},{1,8},{4,13},{5,12},{8,1},{9,0},{12,5},{13,4},{2,11},{3,10},... | collective-permute-start | bytes 2312 | tf_op jit(solution)/shard_map/ppermute | solution.py:69
  17.2 4.8 %collective-permute-start.11 = (bf16[4,96]{1,0:T(4,128)(2,1)S(1)}, bf16[4,96]{1,0:T(4,128)(2,1)S(1)}, u32[]{:S(2)}, u32[]{:S(2)}) collective-permute-start(bf16[4,96]{1,0:T(4,128)(2,1)S(1)} %get-tuple-element.47), channel_id=1, source_target_pairs={{0,13},{1,12},{4,9},{5,8},{8,5},{9,4},{12,1},{13,0},{2,15},{3,14},... | collective-permute-start | bytes 2312 | tf_op jit(solution)/shard_map/ppermute | solution.py:69
  18.9 3.1 %collective-permute-start.12 = (bf16[4,96]{1,0:T(4,128)(2,1)S(1)}, bf16[4,96]{1,0:T(4,128)(2,1)S(1)}, u32[]{:S(2)}, u32[]{:S(2)}) collective-permute-start(bf16[4,96]{1,0:T(4,128)(2,1)S(1)} %get-tuple-element.48), channel_id=1, source_target_pairs={{0,5},{1,4},{4,1},{5,0},{8,13},{9,12},{12,9},{13,8},{2,7},{3,6},{6... | collective-permute-start | bytes 2312 | tf_op jit(solution)/shard_map/ppermute | solution.py:69
  18.9 3.1 %collective-permute-start.9 = (bf16[4,96]{1,0:T(4,128)(2,1)S(1)}, bf16[4,96]{1,0:T(4,128)(2,1)S(1)}, u32[]{:S(2)}, u32[]{:S(2)}) collective-permute-start(bf16[4,96]{1,0:T(4,128)(2,1)S(1)} %get-tuple-element.45), channel_id=1, source_target_pairs={{0,1},{1,0},{2,3},{3,2},{4,5},{5,4},{6,7},{7,6},{8,9},{9,8},{10,11... | collective-permute-start | bytes 2312 | tf_op jit(solution)/shard_map/ppermute | solution.py:405
  22.4 1.3 %collective-permute-start.13 = (f32[4,2048]{1,0:T(4,128)S(1)}, f32[4,2048]{1,0:T(4,128)S(1)}, u32[]{:S(2)}, u32[]{:S(2)}) collective-permute-start(f32[4,2048]{1,0:T(4,128)S(1)} %shard_map.146), channel_id=1, source_target_pairs={{0,1},{1,0},{2,3},{3,2},{4,5},{5,4},{6,7},{7,6},{8,9},{9,8},{10,11... | collective-permute-start | bytes 98312 | tf_op jit(solution)/shard_map/ppermute | solution.py:68
  23.6 3.2 %collective-permute-start.14 = (bf16[4,2048]{1,0:T(4,128)(2,1)S(1)}, bf16[4,2048]{1,0:T(4,128)(2,1)S(1)}, u32[]{:S(2)}, u32[]{:S(2)}) collective-permute-start(bf16[4,2048]{1,0:T(4,128)(2,1)S(1)} %get-tuple-element.56), channel_id=1, source_target_pairs={{0,3},{1,2},{2,1},{3,0},{4,7},{5,6},{6,5},{7,4},{8,11},{9,10},{10,... | collective-permute-start | bytes 49160 | tf_op jit(solution)/shard_map/ppermute | solution.py:69
  26.9 4.2 %collective-permute-start.15 = (bf16[4,2048]{1,0:T(4,128)(2,1)S(1)}, bf16[4,2048]{1,0:T(4,128)(2,1)S(1)}, u32[]{:S(2)}, u32[]{:S(2)}) collective-permute-start(bf16[4,2048]{1,0:T(4,128)(2,1)S(1)} %get-tuple-element.54), channel_id=1, source_target_pairs={{0,9},{1,8},{4,13},{5,12},{8,1},{9,0},{12,5},{13,4},{2,11},{3,10},... | collective-permute-start | bytes 49160 | tf_op jit(solution)/shard_map/ppermute | solution.py:69
  28.1 5.0 %collective-permute-start.16 = (bf16[4,2048]{1,0:T(4,128)(2,1)S(1)}, bf16[4,2048]{1,0:T(4,128)(2,1)S(1)}, u32[]{:S(2)}, u32[]{:S(2)}) collective-permute-start(bf16[4,2048]{1,0:T(4,128)(2,1)S(1)} %get-tuple-element.54), channel_id=1, source_target_pairs={{0,13},{1,12},{4,9},{5,8},{8,5},{9,4},{12,1},{13,0},{2,15},{3,14},... | collective-permute-start | bytes 49160 | tf_op jit(solution)/shard_map/ppermute | solution.py:69
  29.1 4.0 %collective-permute-start.17 = (bf16[4,2048]{1,0:T(4,128)(2,1)S(1)}, bf16[4,2048]{1,0:T(4,128)(2,1)S(1)}, u32[]{:S(2)}, u32[]{:S(2)}) collective-permute-start(bf16[4,2048]{1,0:T(4,128)(2,1)S(1)} %get-tuple-element.54), channel_id=1, source_target_pairs={{0,5},{1,4},{4,1},{5,0},{8,13},{9,12},{12,9},{13,8},{2,7},{3,6},{6... | collective-permute-start | bytes 49160 | tf_op jit(solution)/shard_map/ppermute | solution.py:69
  33.5 4.8 %collective-permute-start.18 = (bf16[4,96]{1,0:T(4,128)(2,1)S(1)}, bf16[4,96]{1,0:T(4,128)(2,1)S(1)}, u32[]{:S(2)}, u32[]{:S(2)}) collective-permute-start(bf16[4,96]{1,0:T(4,128)(2,1)S(1)} %get-tuple-element.49), channel_id=1, source_target_pairs={{0,13},{1,12},{4,9},{5,8},{8,5},{9,4},{12,1},{13,0},{2,15},{3,14},... | collective-permute-start | bytes 2312 | tf_op jit(solution)/shard_map/ppermute | solution.py:69
  35.2 3.9 %collective-permute-start.19 = (bf16[4,96]{1,0:T(4,128)(2,1)S(1)}, bf16[4,96]{1,0:T(4,128)(2,1)S(1)}, u32[]{:S(2)}, u32[]{:S(2)}) collective-permute-start(bf16[4,96]{1,0:T(4,128)(2,1)S(1)} %get-tuple-element.50), channel_id=1, source_target_pairs={{0,9},{1,8},{4,13},{5,12},{8,1},{9,0},{12,5},{13,4},{2,11},{3,10},... | collective-permute-start | bytes 2312 | tf_op jit(solution)/shard_map/ppermute | solution.py:69
  35.2 3.9 %collective-permute-start.20 = (bf16[4,96]{1,0:T(4,128)(2,1)S(1)}, bf16[4,96]{1,0:T(4,128)(2,1)S(1)}, u32[]{:S(2)}, u32[]{:S(2)}) collective-permute-start(bf16[4,96]{1,0:T(4,128)(2,1)S(1)} %get-tuple-element.51), channel_id=1, source_target_pairs={{0,5},{1,4},{4,1},{5,0},{8,13},{9,12},{12,9},{13,8},{2,7},{3,6},{6... | collective-permute-start | bytes 2312 | tf_op jit(solution)/shard_map/ppermute | solution.py:69
  37.4 1.7 %collective-permute-start.21 = (bf16[4,96]{1,0:T(4,128)(2,1)S(1)}, bf16[4,96]{1,0:T(4,128)(2,1)S(1)}, u32[]{:S(2)}, u32[]{:S(2)}) collective-permute-start(bf16[4,96]{1,0:T(4,128)(2,1)S(1)} %get-tuple-element.52), channel_id=1, source_target_pairs={{0,1},{1,0},{2,3},{3,2},{4,5},{5,4},{6,7},{7,6},{8,9},{9,8},{10,11... | collective-permute-start | bytes 2312 | tf_op jit(solution)/shard_map/ppermute | solution.py:405
  (4 other events, 13.6 us)

commit v10 on v9

--- a/solution.py
+++ b/solution.py
@@ -303,9 +303,10 @@
             lap = lap + edge_of(k, edge)
             mask = inside_low if k < STEPS else inside_high if k >= STEPS + layers else inside
             updated = advance(here, before, coef[k], lap, lap_before, mask)
-            now[k] = updated
-            ago[k] = here
-            lapped[k] = viscous * lap
+            if step < STEPS - 1:
+                now[k] = updated
+                ago[k] = here
+                lapped[k] = viscous * lap
             own = k - STEPS
             if 0 <= own < layers:
                 core = updated[:rows]
@@ -518,7 +519,7 @@
     )
     share = modes // (buckets * subs * reps)
     modal_state = lax.dynamic_slice_in_dim(state, lax.axis_index(("tile", "sub", "rep")) * share, share, 1)
-    order = [k for k in (3, 2, 1, 0) if k < parts]
+    order = [k for k in (2, 3, 1, 0) if k < parts]
     surface = call(
         functools.partial(return_kernel, order), shape_of((STEPS, slots), bf16), (route, *exchange(sends, order, crossed))
     )

time: 40 us -> 39.8 us (level)
  starting transfers between devices: 20.5 us -> 19.6 us
  waiting for transfers between devices: 11.1 us -> 11.8 us
    ppermute x13, starting transfers between devices: 18 us -> 17.1 us  [send(): lax.ppermute(value, (axis, 'rep'), [(2 * i + r, 2 * j + 1 - r) for i, j i...]
    ppermute x13, waiting for transfers between devices: 9.44 us -> 10.1 us  [send(): lax.ppermute(value, (axis, 'rep'), [(2 * i + r, 2 * j + 1 - r) for i, j i...]
where the time goes in v10:
time: 39.8 us; the launch traced here: 39.7 us
  starting transfers between devices  19.6 us (49%)
  waiting for transfers between devices  11.8 us (30%)
  Pallas kernels  5.2 us (13%)
  between operations  1.43 us (4%)
  other arithmetic  0.94 us (2%)
  local copies, waits for them, and re-layouts  0.6 us (2%)
    ppermute x13, starting transfers between devices, send(): lax.ppermute(value, (axis, 'rep'), [(2 * i + r, 2 * j + 1 - r) for i, j i...  17.1 us
    ppermute x13, waiting for transfers between devices, send(): lax.ppermute(value, (axis, 'rep'), [(2 * i + r, 2 * j + 1 - r) for i, j i...  10.1 us
    pallas_call x11, Pallas kernels, call(): pl.pallas_call(kernel, out_shape=out_shape, in_specs=specs or [VMEM] * le...  5.2 us
    ppermute x2, starting transfers between devices, body(): lax.ppermute(value, 'rep', swaps(2, 1))  1.01 us
    another operation x1, other arithmetic, body(): fields = jnp.stack([pressure, previous_pressure, courant_square])  0.92 us
    ppermute x1, waiting for transfers between devices, send(): return lax.ppermute(value, axis, places)  0.86 us
    ppermute x1, waiting for transfers between devices, body(): rep_halo = (lax.ppermute(ends, 'rep', swaps(2, 1)),) * 2  0.83 us
  transfers between devices with their start and end apart: 22, of which 11 were waited for; matrix products, arithmetic and copies ran while one was open for 4% of the time, Pallas kernels for 6%

profile of v10, /device:TPU:0, one launch (start us, length us, event | category | flops | bytes accessed | tf_op | source)
XLA Modules:
  0.0 39.7 jit_solution(16074112465524706818)
XLA Ops:
  1.1 0.9 %pad_maximum_fusion.fields = f32[3,8,16,128]{3,2,1,0:T(8,128)S(1)} fusion(f32[1,8,16,128]{3,2,1,0:T(8,128)} %bitcast.14, f32[1,8,16,128]{3,2,1,0:T(8,128)} %bitcast.15, f32[1,8,16,128]{3,2,1,0:T(8,128)} %bitcast.16), kind=kLoop, calls=%fused_computation | loop fusion | flops 98304 | bytes 393216 | tf_op jit(solution)/shard_map/stack | solution.py:442
  2.1 2.7 %collective-permute-start = (bf16[11,16,128]{2,1,0:T(8,128)(2,1)S(1)}, bf16[11,16,128]{2,1,0:T(8,128)(2,1)S(1)}, u32[]{:S(2)}, u32[]{:S(2)}) collective-permute-start(bf16[11,16,128]{2,1,0:T(8,128)(2,1)S(1)} %get-tuple-element.29.after_ref), channel_id=1, source_target_pairs={{0,5},{1,4},{4,9},{5,8},{8,13},{9,12},{12,1},{13,0},{2,7},{3,6},{6... | collective-permute-start | bytes 135176 | tf_op jit(solution)/shard_map/ppermute | solution.py:69
  4.9 2.1 %collective-permute-start.2 = (bf16[11,16,128]{2,1,0:T(8,128)(2,1)S(1)}, bf16[11,16,128]{2,1,0:T(8,128)(2,1)S(1)}, u32[]{:S(2)}, u32[]{:S(2)}) collective-permute-start(bf16[11,16,128]{2,1,0:T(8,128)(2,1)S(1)} %get-tuple-element.30), channel_id=1, source_target_pairs={{0,13},{1,12},{4,1},{5,0},{8,5},{9,4},{12,9},{13,8},{2,15},{3,14},... | collective-permute-start | bytes 135176 | tf_op jit(solution)/shard_map/ppermute | solution.py:69
  9.6 1.3 %collective-permute-start.5 = (bf16[3,48,128]{2,1,0:T(8,128)(2,1)S(1)}, bf16[3,48,128]{2,1,0:T(8,128)(2,1)S(1)}, u32[]{:S(2)}, u32[]{:S(2)}) collective-permute-start(bf16[3,48,128]{2,1,0:T(8,128)(2,1)S(1)} %shard_map.140.ready_ref), channel_id=1, source_target_pairs={{0,3},{1,2},{2,1},{3,0},{4,7},{5,6},{6,5},{7,4},{8,11},{9,10},{10,... | collective-permute-start | bytes 110600 | tf_op jit(solution)/shard_map/ppermute | solution.py:69
  11.4 0.7 %shard_map.141 = (bf16[384,2048]{1,0:T(8,128)(2,1)S(1)}, bf16[2048,384]{1,0:T(8,128)(2,1)S(1)}, f32[1,384]{1,0:T(1,128)S(1)}) custom-call(bf16[3,48,128]{2,1,0:T(8,128)(2,1)S(1)} %shard_map.140.ready_ref, bf16[384,2048]{1,0:T(8,128)(2,1)S(1)} %collective-permute-done.6.shapes_ref, f32[1,384]{1,0:T(1,128)S(1)} %reshape.32.area_ref), custom_call_target="tpu_custom_call" | custom-call | flops 1000000000 | tf_op jit(solution)/shard_map/pallas_call | solution.py:44
  12.2 1.0 %collective-permute-done.5.sub_after.sub_before = bf16[3,48,128]{2,1,0:T(8,128)(2,1)S(1)} collective-permute-done((bf16[3,48,128]{2,1,0:T(8,128)(2,1)S(1)}, bf16[3,48,128]{2,1,0:T(8,128)(2,1)S(1)}, u32[]{:S(2)}, u32[]{:S(2)}) %collective-permute-start.5) | collective-permute-done | bytes 36896 | tf_op jit(solution)/shard_map/ppermute | solution.py:69
  13.8 0.8 %collective-permute-done.8.rep_after.rep_before = f32[3,24,128]{2,1,0:T(8,128)S(1)} collective-permute-done((f32[3,24,128]{2,1,0:T(8,128)S(1)}, f32[3,24,128]{2,1,0:T(8,128)S(1)}, u32[]{:S(2)}, u32[]{:S(2)}) %collective-permute-start.8) | collective-permute-done | bytes 36896 | tf_op jit(solution)/shard_map/ppermute | solution.py:477
  14.6 1.2 %shard_map.144 = (f32[2,8,16,128]{3,2,1,0:T(8,128)S(1)}, bf16[4,96]{1,0:T(4,128)(2,1)S(1)}, bf16[4,96]{1,0:T(4,128)(2,1)S(1)}, bf16[4,96]{1,0:T(4,128)(2,1)S(1)}, bf16[4,96]{1,0:T(4,128)(2,1)S(1)}) custom-call(f32[16,24,128]{2,1,0:T(8,128)S(1)} %get-tuple-element.34.now_in, f32[16,24,128]{2,1,0:T(8,128)S(1)} %get-tuple-element.35.ago_in, ...), custom_call_target="tpu_custom_call" | custom-call | flops 2000000000 | tf_op jit(solution)/shard_map/pallas_call | solution.py:44
  15.8 1.4 %collective-permute-start.10 = (bf16[4,96]{1,0:T(4,128)(2,1)S(1)}, bf16[4,96]{1,0:T(4,128)(2,1)S(1)}, u32[]{:S(2)}, u32[]{:S(2)}) collective-permute-start(bf16[4,96]{1,0:T(4,128)(2,1)S(1)} %get-tuple-element.46), channel_id=1, source_target_pairs={{0,9},{1,8},{4,13},{5,12},{8,1},{9,0},{12,5},{13,4},{2,11},{3,10},... | collective-permute-start | bytes 2312 | tf_op jit(solution)/shard_map/ppermute | solution.py:69
  17.2 1.7 %collective-permute-start.11 = (bf16[4,96]{1,0:T(4,128)(2,1)S(1)}, bf16[4,96]{1,0:T(4,128)(2,1)S(1)}, u32[]{:S(2)}, u32[]{:S(2)}) collective-permute-start(bf16[4,96]{1,0:T(4,128)(2,1)S(1)} %get-tuple-element.47), channel_id=1, source_target_pairs={{0,13},{1,12},{4,9},{5,8},{8,5},{9,4},{12,1},{13,0},{2,15},{3,14},... | collective-permute-start | bytes 2312 | tf_op jit(solution)/shard_map/ppermute | solution.py:69
  19.7 2.3 %collective-permute-done.11.rest_2_ = bf16[4,96]{1,0:T(4,128)(2,1)S(1)} collective-permute-done((bf16[4,96]{1,0:T(4,128)(2,1)S(1)}, bf16[4,96]{1,0:T(4,128)(2,1)S(1)}, u32[]{:S(2)}, u32[]{:S(2)}) %collective-permute-start.11) | collective-permute-done | bytes 800 | tf_op jit(solution)/shard_map/ppermute | solution.py:69
  22.8 0.9 %collective-permute-done.13 = f32[4,2048]{1,0:T(4,128)S(1)} collective-permute-done((f32[4,2048]{1,0:T(4,128)S(1)}, f32[4,2048]{1,0:T(4,128)S(1)}, u32[]{:S(2)}, u32[]{:S(2)}) %collective-permute-start.13) | collective-permute-done | bytes 32800 | tf_op jit(solution)/shard_map/ppermute | solution.py:68
  23.6 1.5 %collective-permute-start.14 = (bf16[4,2048]{1,0:T(4,128)(2,1)S(1)}, bf16[4,2048]{1,0:T(4,128)(2,1)S(1)}, u32[]{:S(2)}, u32[]{:S(2)}) collective-permute-start(bf16[4,2048]{1,0:T(4,128)(2,1)S(1)} %get-tuple-element.56), channel_id=1, source_target_pairs={{0,3},{1,2},{2,1},{3,0},{4,7},{5,6},{6,5},{7,4},{8,11},{9,10},{10,... | collective-permute-start | bytes 49160 | tf_op jit(solution)/shard_map/ppermute | solution.py:69
  25.2 1.7 %collective-permute-done.14 = bf16[4,2048]{1,0:T(4,128)(2,1)S(1)} collective-permute-done((bf16[4,2048]{1,0:T(4,128)(2,1)S(1)}, bf16[4,2048]{1,0:T(4,128)(2,1)S(1)}, u32[]{:S(2)}, u32[]{:S(2)}) %collective-permute-start.14) | collective-permute-done | bytes 16416 | tf_op jit(solution)/shard_map/ppermute | solution.py:69
  26.9 1.2 %collective-permute-start.15 = (bf16[4,2048]{1,0:T(4,128)(2,1)S(1)}, bf16[4,2048]{1,0:T(4,128)(2,1)S(1)}, u32[]{:S(2)}, u32[]{:S(2)}) collective-permute-start(bf16[4,2048]{1,0:T(4,128)(2,1)S(1)} %get-tuple-element.54), channel_id=1, source_target_pairs={{0,9},{1,8},{4,13},{5,12},{8,1},{9,0},{12,5},{13,4},{2,11},{3,10},... | collective-permute-start | bytes 49160 | tf_op jit(solution)/shard_map/ppermute | solution.py:69
  28.1 1.0 %collective-permute-start.16 = (bf16[4,2048]{1,0:T(4,128)(2,1)S(1)}, bf16[4,2048]{1,0:T(4,128)(2,1)S(1)}, u32[]{:S(2)}, u32[]{:S(2)}) collective-permute-start(bf16[4,2048]{1,0:T(4,128)(2,1)S(1)} %get-tuple-element.54), channel_id=1, source_target_pairs={{0,13},{1,12},{4,9},{5,8},{8,5},{9,4},{12,1},{13,0},{2,15},{3,14},... | collective-permute-start | bytes 49160 | tf_op jit(solution)/shard_map/ppermute | solution.py:69
  29.1 1.1 %collective-permute-start.17 = (bf16[4,2048]{1,0:T(4,128)(2,1)S(1)}, bf16[4,2048]{1,0:T(4,128)(2,1)S(1)}, u32[]{:S(2)}, u32[]{:S(2)}) collective-permute-start(bf16[4,2048]{1,0:T(4,128)(2,1)S(1)} %get-tuple-element.54), channel_id=1, source_target_pairs={{0,5},{1,4},{4,1},{5,0},{8,13},{9,12},{12,9},{13,8},{2,7},{3,6},{6... | collective-permute-start | bytes 49160 | tf_op jit(solution)/shard_map/ppermute | solution.py:69
  30.1 0.7 %shard_map.145 = (f32[8,16,128]{2,1,0:T(8,128)}, f32[8,16,128]{2,1,0:T(8,128)}) custom-call(f32[2,8,16,128]{3,2,1,0:T(8,128)S(1)} %get-tuple-element.40.states), custom_call_target="tpu_custom_call" | custom-call | flops 1000000000 | tf_op jit(solution)/shard_map/pallas_call | solution.py:44
  31.1 1.9 %collective-permute-done.16.rest_2_ = bf16[4,2048]{1,0:T(4,128)(2,1)S(1)} collective-permute-done((bf16[4,2048]{1,0:T(4,128)(2,1)S(1)}, bf16[4,2048]{1,0:T(4,128)(2,1)S(1)}, u32[]{:S(2)}, u32[]{:S(2)}) %collective-permute-start.16) | collective-permute-done | bytes 16416 | tf_op jit(solution)/shard_map/ppermute | solution.py:69
  33.5 0.7 %collective-permute-start.18 = (bf16[4,96]{1,0:T(4,128)(2,1)S(1)}, bf16[4,96]{1,0:T(4,128)(2,1)S(1)}, u32[]{:S(2)}, u32[]{:S(2)}) collective-permute-start(bf16[4,96]{1,0:T(4,128)(2,1)S(1)} %get-tuple-element.49), channel_id=1, source_target_pairs={{0,9},{1,8},{4,13},{5,12},{8,1},{9,0},{12,5},{13,4},{2,11},{3,10},... | collective-permute-start | bytes 2312 | tf_op jit(solution)/shard_map/ppermute | solution.py:69
  34.1 1.8 %collective-permute-start.19 = (bf16[4,96]{1,0:T(4,128)(2,1)S(1)}, bf16[4,96]{1,0:T(4,128)(2,1)S(1)}, u32[]{:S(2)}, u32[]{:S(2)}) collective-permute-start(bf16[4,96]{1,0:T(4,128)(2,1)S(1)} %get-tuple-element.50), channel_id=1, source_target_pairs={{0,13},{1,12},{4,9},{5,8},{8,5},{9,4},{12,1},{13,0},{2,15},{3,14},... | collective-permute-start | bytes 2312 | tf_op jit(solution)/shard_map/ppermute | solution.py:69
  35.9 0.7 %collective-permute-start.20 = (bf16[4,96]{1,0:T(4,128)(2,1)S(1)}, bf16[4,96]{1,0:T(4,128)(2,1)S(1)}, u32[]{:S(2)}, u32[]{:S(2)}) collective-permute-start(bf16[4,96]{1,0:T(4,128)(2,1)S(1)} %get-tuple-element.51), channel_id=1, source_target_pairs={{0,5},{1,4},{4,1},{5,0},{8,13},{9,12},{12,9},{13,8},{2,7},{3,6},{6... | collective-permute-start | bytes 2312 | tf_op jit(solution)/shard_map/ppermute | solution.py:69
  37.4 1.5 %collective-permute-done.19.rest_1_ = bf16[4,96]{1,0:T(4,128)(2,1)S(1)} collective-permute-done((bf16[4,96]{1,0:T(4,128)(2,1)S(1)}, bf16[4,96]{1,0:T(4,128)(2,1)S(1)}, u32[]{:S(2)}, u32[]{:S(2)}) %collective-permute-start.19) | collective-permute-done | bytes 800 | tf_op jit(solution)/shard_map/ppermute | solution.py:69
  38.9 0.8 %shard_map.148 = bf16[4,384]{1,0:T(4,128)(2,1)} custom-call(bf16[384,384]{1,0:T(8,128)(2,1)S(1)} %get-tuple-element.31.ready_ref.route_ref, bf16[4,96]{1,0:T(4,128)(2,1)S(1)} %collective-permute-done.18.rest_0_, bf16[4,96]{1,0:T(4,128)(2,1)S(1)} %collective-permute-done.19.rest_1_, bf16[4,96]{1,0:T(4,128)(2,1)S(1)} %collective-permute-done.20.rest_2_, ...), custom_call_target="tpu_custom_call" | custom-call | flops 1000000000 | tf_op jit(solution)/shard_map/pallas_call | solution.py:44
  (48 shorter events, 6.8 us)
Async XLA Ops:
  0.6 10.8 %collective-permute-start.6 = (bf16[384,2048]{1,0:T(8,128)(2,1)}, bf16[384,2048]{1,0:T(8,128)(2,1)S(1)}, u32[]{:S(2)}, u32[]{:S(2)}) collective-permute-start(bf16[384,2048]{1,0:T(8,128)(2,1)} %param.15), channel_id=1, source_target_pairs={{0,1},{1,0},{2,3},{3,2},{4,5},{5,4},{6,7},{7,6},{8,9},{9,8},{10,11... | collective-permute-start | bytes 4718600 | tf_op jit(solution)/shard_map/ppermute | solution.py:439
  2.1 6.0 %copy-start.3 = (s32[1,1,1,384,1]{3,4,2,1,0:T(1,128)S(1)}, s32[1,1,1,384,1]{3,4,2,1,0:T(1,128)}, u32[]{:S(2)}) copy-start(s32[1,1,1,384,1]{3,4,2,1,0:T(1,128)} %param.20) | copy-start | bytes 4612
  2.1 6.0 %copy-start.4 = (s32[1,1,1,384]{3,2,1,0:T(1,128)S(1)}, s32[1,1,1,384]{3,2,1,0:T(1,128)}, u32[]{:S(2)}) copy-start(s32[1,1,1,384]{3,2,1,0:T(1,128)} %param.19) | copy-start | bytes 4612
  2.1 6.9 %collective-permute-start = (bf16[11,16,128]{2,1,0:T(8,128)(2,1)S(1)}, bf16[11,16,128]{2,1,0:T(8,128)(2,1)S(1)}, u32[]{:S(2)}, u32[]{:S(2)}) collective-permute-start(bf16[11,16,128]{2,1,0:T(8,128)(2,1)S(1)} %get-tuple-element.29.after_ref), channel_id=1, source_target_pairs={{0,5},{1,4},{4,9},{5,8},{8,13},{9,12},{12,1},{13,0},{2,7},{3,6},{6... | collective-permute-start | bytes 135176 | tf_op jit(solution)/shard_map/ppermute | solution.py:69
  4.9 4.7 %collective-permute-start.2 = (bf16[11,16,128]{2,1,0:T(8,128)(2,1)S(1)}, bf16[11,16,128]{2,1,0:T(8,128)(2,1)S(1)}, u32[]{:S(2)}, u32[]{:S(2)}) collective-permute-start(bf16[11,16,128]{2,1,0:T(8,128)(2,1)S(1)} %get-tuple-element.30), channel_id=1, source_target_pairs={{0,13},{1,12},{4,1},{5,0},{8,5},{9,4},{12,9},{13,8},{2,15},{3,14},... | collective-permute-start | bytes 135176 | tf_op jit(solution)/shard_map/ppermute | solution.py:69
  7.0 1.8 %collective-permute-start.4 = (bf16[3,32,128]{2,1,0:T(8,128)(2,1)S(1)}, bf16[3,32,128]{2,1,0:T(8,128)(2,1)S(1)}, u32[]{:S(2)}, u32[]{:S(2)}) collective-permute-start(bf16[3,32,128]{2,1,0:T(8,128)(2,1)S(1)} %get-tuple-element.32), channel_id=1, source_target_pairs={{0,1},{1,0},{2,3},{3,2},{4,5},{5,4},{6,7},{7,6},{8,9},{9,8},{10,11... | collective-permute-start | bytes 73736 | tf_op jit(solution)/shard_map/ppermute | solution.py:455
  7.0 1.8 %collective-permute-start.7 = (f32[384]{0:T(512)S(1)}, f32[384]{0:T(512)S(1)}, u32[]{:S(2)}, u32[]{:S(2)}) collective-permute-start(f32[384]{0:T(512)S(1)} %copy-done.5), channel_id=1, source_target_pairs={{0,1},{1,0},{2,3},{3,2},{4,5},{5,4},{6,7},{7,6},{8,9},{9,8},{10,11... | collective-permute-start | bytes 4616 | tf_op jit(solution)/shard_map/ppermute | solution.py:439
  9.6 3.5 %collective-permute-start.5 = (bf16[3,48,128]{2,1,0:T(8,128)(2,1)S(1)}, bf16[3,48,128]{2,1,0:T(8,128)(2,1)S(1)}, u32[]{:S(2)}, u32[]{:S(2)}) collective-permute-start(bf16[3,48,128]{2,1,0:T(8,128)(2,1)S(1)} %shard_map.140.ready_ref), channel_id=1, source_target_pairs={{0,3},{1,2},{2,1},{3,0},{4,7},{5,6},{6,5},{7,4},{8,11},{9,10},{10,... | collective-permute-start | bytes 110600 | tf_op jit(solution)/shard_map/ppermute | solution.py:69
  10.9 2.3 %collective-permute-start.1 = (bf16[11,16,128]{2,1,0:T(8,128)(2,1)S(1)}, bf16[11,16,128]{2,1,0:T(8,128)(2,1)S(1)}, u32[]{:S(2)}, u32[]{:S(2)}) collective-permute-start(bf16[11,16,128]{2,1,0:T(8,128)(2,1)S(1)} %collective-permute-done.tile_before), channel_id=1, source_target_pairs={{0,1},{1,0},{2,3},{3,2},{4,5},{5,4},{6,7},{7,6},{8,9},{9,8},{10,11... | collective-permute-start | bytes 135176 | tf_op jit(solution)/shard_map/ppermute | solution.py:463
  11.3 1.9 %collective-permute-start.3 = (bf16[11,16,128]{2,1,0:T(8,128)(2,1)S(1)}, bf16[11,16,128]{2,1,0:T(8,128)(2,1)S(1)}, u32[]{:S(2)}, u32[]{:S(2)}) collective-permute-start(bf16[11,16,128]{2,1,0:T(8,128)(2,1)S(1)} %collective-permute-done.2.tile_after), channel_id=1, source_target_pairs={{0,1},{1,0},{2,3},{3,2},{4,5},{5,4},{6,7},{7,6},{8,9},{9,8},{10,11... | collective-permute-start | bytes 135176 | tf_op jit(solution)/shard_map/ppermute | solution.py:463
  13.4 1.3 %collective-permute-start.8 = (f32[3,24,128]{2,1,0:T(8,128)S(1)}, f32[3,24,128]{2,1,0:T(8,128)S(1)}, u32[]{:S(2)}, u32[]{:S(2)}) collective-permute-start(f32[3,24,128]{2,1,0:T(8,128)S(1)} %shard_map.142.ready_ref.ends_ref), channel_id=1, source_target_pairs={{0,1},{1,0},{2,3},{3,2},{4,5},{5,4},{6,7},{7,6},{8,9},{9,8},{10,11... | collective-permute-start | bytes 110600 | tf_op jit(solution)/shard_map/ppermute | solution.py:477
  15.8 3.9 %collective-permute-start.10 = (bf16[4,96]{1,0:T(4,128)(2,1)S(1)}, bf16[4,96]{1,0:T(4,128)(2,1)S(1)}, u32[]{:S(2)}, u32[]{:S(2)}) collective-permute-start(bf16[4,96]{1,0:T(4,128)(2,1)S(1)} %get-tuple-element.46), channel_id=1, source_target_pairs={{0,9},{1,8},{4,13},{5,12},{8,1},{9,0},{12,5},{13,4},{2,11},{3,10},... | collective-permute-start | bytes 2312 | tf_op jit(solution)/shard_map/ppermute | solution.py:69
  17.2 4.8 %collective-permute-start.11 = (bf16[4,96]{1,0:T(4,128)(2,1)S(1)}, bf16[4,96]{1,0:T(4,128)(2,1)S(1)}, u32[]{:S(2)}, u32[]{:S(2)}) collective-permute-start(bf16[4,96]{1,0:T(4,128)(2,1)S(1)} %get-tuple-element.47), channel_id=1, source_target_pairs={{0,13},{1,12},{4,9},{5,8},{8,5},{9,4},{12,1},{13,0},{2,15},{3,14},... | collective-permute-start | bytes 2312 | tf_op jit(solution)/shard_map/ppermute | solution.py:69
  18.9 3.1 %collective-permute-start.12 = (bf16[4,96]{1,0:T(4,128)(2,1)S(1)}, bf16[4,96]{1,0:T(4,128)(2,1)S(1)}, u32[]{:S(2)}, u32[]{:S(2)}) collective-permute-start(bf16[4,96]{1,0:T(4,128)(2,1)S(1)} %get-tuple-element.48), channel_id=1, source_target_pairs={{0,5},{1,4},{4,1},{5,0},{8,13},{9,12},{12,9},{13,8},{2,7},{3,6},{6... | collective-permute-start | bytes 2312 | tf_op jit(solution)/shard_map/ppermute | solution.py:69
  18.9 3.1 %collective-permute-start.9 = (bf16[4,96]{1,0:T(4,128)(2,1)S(1)}, bf16[4,96]{1,0:T(4,128)(2,1)S(1)}, u32[]{:S(2)}, u32[]{:S(2)}) collective-permute-start(bf16[4,96]{1,0:T(4,128)(2,1)S(1)} %get-tuple-element.45), channel_id=1, source_target_pairs={{0,1},{1,0},{2,3},{3,2},{4,5},{5,4},{6,7},{7,6},{8,9},{9,8},{10,11... | collective-permute-start | bytes 2312 | tf_op jit(solution)/shard_map/ppermute | solution.py:406
  22.4 1.3 %collective-permute-start.13 = (f32[4,2048]{1,0:T(4,128)S(1)}, f32[4,2048]{1,0:T(4,128)S(1)}, u32[]{:S(2)}, u32[]{:S(2)}) collective-permute-start(f32[4,2048]{1,0:T(4,128)S(1)} %shard_map.146), channel_id=1, source_target_pairs={{0,1},{1,0},{2,3},{3,2},{4,5},{5,4},{6,7},{7,6},{8,9},{9,8},{10,11... | collective-permute-start | bytes 98312 | tf_op jit(solution)/shard_map/ppermute | solution.py:68
  23.6 3.2 %collective-permute-start.14 = (bf16[4,2048]{1,0:T(4,128)(2,1)S(1)}, bf16[4,2048]{1,0:T(4,128)(2,1)S(1)}, u32[]{:S(2)}, u32[]{:S(2)}) collective-permute-start(bf16[4,2048]{1,0:T(4,128)(2,1)S(1)} %get-tuple-element.56), channel_id=1, source_target_pairs={{0,3},{1,2},{2,1},{3,0},{4,7},{5,6},{6,5},{7,4},{8,11},{9,10},{10,... | collective-permute-start | bytes 49160 | tf_op jit(solution)/shard_map/ppermute | solution.py:69
  26.9 4.2 %collective-permute-start.15 = (bf16[4,2048]{1,0:T(4,128)(2,1)S(1)}, bf16[4,2048]{1,0:T(4,128)(2,1)S(1)}, u32[]{:S(2)}, u32[]{:S(2)}) collective-permute-start(bf16[4,2048]{1,0:T(4,128)(2,1)S(1)} %get-tuple-element.54), channel_id=1, source_target_pairs={{0,9},{1,8},{4,13},{5,12},{8,1},{9,0},{12,5},{13,4},{2,11},{3,10},... | collective-permute-start | bytes 49160 | tf_op jit(solution)/shard_map/ppermute | solution.py:69
  28.1 5.0 %collective-permute-start.16 = (bf16[4,2048]{1,0:T(4,128)(2,1)S(1)}, bf16[4,2048]{1,0:T(4,128)(2,1)S(1)}, u32[]{:S(2)}, u32[]{:S(2)}) collective-permute-start(bf16[4,2048]{1,0:T(4,128)(2,1)S(1)} %get-tuple-element.54), channel_id=1, source_target_pairs={{0,13},{1,12},{4,9},{5,8},{8,5},{9,4},{12,1},{13,0},{2,15},{3,14},... | collective-permute-start | bytes 49160 | tf_op jit(solution)/shard_map/ppermute | solution.py:69
  29.1 4.0 %collective-permute-start.17 = (bf16[4,2048]{1,0:T(4,128)(2,1)S(1)}, bf16[4,2048]{1,0:T(4,128)(2,1)S(1)}, u32[]{:S(2)}, u32[]{:S(2)}) collective-permute-start(bf16[4,2048]{1,0:T(4,128)(2,1)S(1)} %get-tuple-element.54), channel_id=1, source_target_pairs={{0,5},{1,4},{4,1},{5,0},{8,13},{9,12},{12,9},{13,8},{2,7},{3,6},{6... | collective-permute-start | bytes 49160 | tf_op jit(solution)/shard_map/ppermute | solution.py:69
  33.5 3.9 %collective-permute-start.18 = (bf16[4,96]{1,0:T(4,128)(2,1)S(1)}, bf16[4,96]{1,0:T(4,128)(2,1)S(1)}, u32[]{:S(2)}, u32[]{:S(2)}) collective-permute-start(bf16[4,96]{1,0:T(4,128)(2,1)S(1)} %get-tuple-element.49), channel_id=1, source_target_pairs={{0,9},{1,8},{4,13},{5,12},{8,1},{9,0},{12,5},{13,4},{2,11},{3,10},... | collective-permute-start | bytes 2312 | tf_op jit(solution)/shard_map/ppermute | solution.py:69
  34.1 4.8 %collective-permute-start.19 = (bf16[4,96]{1,0:T(4,128)(2,1)S(1)}, bf16[4,96]{1,0:T(4,128)(2,1)S(1)}, u32[]{:S(2)}, u32[]{:S(2)}) collective-permute-start(bf16[4,96]{1,0:T(4,128)(2,1)S(1)} %get-tuple-element.50), channel_id=1, source_target_pairs={{0,13},{1,12},{4,9},{5,8},{8,5},{9,4},{12,1},{13,0},{2,15},{3,14},... | collective-permute-start | bytes 2312 | tf_op jit(solution)/shard_map/ppermute | solution.py:69
  35.9 3.0 %collective-permute-start.20 = (bf16[4,96]{1,0:T(4,128)(2,1)S(1)}, bf16[4,96]{1,0:T(4,128)(2,1)S(1)}, u32[]{:S(2)}, u32[]{:S(2)}) collective-permute-start(bf16[4,96]{1,0:T(4,128)(2,1)S(1)} %get-tuple-element.51), channel_id=1, source_target_pairs={{0,5},{1,4},{4,1},{5,0},{8,13},{9,12},{12,9},{13,8},{2,7},{3,6},{6... | collective-permute-start | bytes 2312 | tf_op jit(solution)/shard_map/ppermute | solution.py:69
  36.6 2.4 %collective-permute-start.21 = (bf16[4,96]{1,0:T(4,128)(2,1)S(1)}, bf16[4,96]{1,0:T(4,128)(2,1)S(1)}, u32[]{:S(2)}, u32[]{:S(2)}) collective-permute-start(bf16[4,96]{1,0:T(4,128)(2,1)S(1)} %get-tuple-element.52), channel_id=1, source_target_pairs={{0,1},{1,0},{2,3},{3,2},{4,5},{5,4},{6,7},{7,6},{8,9},{9,8},{10,11... | collective-permute-start | bytes 2312 | tf_op jit(solution)/shard_map/ppermute | solution.py:406
  (4 other events, 13.6 us)

commit v11 on v10

--- a/solution.py
+++ b/solution.py
@@ -334,7 +334,7 @@
         copy.wait()
 
 
-def turn_kernel(buckets, ready_ref, shapes_ref, area_ref, turned_ref, flipped_ref, area_out):
+def turn_kernel(buckets, ready_ref, shapes_ref, area_ref, turned_ref, area_out):
     total = shapes_ref.shape[0]
     bucket = total // buckets
     me = lax.axis_index("tile")
@@ -355,6 +355,9 @@
         area_out[...] = lax.dot_general(
             area_ref[...], picks, (((1,), (1,)), ((), ())), precision=lax.Precision.HIGHEST, preferred_element_type=f32
         )
+
+
+def flip_kernel(ready_ref, turned_ref, flipped_ref):
     flipped_ref[...] = turned_ref[...].astype(f32).T.astype(bf16)
 
 
@@ -462,9 +465,9 @@
     if two:
         tile_halo = [lax.ppermute(value, "rep", swaps(2, 1)) for value in tile_halo]
 
-    turned, flipped, area = call(
+    turned, area = call(
         functools.partial(turn_kernel, buckets),
-        (shape_of(mode_shapes.shape, bf16), shape_of(mode_shapes.shape[::-1], bf16), shape_of((1, slots), f32)),
+        (shape_of(mode_shapes.shape, bf16), shape_of((1, slots), f32)),
         (packed[0], mode_shapes, node_area.reshape(1, slots)),
     )
 
@@ -506,6 +509,8 @@
         forces = functools.reduce(jnp.add, addends)
         if count in (2, 4):
             sent = forces.astype(bf16) if axis != "rep" else forces
+            if axis == "sub":
+                flipped = call(flip_kernel, shape_of(mode_shapes.shape[::-1], bf16), (sent, turned))
             places = [swaps(count, k) for k in (2, 3, 1) if k < count]
             addends = [forces] + [send(sent, axis, swap, reps == 2 and axis != "rep") for swap in places]
         else:

time: 39.8 us -> 39.9 us (level)
    pallas_call x11 -> x12, Pallas kernels: 5.2 us -> 5.25 us  [call(): pl.pallas_call(kernel, out_shape=out_shape, in_specs=specs or [VMEM] * le...]
where the time goes in v11:
time: 39.9 us; the launch traced here: 39.7 us
  starting transfers between devices  19.6 us (49%)
  waiting for transfers between devices  11.8 us (30%)
  Pallas kernels  5.25 us (13%)
  between operations  1.46 us (4%)
  other arithmetic  0.94 us (2%)
  local copies, waits for them, and re-layouts  0.6 us (2%)
    ppermute x13, starting transfers between devices, send(): lax.ppermute(value, (axis, 'rep'), [(2 * i + r, 2 * j + 1 - r) for i, j i...  17.1 us
    ppermute x13, waiting for transfers between devices, send(): lax.ppermute(value, (axis, 'rep'), [(2 * i + r, 2 * j + 1 - r) for i, j i...  10.1 us
    pallas_call x12, Pallas kernels, call(): pl.pallas_call(kernel, out_shape=out_shape, in_specs=specs or [VMEM] * le...  5.25 us
    ppermute x2, starting transfers between devices, body(): lax.ppermute(value, 'rep', swaps(2, 1))  1.01 us
    another operation x1, other arithmetic, body(): fields = jnp.stack([pressure, previous_pressure, courant_square])  0.92 us
    ppermute x1, waiting for transfers between devices, send(): return lax.ppermute(value, axis, places)  0.86 us
    ppermute x1, waiting for transfers between devices, body(): rep_halo = (lax.ppermute(ends, 'rep', swaps(2, 1)),) * 2  0.83 us
  transfers between devices with their start and end apart: 22, of which 11 were waited for; matrix products, arithmetic and copies ran while one was open for 4% of the time, Pallas kernels for 6%

profile of v11, /device:TPU:0, one launch (start us, length us, event | category | flops | bytes accessed | tf_op | source)
XLA Modules:
  0.0 39.7 jit_solution(16793089202799062278)
XLA Ops:
  1.1 0.9 %pad_maximum_fusion.fields = f32[3,8,16,128]{3,2,1,0:T(8,128)S(1)} fusion(f32[1,8,16,128]{3,2,1,0:T(8,128)} %bitcast.14, f32[1,8,16,128]{3,2,1,0:T(8,128)} %bitcast.15, f32[1,8,16,128]{3,2,1,0:T(8,128)} %bitcast.16), kind=kLoop, calls=%fused_computation | loop fusion | flops 98304 | bytes 393216 | tf_op jit(solution)/shard_map/stack | solution.py:445
  2.1 2.7 %collective-permute-start = (bf16[11,16,128]{2,1,0:T(8,128)(2,1)S(1)}, bf16[11,16,128]{2,1,0:T(8,128)(2,1)S(1)}, u32[]{:S(2)}, u32[]{:S(2)}) collective-permute-start(bf16[11,16,128]{2,1,0:T(8,128)(2,1)S(1)} %get-tuple-element.28.after_ref), channel_id=1, source_target_pairs={{0,5},{1,4},{4,9},{5,8},{8,13},{9,12},{12,1},{13,0},{2,7},{3,6},{6... | collective-permute-start | bytes 135176 | tf_op jit(solution)/shard_map/ppermute | solution.py:69
  4.9 2.1 %collective-permute-start.2 = (bf16[11,16,128]{2,1,0:T(8,128)(2,1)S(1)}, bf16[11,16,128]{2,1,0:T(8,128)(2,1)S(1)}, u32[]{:S(2)}, u32[]{:S(2)}) collective-permute-start(bf16[11,16,128]{2,1,0:T(8,128)(2,1)S(1)} %get-tuple-element.29), channel_id=1, source_target_pairs={{0,13},{1,12},{4,1},{5,0},{8,5},{9,4},{12,9},{13,8},{2,15},{3,14},... | collective-permute-start | bytes 135176 | tf_op jit(solution)/shard_map/ppermute | solution.py:69
  8.1 0.6 %shard_map.139 = (bf16[384,384]{1,0:T(8,128)(2,1)S(1)}, bf16[256,384]{1,0:T(8,128)(2,1)S(1)}) custom-call(bf16[11,16,128]{2,1,0:T(8,128)(2,1)S(1)} %get-tuple-element.28.after_ref, s32[1,384]{1,0:T(1,128)S(1)} %bitcast.12, s32[1,384]{1,0:T(1,128)S(1)} %bitcast.13, s32[1,1]{1,0:T(1,128)} %bitcast.9.count_ref), custom_call_target="tpu_custom_call" | custom-call | flops 1000000000 | tf_op jit(solution)/shard_map/pallas_call | solution.py:44
  9.6 1.3 %collective-permute-start.5 = (bf16[3,48,128]{2,1,0:T(8,128)(2,1)S(1)}, bf16[3,48,128]{2,1,0:T(8,128)(2,1)S(1)}, u32[]{:S(2)}, u32[]{:S(2)}) collective-permute-start(bf16[3,48,128]{2,1,0:T(8,128)(2,1)S(1)} %shard_map.140.ready_ref), channel_id=1, source_target_pairs={{0,3},{1,2},{2,1},{3,0},{4,7},{5,6},{6,5},{7,4},{8,11},{9,10},{10,... | collective-permute-start | bytes 110600 | tf_op jit(solution)/shard_map/ppermute | solution.py:69
  11.7 1.4 %collective-permute-done.5.sub_after.sub_before = bf16[3,48,128]{2,1,0:T(8,128)(2,1)S(1)} collective-permute-done((bf16[3,48,128]{2,1,0:T(8,128)(2,1)S(1)}, bf16[3,48,128]{2,1,0:T(8,128)(2,1)S(1)}, u32[]{:S(2)}, u32[]{:S(2)}) %collective-permute-start.5) | collective-permute-done | bytes 36896 | tf_op jit(solution)/shard_map/ppermute | solution.py:69
  13.8 0.8 %collective-permute-done.8.rep_after.rep_before = f32[3,24,128]{2,1,0:T(8,128)S(1)} collective-permute-done((f32[3,24,128]{2,1,0:T(8,128)S(1)}, f32[3,24,128]{2,1,0:T(8,128)S(1)}, u32[]{:S(2)}, u32[]{:S(2)}) %collective-permute-start.8) | collective-permute-done | bytes 36896 | tf_op jit(solution)/shard_map/ppermute | solution.py:480
  14.6 1.2 %shard_map.144 = (f32[2,8,16,128]{3,2,1,0:T(8,128)S(1)}, bf16[4,96]{1,0:T(4,128)(2,1)S(1)}, bf16[4,96]{1,0:T(4,128)(2,1)S(1)}, bf16[4,96]{1,0:T(4,128)(2,1)S(1)}, bf16[4,96]{1,0:T(4,128)(2,1)S(1)}) custom-call(f32[16,24,128]{2,1,0:T(8,128)S(1)} %get-tuple-element.33.now_in, f32[16,24,128]{2,1,0:T(8,128)S(1)} %get-tuple-element.34.ago_in, ...), custom_call_target="tpu_custom_call" | custom-call | flops 2000000000 | tf_op jit(solution)/shard_map/pallas_call | solution.py:44
  15.8 1.4 %collective-permute-start.10 = (bf16[4,96]{1,0:T(4,128)(2,1)S(1)}, bf16[4,96]{1,0:T(4,128)(2,1)S(1)}, u32[]{:S(2)}, u32[]{:S(2)}) collective-permute-start(bf16[4,96]{1,0:T(4,128)(2,1)S(1)} %get-tuple-element.44), channel_id=1, source_target_pairs={{0,9},{1,8},{4,13},{5,12},{8,1},{9,0},{12,5},{13,4},{2,11},{3,10},... | collective-permute-start | bytes 2312 | tf_op jit(solution)/shard_map/ppermute | solution.py:69
  17.2 1.7 %collective-permute-start.11 = (bf16[4,96]{1,0:T(4,128)(2,1)S(1)}, bf16[4,96]{1,0:T(4,128)(2,1)S(1)}, u32[]{:S(2)}, u32[]{:S(2)}) collective-permute-start(bf16[4,96]{1,0:T(4,128)(2,1)S(1)} %get-tuple-element.45), channel_id=1, source_target_pairs={{0,13},{1,12},{4,9},{5,8},{8,5},{9,4},{12,1},{13,0},{2,15},{3,14},... | collective-permute-start | bytes 2312 | tf_op jit(solution)/shard_map/ppermute | solution.py:69
  19.7 2.3 %collective-permute-done.11.rest_2_ = bf16[4,96]{1,0:T(4,128)(2,1)S(1)} collective-permute-done((bf16[4,96]{1,0:T(4,128)(2,1)S(1)}, bf16[4,96]{1,0:T(4,128)(2,1)S(1)}, u32[]{:S(2)}, u32[]{:S(2)}) %collective-permute-start.11) | collective-permute-done | bytes 800 | tf_op jit(solution)/shard_map/ppermute | solution.py:69
  22.8 0.9 %collective-permute-done.13 = f32[4,2048]{1,0:T(4,128)S(1)} collective-permute-done((f32[4,2048]{1,0:T(4,128)S(1)}, f32[4,2048]{1,0:T(4,128)S(1)}, u32[]{:S(2)}, u32[]{:S(2)}) %collective-permute-start.13) | collective-permute-done | bytes 32800 | tf_op jit(solution)/shard_map/ppermute | solution.py:68
  23.6 1.5 %collective-permute-start.14 = (bf16[4,2048]{1,0:T(4,128)(2,1)S(1)}, bf16[4,2048]{1,0:T(4,128)(2,1)S(1)}, u32[]{:S(2)}, u32[]{:S(2)}) collective-permute-start(bf16[4,2048]{1,0:T(4,128)(2,1)S(1)} %get-tuple-element.54.ready_ref), channel_id=1, source_target_pairs={{0,3},{1,2},{2,1},{3,0},{4,7},{5,6},{6,5},{7,4},{8,11},{9,10},{10,... | collective-permute-start | bytes 49160 | tf_op jit(solution)/shard_map/ppermute | solution.py:69
  25.2 0.7 %shard_map.145 = (f32[8,16,128]{2,1,0:T(8,128)}, f32[8,16,128]{2,1,0:T(8,128)}) custom-call(f32[2,8,16,128]{3,2,1,0:T(8,128)S(1)} %get-tuple-element.39.states), custom_call_target="tpu_custom_call" | custom-call | flops 1000000000 | tf_op jit(solution)/shard_map/pallas_call | solution.py:44
  25.8 1.0 %collective-permute-done.14 = bf16[4,2048]{1,0:T(4,128)(2,1)S(1)} collective-permute-done((bf16[4,2048]{1,0:T(4,128)(2,1)S(1)}, bf16[4,2048]{1,0:T(4,128)(2,1)S(1)}, u32[]{:S(2)}, u32[]{:S(2)}) %collective-permute-start.14) | collective-permute-done | bytes 16416 | tf_op jit(solution)/shard_map/ppermute | solution.py:69
  26.9 1.2 %collective-permute-start.15 = (bf16[4,2048]{1,0:T(4,128)(2,1)S(1)}, bf16[4,2048]{1,0:T(4,128)(2,1)S(1)}, u32[]{:S(2)}, u32[]{:S(2)}) collective-permute-start(bf16[4,2048]{1,0:T(4,128)(2,1)S(1)} %get-tuple-element.52), channel_id=1, source_target_pairs={{0,9},{1,8},{4,13},{5,12},{8,1},{9,0},{12,5},{13,4},{2,11},{3,10},... | collective-permute-start | bytes 49160 | tf_op jit(solution)/shard_map/ppermute | solution.py:69
  28.1 1.0 %collective-permute-start.16 = (bf16[4,2048]{1,0:T(4,128)(2,1)S(1)}, bf16[4,2048]{1,0:T(4,128)(2,1)S(1)}, u32[]{:S(2)}, u32[]{:S(2)}) collective-permute-start(bf16[4,2048]{1,0:T(4,128)(2,1)S(1)} %get-tuple-element.52), channel_id=1, source_target_pairs={{0,13},{1,12},{4,9},{5,8},{8,5},{9,4},{12,1},{13,0},{2,15},{3,14},... | collective-permute-start | bytes 49160 | tf_op jit(solution)/shard_map/ppermute | solution.py:69
  29.1 1.1 %collective-permute-start.17 = (bf16[4,2048]{1,0:T(4,128)(2,1)S(1)}, bf16[4,2048]{1,0:T(4,128)(2,1)S(1)}, u32[]{:S(2)}, u32[]{:S(2)}) collective-permute-start(bf16[4,2048]{1,0:T(4,128)(2,1)S(1)} %get-tuple-element.52), channel_id=1, source_target_pairs={{0,5},{1,4},{4,1},{5,0},{8,13},{9,12},{12,9},{13,8},{2,7},{3,6},{6... | collective-permute-start | bytes 49160 | tf_op jit(solution)/shard_map/ppermute | solution.py:69
  31.2 1.9 %collective-permute-done.16.rest_2_ = bf16[4,2048]{1,0:T(4,128)(2,1)S(1)} collective-permute-done((bf16[4,2048]{1,0:T(4,128)(2,1)S(1)}, bf16[4,2048]{1,0:T(4,128)(2,1)S(1)}, u32[]{:S(2)}, u32[]{:S(2)}) %collective-permute-start.16) | collective-permute-done | bytes 16416 | tf_op jit(solution)/shard_map/ppermute | solution.py:69
  33.5 0.7 %collective-permute-start.18 = (bf16[4,96]{1,0:T(4,128)(2,1)S(1)}, bf16[4,96]{1,0:T(4,128)(2,1)S(1)}, u32[]{:S(2)}, u32[]{:S(2)}) collective-permute-start(bf16[4,96]{1,0:T(4,128)(2,1)S(1)} %get-tuple-element.47), channel_id=1, source_target_pairs={{0,9},{1,8},{4,13},{5,12},{8,1},{9,0},{12,5},{13,4},{2,11},{3,10},... | collective-permute-start | bytes 2312 | tf_op jit(solution)/shard_map/ppermute | solution.py:69
  34.1 1.8 %collective-permute-start.19 = (bf16[4,96]{1,0:T(4,128)(2,1)S(1)}, bf16[4,96]{1,0:T(4,128)(2,1)S(1)}, u32[]{:S(2)}, u32[]{:S(2)}) collective-permute-start(bf16[4,96]{1,0:T(4,128)(2,1)S(1)} %get-tuple-element.48), channel_id=1, source_target_pairs={{0,13},{1,12},{4,9},{5,8},{8,5},{9,4},{12,1},{13,0},{2,15},{3,14},... | collective-permute-start | bytes 2312 | tf_op jit(solution)/shard_map/ppermute | solution.py:69
  35.9 0.7 %collective-permute-start.20 = (bf16[4,96]{1,0:T(4,128)(2,1)S(1)}, bf16[4,96]{1,0:T(4,128)(2,1)S(1)}, u32[]{:S(2)}, u32[]{:S(2)}) collective-permute-start(bf16[4,96]{1,0:T(4,128)(2,1)S(1)} %get-tuple-element.49), channel_id=1, source_target_pairs={{0,5},{1,4},{4,1},{5,0},{8,13},{9,12},{12,9},{13,8},{2,7},{3,6},{6... | collective-permute-start | bytes 2312 | tf_op jit(solution)/shard_map/ppermute | solution.py:69
  37.4 1.5 %collective-permute-done.19.rest_1_ = bf16[4,96]{1,0:T(4,128)(2,1)S(1)} collective-permute-done((bf16[4,96]{1,0:T(4,128)(2,1)S(1)}, bf16[4,96]{1,0:T(4,128)(2,1)S(1)}, u32[]{:S(2)}, u32[]{:S(2)}) %collective-permute-start.19) | collective-permute-done | bytes 800 | tf_op jit(solution)/shard_map/ppermute | solution.py:69
  38.9 0.8 %shard_map.149 = bf16[4,384]{1,0:T(4,128)(2,1)} custom-call(bf16[384,384]{1,0:T(8,128)(2,1)S(1)} %get-tuple-element.30.ready_ref.route_ref, bf16[4,96]{1,0:T(4,128)(2,1)S(1)} %collective-permute-done.18.rest_0_, bf16[4,96]{1,0:T(4,128)(2,1)S(1)} %collective-permute-done.19.rest_1_, bf16[4,96]{1,0:T(4,128)(2,1)S(1)} %collective-permute-done.20.rest_2_, ...), custom_call_target="tpu_custom_call" | custom-call | flops 1000000000 | tf_op jit(solution)/shard_map/pallas_call | solution.py:44
  (49 shorter events, 7.2 us)
Async XLA Ops:
  0.6 10.8 %collective-permute-start.6 = (bf16[384,2048]{1,0:T(8,128)(2,1)}, bf16[384,2048]{1,0:T(8,128)(2,1)S(1)}, u32[]{:S(2)}, u32[]{:S(2)}) collective-permute-start(bf16[384,2048]{1,0:T(8,128)(2,1)} %param.15), channel_id=1, source_target_pairs={{0,1},{1,0},{2,3},{3,2},{4,5},{5,4},{6,7},{7,6},{8,9},{9,8},{10,11... | collective-permute-start | bytes 4718600 | tf_op jit(solution)/shard_map/ppermute | solution.py:442
  2.1 6.9 %collective-permute-start = (bf16[11,16,128]{2,1,0:T(8,128)(2,1)S(1)}, bf16[11,16,128]{2,1,0:T(8,128)(2,1)S(1)}, u32[]{:S(2)}, u32[]{:S(2)}) collective-permute-start(bf16[11,16,128]{2,1,0:T(8,128)(2,1)S(1)} %get-tuple-element.28.after_ref), channel_id=1, source_target_pairs={{0,5},{1,4},{4,9},{5,8},{8,13},{9,12},{12,1},{13,0},{2,7},{3,6},{6... | collective-permute-start | bytes 135176 | tf_op jit(solution)/shard_map/ppermute | solution.py:69
  4.9 4.7 %collective-permute-start.2 = (bf16[11,16,128]{2,1,0:T(8,128)(2,1)S(1)}, bf16[11,16,128]{2,1,0:T(8,128)(2,1)S(1)}, u32[]{:S(2)}, u32[]{:S(2)}) collective-permute-start(bf16[11,16,128]{2,1,0:T(8,128)(2,1)S(1)} %get-tuple-element.29), channel_id=1, source_target_pairs={{0,13},{1,12},{4,1},{5,0},{8,5},{9,4},{12,9},{13,8},{2,15},{3,14},... | collective-permute-start | bytes 135176 | tf_op jit(solution)/shard_map/ppermute | solution.py:69
  7.0 1.8 %collective-permute-start.4 = (bf16[3,32,128]{2,1,0:T(8,128)(2,1)S(1)}, bf16[3,32,128]{2,1,0:T(8,128)(2,1)S(1)}, u32[]{:S(2)}, u32[]{:S(2)}) collective-permute-start(bf16[3,32,128]{2,1,0:T(8,128)(2,1)S(1)} %get-tuple-element.31), channel_id=1, source_target_pairs={{0,1},{1,0},{2,3},{3,2},{4,5},{5,4},{6,7},{7,6},{8,9},{9,8},{10,11... | collective-permute-start | bytes 73736 | tf_op jit(solution)/shard_map/ppermute | solution.py:458
  7.0 1.8 %collective-permute-start.7 = (f32[384]{0:T(512)S(1)}, f32[384]{0:T(512)S(1)}, u32[]{:S(2)}, u32[]{:S(2)}) collective-permute-start(f32[384]{0:T(512)S(1)} %copy-done.5), channel_id=1, source_target_pairs={{0,1},{1,0},{2,3},{3,2},{4,5},{5,4},{6,7},{7,6},{8,9},{9,8},{10,11... | collective-permute-start | bytes 4616 | tf_op jit(solution)/shard_map/ppermute | solution.py:442
  9.6 3.5 %collective-permute-start.5 = (bf16[3,48,128]{2,1,0:T(8,128)(2,1)S(1)}, bf16[3,48,128]{2,1,0:T(8,128)(2,1)S(1)}, u32[]{:S(2)}, u32[]{:S(2)}) collective-permute-start(bf16[3,48,128]{2,1,0:T(8,128)(2,1)S(1)} %shard_map.140.ready_ref), channel_id=1, source_target_pairs={{0,3},{1,2},{2,1},{3,0},{4,7},{5,6},{6,5},{7,4},{8,11},{9,10},{10,... | collective-permute-start | bytes 110600 | tf_op jit(solution)/shard_map/ppermute | solution.py:69
  10.9 2.3 %collective-permute-start.1 = (bf16[11,16,128]{2,1,0:T(8,128)(2,1)S(1)}, bf16[11,16,128]{2,1,0:T(8,128)(2,1)S(1)}, u32[]{:S(2)}, u32[]{:S(2)}) collective-permute-start(bf16[11,16,128]{2,1,0:T(8,128)(2,1)S(1)} %collective-permute-done.tile_before), channel_id=1, source_target_pairs={{0,1},{1,0},{2,3},{3,2},{4,5},{5,4},{6,7},{7,6},{8,9},{9,8},{10,11... | collective-permute-start | bytes 135176 | tf_op jit(solution)/shard_map/ppermute | solution.py:466
  11.3 1.9 %collective-permute-start.3 = (bf16[11,16,128]{2,1,0:T(8,128)(2,1)S(1)}, bf16[11,16,128]{2,1,0:T(8,128)(2,1)S(1)}, u32[]{:S(2)}, u32[]{:S(2)}) collective-permute-start(bf16[11,16,128]{2,1,0:T(8,128)(2,1)S(1)} %collective-permute-done.2.tile_after), channel_id=1, source_target_pairs={{0,1},{1,0},{2,3},{3,2},{4,5},{5,4},{6,7},{7,6},{8,9},{9,8},{10,11... | collective-permute-start | bytes 135176 | tf_op jit(solution)/shard_map/ppermute | solution.py:466
  13.4 1.3 %collective-permute-start.8 = (f32[3,24,128]{2,1,0:T(8,128)S(1)}, f32[3,24,128]{2,1,0:T(8,128)S(1)}, u32[]{:S(2)}, u32[]{:S(2)}) collective-permute-start(f32[3,24,128]{2,1,0:T(8,128)S(1)} %shard_map.142.ready_ref.ends_ref), channel_id=1, source_target_pairs={{0,1},{1,0},{2,3},{3,2},{4,5},{5,4},{6,7},{7,6},{8,9},{9,8},{10,11... | collective-permute-start | bytes 110600 | tf_op jit(solution)/shard_map/ppermute | solution.py:480
  15.8 3.9 %collective-permute-start.10 = (bf16[4,96]{1,0:T(4,128)(2,1)S(1)}, bf16[4,96]{1,0:T(4,128)(2,1)S(1)}, u32[]{:S(2)}, u32[]{:S(2)}) collective-permute-start(bf16[4,96]{1,0:T(4,128)(2,1)S(1)} %get-tuple-element.44), channel_id=1, source_target_pairs={{0,9},{1,8},{4,13},{5,12},{8,1},{9,0},{12,5},{13,4},{2,11},{3,10},... | collective-permute-start | bytes 2312 | tf_op jit(solution)/shard_map/ppermute | solution.py:69
  17.2 4.8 %collective-permute-start.11 = (bf16[4,96]{1,0:T(4,128)(2,1)S(1)}, bf16[4,96]{1,0:T(4,128)(2,1)S(1)}, u32[]{:S(2)}, u32[]{:S(2)}) collective-permute-start(bf16[4,96]{1,0:T(4,128)(2,1)S(1)} %get-tuple-element.45), channel_id=1, source_target_pairs={{0,13},{1,12},{4,9},{5,8},{8,5},{9,4},{12,1},{13,0},{2,15},{3,14},... | collective-permute-start | bytes 2312 | tf_op jit(solution)/shard_map/ppermute | solution.py:69
  18.9 3.1 %collective-permute-start.12 = (bf16[4,96]{1,0:T(4,128)(2,1)S(1)}, bf16[4,96]{1,0:T(4,128)(2,1)S(1)}, u32[]{:S(2)}, u32[]{:S(2)}) collective-permute-start(bf16[4,96]{1,0:T(4,128)(2,1)S(1)} %get-tuple-element.46), channel_id=1, source_target_pairs={{0,5},{1,4},{4,1},{5,0},{8,13},{9,12},{12,9},{13,8},{2,7},{3,6},{6... | collective-permute-start | bytes 2312 | tf_op jit(solution)/shard_map/ppermute | solution.py:69
  18.9 3.1 %collective-permute-start.9 = (bf16[4,96]{1,0:T(4,128)(2,1)S(1)}, bf16[4,96]{1,0:T(4,128)(2,1)S(1)}, u32[]{:S(2)}, u32[]{:S(2)}) collective-permute-start(bf16[4,96]{1,0:T(4,128)(2,1)S(1)} %get-tuple-element.43), channel_id=1, source_target_pairs={{0,1},{1,0},{2,3},{3,2},{4,5},{5,4},{6,7},{7,6},{8,9},{9,8},{10,11... | collective-permute-start | bytes 2312 | tf_op jit(solution)/shard_map/ppermute | solution.py:409
  22.4 1.3 %collective-permute-start.13 = (f32[4,2048]{1,0:T(4,128)S(1)}, f32[4,2048]{1,0:T(4,128)S(1)}, u32[]{:S(2)}, u32[]{:S(2)}) collective-permute-start(f32[4,2048]{1,0:T(4,128)S(1)} %shard_map.146), channel_id=1, source_target_pairs={{0,1},{1,0},{2,3},{3,2},{4,5},{5,4},{6,7},{7,6},{8,9},{9,8},{10,11... | collective-permute-start | bytes 98312 | tf_op jit(solution)/shard_map/ppermute | solution.py:68
  23.6 3.2 %collective-permute-start.14 = (bf16[4,2048]{1,0:T(4,128)(2,1)S(1)}, bf16[4,2048]{1,0:T(4,128)(2,1)S(1)}, u32[]{:S(2)}, u32[]{:S(2)}) collective-permute-start(bf16[4,2048]{1,0:T(4,128)(2,1)S(1)} %get-tuple-element.54.ready_ref), channel_id=1, source_target_pairs={{0,3},{1,2},{2,1},{3,0},{4,7},{5,6},{6,5},{7,4},{8,11},{9,10},{10,... | collective-permute-start | bytes 49160 | tf_op jit(solution)/shard_map/ppermute | solution.py:69
  26.9 6.2 %copy-start = (f32[2,2048]{1,0:T(2,128)S(1)}, f32[2,2048]{1,0:T(2,128)}, u32[]{:S(2)}) copy-start(f32[2,2048]{1,0:T(2,128)} %start_ref.1) | copy-start | bytes 49156
  26.9 6.2 %copy-start.1 = (f32[2048]{0:T(1024)S(1)}, f32[2048]{0:T(1024)}, u32[]{:S(2)}) copy-start(f32[2048]{0:T(1024)} %param.16) | copy-start | bytes 24580
  26.9 4.2 %collective-permute-start.15 = (bf16[4,2048]{1,0:T(4,128)(2,1)S(1)}, bf16[4,2048]{1,0:T(4,128)(2,1)S(1)}, u32[]{:S(2)}, u32[]{:S(2)}) collective-permute-start(bf16[4,2048]{1,0:T(4,128)(2,1)S(1)} %get-tuple-element.52), channel_id=1, source_target_pairs={{0,9},{1,8},{4,13},{5,12},{8,1},{9,0},{12,5},{13,4},{2,11},{3,10},... | collective-permute-start | bytes 49160 | tf_op jit(solution)/shard_map/ppermute | solution.py:69
  28.1 5.0 %collective-permute-start.16 = (bf16[4,2048]{1,0:T(4,128)(2,1)S(1)}, bf16[4,2048]{1,0:T(4,128)(2,1)S(1)}, u32[]{:S(2)}, u32[]{:S(2)}) collective-permute-start(bf16[4,2048]{1,0:T(4,128)(2,1)S(1)} %get-tuple-element.52), channel_id=1, source_target_pairs={{0,13},{1,12},{4,9},{5,8},{8,5},{9,4},{12,1},{13,0},{2,15},{3,14},... | collective-permute-start | bytes 49160 | tf_op jit(solution)/shard_map/ppermute | solution.py:69
  29.1 4.0 %collective-permute-start.17 = (bf16[4,2048]{1,0:T(4,128)(2,1)S(1)}, bf16[4,2048]{1,0:T(4,128)(2,1)S(1)}, u32[]{:S(2)}, u32[]{:S(2)}) collective-permute-start(bf16[4,2048]{1,0:T(4,128)(2,1)S(1)} %get-tuple-element.52), channel_id=1, source_target_pairs={{0,5},{1,4},{4,1},{5,0},{8,13},{9,12},{12,9},{13,8},{2,7},{3,6},{6... | collective-permute-start | bytes 49160 | tf_op jit(solution)/shard_map/ppermute | solution.py:69
  33.5 3.9 %collective-permute-start.18 = (bf16[4,96]{1,0:T(4,128)(2,1)S(1)}, bf16[4,96]{1,0:T(4,128)(2,1)S(1)}, u32[]{:S(2)}, u32[]{:S(2)}) collective-permute-start(bf16[4,96]{1,0:T(4,128)(2,1)S(1)} %get-tuple-element.47), channel_id=1, source_target_pairs={{0,9},{1,8},{4,13},{5,12},{8,1},{9,0},{12,5},{13,4},{2,11},{3,10},... | collective-permute-start | bytes 2312 | tf_op jit(solution)/shard_map/ppermute | solution.py:69
  34.1 4.8 %collective-permute-start.19 = (bf16[4,96]{1,0:T(4,128)(2,1)S(1)}, bf16[4,96]{1,0:T(4,128)(2,1)S(1)}, u32[]{:S(2)}, u32[]{:S(2)}) collective-permute-start(bf16[4,96]{1,0:T(4,128)(2,1)S(1)} %get-tuple-element.48), channel_id=1, source_target_pairs={{0,13},{1,12},{4,9},{5,8},{8,5},{9,4},{12,1},{13,0},{2,15},{3,14},... | collective-permute-start | bytes 2312 | tf_op jit(solution)/shard_map/ppermute | solution.py:69
  35.9 3.0 %collective-permute-start.20 = (bf16[4,96]{1,0:T(4,128)(2,1)S(1)}, bf16[4,96]{1,0:T(4,128)(2,1)S(1)}, u32[]{:S(2)}, u32[]{:S(2)}) collective-permute-start(bf16[4,96]{1,0:T(4,128)(2,1)S(1)} %get-tuple-element.49), channel_id=1, source_target_pairs={{0,5},{1,4},{4,1},{5,0},{8,13},{9,12},{12,9},{13,8},{2,7},{3,6},{6... | collective-permute-start | bytes 2312 | tf_op jit(solution)/shard_map/ppermute | solution.py:69
  36.6 2.4 %collective-permute-start.21 = (bf16[4,96]{1,0:T(4,128)(2,1)S(1)}, bf16[4,96]{1,0:T(4,128)(2,1)S(1)}, u32[]{:S(2)}, u32[]{:S(2)}) collective-permute-start(bf16[4,96]{1,0:T(4,128)(2,1)S(1)} %get-tuple-element.50), channel_id=1, source_target_pairs={{0,1},{1,0},{2,3},{3,2},{4,5},{5,4},{6,7},{7,6},{8,9},{9,8},{10,11... | collective-permute-start | bytes 2312 | tf_op jit(solution)/shard_map/ppermute | solution.py:409
  (4 other events, 23.2 us)
